TPU v7x, 128 devices: a whole 4x4x4 slice. The times are simulated.
128 devices in a mesh: sub: 16 (over y, x), lam: 8 (over z, core).
Axes of the slice: x: 4, y: 4, z: 4, core: 2. Of those that a mesh axis runs over, the one named last changes fastest.
Arguments:
- edge_field: bfloat16 [8, 65536, 128], P('lam', 'sub'), may hold values from -6 to 6
- coupling: float32 [8, 65536], P('lam', 'sub'), may hold values from 0.3 to 3
- owner_map: int32 [8, 65536, 1], P('lam', 'sub'), may hold values from 0 to 127; in each aligned block of 4096 rows (0 to 4095, 4096 to 8191, ..., all dimensions but the last counted through in order) at most 48 rows name the same one
- in_plane: bfloat16 [128, 128], replicated, may hold values from -0.5 to 0.5
- profile_op: bfloat16 [128, 128, 128], P(('sub', 'lam')), may hold values from -0.5 to 0.5
Outputs:
- field_next: float32 [8, 65536, 128], P('lam', 'sub')
Inputs may be any that keep to these rules, and one draw needn't show every extreme that they name: `owner_map`: within the 4096 elements of one device no owner is named more than 48 times, a bound that some block reaches.
All inputs are finite; a program needn't handle non-finite values.
Results may differ from a plain program's by a relative error of at most 0.0018.
Values may be sent and summed in bfloat16 or wider, within the bound.
No kernel may reach another device: no remote copies, remote signals or barrier semaphores. Data moves between devices by JAX's collectives and lax.ppermute only.
A program may use at most 64 MiB of HBM per device.

v0:
```python
import jax
import jax.numpy as jnp
from jax import lax
from jax.sharding import PartitionSpec as P

step_size = 0.25


def extended(cells, sides, width):
    for axis, dim in sides:
        count = lax.axis_size(axis)
        ends = count - 1
        head = lax.slice_in_dim(cells, 0, width, axis=dim)
        tail = lax.slice_in_dim(cells, cells.shape[dim] - width, cells.shape[dim], axis=dim)
        cells = jnp.concatenate(
            [
                lax.ppermute(tail, axis, [(i, (i + 1) % count) for i in range(ends)]),
                cells,
                lax.ppermute(head, axis, [((i + 1) % count, i) for i in range(ends)]),
            ],
            axis=dim,
        )
    return cells


def profile_response(response_raw, half_width):
    real_part = response_raw[:, :half_width]
    imag_part = response_raw[:, half_width:]
    magnitude = real_part * real_part + imag_part * imag_part
    reluct = 1.0 + 4.0 * magnitude / (1.0 + magnitude)
    return (response_raw * jnp.concatenate([reluct, reluct], axis=1)).astype(jnp.bfloat16)


def per_device(edge_field, coupling, owner_map, in_plane, profile_op):
    element_rows = edge_field[0]
    elem_count = element_rows.shape[0]
    columns = element_rows.shape[1]
    half_width = columns // 2
    owner_ids = owner_map[0, :, 0]
    sub_count = lax.axis_size("sub")
    lam_count = lax.axis_size("lam")
    device_count = sub_count * lam_count
    capacity = max(2, 3 * elem_count // (2 * device_count))
    owner_table = (owner_ids[:, None] == jnp.arange(device_count, dtype=jnp.int32)[None, :]).astype(
        jnp.int32
    )
    earlier = jnp.cumsum(owner_table, axis=0) - owner_table
    position = jnp.sum(earlier * owner_table, axis=1)
    slot_index = owner_ids * capacity + position
    source_rows = (
        jnp.full((device_count * capacity,), elem_count, jnp.int32)
        .at[slot_index]
        .set(jnp.arange(elem_count, dtype=jnp.int32))
    )
    padded_source = jnp.concatenate(
        [element_rows, jnp.zeros((1, columns), element_rows.dtype)], axis=0
    )
    outgoing = padded_source[source_rows].reshape(device_count, capacity, columns)
    arrived = lax.all_to_all(outgoing, ("sub", "lam"), split_axis=0, concat_axis=0, tiled=True)
    response_raw = jnp.dot(
        arrived.reshape(-1, columns), profile_op[0], preferred_element_type=jnp.float32
    )
    effect_slots = profile_response(response_raw, half_width)
    returned = lax.all_to_all(
        effect_slots.reshape(device_count, capacity, columns),
        ("sub", "lam"),
        split_axis=0,
        concat_axis=0,
        tiled=True,
    )
    effective = returned.reshape(-1, columns)[slot_index].astype(jnp.float32)
    padded_rows = extended(element_rows, (("sub", 0),), 1)
    projected = jnp.dot(padded_rows, in_plane, preferred_element_type=jnp.float32)
    stiffness = coupling[0][:, None] * (2.0 * projected[1:-1] - projected[:-2] - projected[2:])
    field_next = element_rows.astype(jnp.float32) - step_size * (stiffness + effective)
    return field_next[None]


def solution(mesh):
    placed = (
        P("lam", "sub", None),
        P("lam", "sub"),
        P("lam", "sub", None),
        P(),
        P(("sub", "lam"), None, None),
    )
    return jax.shard_map(
        per_device, mesh=mesh, in_specs=placed, out_specs=P("lam", "sub", None), check_vma=False
    )
```

profile of v0, /device:TPU:1, one launch (start us, length us, event | category | flops | bytes accessed | tf_op | source)
XLA Modules:
  0.0 134.9 jit_solution(15928244309579006194)
XLA Ops:
  0.0 0.8 copy.8
  0.8 0.6 fusion.8
  1.5 0.1 reduce-window.9
  1.5 0.2 broadcast_add_fusion
  1.8 1.2 copy.9
  3.0 0.0 copy-start.1
  3.0 1.4 %fusion.7 = s32[4096]{0:T(1024)S(1)} fusion(s32[128,32,128]{0,2,1:T(8,128)S(1)} %copy.9, s32[4096]{0:T(1024)S(1)} %bitcast.44), kind=kLoop, calls=%fused_computation.15 | loop fusion | flops 2617344 | bytes 2129920 | tf_op jit(solution)/shard_map/reduce_sum | solution.py:48
  4.5 15.5 %scatter_custom_fusion = s32[6144]{0:T(1024)S(1)} fusion(s32[4096]{0:T(1024)S(1)} %bitcast.46, s32[4096]{0:T(1024)S(1)} %iota.11, s32[]{:T(128)} %constant.12.clone.1), kind=kCustom, calls=%fused_computation.33 | custom fusion | bytes 24580 | tf_op jit(solution)/shard_map/scatter | solution.py:53
  20.1 0.1 concatenate.10
  20.2 22.3 %gather_fusion = bf16[6144,128]{1,0:T(8,128)(2,1)} fusion(bf16[4097,128]{1,0:T(8,128)(2,1)S(1)} %concatenate.10, s32[6144]{0:T(1024)S(1)} %fusion.14), kind=kCustom, calls=%fused_computation | custom fusion | bytes 3170304 | tf_op jit(solution)/shard_map/gather | solution.py:58
  42.4 36.2 %all_to_all.10 = bf16[128,48,128]{2,1,0:T(8,128)(2,1)S(1)} all-to-all(bf16[128,48,128]{2,1,0:T(8,128)(2,1)} %bitcast.42), channel_id=1, replica_groups=mesh['sub'=16,'lam'=8] {'sub','lam'}, dimensions={0} | all-to-all | bytes 3145728 | tf_op jit(solution)/shard_map/all_to_all | solution.py:59
  78.6 0.6 fusion.12
  79.2 0.4 divide_add_fusion
  79.6 0.2 fusion
  79.9 1.6 %copy.10 = bf16[6144,128]{1,0:T(8,128)(2,1)} copy(bf16[6144,128]{0,1:T(8,128)(2,1)S(1)} %fusion) | data formatting | bytes 3145728 | tf_op jit(solution)/shard_map/convert_element_type | solution.py:31
  81.5 4.8 %all-to-all-start.1 = ((bf16[128,48,128]{2,1,0:T(8,128)(2,1)}), bf16[128,48,128]{2,1,0:T(8,128)(2,1)S(1)}, u32[]{:S(2)}, u32[]{:S(2)}) async-start(bf16[128,48,128]{2,1,0:T(8,128)(2,1)} %bitcast.40), calls=%async_computation.1 | async-start | bytes 3145728 | tf_op jit(solution)/shard_map/all_to_all | solution.py:64
  86.3 3.3 %collective-permute-start = (bf16[1,128]{1,0:T(2,128)(2,1)S(1)}, bf16[1,128]{1,0:T(2,128)(2,1)S(1)}, u32[]{:S(2)}, u32[]{:S(2)}) collective-permute-start(bf16[1,128]{1,0:T(2,128)(2,1)S(1)} %get-tuple-element.6), channel_id=1, source_target_pairs={{0,8},{8,16},{16,24},{24,32},{32,40},{40,48},{48,56},{56,64},{64,7... | collective-permute-start | bytes 776 | tf_op jit(solution)/shard_map/ppermute | solution.py:17
  89.6 1.3 collective-permute-start.1
  90.9 10.8 %collective-permute-done = bf16[1,128]{1,0:T(2,128)(2,1)S(1)} collective-permute-done((bf16[1,128]{1,0:T(2,128)(2,1)S(1)}, bf16[1,128]{1,0:T(2,128)(2,1)S(1)}, u32[]{:S(2)}, u32[]{:S(2)}) %collective-permute-start) | collective-permute-done | bytes 288 | tf_op jit(solution)/shard_map/ppermute | solution.py:17
  101.7 2.9 %collective-permute-done.1 = bf16[1,128]{1,0:T(2,128)(2,1)S(1)} collective-permute-done((bf16[1,128]{1,0:T(2,128)(2,1)S(1)}, bf16[1,128]{1,0:T(2,128)(2,1)S(1)}, u32[]{:S(2)}, u32[]{:S(2)}) %collective-permute-start.1) | collective-permute-done | bytes 288 | tf_op jit(solution)/shard_map/ppermute | solution.py:19
  104.6 6.8 %concatenate.9 = bf16[4098,128]{1,0:T(8,128)(2,1)} concatenate(bf16[1,128]{1,0:T(2,128)(2,1)S(1)} %collective-permute-done, bf16[4096,128]{1,0:T(8,128)(2,1)S(1)} %bitcast.39, bf16[1,128]{1,0:T(2,128)(2,1)S(1)} %collective-permute-done.1), dimensions={0} | concatenate | bytes 2098176 | tf_op jit(solution)/shard_map/concatenate | solution.py:15
  111.5 3.3 %fusion.17 = f32[4098,128]{1,0:T(8,128)} fusion(bf16[4098,128]{1,0:T(8,128)(2,1)} %concatenate.9, bf16[128,128]{1,0:T(8,128)(2,1)S(1)} %copy-done.3), kind=kOutput, calls=%fused_computation.38 | convolution fusion | flops 134283264 | bytes 3180032 | tf_op jit(solution)/shard_map/dot_general | solution.py:73
  114.7 15.0 %gather_fusion.1 = bf16[4096,128]{1,0:T(8,128)(2,1)} fusion(bf16[6144,128]{1,0:T(8,128)(2,1)S(1)} %bitcast.37, s32[4096]{0:T(1024)S(1)} %broadcast_clamp_fusion), kind=kCustom, calls=%fused_computation.1 | custom fusion | bytes 2113536 | tf_op jit(solution)/shard_map/gather | solution.py:71
  129.7 5.1 %fusion.5 = f32[1,4096,128]{2,1,0:T(8,128)} fusion(f32[4098,128]{1,0:T(8,128)} %fusion.17, bf16[4096,128]{1,0:T(8,128)(2,1)} %gather_fusion.1, f32[4096]{0:T(1024)S(1)} %bitcast.48, bf16[1,4096,128]{2,1,0:T(8,128)(2,1)S(1)} %copy-done.1), kind=kLoop, calls=%fused_computation.10 | loop fusion | flops 4718592 | bytes 10502144 | tf_op jit(solution)/shard_map/broadcast_in_dim | solution.py:76
  (17 shorter events, 0.1 us)
Async XLA Ops:
  0.0 78.6 %copy-start = (bf16[1,128,128]{2,1,0:T(8,128)(2,1)S(1)}, bf16[1,128,128]{2,1,0:T(8,128)(2,1)}, u32[]{:S(2)}) copy-start(bf16[1,128,128]{2,1,0:T(8,128)(2,1)} %param.9) | copy-start | bytes 98308
  1.7 1.3 copy-start.2
  3.0 17.1 %copy-start.1 = (bf16[1,4096,128]{2,1,0:T(8,128)(2,1)S(1)}, bf16[1,4096,128]{2,1,0:T(8,128)(2,1)}, u32[]{:S(2)}) copy-start(bf16[1,4096,128]{2,1,0:T(8,128)(2,1)} %param.5) | copy-start | bytes 3145732
  81.5 30.0 %copy-start.3 = (bf16[128,128]{1,0:T(8,128)(2,1)S(1)}, bf16[128,128]{1,0:T(8,128)(2,1)}, u32[]{:S(2)}) copy-start(bf16[128,128]{1,0:T(8,128)(2,1)} %param.8) | copy-start | bytes 98308
  81.5 33.3 %all-to-all-start.1 = ((bf16[128,48,128]{2,1,0:T(8,128)(2,1)}), bf16[128,48,128]{2,1,0:T(8,128)(2,1)S(1)}, u32[]{:S(2)}, u32[]{:S(2)}) async-start(bf16[128,48,128]{2,1,0:T(8,128)(2,1)} %bitcast.40), calls=%async_computation.1 | async-start | bytes 3145728 | tf_op jit(solution)/shard_map/all_to_all | solution.py:64
  86.3 15.4 %collective-permute-start = (bf16[1,128]{1,0:T(2,128)(2,1)S(1)}, bf16[1,128]{1,0:T(2,128)(2,1)S(1)}, u32[]{:S(2)}, u32[]{:S(2)}) collective-permute-start(bf16[1,128]{1,0:T(2,128)(2,1)S(1)} %get-tuple-element.6), channel_id=1, source_target_pairs={{0,8},{8,16},{16,24},{24,32},{32,40},{40,48},{48,56},{56,64},{64,7... | collective-permute-start | bytes 776 | tf_op jit(solution)/shard_map/ppermute | solution.py:17
  89.6 15.0 %collective-permute-start.1 = (bf16[1,128]{1,0:T(2,128)(2,1)S(1)}, bf16[1,128]{1,0:T(2,128)(2,1)S(1)}, u32[]{:S(2)}, u32[]{:S(2)}) collective-permute-start(bf16[1,128]{1,0:T(2,128)(2,1)S(1)} %get-tuple-element.5), channel_id=1, source_target_pairs={{8,0},{16,8},{24,16},{32,24},{40,32},{48,40},{56,48},{64,56},{72,6... | collective-permute-start | bytes 776 | tf_op jit(solution)/shard_map/ppermute | solution.py:19
  114.7 15.0 %copy-start.4 = (f32[1,4096]{1,0:T(1,128)S(1)}, f32[1,4096]{1,0:T(1,128)}, u32[]{:S(2)}) copy-start(f32[1,4096]{1,0:T(1,128)} %param.6) | copy-start | bytes 49156
where the time goes:
time: 136 us; the launch traced here: 135 us
  local copies, waits for them, and re-layouts  63.4 us (47%)
  blocking collectives  36.2 us (27%)
  waiting for transfers between devices  13.7 us (10%)
  starting transfers between devices  9.4 us (7%)
  other arithmetic  8.15 us (6%)
  matrix products  3.88 us (3%)
    all_to_all x1, blocking collectives, per_device(): lax.all_to_all(outgoing, ('sub', 'lam'), split_axis=0, concat_axis=0, til...  36.2 us
    gather x1, local copies, waits for them, and re-layouts, per_device(): padded_source[source_rows].reshape(device_count, capacity, columns)  22.3 us
    scatter x1, local copies, waits for them, and re-layouts, per_device(): source_rows = jnp.full((device_count * capacity,), elem_count, jnp.int32)...  15.5 us
    gather x1, local copies, waits for them, and re-layouts, per_device(): effective = returned.reshape(-1, columns)[slot_index].astype(jnp.float32)  15 us
    ppermute x1, waiting for transfers between devices, extended(): lax.ppermute(tail, axis, [(i, (i + 1) % count) for i in range(ends)])  10.8 us
    concatenate x1, local copies, waits for them, and re-layouts, extended(): jnp.concatenate([lax.ppermute(tail, axis, [(i, (i + 1) % count) for i in...  6.84 us
    broadcast_in_dim x1, other arithmetic, per_device(): return field_next[None]  5.12 us
    all_to_all x1, starting transfers between devices, per_device(): lax.all_to_all(effect_slots.reshape(device_count, capacity, columns), ('s...  4.81 us
  transfers between devices with their start and end apart: 3, of which 2 were waited for; matrix products, arithmetic and copies ran while one was open for 7% of the time, Pallas kernels for 0%

commit v1 on v0

v1 whole, which is shorter than its diff:
```python
import functools

import jax
import jax.numpy as jnp
import numpy as np
from jax import lax
from jax.experimental import pallas as pl
from jax.experimental.pallas import tpu as pltpu
from jax.sharding import PartitionSpec as P

step_size = 0.25
axes_all = ("sub", "lam")
owners = 128
cap = 48
rows = 4096
vals = 128
slots = owners * cap
chunk = 256
offsets = np.array([0, -1, 1, 2])
vmem_bytes = 40 * 1024 * 1024


def params():
    return pltpu.CompilerParams(vmem_limit_bytes=vmem_bytes)


def device(y, x, z, c):
    return ((y % 4) * 4 + (x % 4)) * 8 + (z % 4) * 2 + (c % 2)


def shifted(value, step, axes):
    pairs = []
    for y in range(4):
        for x in range(4):
            for z in range(4):
                for c in range(2):
                    place = dict(y=y, x=x, z=z, c=c)
                    place[axes[c]] += step
                    pairs.append((device(y, x, z, c), device(**place)))
    return lax.ppermute(value, axes_all, pairs)


def core_swap(value):
    pairs = [(d, d ^ 1) for d in range(owners)]
    return lax.ppermute(value, axes_all, pairs)


def around(value, axes):
    return [value] + [shifted(value, step, axes) for step in (1, -1, 2)]


def gather_operators(block):
    near = jnp.concatenate(around(block, "zz"), axis=0)
    plane = jnp.concatenate(around(near, "xy"), axis=0)
    parts = around(plane, "yx")
    return [(part, core_swap(part)) for part in parts]


def slot_owners():
    sub, lam = lax.axis_index("sub"), lax.axis_index("lam")
    y, x, z, c = sub // 4, sub % 4, lam // 2, lam % 2
    index = np.arange(owners)
    third, group = index // 32, (index // 16) % 2
    second, first = (index // 4) % 4, index % 4
    core = jnp.asarray(group, jnp.int32) ^ c
    by_second = jnp.asarray(offsets[second], jnp.int32)
    by_third = jnp.asarray(offsets[third], jnp.int32)
    even = core == 0
    dx = jnp.where(even, by_second, by_third)
    dy = jnp.where(even, by_third, by_second)
    dz = jnp.asarray(offsets[first], jnp.int32)
    return (((y + dy + 4) % 4) * 4 + (x + dx + 4) % 4) * 8 + ((z + dz + 4) % 4) * 2 + core


def rank_kernel(owner_ref, table_ref, slot_ref):
    table = table_ref[...]
    row = lax.broadcasted_iota(jnp.int32, (chunk, chunk + owners), 0)
    col = lax.broadcasted_iota(jnp.int32, (chunk, chunk + owners), 1)
    earlier = jnp.where((row < col) | (col >= chunk), 1.0, 0.0).astype(jnp.bfloat16)
    start = cap * lax.broadcasted_iota(jnp.int32, (owners, owners), 0).astype(jnp.float32)
    for j in range(rows // chunk):
        hit = table == owner_ref[j : j + 1, :]
        count = jnp.dot(
            jnp.where(hit, 1.0, 0.0).astype(jnp.bfloat16), earlier, preferred_element_type=jnp.float32
        )
        place = count[:, :chunk] + jnp.concatenate([start, start], axis=1)
        slot = jnp.sum(jnp.where(hit, place, 0.0), axis=0, keepdims=True)
        slot_ref[j : j + 1, :] = slot.astype(jnp.int32)
        start = start + count[:, chunk:]


def rank(owner, table):
    return pl.pallas_call(
        rank_kernel,
        out_shape=jax.ShapeDtypeStruct((rows // chunk, chunk), jnp.int32),
        compiler_params=params(),
        cost_estimate=pl.CostEstimate(flops=2 * 128 * 4096 * 384, bytes_accessed=100000, transcendentals=0),
    )(owner, table)


def sort_kernel(slot_ref, field_ref, sorted_ref, wide, placed):
    wide[...] = field_ref[...].astype(jnp.float32)

    def body(i, carry):
        first = pl.multiple_of(i * 32, 32)
        for j in range(32):
            placed[pl.ds(slot_ref[first + j], 1), :] = wide[pl.ds(first + j, 1), :]
        return carry

    lax.fori_loop(0, rows // 32, body, 0)
    sorted_ref[...] = placed[...].astype(jnp.bfloat16)


def sort_rows(slot, field):
    return pl.pallas_call(
        sort_kernel,
        in_specs=[pl.BlockSpec(memory_space=pltpu.SMEM), pl.BlockSpec(memory_space=pltpu.VMEM)],
        out_shape=jax.ShapeDtypeStruct((slots, vals), jnp.bfloat16),
        scratch_shapes=[pltpu.VMEM((rows, vals), jnp.float32), pltpu.VMEM((slots, vals), jnp.float32)],
        compiler_params=params(),
        cost_estimate=pl.CostEstimate(flops=0, bytes_accessed=20000000, transcendentals=0),
    )(slot, field)


def stencil_kernel(field_ref, halo_ref, coupling_ref, plane_ref, base_ref, projected):
    plane = plane_ref[...]
    ends = jnp.dot(halo_ref[...], plane, preferred_element_type=jnp.float32)
    projected[0:8, :] = ends[0:8]
    projected[rows + 8 : rows + 16, :] = ends[8:16]
    for j in range(rows // 512):
        projected[8 + j * 512 : 8 + (j + 1) * 512, :] = jnp.dot(
            field_ref[j * 512 : (j + 1) * 512, :], plane, preferred_element_type=jnp.float32
        )
    for j in range(rows // vals):
        lo = j * vals
        weight = jnp.broadcast_to(coupling_ref[j : j + 1, :], (vals, vals)).T
        here = projected[lo + 8 : lo + 8 + vals, :]
        before = projected[lo + 7 : lo + 7 + vals, :]
        after = projected[lo + 9 : lo + 9 + vals, :]
        field = field_ref[lo : lo + vals, :].astype(jnp.float32)
        base_ref[lo : lo + vals, :] = field - step_size * (weight * (2.0 * here - before - after))


def stencil(field, halo, coupling, plane):
    return pl.pallas_call(
        stencil_kernel,
        out_shape=jax.ShapeDtypeStruct((rows, vals), jnp.float32),
        scratch_shapes=[pltpu.VMEM((rows + 16, vals), jnp.float32)],
        compiler_params=params(),
        cost_estimate=pl.CostEstimate(flops=2 * 4096 * 128 * 128, bytes_accessed=10000000, transcendentals=0),
    )(field, halo, coupling, plane)


def respond(block, operator):
    response = jnp.dot(block, operator, preferred_element_type=jnp.float32)
    square = response * response
    magnitude = square + pltpu.roll(square, vals // 2, 1)
    reluct = 5.0 - 4.0 / (1.0 + magnitude)
    return reluct * response


def effect_kernel(*refs):
    sorted_ref, near_ref, far_ref = refs[:3]
    effect_ref = refs[-1]
    for g, operator_ref in enumerate((near_ref, far_ref)):
        for k in range(16):
            lo = (g * 16 + k) * cap
            effect_ref[lo : lo + cap, :] = respond(
                sorted_ref[lo : lo + cap, :], operator_ref[k * vals : (k + 1) * vals, :]
            )


def effects(sorted_rows, near, far, number, previous):
    block = 32 * cap
    whole = pl.BlockSpec((16 * vals, vals), lambda i: (0, 0))
    specs = [pl.BlockSpec((block, vals), lambda i: (number, 0)), whole, whole]
    operands = [sorted_rows, near, far]
    if previous is not None:
        specs.append(pl.BlockSpec(memory_space=pl.ANY))
        operands.append(previous)
    return pl.pallas_call(
        effect_kernel,
        grid=(1,),
        in_specs=specs,
        out_specs=pl.BlockSpec((block, vals), lambda i: (number, 0)),
        out_shape=jax.ShapeDtypeStruct((slots, vals), jnp.float32),
        input_output_aliases={} if previous is None else {3: 0},
        compiler_params=params(),
        cost_estimate=pl.CostEstimate(
            flops=2 * block * 128 * 128, bytes_accessed=4000000, transcendentals=0
        ),
    )(*operands)


def combine_kernel(slot_ref, effect_ref, base_ref, out_ref):
    top = pl.program_id(0) * 512

    def body(i, carry):
        first = pl.multiple_of(i * 32, 32)
        for j in range(32):
            effect = effect_ref[pl.ds(slot_ref[top + first + j], 1), :]
            out_ref[pl.ds(first + j, 1), :] = base_ref[pl.ds(first + j, 1), :] - step_size * effect
        return carry

    lax.fori_loop(0, 512 // 32, body, 0)


def combine(slot, effect, base):
    part = pl.BlockSpec((512, vals), lambda i: (i, 0))
    return pl.pallas_call(
        combine_kernel,
        grid=(rows // 512,),
        in_specs=[
            pl.BlockSpec(memory_space=pltpu.SMEM),
            pl.BlockSpec((slots, vals), lambda i: (0, 0)),
            part,
        ],
        out_specs=part,
        out_shape=jax.ShapeDtypeStruct((rows, vals), jnp.float32),
        compiler_params=params(),
        cost_estimate=pl.CostEstimate(flops=4096 * 128, bytes_accessed=10000000, transcendentals=0),
    )(slot, effect, base)


def halo_rows(field):
    ends = lax.axis_size("sub") - 1
    before = lax.ppermute(field[rows - 16 :], "sub", [(i, i + 1) for i in range(ends)])
    after = lax.ppermute(field[:16], "sub", [(i + 1, i) for i in range(ends)])
    return jnp.concatenate([before[8:], after[:8]], axis=0)


def per_device(edge_field, coupling, owner_map, in_plane, profile_op):
    field = edge_field[0]
    parts = gather_operators(profile_op[0])
    table = slot_owners()[:, None]
    slot = rank(owner_map.reshape(rows // chunk, chunk), table).reshape(rows)
    sorted_rows = sort_rows(slot, field)
    base = stencil(field, halo_rows(field), coupling.reshape(rows // vals, vals), in_plane)
    effect = None
    for number, (near, far) in enumerate(parts):
        effect = effects(sorted_rows, near, far, number, effect)
    return combine(slot, effect, base)[None]


def solution(mesh):
    placed = (
        P("lam", "sub", None),
        P("lam", "sub"),
        P("lam", "sub", None),
        P(),
        P(("sub", "lam"), None, None),
    )
    return jax.shard_map(
        per_device, mesh=mesh, in_specs=placed, out_specs=P("lam", "sub", None), check_vma=False
    )
```

time: 136 us -> 68.9 us (0.51)
  the two profiles are of different devices: /device:TPU:1 before, /device:TPU:9 now
where the time goes in v1:
time: 68.9 us; the launch traced here: 68.3 us
  starting transfers between devices  33.6 us (49%)
  Pallas kernels  18.9 us (27%)
  waiting for transfers between devices  10.5 us (15%)
  other arithmetic  2.9 us (4%)
  local copies, waits for them, and re-layouts  2.24 us (3%)
    ppermute x4, starting transfers between devices, core_swap(): return lax.ppermute(value, axes_all, pairs)  15.2 us
    ppermute x9, starting transfers between devices, shifted(): return lax.ppermute(value, axes_all, pairs)  12.7 us
    ppermute x9, waiting for transfers between devices, shifted(): return lax.ppermute(value, axes_all, pairs)  8.74 us
    pallas_call x1, Pallas kernels, combine(): pl.pallas_call(combine_kernel, grid=(rows // 512,), in_specs=[pl.BlockSpe...  6.41 us
    pallas_call x4, Pallas kernels, effects(): pl.pallas_call(effect_kernel, grid=(1,), in_specs=specs, out_specs=pl.Blo...  6.16 us
    pallas_call x1, Pallas kernels, sort_rows(): pl.pallas_call(sort_kernel, in_specs=[pl.BlockSpec(memory_space=pltpu.SME...  4.86 us
    ppermute x1, starting transfers between devices, halo_rows(): after = lax.ppermute(field[:16], 'sub', [(i + 1, i) for i in range(ends)])  3.76 us
    ppermute x1, starting transfers between devices, halo_rows(): lax.ppermute(field[rows - 16:], 'sub', [(i, i + 1) for i in range(ends)])  1.91 us
  transfers between devices with their start and end apart: 15, of which 8 were waited for; matrix products, arithmetic and copies ran while one was open for 6% of the time, Pallas kernels for 16%

profile of v1, /device:TPU:9, one launch (start us, length us, event | category | flops | bytes accessed | tf_op | source)
XLA Modules:
  0.0 68.3 jit_solution(12551053834441779991)
XLA Ops:
  0.0 1.7 %collective-permute-start = (bf16[128,128]{1,0:T(8,128)(2,1)}, bf16[128,128]{1,0:T(8,128)(2,1)S(1)}, u32[]{:S(2)}, u32[]{:S(2)}) collective-permute-start(bf16[128,128]{1,0:T(8,128)(2,1)} %bitcast.20), channel_id=1, source_target_pairs={{0,2},{1,3},{2,4},{3,5},{4,6},{5,7},{6,0},{7,1},{8,10},{9,11},{10,... | collective-permute-start | bytes 98312 | tf_op jit(solution)/shard_map/ppermute | solution.py:40
  1.7 2.2 %collective-permute-start.1 = (bf16[128,128]{1,0:T(8,128)(2,1)}, bf16[128,128]{1,0:T(8,128)(2,1)S(1)}, u32[]{:S(2)}, u32[]{:S(2)}) collective-permute-start(bf16[128,128]{1,0:T(8,128)(2,1)} %bitcast.21), channel_id=1, source_target_pairs={{0,6},{1,7},{2,0},{3,1},{4,2},{5,3},{6,4},{7,5},{8,14},{9,15},{10,... | collective-permute-start | bytes 98312 | tf_op jit(solution)/shard_map/ppermute | solution.py:40
  3.9 1.2 %collective-permute-start.2 = (bf16[128,128]{1,0:T(8,128)(2,1)}, bf16[128,128]{1,0:T(8,128)(2,1)S(1)}, u32[]{:S(2)}, u32[]{:S(2)}) collective-permute-start(bf16[128,128]{1,0:T(8,128)(2,1)} %bitcast.22), channel_id=1, source_target_pairs={{0,4},{1,5},{2,6},{3,7},{4,0},{5,1},{6,2},{7,3},{8,12},{9,13},{10,... | collective-permute-start | bytes 98312 | tf_op jit(solution)/shard_map/ppermute | solution.py:40
  5.9 2.5 %collective-permute-done.2 = bf16[128,128]{1,0:T(8,128)(2,1)S(1)} collective-permute-done((bf16[128,128]{1,0:T(8,128)(2,1)}, bf16[128,128]{1,0:T(8,128)(2,1)S(1)}, u32[]{:S(2)}, u32[]{:S(2)}) %collective-permute-start.2) | collective-permute-done | bytes 32800 | tf_op jit(solution)/shard_map/ppermute | solution.py:40
  9.2 1.4 %collective-permute-start.3 = (bf16[512,128]{1,0:T(8,128)(2,1)S(1)}, bf16[512,128]{1,0:T(8,128)(2,1)S(1)}, u32[]{:S(2)}, u32[]{:S(2)}) collective-permute-start(bf16[512,128]{1,0:T(8,128)(2,1)S(1)} %pad_maximum_fusion), channel_id=1, source_target_pairs={{0,8},{1,33},{2,10},{3,35},{4,12},{5,37},{6,14},{7,39},{8,16},{9,4... | collective-permute-start | bytes 393224 | tf_op jit(solution)/shard_map/ppermute | solution.py:40
  10.7 2.0 %collective-permute-start.5 = (bf16[512,128]{1,0:T(8,128)(2,1)S(1)}, bf16[512,128]{1,0:T(8,128)(2,1)S(1)}, u32[]{:S(2)}, u32[]{:S(2)}) collective-permute-start(bf16[512,128]{1,0:T(8,128)(2,1)S(1)} %pad_maximum_fusion), channel_id=1, source_target_pairs={{0,16},{1,65},{2,18},{3,67},{4,20},{5,69},{6,22},{7,71},{8,24},{9,... | collective-permute-start | bytes 393224 | tf_op jit(solution)/shard_map/ppermute | solution.py:40
  13.1 1.3 %collective-permute-done.4 = bf16[512,128]{1,0:T(8,128)(2,1)S(1)} collective-permute-done((bf16[512,128]{1,0:T(8,128)(2,1)S(1)}, bf16[512,128]{1,0:T(8,128)(2,1)S(1)}, u32[]{:S(2)}, u32[]{:S(2)}) %collective-permute-start.4) | collective-permute-done | bytes 131104 | tf_op jit(solution)/shard_map/ppermute | solution.py:40
  14.4 2.4 %collective-permute-done.5 = bf16[512,128]{1,0:T(8,128)(2,1)S(1)} collective-permute-done((bf16[512,128]{1,0:T(8,128)(2,1)S(1)}, bf16[512,128]{1,0:T(8,128)(2,1)S(1)}, u32[]{:S(2)}, u32[]{:S(2)}) %collective-permute-start.5) | collective-permute-done | bytes 131104 | tf_op jit(solution)/shard_map/ppermute | solution.py:40
  16.8 1.0 %collective-permute-start.10 = (bf16[2048,128]{1,0:T(8,128)(2,1)S(1)}, bf16[2048,128]{1,0:T(8,128)(2,1)S(1)}, u32[]{:S(2)}, u32[]{:S(2)}) collective-permute-start(bf16[2048,128]{1,0:T(8,128)(2,1)S(1)} %constant_dynamic-update-slice_fusion.refs_1_), channel_id=1, source_target_pairs={{0,32},{1,9},{2,34},{3,11},{4,36},{5,13},{6,38},{7,15},{8,40},{9,1... | collective-permute-start | bytes 1572872 | tf_op jit(solution)/shard_map/ppermute | solution.py:40
  17.8 1.8 %collective-permute-start.8 = (bf16[2048,128]{1,0:T(8,128)(2,1)S(1)}, bf16[2048,128]{1,0:T(8,128)(2,1)S(1)}, u32[]{:S(2)}, u32[]{:S(2)}) collective-permute-start(bf16[2048,128]{1,0:T(8,128)(2,1)S(1)} %constant_dynamic-update-slice_fusion.refs_1_), channel_id=1, source_target_pairs={{0,96},{1,25},{2,98},{3,27},{4,100},{5,29},{6,102},{7,31},{8,104},... | collective-permute-start | bytes 1572872 | tf_op jit(solution)/shard_map/ppermute | solution.py:40
  19.5 1.2 %collective-permute-start.6 = (bf16[2048,128]{1,0:T(8,128)(2,1)S(1)}, bf16[2048,128]{1,0:T(8,128)(2,1)S(1)}, u32[]{:S(2)}, u32[]{:S(2)}) collective-permute-start(bf16[2048,128]{1,0:T(8,128)(2,1)S(1)} %constant_dynamic-update-slice_fusion.refs_1_), channel_id=1, source_target_pairs={{0,64},{1,17},{2,66},{3,19},{4,68},{5,21},{6,70},{7,23},{8,72},{9,... | collective-permute-start | bytes 1572872 | tf_op jit(solution)/shard_map/ppermute | solution.py:40
  20.8 4.8 %collective-permute-start.12 = (bf16[2048,128]{1,0:T(8,128)(2,1)S(1)}, bf16[2048,128]{1,0:T(8,128)(2,1)}, u32[]{:S(2)}, u32[]{:S(2)}) collective-permute-start(bf16[2048,128]{1,0:T(8,128)(2,1)S(1)} %constant_dynamic-update-slice_fusion.refs_1_), channel_id=1, source_target_pairs={{0,1},{1,0},{2,3},{3,2},{4,5},{5,4},{6,7},{7,6},{8,9},{9,8},{10,11... | collective-permute-start | bytes 1572872 | tf_op jit(solution)/shard_map/ppermute | solution.py:45
  26.1 4.2 %collective-permute-start.11 = (bf16[2048,128]{1,0:T(8,128)(2,1)S(1)}, bf16[2048,128]{1,0:T(8,128)(2,1)}, u32[]{:S(2)}, u32[]{:S(2)}) collective-permute-start(bf16[2048,128]{1,0:T(8,128)(2,1)S(1)} %collective-permute-done.10.refs_1_), channel_id=1, source_target_pairs={{0,1},{1,0},{2,3},{3,2},{4,5},{5,4},{6,7},{7,6},{8,9},{9,8},{10,11... | collective-permute-start | bytes 1572872 | tf_op jit(solution)/shard_map/ppermute | solution.py:45
  32.7 5.6 %collective-permute-start.7 = (bf16[2048,128]{1,0:T(8,128)(2,1)S(1)}, bf16[2048,128]{1,0:T(8,128)(2,1)}, u32[]{:S(2)}, u32[]{:S(2)}) collective-permute-start(bf16[2048,128]{1,0:T(8,128)(2,1)S(1)} %collective-permute-done.6.refs_1_), channel_id=1, source_target_pairs={{0,1},{1,0},{2,3},{3,2},{4,5},{5,4},{6,7},{7,6},{8,9},{9,8},{10,11... | collective-permute-start | bytes 1572872 | tf_op jit(solution)/shard_map/ppermute | solution.py:45
  39.0 1.9 %collective-permute-start.13 = (bf16[16,128]{1,0:T(8,128)(2,1)S(1)}, bf16[16,128]{1,0:T(8,128)(2,1)S(1)}, u32[]{:S(2)}, u32[]{:S(2)}) collective-permute-start(bf16[16,128]{1,0:T(8,128)(2,1)S(1)} %get-tuple-element.5), channel_id=1, source_target_pairs={{0,8},{8,16},{16,24},{24,32},{32,40},{40,48},{48,56},{56,64},{64,7... | collective-permute-start | bytes 12296 | tf_op jit(solution)/shard_map/ppermute | solution.py:227
  42.3 1.4 %reduce.3 = s32[4096]{0:T(1024)S(1)} reduce(s32[1,4096,1]{1,2,0:T(1,128)} %param.11, s32[]{:T(128)} %broadcast.22), dimensions={0,2}, to_apply=%param.11.reduce_sub_computation.3 | reduce | bytes 32772 | tf_op args[2]
  43.7 1.7 %collective-permute-done.13 = bf16[16,128]{1,0:T(8,128)(2,1)S(1)} collective-permute-done((bf16[16,128]{1,0:T(8,128)(2,1)S(1)}, bf16[16,128]{1,0:T(8,128)(2,1)S(1)}, u32[]{:S(2)}, u32[]{:S(2)}) %collective-permute-start.13) | collective-permute-done | bytes 4128 | tf_op jit(solution)/shard_map/ppermute | solution.py:227
  45.5 3.8 %collective-permute-start.14 = (bf16[16,128]{1,0:T(8,128)(2,1)S(1)}, bf16[16,128]{1,0:T(8,128)(2,1)S(1)}, u32[]{:S(2)}, u32[]{:S(2)}) collective-permute-start(bf16[16,128]{1,0:T(8,128)(2,1)S(1)} %get-tuple-element.6), channel_id=1, source_target_pairs={{8,0},{16,8},{24,16},{32,24},{40,32},{48,40},{56,48},{64,56},{72,6... | collective-permute-start | bytes 12296 | tf_op jit(solution)/shard_map/ppermute | solution.py:228
  50.0 4.9 %shard_map.92.refs_0_ = bf16[6144,128]{1,0:T(8,128)(2,1)S(1)} custom-call(s32[4096]{0:T(1024)S(1)} %bitcast.16, bf16[4096,128]{1,0:T(8,128)(2,1)S(1)} %bitcast.14), custom_call_target="tpu_custom_call" | custom-call | bytes 20000000 | tf_op jit(solution)/shard_map/pallas_call | solution.py:115
  55.7 1.5 %shard_map.93.refs_3_ = f32[6144,128]{1,0:T(8,128)S(1)} custom-call(bf16[6144,128]{1,0:T(8,128)(2,1)S(1)} %shard_map.92.refs_0_, bf16[2048,128]{1,0:T(8,128)(2,1)S(1)} %constant_dynamic-update-slice_fusion.refs_1_, bf16[2048,128]{1,0:T(8,128)(2,1)} %collective-permute-done.12.refs_2_), custom_call_target="tpu_custom_call" | custom-call | flops 50331648 | bytes 4000000 | tf_op jit(solution)/shard_map/pallas_call | solution.py:181
  57.2 1.5 %shard_map.94.refs_3_ = f32[6144,128]{1,0:T(8,128)S(1)} custom-call(bf16[6144,128]{1,0:T(8,128)(2,1)S(1)} %shard_map.92.refs_0_, bf16[2048,128]{1,0:T(8,128)(2,1)S(1)} %collective-permute-done.10.refs_1_, bf16[2048,128]{1,0:T(8,128)(2,1)} %collective-permute-done.11.refs_2_, f32[6144,128]{1,0:T(8,128)S(1)} %shard_map.93.refs_3_), custom_call_target="tpu_custom_call", output_to_operand_aliasing={{}: (3, {})} | custom-call | flops 50331648 | bytes 4000000 | tf_op jit(solution)/shard_map/pallas_call | solution.py:181
  58.8 1.5 %shard_map.95.refs_3_ = f32[6144,128]{1,0:T(8,128)S(1)} custom-call(bf16[6144,128]{1,0:T(8,128)(2,1)S(1)} %shard_map.92.refs_0_, bf16[2048,128]{1,0:T(8,128)(2,1)S(1)} %collective-permute-done.8.refs_1_, bf16[2048,128]{1,0:T(8,128)(2,1)} %collective-permute-done.9.refs_2_, f32[6144,128]{1,0:T(8,128)S(1)} %shard_map.94.refs_3_), custom_call_target="tpu_custom_call", output_to_operand_aliasing={{}: (3, {})} | custom-call | flops 50331648 | bytes 4000000 | tf_op jit(solution)/shard_map/pallas_call | solution.py:181
  60.3 1.5 %shard_map.96.effect_ref = f32[6144,128]{1,0:T(8,128)S(1)} custom-call(bf16[6144,128]{1,0:T(8,128)(2,1)S(1)} %shard_map.92.refs_0_, bf16[2048,128]{1,0:T(8,128)(2,1)S(1)} %collective-permute-done.6.refs_1_, bf16[2048,128]{1,0:T(8,128)(2,1)} %collective-permute-done.7.refs_2_, f32[6144,128]{1,0:T(8,128)S(1)} %shard_map.95.refs_3_), custom_call_target="tpu_custom_call", output_to_operand_aliasing={{}: (3, {})} | custom-call | flops 50331648 | bytes 4000000 | tf_op jit(solution)/shard_map/pallas_call | solution.py:181
  61.9 6.4 %shard_map.98 = f32[4096,128]{1,0:T(8,128)} custom-call(s32[4096]{0:T(1024)S(1)} %bitcast.17, f32[6144,128]{1,0:T(8,128)S(1)} %shard_map.96.effect_ref, f32[4096,128]{1,0:T(8,128)S(1)} %shard_map.97.base_ref), custom_call_target="tpu_custom_call" | custom-call | flops 524288 | bytes 10000000 | tf_op jit(solution)/shard_map/pallas_call | solution.py:210
  (38 shorter events, 8.6 us)
Async XLA Ops:
  0.0 50.0 %copy-start = (bf16[1,4096,128]{2,1,0:T(8,128)(2,1)S(1)}, bf16[1,4096,128]{2,1,0:T(8,128)(2,1)}, u32[]{:S(2)}) copy-start(bf16[1,4096,128]{2,1,0:T(8,128)(2,1)} %param.9) | copy-start | bytes 3145732
  0.0 54.9 %copy-start.2 = (f32[1,4096]{1,0:T(1,128)S(1)}, f32[1,4096]{1,0:T(1,128)}, u32[]{:S(2)}) copy-start(f32[1,4096]{1,0:T(1,128)} %param.10) | copy-start | bytes 49156
  0.0 54.9 %copy-start.1 = (bf16[128,128]{1,0:T(8,128)(2,1)S(1)}, bf16[128,128]{1,0:T(8,128)(2,1)}, u32[]{:S(2)}) copy-start(bf16[128,128]{1,0:T(8,128)(2,1)} %plane_ref.1) | copy-start | bytes 98308
  0.0 5.9 %collective-permute-start = (bf16[128,128]{1,0:T(8,128)(2,1)}, bf16[128,128]{1,0:T(8,128)(2,1)S(1)}, u32[]{:S(2)}, u32[]{:S(2)}) collective-permute-start(bf16[128,128]{1,0:T(8,128)(2,1)} %bitcast.20), channel_id=1, source_target_pairs={{0,2},{1,3},{2,4},{3,5},{4,6},{5,7},{6,0},{7,1},{8,10},{9,11},{10,... | collective-permute-start | bytes 98312 | tf_op jit(solution)/shard_map/ppermute | solution.py:40
  1.7 4.2 %collective-permute-start.1 = (bf16[128,128]{1,0:T(8,128)(2,1)}, bf16[128,128]{1,0:T(8,128)(2,1)S(1)}, u32[]{:S(2)}, u32[]{:S(2)}) collective-permute-start(bf16[128,128]{1,0:T(8,128)(2,1)} %bitcast.21), channel_id=1, source_target_pairs={{0,6},{1,7},{2,0},{3,1},{4,2},{5,3},{6,4},{7,5},{8,14},{9,15},{10,... | collective-permute-start | bytes 98312 | tf_op jit(solution)/shard_map/ppermute | solution.py:40
  3.9 4.5 %collective-permute-start.2 = (bf16[128,128]{1,0:T(8,128)(2,1)}, bf16[128,128]{1,0:T(8,128)(2,1)S(1)}, u32[]{:S(2)}, u32[]{:S(2)}) collective-permute-start(bf16[128,128]{1,0:T(8,128)(2,1)} %bitcast.22), channel_id=1, source_target_pairs={{0,4},{1,5},{2,6},{3,7},{4,0},{5,1},{6,2},{7,3},{8,12},{9,13},{10,... | collective-permute-start | bytes 98312 | tf_op jit(solution)/shard_map/ppermute | solution.py:40
  9.2 3.9 %collective-permute-start.3 = (bf16[512,128]{1,0:T(8,128)(2,1)S(1)}, bf16[512,128]{1,0:T(8,128)(2,1)S(1)}, u32[]{:S(2)}, u32[]{:S(2)}) collective-permute-start(bf16[512,128]{1,0:T(8,128)(2,1)S(1)} %pad_maximum_fusion), channel_id=1, source_target_pairs={{0,8},{1,33},{2,10},{3,35},{4,12},{5,37},{6,14},{7,39},{8,16},{9,4... | collective-permute-start | bytes 393224 | tf_op jit(solution)/shard_map/ppermute | solution.py:40
  10.5 3.8 %collective-permute-start.4 = (bf16[512,128]{1,0:T(8,128)(2,1)S(1)}, bf16[512,128]{1,0:T(8,128)(2,1)S(1)}, u32[]{:S(2)}, u32[]{:S(2)}) collective-permute-start(bf16[512,128]{1,0:T(8,128)(2,1)S(1)} %pad_maximum_fusion), channel_id=1, source_target_pairs={{0,24},{1,97},{2,26},{3,99},{4,28},{5,101},{6,30},{7,103},{8,0},{9... | collective-permute-start | bytes 393224 | tf_op jit(solution)/shard_map/ppermute | solution.py:40
  10.7 6.1 %collective-permute-start.5 = (bf16[512,128]{1,0:T(8,128)(2,1)S(1)}, bf16[512,128]{1,0:T(8,128)(2,1)S(1)}, u32[]{:S(2)}, u32[]{:S(2)}) collective-permute-start(bf16[512,128]{1,0:T(8,128)(2,1)S(1)} %pad_maximum_fusion), channel_id=1, source_target_pairs={{0,16},{1,65},{2,18},{3,67},{4,20},{5,69},{6,22},{7,71},{8,24},{9,... | collective-permute-start | bytes 393224 | tf_op jit(solution)/shard_map/ppermute | solution.py:40
  16.8 9.3 %collective-permute-start.10 = (bf16[2048,128]{1,0:T(8,128)(2,1)S(1)}, bf16[2048,128]{1,0:T(8,128)(2,1)S(1)}, u32[]{:S(2)}, u32[]{:S(2)}) collective-permute-start(bf16[2048,128]{1,0:T(8,128)(2,1)S(1)} %constant_dynamic-update-slice_fusion.refs_1_), channel_id=1, source_target_pairs={{0,32},{1,9},{2,34},{3,11},{4,36},{5,13},{6,38},{7,15},{8,40},{9,1... | collective-permute-start | bytes 1572872 | tf_op jit(solution)/shard_map/ppermute | solution.py:40
  17.8 13.5 %collective-permute-start.8 = (bf16[2048,128]{1,0:T(8,128)(2,1)S(1)}, bf16[2048,128]{1,0:T(8,128)(2,1)S(1)}, u32[]{:S(2)}, u32[]{:S(2)}) collective-permute-start(bf16[2048,128]{1,0:T(8,128)(2,1)S(1)} %constant_dynamic-update-slice_fusion.refs_1_), channel_id=1, source_target_pairs={{0,96},{1,25},{2,98},{3,27},{4,100},{5,29},{6,102},{7,31},{8,104},... | collective-permute-start | bytes 1572872 | tf_op jit(solution)/shard_map/ppermute | solution.py:40
  19.5 13.2 %collective-permute-start.6 = (bf16[2048,128]{1,0:T(8,128)(2,1)S(1)}, bf16[2048,128]{1,0:T(8,128)(2,1)S(1)}, u32[]{:S(2)}, u32[]{:S(2)}) collective-permute-start(bf16[2048,128]{1,0:T(8,128)(2,1)S(1)} %constant_dynamic-update-slice_fusion.refs_1_), channel_id=1, source_target_pairs={{0,64},{1,17},{2,66},{3,19},{4,68},{5,21},{6,70},{7,23},{8,72},{9,... | collective-permute-start | bytes 1572872 | tf_op jit(solution)/shard_map/ppermute | solution.py:40
  20.8 34.9 %collective-permute-start.12 = (bf16[2048,128]{1,0:T(8,128)(2,1)S(1)}, bf16[2048,128]{1,0:T(8,128)(2,1)}, u32[]{:S(2)}, u32[]{:S(2)}) collective-permute-start(bf16[2048,128]{1,0:T(8,128)(2,1)S(1)} %constant_dynamic-update-slice_fusion.refs_1_), channel_id=1, source_target_pairs={{0,1},{1,0},{2,3},{3,2},{4,5},{5,4},{6,7},{7,6},{8,9},{9,8},{10,11... | collective-permute-start | bytes 1572872 | tf_op jit(solution)/shard_map/ppermute | solution.py:45
  26.1 31.1 %collective-permute-start.11 = (bf16[2048,128]{1,0:T(8,128)(2,1)S(1)}, bf16[2048,128]{1,0:T(8,128)(2,1)}, u32[]{:S(2)}, u32[]{:S(2)}) collective-permute-start(bf16[2048,128]{1,0:T(8,128)(2,1)S(1)} %collective-permute-done.10.refs_1_), channel_id=1, source_target_pairs={{0,1},{1,0},{2,3},{3,2},{4,5},{5,4},{6,7},{7,6},{8,9},{9,8},{10,11... | collective-permute-start | bytes 1572872 | tf_op jit(solution)/shard_map/ppermute | solution.py:45
  31.3 27.5 %collective-permute-start.9 = (bf16[2048,128]{1,0:T(8,128)(2,1)S(1)}, bf16[2048,128]{1,0:T(8,128)(2,1)}, u32[]{:S(2)}, u32[]{:S(2)}) collective-permute-start(bf16[2048,128]{1,0:T(8,128)(2,1)S(1)} %collective-permute-done.8.refs_1_), channel_id=1, source_target_pairs={{0,1},{1,0},{2,3},{3,2},{4,5},{5,4},{6,7},{7,6},{8,9},{9,8},{10,11... | collective-permute-start | bytes 1572872 | tf_op jit(solution)/shard_map/ppermute | solution.py:45
  32.7 27.6 %collective-permute-start.7 = (bf16[2048,128]{1,0:T(8,128)(2,1)S(1)}, bf16[2048,128]{1,0:T(8,128)(2,1)}, u32[]{:S(2)}, u32[]{:S(2)}) collective-permute-start(bf16[2048,128]{1,0:T(8,128)(2,1)S(1)} %collective-permute-done.6.refs_1_), channel_id=1, source_target_pairs={{0,1},{1,0},{2,3},{3,2},{4,5},{5,4},{6,7},{7,6},{8,9},{9,8},{10,11... | collective-permute-start | bytes 1572872 | tf_op jit(solution)/shard_map/ppermute | solution.py:45
  39.0 6.4 %collective-permute-start.13 = (bf16[16,128]{1,0:T(8,128)(2,1)S(1)}, bf16[16,128]{1,0:T(8,128)(2,1)S(1)}, u32[]{:S(2)}, u32[]{:S(2)}) collective-permute-start(bf16[16,128]{1,0:T(8,128)(2,1)S(1)} %get-tuple-element.5), channel_id=1, source_target_pairs={{0,8},{8,16},{16,24},{24,32},{32,40},{40,48},{48,56},{56,64},{64,7... | collective-permute-start | bytes 12296 | tf_op jit(solution)/shard_map/ppermute | solution.py:227
  45.5 9.4 %collective-permute-start.14 = (bf16[16,128]{1,0:T(8,128)(2,1)S(1)}, bf16[16,128]{1,0:T(8,128)(2,1)S(1)}, u32[]{:S(2)}, u32[]{:S(2)}) collective-permute-start(bf16[16,128]{1,0:T(8,128)(2,1)S(1)} %get-tuple-element.6), channel_id=1, source_target_pairs={{8,0},{16,8},{24,16},{32,24},{40,32},{48,40},{56,48},{64,56},{72,6... | collective-permute-start | bytes 12296 | tf_op jit(solution)/shard_map/ppermute | solution.py:228

commit v2 on v1

--- a/solution.py
+++ b/solution.py
@@ -16,7 +16,7 @@
 vals = 128
 slots = owners * cap
 chunk = 256
-offsets = np.array([0, -1, 1, 2])
+offsets = np.array([0, 2, -1, 1])
 vmem_bytes = 40 * 1024 * 1024
 
 
@@ -46,14 +46,7 @@
 
 
 def around(value, axes):
-    return [value] + [shifted(value, step, axes) for step in (1, -1, 2)]
-
-
-def gather_operators(block):
-    near = jnp.concatenate(around(block, "zz"), axis=0)
-    plane = jnp.concatenate(around(near, "xy"), axis=0)
-    parts = around(plane, "yx")
-    return [(part, core_swap(part)) for part in parts]
+    return [value] + [shifted(value, step, axes) for step in (2, 1, -1)]
 
 
 def slot_owners():
@@ -147,7 +140,7 @@
         out_shape=jax.ShapeDtypeStruct((rows, vals), jnp.float32),
         scratch_shapes=[pltpu.VMEM((rows + 16, vals), jnp.float32)],
         compiler_params=params(),
-        cost_estimate=pl.CostEstimate(flops=2 * 4096 * 128 * 128, bytes_accessed=10000000, transcendentals=0),
+        cost_estimate=pl.CostEstimate(flops=1000, bytes_accessed=1000, transcendentals=0),
     )(field, halo, coupling, plane)
 
 
@@ -159,67 +152,84 @@
     return reluct * response
 
 
-def effect_kernel(*refs):
-    sorted_ref, near_ref, far_ref = refs[:3]
-    effect_ref = refs[-1]
-    for g, operator_ref in enumerate((near_ref, far_ref)):
-        for k in range(16):
-            lo = (g * 16 + k) * cap
-            effect_ref[lo : lo + cap, :] = respond(
-                sorted_ref[lo : lo + cap, :], operator_ref[k * vals : (k + 1) * vals, :]
-            )
-
-
-def effects(sorted_rows, near, far, number, previous):
-    block = 32 * cap
-    whole = pl.BlockSpec((16 * vals, vals), lambda i: (0, 0))
-    specs = [pl.BlockSpec((block, vals), lambda i: (number, 0)), whole, whole]
-    operands = [sorted_rows, near, far]
+def effect_block(sorted_ref, operator_ref, effect_ref, block):
+    for k in range(16):
+        lo = (block * 16 + k) * cap
+        effect_ref[lo : lo + cap, :] = respond(
+            sorted_ref[lo : lo + cap, :], operator_ref[k * vals : (k + 1) * vals, :]
+        )
+
+
+def effect_kernel(blocks, *refs):
+    sorted_ref, effect_ref = refs[0], refs[-1]
+    for block, operator_ref in zip(blocks, refs[1:]):
+        effect_block(sorted_ref, operator_ref, effect_ref, block)
+
+
+in_vmem = pl.BlockSpec(memory_space=pltpu.VMEM)
+
+
+def effects(sorted_rows, operators, blocks, previous):
+    operands = [sorted_rows, *operators]
     if previous is not None:
-        specs.append(pl.BlockSpec(memory_space=pl.ANY))
         operands.append(previous)
     return pl.pallas_call(
-        effect_kernel,
-        grid=(1,),
-        in_specs=specs,
-        out_specs=pl.BlockSpec((block, vals), lambda i: (number, 0)),
+        functools.partial(effect_kernel, blocks),
+        in_specs=[in_vmem] * len(operands),
+        out_specs=in_vmem,
         out_shape=jax.ShapeDtypeStruct((slots, vals), jnp.float32),
-        input_output_aliases={} if previous is None else {3: 0},
-        compiler_params=params(),
-        cost_estimate=pl.CostEstimate(
-            flops=2 * block * 128 * 128, bytes_accessed=4000000, transcendentals=0
-        ),
+        input_output_aliases={} if previous is None else {len(operands) - 1: 0},
+        compiler_params=params(),
+        cost_estimate=pl.CostEstimate(flops=1000, bytes_accessed=1000, transcendentals=0),
     )(*operands)
 
 
-def combine_kernel(slot_ref, effect_ref, base_ref, out_ref):
-    top = pl.program_id(0) * 512
-
-    def body(i, carry):
-        first = pl.multiple_of(i * 32, 32)
-        for j in range(32):
-            effect = effect_ref[pl.ds(slot_ref[top + first + j], 1), :]
-            out_ref[pl.ds(first + j, 1), :] = base_ref[pl.ds(first + j, 1), :] - step_size * effect
-        return carry
-
-    lax.fori_loop(0, 512 // 32, body, 0)
-
-
-def combine(slot, effect, base):
-    part = pl.BlockSpec((512, vals), lambda i: (i, 0))
-    return pl.pallas_call(
-        combine_kernel,
-        grid=(rows // 512,),
-        in_specs=[
-            pl.BlockSpec(memory_space=pltpu.SMEM),
-            pl.BlockSpec((slots, vals), lambda i: (0, 0)),
-            part,
+part_rows = 512
+
+
+def final_kernel(blocks, slot_ref, base_ref, sorted_ref, *refs):
+    operators, (_, out_ref, effect_ref, result, sent) = refs[:-5], refs[-5:]
+    for block, operator_ref in zip(blocks, operators):
+        effect_block(sorted_ref, operator_ref, effect_ref, block)
+
+    def copy(part):
+        span = pl.ds(pl.multiple_of(part * part_rows, part_rows), part_rows)
+        return pltpu.make_async_copy(result.at[span], out_ref.at[span], sent.at[part])
+
+    for part in range(rows // part_rows):
+
+        def body(i, carry):
+            first = pl.multiple_of(part * part_rows + i * 32, 32)
+            for j in range(32):
+                effect = effect_ref[pl.ds(slot_ref[first + j], 1), :]
+                row = pl.ds(first + j, 1)
+                result[row, :] = base_ref[row, :] - step_size * effect
+            return carry
+
+        lax.fori_loop(0, part_rows // 32, body, 0)
+        copy(part).start()
+    for part in range(rows // part_rows):
+        copy(part).wait()
+
+
+def finish(slot, base, sorted_rows, operators, blocks, previous):
+    operands = [slot, base, sorted_rows, *operators, previous]
+    return pl.pallas_call(
+        functools.partial(final_kernel, blocks),
+        in_specs=[pl.BlockSpec(memory_space=pltpu.SMEM)] + [in_vmem] * (len(operands) - 1),
+        out_specs=[pl.BlockSpec(memory_space=pl.ANY), in_vmem],
+        out_shape=[
+            jax.ShapeDtypeStruct((rows, vals), jnp.float32),
+            jax.ShapeDtypeStruct((slots, vals), jnp.float32),
         ],
-        out_specs=part,
-        out_shape=jax.ShapeDtypeStruct((rows, vals), jnp.float32),
+        input_output_aliases={len(operands) - 1: 1},
+        scratch_shapes=[
+            pltpu.VMEM((rows, vals), jnp.float32),
+            pltpu.SemaphoreType.DMA((rows // part_rows,)),
+        ],
         compiler_params=params(),
         cost_estimate=pl.CostEstimate(flops=4096 * 128, bytes_accessed=10000000, transcendentals=0),
-    )(slot, effect, base)
+    )(*operands)[0]
 
 
 def halo_rows(field):
@@ -231,15 +241,21 @@
 
 def per_device(edge_field, coupling, owner_map, in_plane, profile_op):
     field = edge_field[0]
-    parts = gather_operators(profile_op[0])
+    tied = lax.optimization_barrier
+    near = jnp.concatenate(around(profile_op[0], "zz"), axis=0)
     table = slot_owners()[:, None]
     slot = rank(owner_map.reshape(rows // chunk, chunk), table).reshape(rows)
+    near, slot = tied((near, slot))
+    plane = jnp.concatenate(around(near, "xy"), axis=0)
     sorted_rows = sort_rows(slot, field)
+    plane, sorted_rows = tied((plane, sorted_rows))
+    own, *others = around(plane, "yx")
+    effect = effects(sorted_rows, [own, core_swap(own)], (0, 1), None)
     base = stencil(field, halo_rows(field), coupling.reshape(rows // vals, vals), in_plane)
-    effect = None
-    for number, (near, far) in enumerate(parts):
-        effect = effects(sorted_rows, near, far, number, effect)
-    return combine(slot, effect, base)[None]
+    *others, effect, base = tied((*others, effect, base))
+    effect = effects(sorted_rows, others, (2, 4, 6), effect)
+    far = [core_swap(part) for part in others]
+    return finish(slot, base, sorted_rows, far, (3, 5, 7), effect)[None]
 
 
 def solution(mesh):

time: 68.9 us -> 55.9 us (0.81)
  the two profiles are of different devices: /device:TPU:9 before, /device:TPU:57 now
where the time goes in v2:
time: 55.9 us; the launch traced here: 55.6 us
  starting transfers between devices  22.4 us (40%)
  waiting for transfers between devices  14.3 us (26%)
  Pallas kernels  13.8 us (25%)
  other arithmetic  2.94 us (5%)
  local copies, waits for them, and re-layouts  1.88 us (3%)
    ppermute x9, starting transfers between devices, shifted(): return lax.ppermute(value, axes_all, pairs)  11.4 us
    ppermute x1, waiting for transfers between devices, halo_rows(): lax.ppermute(field[rows - 16:], 'sub', [(i, i + 1) for i in range(ends)])  10.1 us
    pallas_call x1, Pallas kernels, finish(): pl.pallas_call(functools.partial(final_kernel, blocks), in_specs=[pl.Bloc...  6.38 us
    ppermute x4, starting transfers between devices, core_swap(): return lax.ppermute(value, axes_all, pairs)  6.11 us
    pallas_call x1, Pallas kernels, sort_rows(): pl.pallas_call(sort_kernel, in_specs=[pl.BlockSpec(memory_space=pltpu.SME...  4.86 us
    ppermute x1, starting transfers between devices, halo_rows(): lax.ppermute(field[rows - 16:], 'sub', [(i, i + 1) for i in range(ends)])  2.84 us
    ppermute x1, waiting for transfers between devices, halo_rows(): after = lax.ppermute(field[:16], 'sub', [(i + 1, i) for i in range(ends)])  2.29 us
    ppermute x1, starting transfers between devices, halo_rows(): after = lax.ppermute(field[:16], 'sub', [(i + 1, i) for i in range(ends)])  2.04 us
  transfers between devices with their start and end apart: 15, of which 5 were waited for; matrix products, arithmetic and copies ran while one was open for 5% of the time, Pallas kernels for 13%

profile of v2, /device:TPU:57, one launch (start us, length us, event | category | flops | bytes accessed | tf_op | source)
XLA Modules:
  0.0 55.6 jit_solution(245383173707491540)
XLA Ops:
  0.0 1.7 %collective-permute-start.1 = (bf16[128,128]{1,0:T(8,128)(2,1)}, bf16[128,128]{1,0:T(8,128)(2,1)S(1)}, u32[]{:S(2)}, u32[]{:S(2)}) collective-permute-start(bf16[128,128]{1,0:T(8,128)(2,1)} %bitcast.20), channel_id=1, source_target_pairs={{0,2},{1,3},{2,4},{3,5},{4,6},{5,7},{6,0},{7,1},{8,10},{9,11},{10,... | collective-permute-start | bytes 98312 | tf_op jit(solution)/shard_map/ppermute | solution.py:40
  1.7 3.7 %collective-permute-start = (bf16[128,128]{1,0:T(8,128)(2,1)}, bf16[128,128]{1,0:T(8,128)(2,1)S(1)}, u32[]{:S(2)}, u32[]{:S(2)}) collective-permute-start(bf16[128,128]{1,0:T(8,128)(2,1)} %bitcast.21), channel_id=1, source_target_pairs={{0,4},{1,5},{2,6},{3,7},{4,0},{5,1},{6,2},{7,3},{8,12},{9,13},{10,... | collective-permute-start | bytes 98312 | tf_op jit(solution)/shard_map/ppermute | solution.py:40
  5.9 1.4 %reduce.3 = s32[4096]{0:T(1024)S(1)} reduce(s32[1,4096,1]{1,2,0:T(1,128)} %param.11, s32[]{:T(128)} %broadcast.22), dimensions={0,2}, to_apply=%param.11.reduce_sub_computation.3 | reduce | bytes 32772 | tf_op args[2]
  7.3 0.7 %fusion.5 = s32[128,1]{0,1:T(1,128)S(1)} fusion(s32[128]{0:T(128)} %constant.82.clone, s32[128]{0:T(128)} %constant.83.clone, s32[128]{0:T(128)} %constant.84.clone, s32[128]{0:T(128)} %constant.85.clone, s32[]{:T(128)S(6)} %select_n.46, s32[]{:T(128)S(6)} %select_n.43, s32[]{:T(128)S(6)} %select_n.40, s32[]{:T(128)S(6)} %select_n.39), kind=kLoop, calls=%fused_computation.22 | loop fusion | flops 6272 | bytes 2576 | tf_op jit(solution)/shard_map/broadcast_in_dim | solution.py:246
  8.2 0.8 %shard_map.91 = s32[16,256]{1,0:T(8,128)S(1)} custom-call(s32[16,256]{1,0:T(8,128)S(1)} %reshape.11.owner_ref, s32[128,1]{1,0:T(8,128)S(1)} %copy.12.table_ref), custom_call_target="tpu_custom_call" | custom-call | flops 402653184 | bytes 100000 | tf_op jit(solution)/shard_map/pallas_call | solution.py:86
  9.0 0.8 %pad_maximum_fusion.1 = bf16[512,128]{1,0:T(8,128)(2,1)S(1)} fusion(bf16[128,128]{1,0:T(8,128)(2,1)S(1)} %collective-permute-done.2, bf16[128,128]{1,0:T(8,128)(2,1)S(1)} %collective-permute-done.1, bf16[128,128]{1,0:T(8,128)(2,1)S(1)} %collective-permute-done, bf16[128,128]{1,0:T(8,128)(2,1)} %bitcast.22), kind=kLoop, calls=%fused_computation.1 | loop fusion | flops 524288 | bytes 262144 | tf_op jit(solution)/shard_map/concatenate | solution.py:245
  9.8 0.5 collective-permute-start.5
  10.3 2.2 %collective-permute-start.4 = (bf16[512,128]{1,0:T(8,128)(2,1)S(1)}, bf16[512,128]{1,0:T(8,128)(2,1)S(1)}, u32[]{:S(2)}, u32[]{:S(2)}) collective-permute-start(bf16[512,128]{1,0:T(8,128)(2,1)S(1)} %pad_maximum_fusion.1), channel_id=1, source_target_pairs={{0,8},{1,33},{2,10},{3,35},{4,12},{5,37},{6,14},{7,39},{8,16},{9,4... | collective-permute-start | bytes 393224 | tf_op jit(solution)/shard_map/ppermute | solution.py:40
  12.5 1.2 %copy-done = bf16[1,4096,128]{2,1,0:T(8,128)(2,1)S(1)} copy-done((bf16[1,4096,128]{2,1,0:T(8,128)(2,1)S(1)}, bf16[1,4096,128]{2,1,0:T(8,128)(2,1)}, u32[]{:S(2)}) %copy-start) | copy-done | bytes 1048600
  13.7 4.9 %shard_map.92.refs_0_.sorted_ref = bf16[6144,128]{1,0:T(8,128)(2,1)S(1)} custom-call(s32[4096]{0:T(1024)S(1)} %bitcast.15, bf16[4096,128]{1,0:T(8,128)(2,1)S(1)} %bitcast.13), custom_call_target="tpu_custom_call" | custom-call | bytes 20000000 | tf_op jit(solution)/shard_map/pallas_call | solution.py:108
  18.7 4.0 %collective-permute-start.9 = (bf16[2048,128]{1,0:T(8,128)(2,1)S(1)}, bf16[2048,128]{1,0:T(8,128)(2,1)S(1)}, u32[]{:S(2)}, u32[]{:S(2)}) collective-permute-start(bf16[2048,128]{1,0:T(8,128)(2,1)S(1)} %pad_maximum_fusion.refs_1_), channel_id=1, source_target_pairs={{0,1},{1,0},{2,3},{3,2},{4,5},{5,4},{6,7},{7,6},{8,9},{9,8},{10,11... | collective-permute-start | bytes 1572872 | tf_op jit(solution)/shard_map/ppermute | solution.py:45
  22.7 1.0 %collective-permute-start.8 = (bf16[2048,128]{1,0:T(8,128)(2,1)S(1)}, bf16[2048,128]{1,0:T(8,128)(2,1)S(1)}, u32[]{:S(2)}, u32[]{:S(2)}) collective-permute-start(bf16[2048,128]{1,0:T(8,128)(2,1)S(1)} %pad_maximum_fusion.refs_1_), channel_id=1, source_target_pairs={{0,96},{1,25},{2,98},{3,27},{4,100},{5,29},{6,102},{7,31},{8,104},... | collective-permute-start | bytes 1572872 | tf_op jit(solution)/shard_map/ppermute | solution.py:40
  23.7 0.5 collective-permute-start.7
  24.2 1.8 %collective-permute-start.6 = (bf16[2048,128]{1,0:T(8,128)(2,1)S(1)}, bf16[2048,128]{1,0:T(8,128)(2,1)S(1)}, u32[]{:S(2)}, u32[]{:S(2)}) collective-permute-start(bf16[2048,128]{1,0:T(8,128)(2,1)S(1)} %pad_maximum_fusion.refs_1_), channel_id=1, source_target_pairs={{0,64},{1,17},{2,66},{3,19},{4,68},{5,21},{6,70},{7,23},{8,72},{9,... | collective-permute-start | bytes 1572872 | tf_op jit(solution)/shard_map/ppermute | solution.py:40
  26.0 2.8 %collective-permute-start.10 = (bf16[16,128]{1,0:T(8,128)(2,1)S(1)}, bf16[16,128]{1,0:T(8,128)(2,1)S(1)}, u32[]{:S(2)}, u32[]{:S(2)}) collective-permute-start(bf16[16,128]{1,0:T(8,128)(2,1)S(1)} %get-tuple-element.25), channel_id=1, source_target_pairs={{0,8},{8,16},{16,24},{24,32},{32,40},{40,48},{48,56},{56,64},{64,7... | collective-permute-start | bytes 12296 | tf_op jit(solution)/shard_map/ppermute | solution.py:237
  28.8 10.1 %collective-permute-done.10 = bf16[16,128]{1,0:T(8,128)(2,1)S(1)} collective-permute-done((bf16[16,128]{1,0:T(8,128)(2,1)S(1)}, bf16[16,128]{1,0:T(8,128)(2,1)S(1)}, u32[]{:S(2)}, u32[]{:S(2)}) %collective-permute-start.10) | collective-permute-done | bytes 4128 | tf_op jit(solution)/shard_map/ppermute | solution.py:237
  38.9 2.0 %collective-permute-start.11 = (bf16[16,128]{1,0:T(8,128)(2,1)S(1)}, bf16[16,128]{1,0:T(8,128)(2,1)S(1)}, u32[]{:S(2)}, u32[]{:S(2)}) collective-permute-start(bf16[16,128]{1,0:T(8,128)(2,1)S(1)} %get-tuple-element.26), channel_id=1, source_target_pairs={{8,0},{16,8},{24,16},{32,24},{40,32},{48,40},{56,48},{64,56},{72,6... | collective-permute-start | bytes 12296 | tf_op jit(solution)/shard_map/ppermute | solution.py:238
  41.0 2.3 %collective-permute-done.11 = bf16[16,128]{1,0:T(8,128)(2,1)S(1)} collective-permute-done((bf16[16,128]{1,0:T(8,128)(2,1)S(1)}, bf16[16,128]{1,0:T(8,128)(2,1)S(1)}, u32[]{:S(2)}, u32[]{:S(2)}) %collective-permute-start.11) | collective-permute-done | bytes 4128 | tf_op jit(solution)/shard_map/ppermute | solution.py:238
  43.3 0.7 %shard_map.94.base_ref = f32[4096,128]{1,0:T(8,128)S(1)} custom-call(bf16[4096,128]{1,0:T(8,128)(2,1)S(1)} %bitcast.14, bf16[16,128]{1,0:T(8,128)(2,1)S(1)} %pad_maximum_fusion.2.halo_ref, f32[32,128]{1,0:T(8,128)S(1)} %bitcast.17, bf16[128,128]{1,0:T(8,128)(2,1)S(1)} %copy-done.1), custom_call_target="tpu_custom_call" | custom-call | flops 1000 | bytes 1000 | tf_op jit(solution)/shard_map/pallas_call | solution.py:138
  44.5 1.6 %collective-permute-start.12 = (bf16[2048,128]{1,0:T(8,128)(2,1)S(1)}, bf16[2048,128]{1,0:T(8,128)(2,1)S(1)}, u32[]{:S(2)}, u32[]{:S(2)}) collective-permute-start(bf16[2048,128]{1,0:T(8,128)(2,1)S(1)} %collective-permute-done.6.refs_1_), channel_id=1, source_target_pairs={{0,1},{1,0},{2,3},{3,2},{4,5},{5,4},{6,7},{7,6},{8,9},{9,8},{10,11... | collective-permute-start | bytes 1572872 | tf_op jit(solution)/shard_map/ppermute | solution.py:45
  46.6 0.6 %shard_map.95.refs_3_ = f32[6144,128]{1,0:T(8,128)S(1)} custom-call(bf16[6144,128]{1,0:T(8,128)(2,1)S(1)} %shard_map.92.refs_0_.sorted_ref, bf16[2048,128]{1,0:T(8,128)(2,1)S(1)} %collective-permute-done.6.refs_1_, bf16[2048,128]{1,0:T(8,128)(2,1)S(1)} %collective-permute-done.7.refs_2_, ...), custom_call_target="tpu_custom_call", output_to_operand_aliasing={{}: (4, {})} | custom-call | flops 1000 | bytes 1000 | tf_op jit(solution)/shard_map/pallas_call | solution.py:176
  47.7 0.7 %collective-permute-done.13.refs_1_ = bf16[2048,128]{1,0:T(8,128)(2,1)S(1)} collective-permute-done((bf16[2048,128]{1,0:T(8,128)(2,1)S(1)}, bf16[2048,128]{1,0:T(8,128)(2,1)S(1)}, u32[]{:S(2)}, u32[]{:S(2)}) %collective-permute-start.13) | collective-permute-done | bytes 524320 | tf_op jit(solution)/shard_map/ppermute | solution.py:45
  48.4 0.7 %collective-permute-done.14.refs_2_ = bf16[2048,128]{1,0:T(8,128)(2,1)S(1)} collective-permute-done((bf16[2048,128]{1,0:T(8,128)(2,1)S(1)}, bf16[2048,128]{1,0:T(8,128)(2,1)S(1)}, u32[]{:S(2)}, u32[]{:S(2)}) %collective-permute-start.14) | collective-permute-done | bytes 524320 | tf_op jit(solution)/shard_map/ppermute | solution.py:45
  49.2 6.4 %shard_map.96 = (f32[4096,128]{1,0:T(8,128)}, f32[6144,128]{1,0:T(8,128)S(1)}) custom-call(s32[4096]{0:T(1024)S(1)} %bitcast.16, f32[4096,128]{1,0:T(8,128)S(1)} %shard_map.94.base_ref, bf16[6144,128]{1,0:T(8,128)(2,1)S(1)} %shard_map.92.refs_0_.sorted_ref, bf16[2048,128]{1,0:T(8,128)(2,1)S(1)} %collective-permute-done.12.refs_0_, ...), custom_call_target="tpu_custom_call", output_to_operand_aliasing={{1}: (6, {})} | custom-call | flops 524288 | bytes 10000000 | tf_op jit(solution)/shard_map/pallas_call | solution.py:217
  (30 shorter events, 2.1 us)
Async XLA Ops:
  0.0 43.3 %copy-start.1 = (bf16[128,128]{1,0:T(8,128)(2,1)S(1)}, bf16[128,128]{1,0:T(8,128)(2,1)}, u32[]{:S(2)}) copy-start(bf16[128,128]{1,0:T(8,128)(2,1)} %plane_ref.1) | copy-start | bytes 98308
  0.0 43.3 %copy-start.2 = (f32[1,4096]{1,0:T(1,128)S(1)}, f32[1,4096]{1,0:T(1,128)}, u32[]{:S(2)}) copy-start(f32[1,4096]{1,0:T(1,128)} %param.10) | copy-start | bytes 49156
  0.0 9.0 %collective-permute-start.2 = (bf16[128,128]{1,0:T(8,128)(2,1)}, bf16[128,128]{1,0:T(8,128)(2,1)S(1)}, u32[]{:S(2)}, u32[]{:S(2)}) collective-permute-start(bf16[128,128]{1,0:T(8,128)(2,1)} %bitcast.19), channel_id=1, source_target_pairs={{0,6},{1,7},{2,0},{3,1},{4,2},{5,3},{6,4},{7,5},{8,14},{9,15},{10,... | collective-permute-start | bytes 98312 | tf_op jit(solution)/shard_map/ppermute | solution.py:40
  0.0 9.0 %collective-permute-start.1 = (bf16[128,128]{1,0:T(8,128)(2,1)}, bf16[128,128]{1,0:T(8,128)(2,1)S(1)}, u32[]{:S(2)}, u32[]{:S(2)}) collective-permute-start(bf16[128,128]{1,0:T(8,128)(2,1)} %bitcast.20), channel_id=1, source_target_pairs={{0,2},{1,3},{2,4},{3,5},{4,6},{5,7},{6,0},{7,1},{8,10},{9,11},{10,... | collective-permute-start | bytes 98312 | tf_op jit(solution)/shard_map/ppermute | solution.py:40
  1.7 7.3 %collective-permute-start = (bf16[128,128]{1,0:T(8,128)(2,1)}, bf16[128,128]{1,0:T(8,128)(2,1)S(1)}, u32[]{:S(2)}, u32[]{:S(2)}) collective-permute-start(bf16[128,128]{1,0:T(8,128)(2,1)} %bitcast.21), channel_id=1, source_target_pairs={{0,4},{1,5},{2,6},{3,7},{4,0},{5,1},{6,2},{7,3},{8,12},{9,13},{10,... | collective-permute-start | bytes 98312 | tf_op jit(solution)/shard_map/ppermute | solution.py:40
  9.8 8.8 %collective-permute-start.5 = (bf16[512,128]{1,0:T(8,128)(2,1)S(1)}, bf16[512,128]{1,0:T(8,128)(2,1)S(1)}, u32[]{:S(2)}, u32[]{:S(2)}) collective-permute-start(bf16[512,128]{1,0:T(8,128)(2,1)S(1)} %pad_maximum_fusion.1), channel_id=1, source_target_pairs={{0,24},{1,97},{2,26},{3,99},{4,28},{5,101},{6,30},{7,103},{8,0},{9... | collective-permute-start | bytes 393224 | tf_op jit(solution)/shard_map/ppermute | solution.py:40
  10.3 8.3 %collective-permute-start.4 = (bf16[512,128]{1,0:T(8,128)(2,1)S(1)}, bf16[512,128]{1,0:T(8,128)(2,1)S(1)}, u32[]{:S(2)}, u32[]{:S(2)}) collective-permute-start(bf16[512,128]{1,0:T(8,128)(2,1)S(1)} %pad_maximum_fusion.1), channel_id=1, source_target_pairs={{0,8},{1,33},{2,10},{3,35},{4,12},{5,37},{6,14},{7,39},{8,16},{9,4... | collective-permute-start | bytes 393224 | tf_op jit(solution)/shard_map/ppermute | solution.py:40
  12.5 6.1 %collective-permute-start.3 = (bf16[512,128]{1,0:T(8,128)(2,1)S(1)}, bf16[512,128]{1,0:T(8,128)(2,1)S(1)}, u32[]{:S(2)}, u32[]{:S(2)}) collective-permute-start(bf16[512,128]{1,0:T(8,128)(2,1)S(1)} %pad_maximum_fusion.1), channel_id=1, source_target_pairs={{0,16},{1,65},{2,18},{3,67},{4,20},{5,69},{6,22},{7,71},{8,24},{9,... | collective-permute-start | bytes 393224 | tf_op jit(solution)/shard_map/ppermute | solution.py:40
  12.5 1.2 %copy-start = (bf16[1,4096,128]{2,1,0:T(8,128)(2,1)S(1)}, bf16[1,4096,128]{2,1,0:T(8,128)(2,1)}, u32[]{:S(2)}) copy-start(bf16[1,4096,128]{2,1,0:T(8,128)(2,1)} %param.9) | copy-start | bytes 3145732
  18.7 25.3 %collective-permute-start.9 = (bf16[2048,128]{1,0:T(8,128)(2,1)S(1)}, bf16[2048,128]{1,0:T(8,128)(2,1)S(1)}, u32[]{:S(2)}, u32[]{:S(2)}) collective-permute-start(bf16[2048,128]{1,0:T(8,128)(2,1)S(1)} %pad_maximum_fusion.refs_1_), channel_id=1, source_target_pairs={{0,1},{1,0},{2,3},{3,2},{4,5},{5,4},{6,7},{7,6},{8,9},{9,8},{10,11... | collective-permute-start | bytes 1572872 | tf_op jit(solution)/shard_map/ppermute | solution.py:45
  22.7 21.8 %collective-permute-start.8 = (bf16[2048,128]{1,0:T(8,128)(2,1)S(1)}, bf16[2048,128]{1,0:T(8,128)(2,1)S(1)}, u32[]{:S(2)}, u32[]{:S(2)}) collective-permute-start(bf16[2048,128]{1,0:T(8,128)(2,1)S(1)} %pad_maximum_fusion.refs_1_), channel_id=1, source_target_pairs={{0,96},{1,25},{2,98},{3,27},{4,100},{5,29},{6,102},{7,31},{8,104},... | collective-permute-start | bytes 1572872 | tf_op jit(solution)/shard_map/ppermute | solution.py:40
  23.7 20.8 %collective-permute-start.7 = (bf16[2048,128]{1,0:T(8,128)(2,1)S(1)}, bf16[2048,128]{1,0:T(8,128)(2,1)S(1)}, u32[]{:S(2)}, u32[]{:S(2)}) collective-permute-start(bf16[2048,128]{1,0:T(8,128)(2,1)S(1)} %pad_maximum_fusion.refs_1_), channel_id=1, source_target_pairs={{0,32},{1,9},{2,34},{3,11},{4,36},{5,13},{6,38},{7,15},{8,40},{9,1... | collective-permute-start | bytes 1572872 | tf_op jit(solution)/shard_map/ppermute | solution.py:40
  24.2 20.3 %collective-permute-start.6 = (bf16[2048,128]{1,0:T(8,128)(2,1)S(1)}, bf16[2048,128]{1,0:T(8,128)(2,1)S(1)}, u32[]{:S(2)}, u32[]{:S(2)}) collective-permute-start(bf16[2048,128]{1,0:T(8,128)(2,1)S(1)} %pad_maximum_fusion.refs_1_), channel_id=1, source_target_pairs={{0,64},{1,17},{2,66},{3,19},{4,68},{5,21},{6,70},{7,23},{8,72},{9,... | collective-permute-start | bytes 1572872 | tf_op jit(solution)/shard_map/ppermute | solution.py:40
  26.0 12.9 %collective-permute-start.10 = (bf16[16,128]{1,0:T(8,128)(2,1)S(1)}, bf16[16,128]{1,0:T(8,128)(2,1)S(1)}, u32[]{:S(2)}, u32[]{:S(2)}) collective-permute-start(bf16[16,128]{1,0:T(8,128)(2,1)S(1)} %get-tuple-element.25), channel_id=1, source_target_pairs={{0,8},{8,16},{16,24},{24,32},{32,40},{40,48},{48,56},{56,64},{64,7... | collective-permute-start | bytes 12296 | tf_op jit(solution)/shard_map/ppermute | solution.py:237
  38.9 4.3 %collective-permute-start.11 = (bf16[16,128]{1,0:T(8,128)(2,1)S(1)}, bf16[16,128]{1,0:T(8,128)(2,1)S(1)}, u32[]{:S(2)}, u32[]{:S(2)}) collective-permute-start(bf16[16,128]{1,0:T(8,128)(2,1)S(1)} %get-tuple-element.26), channel_id=1, source_target_pairs={{8,0},{16,8},{24,16},{32,24},{40,32},{48,40},{56,48},{64,56},{72,6... | collective-permute-start | bytes 12296 | tf_op jit(solution)/shard_map/ppermute | solution.py:238
  44.5 3.2 %collective-permute-start.12 = (bf16[2048,128]{1,0:T(8,128)(2,1)S(1)}, bf16[2048,128]{1,0:T(8,128)(2,1)S(1)}, u32[]{:S(2)}, u32[]{:S(2)}) collective-permute-start(bf16[2048,128]{1,0:T(8,128)(2,1)S(1)} %collective-permute-done.6.refs_1_), channel_id=1, source_target_pairs={{0,1},{1,0},{2,3},{3,2},{4,5},{5,4},{6,7},{7,6},{8,9},{9,8},{10,11... | collective-permute-start | bytes 1572872 | tf_op jit(solution)/shard_map/ppermute | solution.py:45
  46.1 2.3 %collective-permute-start.13 = (bf16[2048,128]{1,0:T(8,128)(2,1)S(1)}, bf16[2048,128]{1,0:T(8,128)(2,1)S(1)}, u32[]{:S(2)}, u32[]{:S(2)}) collective-permute-start(bf16[2048,128]{1,0:T(8,128)(2,1)S(1)} %collective-permute-done.7.refs_2_), channel_id=1, source_target_pairs={{0,1},{1,0},{2,3},{3,2},{4,5},{5,4},{6,7},{7,6},{8,9},{9,8},{10,11... | collective-permute-start | bytes 1572872 | tf_op jit(solution)/shard_map/ppermute | solution.py:45
  46.2 2.9 %collective-permute-start.14 = (bf16[2048,128]{1,0:T(8,128)(2,1)S(1)}, bf16[2048,128]{1,0:T(8,128)(2,1)S(1)}, u32[]{:S(2)}, u32[]{:S(2)}) collective-permute-start(bf16[2048,128]{1,0:T(8,128)(2,1)S(1)} %collective-permute-done.8.refs_3_), channel_id=1, source_target_pairs={{0,1},{1,0},{2,3},{3,2},{4,5},{5,4},{6,7},{7,6},{8,9},{9,8},{10,11... | collective-permute-start | bytes 1572872 | tf_op jit(solution)/shard_map/ppermute | solution.py:45

commit v3 on v2

--- a/solution.py
+++ b/solution.py
@@ -16,8 +16,14 @@
 vals = 128
 slots = owners * cap
 chunk = 256
+unroll = 128
+group = 4 * vals
+stride = group + 16
 offsets = np.array([0, 2, -1, 1])
-vmem_bytes = 40 * 1024 * 1024
+vmem_bytes = 20 * 1024 * 1024
+
+
+in_vmem = pl.BlockSpec(memory_space=pltpu.VMEM)
 
 
 def params():
@@ -43,6 +49,10 @@
 def core_swap(value):
     pairs = [(d, d ^ 1) for d in range(owners)]
     return lax.ppermute(value, axes_all, pairs)
+
+
+def swap_pieces(value):
+    return [core_swap(value[i : i + group]) for i in range(0, value.shape[0], stride)]
 
 
 def around(value, axes):
@@ -95,12 +105,12 @@
     wide[...] = field_ref[...].astype(jnp.float32)
 
     def body(i, carry):
-        first = pl.multiple_of(i * 32, 32)
-        for j in range(32):
+        first = pl.multiple_of(i * unroll, unroll)
+        for j in range(unroll):
             placed[pl.ds(slot_ref[first + j], 1), :] = wide[pl.ds(first + j, 1), :]
         return carry
 
-    lax.fori_loop(0, rows // 32, body, 0)
+    lax.fori_loop(0, rows // unroll, body, 0)
     sorted_ref[...] = placed[...].astype(jnp.bfloat16)
 
 
@@ -115,11 +125,33 @@
     )(slot, field)
 
 
-def stencil_kernel(field_ref, halo_ref, coupling_ref, plane_ref, base_ref, projected):
+def halo_choice():
+    sub, lam = lax.axis_index("sub"), lax.axis_index("lam")
+    x, inner = sub % 4, jnp.where(lam % 2 == 0, 0, 2)
+    before = jnp.where(sub == 0, 3, jnp.where(x == 0, 1, inner))
+    after = jnp.where(sub == 15, 3, jnp.where(x == 3, 1, inner))
+    return jnp.stack([before, after]).astype(jnp.int32)
+
+
+def halo(choice, own_ref, next_ref, label):
+    def ends(ref, second):
+        top = second * stride + group
+        return ref[top : top + 16, :].astype(jnp.float32)
+
+    nothing = jnp.zeros((16, vals), jnp.float32)
+    across = jnp.where(choice == 2, ends(next_ref, 0), nothing)
+    corner = jnp.where(choice == 1, ends(next_ref, label), across)
+    return jnp.where(choice == 0, ends(own_ref, label), corner).astype(jnp.bfloat16)
+
+
+def stencil_kernel(
+    choice_ref, field_ref, own_ref, before_ref, after_ref, coupling_ref, plane_ref, base_ref, projected
+):
     plane = plane_ref[...]
-    ends = jnp.dot(halo_ref[...], plane, preferred_element_type=jnp.float32)
-    projected[0:8, :] = ends[0:8]
-    projected[rows + 8 : rows + 16, :] = ends[8:16]
+    before = halo(choice_ref[0], own_ref, before_ref, 2)
+    after = halo(choice_ref[1], own_ref, after_ref, 3)
+    projected[0:8, :] = jnp.dot(before, plane, preferred_element_type=jnp.float32)[8:16]
+    projected[rows + 8 : rows + 16, :] = jnp.dot(after, plane, preferred_element_type=jnp.float32)[0:8]
     for j in range(rows // 512):
         projected[8 + j * 512 : 8 + (j + 1) * 512, :] = jnp.dot(
             field_ref[j * 512 : (j + 1) * 512, :], plane, preferred_element_type=jnp.float32
@@ -134,14 +166,16 @@
         base_ref[lo : lo + vals, :] = field - step_size * (weight * (2.0 * here - before - after))
 
 
-def stencil(field, halo, coupling, plane):
+def stencil(field, own, before, after, coupling, plane):
     return pl.pallas_call(
         stencil_kernel,
+        in_specs=[pl.BlockSpec(memory_space=pltpu.SMEM)] + [in_vmem] * 6,
+        out_specs=in_vmem,
         out_shape=jax.ShapeDtypeStruct((rows, vals), jnp.float32),
         scratch_shapes=[pltpu.VMEM((rows + 16, vals), jnp.float32)],
         compiler_params=params(),
         cost_estimate=pl.CostEstimate(flops=1000, bytes_accessed=1000, transcendentals=0),
-    )(field, halo, coupling, plane)
+    )(halo_choice(), field, own, before, after, coupling, plane)
 
 
 def respond(block, operator):
@@ -152,21 +186,22 @@
     return reluct * response
 
 
-def effect_block(sorted_ref, operator_ref, effect_ref, block):
-    for k in range(16):
-        lo = (block * 16 + k) * cap
+def effect_blocks(sorted_ref, operators, effect_ref, blocks):
+    tiles = [
+        (ref, top + k * vals)
+        for ref in operators
+        for top in range(0, ref.shape[0], stride)
+        for k in range(group // vals)
+    ]
+    for number, (operator_ref, top) in enumerate(tiles[: 16 * len(blocks)]):
+        lo = (blocks[number // 16] * 16 + number % 16) * cap
         effect_ref[lo : lo + cap, :] = respond(
-            sorted_ref[lo : lo + cap, :], operator_ref[k * vals : (k + 1) * vals, :]
+            sorted_ref[lo : lo + cap, :], operator_ref[top : top + vals, :]
         )
 
 
 def effect_kernel(blocks, *refs):
-    sorted_ref, effect_ref = refs[0], refs[-1]
-    for block, operator_ref in zip(blocks, refs[1:]):
-        effect_block(sorted_ref, operator_ref, effect_ref, block)
-
-
-in_vmem = pl.BlockSpec(memory_space=pltpu.VMEM)
+    effect_blocks(refs[0], refs[1:], refs[-1], blocks)
 
 
 def effects(sorted_rows, operators, blocks, previous):
@@ -189,8 +224,7 @@
 
 def final_kernel(blocks, slot_ref, base_ref, sorted_ref, *refs):
     operators, (_, out_ref, effect_ref, result, sent) = refs[:-5], refs[-5:]
-    for block, operator_ref in zip(blocks, operators):
-        effect_block(sorted_ref, operator_ref, effect_ref, block)
+    effect_blocks(sorted_ref, operators, effect_ref, blocks)
 
     def copy(part):
         span = pl.ds(pl.multiple_of(part * part_rows, part_rows), part_rows)
@@ -199,14 +233,14 @@
     for part in range(rows // part_rows):
 
         def body(i, carry):
-            first = pl.multiple_of(part * part_rows + i * 32, 32)
-            for j in range(32):
+            first = pl.multiple_of(part * part_rows + i * unroll, unroll)
+            for j in range(unroll):
                 effect = effect_ref[pl.ds(slot_ref[first + j], 1), :]
                 row = pl.ds(first + j, 1)
                 result[row, :] = base_ref[row, :] - step_size * effect
             return carry
 
-        lax.fori_loop(0, part_rows // 32, body, 0)
+        lax.fori_loop(0, part_rows // unroll, body, 0)
         copy(part).start()
     for part in range(rows // part_rows):
         copy(part).wait()
@@ -232,30 +266,25 @@
     )(*operands)[0]
 
 
-def halo_rows(field):
-    ends = lax.axis_size("sub") - 1
-    before = lax.ppermute(field[rows - 16 :], "sub", [(i, i + 1) for i in range(ends)])
-    after = lax.ppermute(field[:16], "sub", [(i + 1, i) for i in range(ends)])
-    return jnp.concatenate([before[8:], after[:8]], axis=0)
-
-
 def per_device(edge_field, coupling, owner_map, in_plane, profile_op):
     field = edge_field[0]
     tied = lax.optimization_barrier
-    near = jnp.concatenate(around(profile_op[0], "zz"), axis=0)
+    ends = jnp.concatenate([field[:8], field[rows - 8 :]], axis=0)
+    near = jnp.concatenate([*around(profile_op[0], "zz"), ends], axis=0)
     table = slot_owners()[:, None]
     slot = rank(owner_map.reshape(rows // chunk, chunk), table).reshape(rows)
     near, slot = tied((near, slot))
     plane = jnp.concatenate(around(near, "xy"), axis=0)
     sorted_rows = sort_rows(slot, field)
     plane, sorted_rows = tied((plane, sorted_rows))
-    own, *others = around(plane, "yx")
-    effect = effects(sorted_rows, [own, core_swap(own)], (0, 1), None)
-    base = stencil(field, halo_rows(field), coupling.reshape(rows // vals, vals), in_plane)
-    *others, effect, base = tied((*others, effect, base))
-    effect = effects(sorted_rows, others, (2, 4, 6), effect)
-    far = [core_swap(part) for part in others]
-    return finish(slot, base, sorted_rows, far, (3, 5, 7), effect)[None]
+    own, across, plus, minus = around(plane, "yx")
+    effect = effects(sorted_rows, [own, *swap_pieces(own)], (0, 1), None)
+    minus, plus, effect = tied((minus, plus, effect))
+    effect = effects(sorted_rows, [plus, minus], (4, 6), effect)
+    base = stencil(field, own, plus, minus, coupling.reshape(rows // vals, vals), in_plane)
+    effect = effects(sorted_rows, [*swap_pieces(plus), *swap_pieces(minus)], (5, 7), effect)
+    across, effect, base = tied((across, effect, base))
+    return finish(slot, base, sorted_rows, [across, *swap_pieces(across)], (2, 3), effect)[None]
 
 
 def solution(mesh):

time: 55.9 us -> 62.4 us (1.12)
  waiting for transfers between devices: 14.3 us -> 2.77 us
  local copies, waits for them, and re-layouts: 1.88 us -> 10.7 us
  starting transfers between devices: 22.4 us -> 28.2 us
  Pallas kernels: 13.8 us -> 16.9 us
    ppermute x2 -> x0, waiting for transfers between devices: 12.4 us -> none  [the longest x1 10.1 us: halo_rows(): lax.ppermute(field[rows - 16:], 'sub', [(i, i + 1) for i in range(ends)])]
    ppermute x4 -> x16, starting transfers between devices: 6.11 us -> 16.5 us  [core_swap(): return lax.ppermute(value, axes_all, pairs)]
    unnamed x8 -> x37, local copies, waits for them, and re-layouts: 1.75 us -> 7.41 us
    ppermute x2 -> x0, starting transfers between devices: 4.88 us -> none  [the longest x1 2.84 us: halo_rows(): lax.ppermute(field[rows - 16:], 'sub', [(i, i + 1) for i in range(ends)])]
    slice x3 -> x4, local copies, waits for them, and re-layouts: 0.01 us -> 3.11 us  [swap_pieces(): value[i:i + group]]
    pallas_call x2 -> x3, Pallas kernels: 1.14 us -> 3.64 us  [effects(): pl.pallas_call(functools.partial(effect_kernel, blocks), in_specs=[in_vme...]
    pallas_call x1, Pallas kernels: 0.69 us -> 1.99 us  [stencil(): pl.pallas_call(stencil_kernel, in_specs=[pl.BlockSpec(memory_space=pltpu....]
    ppermute x9, waiting for transfers between devices: 0.02 us -> 0.88 us  [shifted(): return lax.ppermute(value, axes_all, pairs)]
  transfers between devices with their start and end apart: 15 -> 25, of which waited for: 5 -> 7; matrix products, arithmetic and copies ran while one was open for 5% -> 9% of each run, Pallas kernels for 13% -> 18%
where the time goes in v3:
time: 62.4 us; the launch traced here: 61.9 us
  starting transfers between devices  28.2 us (45%)
  Pallas kernels  16.9 us (27%)
  local copies, waits for them, and re-layouts  10.7 us (17%)
  other arithmetic  3.04 us (5%)
  waiting for transfers between devices  2.77 us (4%)
    ppermute x16, starting transfers between devices, core_swap(): return lax.ppermute(value, axes_all, pairs)  16.5 us
    ppermute x9, starting transfers between devices, shifted(): return lax.ppermute(value, axes_all, pairs)  11.7 us
    unnamed x37, local copies, waits for them, and re-layouts  7.41 us
    pallas_call x1, Pallas kernels, finish(): pl.pallas_call(functools.partial(final_kernel, blocks), in_specs=[pl.Bloc...  6.04 us
    pallas_call x1, Pallas kernels, sort_rows(): pl.pallas_call(sort_kernel, in_specs=[pl.BlockSpec(memory_space=pltpu.SME...  4.46 us
    pallas_call x3, Pallas kernels, effects(): pl.pallas_call(functools.partial(effect_kernel, blocks), in_specs=[in_vme...  3.64 us
    slice x4, local copies, waits for them, and re-layouts, swap_pieces(): value[i:i + group]  3.11 us
    pallas_call x1, Pallas kernels, stencil(): pl.pallas_call(stencil_kernel, in_specs=[pl.BlockSpec(memory_space=pltpu....  1.99 us
  transfers between devices with their start and end apart: 25, of which 7 were waited for; matrix products, arithmetic and copies ran while one was open for 9% of the time, Pallas kernels for 18%

profile of v3, /device:TPU:57, one launch (start us, length us, event | category | flops | bytes accessed | tf_op | source)
XLA Modules:
  0.0 61.9 jit_solution(15881473830367811525)
XLA Ops:
  0.0 1.7 %collective-permute-start.1 = (bf16[128,128]{1,0:T(8,128)(2,1)}, bf16[128,128]{1,0:T(8,128)(2,1)S(1)}, u32[]{:S(2)}, u32[]{:S(2)}) collective-permute-start(bf16[128,128]{1,0:T(8,128)(2,1)} %bitcast.23), channel_id=1, source_target_pairs={{0,2},{1,3},{2,4},{3,5},{4,6},{5,7},{6,0},{7,1},{8,10},{9,11},{10,... | collective-permute-start | bytes 98312 | tf_op jit(solution)/shard_map/ppermute | solution.py:46
  1.7 3.7 %collective-permute-start = (bf16[128,128]{1,0:T(8,128)(2,1)}, bf16[128,128]{1,0:T(8,128)(2,1)S(1)}, u32[]{:S(2)}, u32[]{:S(2)}) collective-permute-start(bf16[128,128]{1,0:T(8,128)(2,1)} %bitcast.24), channel_id=1, source_target_pairs={{0,4},{1,5},{2,6},{3,7},{4,0},{5,1},{6,2},{7,3},{8,12},{9,13},{10,... | collective-permute-start | bytes 98312 | tf_op jit(solution)/shard_map/ppermute | solution.py:46
  5.4 0.8 %constant_dynamic-update-slice_fusion.5 = bf16[528,128]{1,0:T(8,128)(2,1)S(1)} fusion(bf16[1,128,128]{2,1,0:T(8,128)(2,1)} %param.13), kind=kLoop, calls=%fused_computation.6 | loop fusion | bytes 65536
  6.7 1.4 %reduce.3 = s32[4096]{0:T(1024)S(1)} reduce(s32[1,4096,1]{1,2,0:T(1,128)} %param.11, s32[]{:T(128)} %broadcast.22), dimensions={0,2}, to_apply=%param.11.reduce_sub_computation.3 | reduce | bytes 32772 | tf_op args[2]
  10.4 2.2 %collective-permute-start.4 = (bf16[528,128]{1,0:T(8,128)(2,1)S(1)}, bf16[528,128]{1,0:T(8,128)(2,1)S(1)}, u32[]{:S(2)}, u32[]{:S(2)}) collective-permute-start(bf16[528,128]{1,0:T(8,128)(2,1)S(1)} %constant_dynamic-update-slice_fusion), channel_id=1, source_target_pairs={{0,8},{1,33},{2,10},{3,35},{4,12},{5,37},{6,14},{7,39},{8,16},{9,4... | collective-permute-start | bytes 405512 | tf_op jit(solution)/shard_map/ppermute | solution.py:46
  12.6 4.5 %shard_map.92.refs_0_.sorted_ref = bf16[6144,128]{1,0:T(8,128)(2,1)S(1)} custom-call(s32[4096]{0:T(1024)S(1)} %bitcast.18, bf16[4096,128]{1,0:T(8,128)(2,1)S(1)} %bitcast.16), custom_call_target="tpu_custom_call" | custom-call | bytes 20000000 | tf_op jit(solution)/shard_map/pallas_call | solution.py:118
  17.1 0.9 %collective-permute-done.3 = bf16[528,128]{1,0:T(8,128)(2,1)S(1)} collective-permute-done((bf16[528,128]{1,0:T(8,128)(2,1)S(1)}, bf16[528,128]{1,0:T(8,128)(2,1)S(1)}, u32[]{:S(2)}, u32[]{:S(2)}) %collective-permute-start.3) | collective-permute-done | bytes 135200 | tf_op jit(solution)/shard_map/ppermute | solution.py:46
  18.0 0.8 %pad_maximum_fusion.refs_1_.own_ref = bf16[2112,128]{1,0:T(8,128)(2,1)} fusion(bf16[528,128]{1,0:T(8,128)(2,1)S(1)} %collective-permute-done.5, bf16[528,128]{1,0:T(8,128)(2,1)S(1)} %collective-permute-done.4, bf16[528,128]{1,0:T(8,128)(2,1)S(1)} %collective-permute-done.3, bf16[528,128]{1,0:T(8,128)(2,1)S(1)} %constant_dynamic-update-slice_fusion), kind=kLoop, calls=%fused_computation | loop fusion | flops 2162688 | bytes 1081344 | tf_op jit(solution)/shard_map/concatenate | solution.py:277
  18.8 1.2 %collective-permute-start.8 = (bf16[2112,128]{1,0:T(8,128)(2,1)}, bf16[2112,128]{1,0:T(8,128)(2,1)S(1)}, u32[]{:S(2)}, u32[]{:S(2)}) collective-permute-start(bf16[2112,128]{1,0:T(8,128)(2,1)} %pad_maximum_fusion.refs_1_.own_ref), channel_id=1, source_target_pairs={{0,32},{1,9},{2,34},{3,11},{4,36},{5,13},{6,38},{7,15},{8,40},{9,1... | collective-permute-start | bytes 1622024 | tf_op jit(solution)/shard_map/ppermute | solution.py:46
  20.0 1.5 %collective-permute-start.7 = (bf16[2112,128]{1,0:T(8,128)(2,1)}, bf16[2112,128]{1,0:T(8,128)(2,1)S(1)}, u32[]{:S(2)}, u32[]{:S(2)}) collective-permute-start(bf16[2112,128]{1,0:T(8,128)(2,1)} %pad_maximum_fusion.refs_1_.own_ref), channel_id=1, source_target_pairs={{0,96},{1,25},{2,98},{3,27},{4,100},{5,29},{6,102},{7,31},{8,104},... | collective-permute-start | bytes 1622024 | tf_op jit(solution)/shard_map/ppermute | solution.py:46
  21.5 1.1 %fusion.16 = (bf16[512,128]{1,0:T(8,128)(2,1)S(1)}, bf16[512,128]{1,0:T(8,128)(2,1)S(1)}, bf16[512,128]{1,0:T(8,128)(2,1)S(1)}, bf16[512,128]{1,0:T(8,128)(2,1)S(1)}) fusion(bf16[2112,128]{1,0:T(8,128)(2,1)} %pad_maximum_fusion.refs_1_.own_ref), kind=kLoop, calls=%fused_computation.36 | loop fusion | bytes 1048576 | tf_op jit(solution)/shard_map/slice | solution.py:55
  22.6 3.3 %collective-permute-start.12 = (bf16[512,128]{1,0:T(8,128)(2,1)S(1)}, bf16[512,128]{1,0:T(8,128)(2,1)S(1)}, u32[]{:S(2)}, u32[]{:S(2)}) collective-permute-start(bf16[512,128]{1,0:T(8,128)(2,1)S(1)} %get-tuple-element.39), channel_id=1, source_target_pairs={{0,1},{1,0},{2,3},{3,2},{4,5},{5,4},{6,7},{7,6},{8,9},{9,8},{10,11... | collective-permute-start | bytes 393224 | tf_op jit(solution)/shard_map/ppermute | solution.py:51
  27.3 0.9 %collective-permute-start.6 = (bf16[2112,128]{1,0:T(8,128)(2,1)}, bf16[2112,128]{1,0:T(8,128)(2,1)}, u32[]{:S(2)}, u32[]{:S(2)}) collective-permute-start(bf16[2112,128]{1,0:T(8,128)(2,1)} %pad_maximum_fusion.refs_1_.own_ref), channel_id=1, source_target_pairs={{0,64},{1,17},{2,66},{3,19},{4,68},{5,21},{6,70},{7,23},{8,72},{9,... | collective-permute-start | bytes 1622024 | tf_op jit(solution)/shard_map/ppermute | solution.py:46
  28.3 1.5 %shard_map.93.refs_3_ = f32[6144,128]{1,0:T(8,128)S(1)} custom-call(bf16[6144,128]{1,0:T(8,128)(2,1)S(1)} %shard_map.92.refs_0_.sorted_ref, bf16[2112,128]{1,0:T(8,128)(2,1)} %pad_maximum_fusion.refs_1_.own_ref, bf16[512,128]{1,0:T(8,128)(2,1)S(1)} %collective-permute-done.9.refs_2_, bf16[512,128]{1,0:T(8,128)(2,1)S(1)} %collective-permute-done.10.refs_3_, ...), custom_call_target="tpu_custom_call" | custom-call | flops 1000 | bytes 1000 | tf_op jit(solution)/shard_map/pallas_call | solution.py:211
  29.9 0.9 %copy-done.3 = bf16[2112,128]{1,0:T(8,128)(2,1)} copy-done((bf16[2112,128]{1,0:T(8,128)(2,1)}, bf16[2112,128]{1,0:T(8,128)(2,1)S(1)}, u32[]{:S(2)}) %copy-start.3) | copy-done | bytes 540696
  30.8 9.6 %collective-permute-start.16 = (bf16[512,128]{1,0:T(8,128)(2,1)S(1)}, bf16[512,128]{1,0:T(8,128)(2,1)S(1)}, u32[]{:S(2)}, u32[]{:S(2)}) collective-permute-start(bf16[512,128]{1,0:T(8,128)(2,1)S(1)} %get-tuple-element.35), channel_id=1, source_target_pairs={{0,1},{1,0},{2,3},{3,2},{4,5},{5,4},{6,7},{7,6},{8,9},{9,8},{10,11... | collective-permute-start | bytes 393224 | tf_op jit(solution)/shard_map/ppermute | solution.py:51
  40.9 0.8 %fusion.14 = (bf16[512,128]{1,0:T(8,128)(2,1)}, bf16[512,128]{1,0:T(8,128)(2,1)}, bf16[512,128]{1,0:T(8,128)(2,1)}, bf16[512,128]{1,0:T(8,128)(2,1)}) fusion(bf16[2112,128]{1,0:T(8,128)(2,1)S(1)} %collective-permute-done.7.refs_2_.after_ref), kind=kLoop, calls=%fused_computation.34 | loop fusion | bytes 1048576 | tf_op jit(solution)/shard_map/slice | solution.py:55
  43.6 1.4 %copy-done.1 = bf16[6144,128]{1,0:T(8,128)(2,1)S(1)} copy-done((bf16[6144,128]{1,0:T(8,128)(2,1)S(1)}, bf16[6144,128]{1,0:T(8,128)(2,1)}, u32[]{:S(2)}) %copy-start.1) | copy-done | bytes 1572888
  45.0 1.0 %copy-done.4 = bf16[2112,128]{1,0:T(8,128)(2,1)S(1)} copy-done((bf16[2112,128]{1,0:T(8,128)(2,1)S(1)}, bf16[2112,128]{1,0:T(8,128)(2,1)}, u32[]{:S(2)}) %copy-start.4) | copy-done | bytes 540696
  46.0 1.0 %copy-done.7 = bf16[2112,128]{1,0:T(8,128)(2,1)S(1)} copy-done((bf16[2112,128]{1,0:T(8,128)(2,1)S(1)}, bf16[2112,128]{1,0:T(8,128)(2,1)}, u32[]{:S(2)}) %copy-start.7) | copy-done | bytes 540696
  48.6 2.0 %shard_map.96.base_ref = f32[4096,128]{1,0:T(8,128)S(1)} custom-call(s32[2]{0:T(128)S(1)} %pad_add_fusion.choice_ref, bf16[4096,128]{1,0:T(8,128)(2,1)S(1)} %bitcast.17, bf16[2112,128]{1,0:T(8,128)(2,1)} %pad_maximum_fusion.refs_1_.own_ref, bf16[2112,128]{1,0:T(8,128)(2,1)S(1)} %copy-done.5, bf16[2112,128]{1,0:T(8,128)(2,1)S(1)} %copy-done.8, ...), custom_call_target="tpu_custom_call" | custom-call | flops 1000 | bytes 1000 | tf_op jit(solution)/shard_map/pallas_call | solution.py:170
  50.7 1.6 %shard_map.95.refs_5_ = f32[6144,128]{1,0:T(8,128)S(1)} custom-call(bf16[6144,128]{1,0:T(8,128)(2,1)S(1)} %copy-done.2, bf16[512,128]{1,0:T(8,128)(2,1)S(1)} %copy-done.12, bf16[512,128]{1,0:T(8,128)(2,1)S(1)} %collective-permute-done.14.refs_2_, bf16[512,128]{1,0:T(8,128)(2,1)S(1)} %collective-permute-done.15.refs_3_, ...), custom_call_target="tpu_custom_call", output_to_operand_aliasing={{}: (9, {})} | custom-call | flops 1000 | bytes 1000 | tf_op jit(solution)/shard_map/pallas_call | solution.py:211
  52.3 1.1 %fusion.13 = (bf16[512,128]{1,0:T(8,128)(2,1)S(1)}, bf16[512,128]{1,0:T(8,128)(2,1)S(1)}, bf16[512,128]{1,0:T(8,128)(2,1)S(1)}, bf16[512,128]{1,0:T(8,128)(2,1)S(1)}) fusion(bf16[2112,128]{1,0:T(8,128)(2,1)} %collective-permute-done.6.refs_0_), kind=kLoop, calls=%fused_computation.33 | loop fusion | bytes 1048576 | tf_op jit(solution)/shard_map/slice | solution.py:55
  55.8 6.0 %shard_map.97 = (f32[4096,128]{1,0:T(8,128)}, f32[6144,128]{1,0:T(8,128)S(1)}) custom-call(s32[4096]{0:T(1024)S(1)} %bitcast.19, f32[4096,128]{1,0:T(8,128)S(1)} %shard_map.96.base_ref, bf16[6144,128]{1,0:T(8,128)(2,1)S(1)} %copy-done.2, bf16[2112,128]{1,0:T(8,128)(2,1)} %collective-permute-done.6.refs_0_, ...), custom_call_target="tpu_custom_call", output_to_operand_aliasing={{1}: (8, {})} | custom-call | flops 524288 | bytes 10000000 | tf_op jit(solution)/shard_map/pallas_call | solution.py:251
  (81 shorter events, 10.5 us)
Async XLA Ops:
  0.0 9.8 %collective-permute-start.2 = (bf16[128,128]{1,0:T(8,128)(2,1)}, bf16[128,128]{1,0:T(8,128)(2,1)S(1)}, u32[]{:S(2)}, u32[]{:S(2)}) collective-permute-start(bf16[128,128]{1,0:T(8,128)(2,1)} %bitcast.22), channel_id=1, source_target_pairs={{0,6},{1,7},{2,0},{3,1},{4,2},{5,3},{6,4},{7,5},{8,14},{9,15},{10,... | collective-permute-start | bytes 98312 | tf_op jit(solution)/shard_map/ppermute | solution.py:46
  0.0 9.8 %collective-permute-start.1 = (bf16[128,128]{1,0:T(8,128)(2,1)}, bf16[128,128]{1,0:T(8,128)(2,1)S(1)}, u32[]{:S(2)}, u32[]{:S(2)}) collective-permute-start(bf16[128,128]{1,0:T(8,128)(2,1)} %bitcast.23), channel_id=1, source_target_pairs={{0,2},{1,3},{2,4},{3,5},{4,6},{5,7},{6,0},{7,1},{8,10},{9,11},{10,... | collective-permute-start | bytes 98312 | tf_op jit(solution)/shard_map/ppermute | solution.py:46
  1.7 8.0 %collective-permute-start = (bf16[128,128]{1,0:T(8,128)(2,1)}, bf16[128,128]{1,0:T(8,128)(2,1)S(1)}, u32[]{:S(2)}, u32[]{:S(2)}) collective-permute-start(bf16[128,128]{1,0:T(8,128)(2,1)} %bitcast.24), channel_id=1, source_target_pairs={{0,4},{1,5},{2,6},{3,7},{4,0},{5,1},{6,2},{7,3},{8,12},{9,13},{10,... | collective-permute-start | bytes 98312 | tf_op jit(solution)/shard_map/ppermute | solution.py:46
  9.9 7.2 %collective-permute-start.5 = (bf16[528,128]{1,0:T(8,128)(2,1)S(1)}, bf16[528,128]{1,0:T(8,128)(2,1)S(1)}, u32[]{:S(2)}, u32[]{:S(2)}) collective-permute-start(bf16[528,128]{1,0:T(8,128)(2,1)S(1)} %constant_dynamic-update-slice_fusion), channel_id=1, source_target_pairs={{0,24},{1,97},{2,26},{3,99},{4,28},{5,101},{6,30},{7,103},{8,0},{9... | collective-permute-start | bytes 405512 | tf_op jit(solution)/shard_map/ppermute | solution.py:46
  10.4 6.7 %collective-permute-start.4 = (bf16[528,128]{1,0:T(8,128)(2,1)S(1)}, bf16[528,128]{1,0:T(8,128)(2,1)S(1)}, u32[]{:S(2)}, u32[]{:S(2)}) collective-permute-start(bf16[528,128]{1,0:T(8,128)(2,1)S(1)} %constant_dynamic-update-slice_fusion), channel_id=1, source_target_pairs={{0,8},{1,33},{2,10},{3,35},{4,12},{5,37},{6,14},{7,39},{8,16},{9,4... | collective-permute-start | bytes 405512 | tf_op jit(solution)/shard_map/ppermute | solution.py:46
  12.6 5.4 %collective-permute-start.3 = (bf16[528,128]{1,0:T(8,128)(2,1)S(1)}, bf16[528,128]{1,0:T(8,128)(2,1)S(1)}, u32[]{:S(2)}, u32[]{:S(2)}) collective-permute-start(bf16[528,128]{1,0:T(8,128)(2,1)S(1)} %constant_dynamic-update-slice_fusion), channel_id=1, source_target_pairs={{0,16},{1,65},{2,18},{3,67},{4,20},{5,69},{6,22},{7,71},{8,24},{9,... | collective-permute-start | bytes 405512 | tf_op jit(solution)/shard_map/ppermute | solution.py:46
  18.8 11.0 %collective-permute-start.8 = (bf16[2112,128]{1,0:T(8,128)(2,1)}, bf16[2112,128]{1,0:T(8,128)(2,1)S(1)}, u32[]{:S(2)}, u32[]{:S(2)}) collective-permute-start(bf16[2112,128]{1,0:T(8,128)(2,1)} %pad_maximum_fusion.refs_1_.own_ref), channel_id=1, source_target_pairs={{0,32},{1,9},{2,34},{3,11},{4,36},{5,13},{6,38},{7,15},{8,40},{9,1... | collective-permute-start | bytes 1622024 | tf_op jit(solution)/shard_map/ppermute | solution.py:46
  20.0 9.8 %collective-permute-start.7 = (bf16[2112,128]{1,0:T(8,128)(2,1)}, bf16[2112,128]{1,0:T(8,128)(2,1)S(1)}, u32[]{:S(2)}, u32[]{:S(2)}) collective-permute-start(bf16[2112,128]{1,0:T(8,128)(2,1)} %pad_maximum_fusion.refs_1_.own_ref), channel_id=1, source_target_pairs={{0,96},{1,25},{2,98},{3,27},{4,100},{5,29},{6,102},{7,31},{8,104},... | collective-permute-start | bytes 1622024 | tf_op jit(solution)/shard_map/ppermute | solution.py:46
  22.6 4.3 %collective-permute-start.12 = (bf16[512,128]{1,0:T(8,128)(2,1)S(1)}, bf16[512,128]{1,0:T(8,128)(2,1)S(1)}, u32[]{:S(2)}, u32[]{:S(2)}) collective-permute-start(bf16[512,128]{1,0:T(8,128)(2,1)S(1)} %get-tuple-element.39), channel_id=1, source_target_pairs={{0,1},{1,0},{2,3},{3,2},{4,5},{5,4},{6,7},{7,6},{8,9},{9,8},{10,11... | collective-permute-start | bytes 393224 | tf_op jit(solution)/shard_map/ppermute | solution.py:51
  26.0 1.4 %collective-permute-start.11 = (bf16[512,128]{1,0:T(8,128)(2,1)S(1)}, bf16[512,128]{1,0:T(8,128)(2,1)S(1)}, u32[]{:S(2)}, u32[]{:S(2)}) collective-permute-start(bf16[512,128]{1,0:T(8,128)(2,1)S(1)} %get-tuple-element.40), channel_id=1, source_target_pairs={{0,1},{1,0},{2,3},{3,2},{4,5},{5,4},{6,7},{7,6},{8,9},{9,8},{10,11... | collective-permute-start | bytes 393224 | tf_op jit(solution)/shard_map/ppermute | solution.py:51
  26.0 2.1 %collective-permute-start.10 = (bf16[512,128]{1,0:T(8,128)(2,1)S(1)}, bf16[512,128]{1,0:T(8,128)(2,1)S(1)}, u32[]{:S(2)}, u32[]{:S(2)}) collective-permute-start(bf16[512,128]{1,0:T(8,128)(2,1)S(1)} %get-tuple-element.41), channel_id=1, source_target_pairs={{0,1},{1,0},{2,3},{3,2},{4,5},{5,4},{6,7},{7,6},{8,9},{9,8},{10,11... | collective-permute-start | bytes 393224 | tf_op jit(solution)/shard_map/ppermute | solution.py:51
  26.9 1.3 %collective-permute-start.9 = (bf16[512,128]{1,0:T(8,128)(2,1)S(1)}, bf16[512,128]{1,0:T(8,128)(2,1)S(1)}, u32[]{:S(2)}, u32[]{:S(2)}) collective-permute-start(bf16[512,128]{1,0:T(8,128)(2,1)S(1)} %get-tuple-element.42), channel_id=1, source_target_pairs={{0,1},{1,0},{2,3},{3,2},{4,5},{5,4},{6,7},{7,6},{8,9},{9,8},{10,11... | collective-permute-start | bytes 393224 | tf_op jit(solution)/shard_map/ppermute | solution.py:51
  27.3 25.0 %collective-permute-start.6 = (bf16[2112,128]{1,0:T(8,128)(2,1)}, bf16[2112,128]{1,0:T(8,128)(2,1)}, u32[]{:S(2)}, u32[]{:S(2)}) collective-permute-start(bf16[2112,128]{1,0:T(8,128)(2,1)} %pad_maximum_fusion.refs_1_.own_ref), channel_id=1, source_target_pairs={{0,64},{1,17},{2,66},{3,19},{4,68},{5,21},{6,70},{7,23},{8,72},{9,... | collective-permute-start | bytes 1622024 | tf_op jit(solution)/shard_map/ppermute | solution.py:46
  30.8 10.9 %collective-permute-start.16 = (bf16[512,128]{1,0:T(8,128)(2,1)S(1)}, bf16[512,128]{1,0:T(8,128)(2,1)S(1)}, u32[]{:S(2)}, u32[]{:S(2)}) collective-permute-start(bf16[512,128]{1,0:T(8,128)(2,1)S(1)} %get-tuple-element.35), channel_id=1, source_target_pairs={{0,1},{1,0},{2,3},{3,2},{4,5},{5,4},{6,7},{7,6},{8,9},{9,8},{10,11... | collective-permute-start | bytes 393224 | tf_op jit(solution)/shard_map/ppermute | solution.py:51
  40.4 1.8 %collective-permute-start.15 = (bf16[512,128]{1,0:T(8,128)(2,1)S(1)}, bf16[512,128]{1,0:T(8,128)(2,1)S(1)}, u32[]{:S(2)}, u32[]{:S(2)}) collective-permute-start(bf16[512,128]{1,0:T(8,128)(2,1)S(1)} %get-tuple-element.36), channel_id=1, source_target_pairs={{0,1},{1,0},{2,3},{3,2},{4,5},{5,4},{6,7},{7,6},{8,9},{9,8},{10,11... | collective-permute-start | bytes 393224 | tf_op jit(solution)/shard_map/ppermute | solution.py:51
  40.4 1.9 %collective-permute-start.14 = (bf16[512,128]{1,0:T(8,128)(2,1)S(1)}, bf16[512,128]{1,0:T(8,128)(2,1)S(1)}, u32[]{:S(2)}, u32[]{:S(2)}) collective-permute-start(bf16[512,128]{1,0:T(8,128)(2,1)S(1)} %get-tuple-element.37), channel_id=1, source_target_pairs={{0,1},{1,0},{2,3},{3,2},{4,5},{5,4},{6,7},{7,6},{8,9},{9,8},{10,11... | collective-permute-start | bytes 393224 | tf_op jit(solution)/shard_map/ppermute | solution.py:51
  40.9 1.9 %collective-permute-start.13 = (bf16[512,128]{1,0:T(8,128)(2,1)S(1)}, bf16[512,128]{1,0:T(8,128)(2,1)S(1)}, u32[]{:S(2)}, u32[]{:S(2)}) collective-permute-start(bf16[512,128]{1,0:T(8,128)(2,1)S(1)} %get-tuple-element.38), channel_id=1, source_target_pairs={{0,1},{1,0},{2,3},{3,2},{4,5},{5,4},{6,7},{7,6},{8,9},{9,8},{10,11... | collective-permute-start | bytes 393224 | tf_op jit(solution)/shard_map/ppermute | solution.py:51
  41.7 8.9 %collective-permute-start.20 = (bf16[512,128]{1,0:T(8,128)(2,1)}, bf16[512,128]{1,0:T(8,128)(2,1)}, u32[]{:S(2)}, u32[]{:S(2)}) collective-permute-start(bf16[512,128]{1,0:T(8,128)(2,1)} %get-tuple-element.31), channel_id=1, source_target_pairs={{0,1},{1,0},{2,3},{3,2},{4,5},{5,4},{6,7},{7,6},{8,9},{9,8},{10,11... | collective-permute-start | bytes 393224 | tf_op jit(solution)/shard_map/ppermute | solution.py:51
  42.3 8.4 %collective-permute-start.19 = (bf16[512,128]{1,0:T(8,128)(2,1)}, bf16[512,128]{1,0:T(8,128)(2,1)}, u32[]{:S(2)}, u32[]{:S(2)}) collective-permute-start(bf16[512,128]{1,0:T(8,128)(2,1)} %get-tuple-element.32), channel_id=1, source_target_pairs={{0,1},{1,0},{2,3},{3,2},{4,5},{5,4},{6,7},{7,6},{8,9},{9,8},{10,11... | collective-permute-start | bytes 393224 | tf_op jit(solution)/shard_map/ppermute | solution.py:51
  42.3 8.3 %collective-permute-start.18 = (bf16[512,128]{1,0:T(8,128)(2,1)}, bf16[512,128]{1,0:T(8,128)(2,1)}, u32[]{:S(2)}, u32[]{:S(2)}) collective-permute-start(bf16[512,128]{1,0:T(8,128)(2,1)} %get-tuple-element.33), channel_id=1, source_target_pairs={{0,1},{1,0},{2,3},{3,2},{4,5},{5,4},{6,7},{7,6},{8,9},{9,8},{10,11... | collective-permute-start | bytes 393224 | tf_op jit(solution)/shard_map/ppermute | solution.py:51
  43.4 7.3 %collective-permute-start.17 = (bf16[512,128]{1,0:T(8,128)(2,1)}, bf16[512,128]{1,0:T(8,128)(2,1)}, u32[]{:S(2)}, u32[]{:S(2)}) collective-permute-start(bf16[512,128]{1,0:T(8,128)(2,1)} %get-tuple-element.34), channel_id=1, source_target_pairs={{0,1},{1,0},{2,3},{3,2},{4,5},{5,4},{6,7},{7,6},{8,9},{9,8},{10,11... | collective-permute-start | bytes 393224 | tf_op jit(solution)/shard_map/ppermute | solution.py:51
  53.5 1.5 %collective-permute-start.24 = (bf16[512,128]{1,0:T(8,128)(2,1)S(1)}, bf16[512,128]{1,0:T(8,128)(2,1)S(1)}, u32[]{:S(2)}, u32[]{:S(2)}) collective-permute-start(bf16[512,128]{1,0:T(8,128)(2,1)S(1)} %get-tuple-element.27), channel_id=1, source_target_pairs={{0,1},{1,0},{2,3},{3,2},{4,5},{5,4},{6,7},{7,6},{8,9},{9,8},{10,11... | collective-permute-start | bytes 393224 | tf_op jit(solution)/shard_map/ppermute | solution.py:51
  54.0 1.3 %collective-permute-start.23 = (bf16[512,128]{1,0:T(8,128)(2,1)S(1)}, bf16[512,128]{1,0:T(8,128)(2,1)S(1)}, u32[]{:S(2)}, u32[]{:S(2)}) collective-permute-start(bf16[512,128]{1,0:T(8,128)(2,1)S(1)} %get-tuple-element.28), channel_id=1, source_target_pairs={{0,1},{1,0},{2,3},{3,2},{4,5},{5,4},{6,7},{7,6},{8,9},{9,8},{10,11... | collective-permute-start | bytes 393224 | tf_op jit(solution)/shard_map/ppermute | solution.py:51
  54.0 1.4 %collective-permute-start.22 = (bf16[512,128]{1,0:T(8,128)(2,1)S(1)}, bf16[512,128]{1,0:T(8,128)(2,1)S(1)}, u32[]{:S(2)}, u32[]{:S(2)}) collective-permute-start(bf16[512,128]{1,0:T(8,128)(2,1)S(1)} %get-tuple-element.29), channel_id=1, source_target_pairs={{0,1},{1,0},{2,3},{3,2},{4,5},{5,4},{6,7},{7,6},{8,9},{9,8},{10,11... | collective-permute-start | bytes 393224 | tf_op jit(solution)/shard_map/ppermute | solution.py:51
  (16 other events, 51.0 us)

commit v4 on v3

--- a/solution.py
+++ b/solution.py
@@ -2,7 +2,6 @@
 
 import jax
 import jax.numpy as jnp
-import numpy as np
 from jax import lax
 from jax.experimental import pallas as pl
 from jax.experimental.pallas import tpu as pltpu
@@ -19,7 +18,6 @@
 unroll = 128
 group = 4 * vals
 stride = group + 16
-offsets = np.array([0, 2, -1, 1])
 vmem_bytes = 20 * 1024 * 1024
 
 
@@ -59,46 +57,46 @@
     return [value] + [shifted(value, step, axes) for step in (2, 1, -1)]
 
 
+def offset(index):
+    return jnp.where(index == 1, 2, jnp.where(index == 2, 3, jnp.where(index == 3, 1, 0)))
+
+
 def slot_owners():
     sub, lam = lax.axis_index("sub"), lax.axis_index("lam")
     y, x, z, c = sub // 4, sub % 4, lam // 2, lam % 2
-    index = np.arange(owners)
-    third, group = index // 32, (index // 16) % 2
-    second, first = (index // 4) % 4, index % 4
-    core = jnp.asarray(group, jnp.int32) ^ c
-    by_second = jnp.asarray(offsets[second], jnp.int32)
-    by_third = jnp.asarray(offsets[third], jnp.int32)
-    even = core == 0
-    dx = jnp.where(even, by_second, by_third)
-    dy = jnp.where(even, by_third, by_second)
-    dz = jnp.asarray(offsets[first], jnp.int32)
-    return (((y + dy + 4) % 4) * 4 + (x + dx + 4) % 4) * 8 + ((z + dz + 4) % 4) * 2 + core
-
-
-def rank_kernel(owner_ref, table_ref, slot_ref):
-    table = table_ref[...]
+    index = lax.broadcasted_iota(jnp.int32, (owners, chunk), 0)
+    third, side = index >> 5, (index >> 4) & 1
+    second, first = (index >> 2) & 3, index & 3
+    core = side ^ c
+    dx = jnp.where(core == 0, offset(second), offset(third))
+    dy = jnp.where(core == 0, offset(third), offset(second))
+    return ((((y + dy) & 3) << 2) + ((x + dx) & 3)) * 8 + ((z + offset(first)) & 3) * 2 + core
+
+
+def rank_kernel(owner_ref, slot_ref):
+    table = slot_owners()
     row = lax.broadcasted_iota(jnp.int32, (chunk, chunk + owners), 0)
     col = lax.broadcasted_iota(jnp.int32, (chunk, chunk + owners), 1)
     earlier = jnp.where((row < col) | (col >= chunk), 1.0, 0.0).astype(jnp.bfloat16)
     start = cap * lax.broadcasted_iota(jnp.int32, (owners, owners), 0).astype(jnp.float32)
-    for j in range(rows // chunk):
-        hit = table == owner_ref[j : j + 1, :]
+    for j in range(0, rows, chunk):
+        hit = table == owner_ref[:, j : j + chunk]
         count = jnp.dot(
             jnp.where(hit, 1.0, 0.0).astype(jnp.bfloat16), earlier, preferred_element_type=jnp.float32
         )
         place = count[:, :chunk] + jnp.concatenate([start, start], axis=1)
         slot = jnp.sum(jnp.where(hit, place, 0.0), axis=0, keepdims=True)
-        slot_ref[j : j + 1, :] = slot.astype(jnp.int32)
+        slot_ref[:, j : j + chunk] = slot.astype(jnp.int32)
         start = start + count[:, chunk:]
 
 
-def rank(owner, table):
+def rank(owner):
     return pl.pallas_call(
         rank_kernel,
-        out_shape=jax.ShapeDtypeStruct((rows // chunk, chunk), jnp.int32),
+        out_shape=jax.ShapeDtypeStruct((1, rows), jnp.int32),
         compiler_params=params(),
         cost_estimate=pl.CostEstimate(flops=2 * 128 * 4096 * 384, bytes_accessed=100000, transcendentals=0),
-    )(owner, table)
+    )(owner)
 
 
 def sort_kernel(slot_ref, field_ref, sorted_ref, wide, placed):
@@ -125,14 +123,6 @@
     )(slot, field)
 
 
-def halo_choice():
-    sub, lam = lax.axis_index("sub"), lax.axis_index("lam")
-    x, inner = sub % 4, jnp.where(lam % 2 == 0, 0, 2)
-    before = jnp.where(sub == 0, 3, jnp.where(x == 0, 1, inner))
-    after = jnp.where(sub == 15, 3, jnp.where(x == 3, 1, inner))
-    return jnp.stack([before, after]).astype(jnp.int32)
-
-
 def halo(choice, own_ref, next_ref, label):
     def ends(ref, second):
         top = second * stride + group
@@ -145,11 +135,15 @@
 
 
 def stencil_kernel(
-    choice_ref, field_ref, own_ref, before_ref, after_ref, coupling_ref, plane_ref, base_ref, projected
+    field_ref, own_ref, before_ref, after_ref, coupling_ref, plane_ref, base_ref, projected
 ):
     plane = plane_ref[...]
-    before = halo(choice_ref[0], own_ref, before_ref, 2)
-    after = halo(choice_ref[1], own_ref, after_ref, 3)
+    sub, lam = lax.axis_index("sub"), lax.axis_index("lam")
+    x, inner = sub % 4, jnp.where(lam % 2 == 0, 0, 2)
+    choice = jnp.where(sub == 0, 3, jnp.where(x == 0, 1, inner))
+    before = halo(choice, own_ref, before_ref, 2)
+    choice = jnp.where(sub == 15, 3, jnp.where(x == 3, 1, inner))
+    after = halo(choice, own_ref, after_ref, 3)
     projected[0:8, :] = jnp.dot(before, plane, preferred_element_type=jnp.float32)[8:16]
     projected[rows + 8 : rows + 16, :] = jnp.dot(after, plane, preferred_element_type=jnp.float32)[0:8]
     for j in range(rows // 512):
@@ -169,13 +163,13 @@
 def stencil(field, own, before, after, coupling, plane):
     return pl.pallas_call(
         stencil_kernel,
-        in_specs=[pl.BlockSpec(memory_space=pltpu.SMEM)] + [in_vmem] * 6,
+        in_specs=[in_vmem] * 6,
         out_specs=in_vmem,
         out_shape=jax.ShapeDtypeStruct((rows, vals), jnp.float32),
         scratch_shapes=[pltpu.VMEM((rows + 16, vals), jnp.float32)],
         compiler_params=params(),
         cost_estimate=pl.CostEstimate(flops=1000, bytes_accessed=1000, transcendentals=0),
-    )(halo_choice(), field, own, before, after, coupling, plane)
+    )(field, own, before, after, coupling, plane)
 
 
 def respond(block, operator):
@@ -271,8 +265,7 @@
     tied = lax.optimization_barrier
     ends = jnp.concatenate([field[:8], field[rows - 8 :]], axis=0)
     near = jnp.concatenate([*around(profile_op[0], "zz"), ends], axis=0)
-    table = slot_owners()[:, None]
-    slot = rank(owner_map.reshape(rows // chunk, chunk), table).reshape(rows)
+    slot = rank(owner_map.transpose(0, 2, 1)[0]).reshape(rows)
     near, slot = tied((near, slot))
     plane = jnp.concatenate(around(near, "xy"), axis=0)
     sorted_rows = sort_rows(slot, field)

time: 62.4 us -> 49.4 us (0.79)
  the two profiles are of different devices: /device:TPU:57 before, /device:TPU:27 now
where the time goes in v4:
time: 49.4 us; the launch traced here: 49.2 us
  starting transfers between devices  30.1 us (61%)
  Pallas kernels  13.2 us (27%)
  waiting for transfers between devices  3.93 us (8%)
  local copies, waits for them, and re-layouts  1.74 us (4%)
    ppermute x16, starting transfers between devices, core_swap(): return lax.ppermute(value, axes_all, pairs)  19 us
    ppermute x9, starting transfers between devices, shifted(): return lax.ppermute(value, axes_all, pairs)  11.1 us
    pallas_call x1, Pallas kernels, finish(): pl.pallas_call(functools.partial(final_kernel, blocks), in_specs=[pl.Bloc...  5.78 us
    pallas_call x1, Pallas kernels, sort_rows(): pl.pallas_call(sort_kernel, in_specs=[pl.BlockSpec(memory_space=pltpu.SME...  4.46 us
    ppermute x9, waiting for transfers between devices, shifted(): return lax.ppermute(value, axes_all, pairs)  1.96 us
    ppermute x16, waiting for transfers between devices, core_swap(): return lax.ppermute(value, axes_all, pairs)  1.96 us
    unnamed x13, local copies, waits for them, and re-layouts  1.59 us
    pallas_call x3, Pallas kernels, effects(): pl.pallas_call(functools.partial(effect_kernel, blocks), in_specs=[in_vme...  1.49 us
  transfers between devices with their start and end apart: 25, of which 9 were waited for; matrix products, arithmetic and copies ran while one was open for 2% of the time, Pallas kernels for 15%

profile of v4, /device:TPU:27, one launch (start us, length us, event | category | flops | bytes accessed | tf_op | source)
XLA Modules:
  0.0 49.2 jit_solution(9526464662769443188)
XLA Ops:
  0.0 3.8 %collective-permute-start.2 = (bf16[128,128]{1,0:T(8,128)(2,1)}, bf16[128,128]{1,0:T(8,128)(2,1)S(1)}, u32[]{:S(2)}, u32[]{:S(2)}) collective-permute-start(bf16[128,128]{1,0:T(8,128)(2,1)} %bitcast.17), channel_id=1, source_target_pairs={{0,6},{1,7},{2,0},{3,1},{4,2},{5,3},{6,4},{7,5},{8,14},{9,15},{10,... | collective-permute-start | bytes 98312 | tf_op jit(solution)/shard_map/ppermute | solution.py:44
  3.8 1.3 %collective-permute-start = (bf16[128,128]{1,0:T(8,128)(2,1)}, bf16[128,128]{1,0:T(8,128)(2,1)S(1)}, u32[]{:S(2)}, u32[]{:S(2)}) collective-permute-start(bf16[128,128]{1,0:T(8,128)(2,1)} %bitcast.19), channel_id=1, source_target_pairs={{0,4},{1,5},{2,6},{3,7},{4,0},{5,1},{6,2},{7,3},{8,12},{9,13},{10,... | collective-permute-start | bytes 98312 | tf_op jit(solution)/shard_map/ppermute | solution.py:44
  5.1 0.8 %constant_dynamic-update-slice_fusion.5 = bf16[528,128]{1,0:T(8,128)(2,1)S(1)} fusion(bf16[1,128,128]{2,1,0:T(8,128)(2,1)} %param.9), kind=kLoop, calls=%fused_computation.6 | loop fusion | bytes 65536
  5.9 0.7 %copy-done.3 = s32[1,4096,1]{1,2,0:T(1,128)S(1)} copy-done((s32[1,4096,1]{1,2,0:T(1,128)S(1)}, s32[1,4096,1]{1,2,0:T(1,128)}, u32[]{:S(2)}) %copy-start.3) | copy-done | bytes 16408
  6.6 0.8 %shard_map.55 = s32[1,4096]{1,0:T(1,128)S(1)} custom-call(s32[1,4096]{1,0:T(1,128)S(1)} %bitcast.16), custom_call_target="tpu_custom_call" | custom-call | flops 402653184 | bytes 100000 | tf_op jit(solution)/shard_map/pallas_call | solution.py:94
  7.3 1.0 %collective-permute-done = bf16[128,128]{1,0:T(8,128)(2,1)S(1)} collective-permute-done((bf16[128,128]{1,0:T(8,128)(2,1)}, bf16[128,128]{1,0:T(8,128)(2,1)S(1)}, u32[]{:S(2)}, u32[]{:S(2)}) %collective-permute-start) | collective-permute-done | bytes 32800 | tf_op jit(solution)/shard_map/ppermute | solution.py:44
  8.4 0.5 %collective-permute-start.5 = (bf16[528,128]{1,0:T(8,128)(2,1)S(1)}, bf16[528,128]{1,0:T(8,128)(2,1)S(1)}, u32[]{:S(2)}, u32[]{:S(2)}) collective-permute-start(bf16[528,128]{1,0:T(8,128)(2,1)S(1)} %constant_dynamic-update-slice_fusion), channel_id=1, source_target_pairs={{0,24},{1,97},{2,26},{3,99},{4,28},{5,101},{6,30},{7,103},{8,0},{9... | collective-permute-start | bytes 405512 | tf_op jit(solution)/shard_map/ppermute | solution.py:44
  9.0 2.2 %collective-permute-start.4 = (bf16[528,128]{1,0:T(8,128)(2,1)S(1)}, bf16[528,128]{1,0:T(8,128)(2,1)S(1)}, u32[]{:S(2)}, u32[]{:S(2)}) collective-permute-start(bf16[528,128]{1,0:T(8,128)(2,1)S(1)} %constant_dynamic-update-slice_fusion), channel_id=1, source_target_pairs={{0,8},{1,33},{2,10},{3,35},{4,12},{5,37},{6,14},{7,39},{8,16},{9,4... | collective-permute-start | bytes 405512 | tf_op jit(solution)/shard_map/ppermute | solution.py:44
  11.2 4.5 %shard_map.56.refs_0_.sorted_ref = bf16[6144,128]{1,0:T(8,128)(2,1)S(1)} custom-call(s32[4096]{0:T(1024)S(1)} %bitcast.13, bf16[4096,128]{1,0:T(8,128)(2,1)S(1)} %bitcast.11), custom_call_target="tpu_custom_call" | custom-call | bytes 20000000 | tf_op jit(solution)/shard_map/pallas_call | solution.py:116
  15.7 0.9 %collective-permute-done.3 = bf16[528,128]{1,0:T(8,128)(2,1)S(1)} collective-permute-done((bf16[528,128]{1,0:T(8,128)(2,1)S(1)}, bf16[528,128]{1,0:T(8,128)(2,1)S(1)}, u32[]{:S(2)}, u32[]{:S(2)}) %collective-permute-start.3) | collective-permute-done | bytes 135200 | tf_op jit(solution)/shard_map/ppermute | solution.py:44
  16.6 1.3 %collective-permute-start.8 = (bf16[2112,128]{1,0:T(8,128)(2,1)S(1)}, bf16[2112,128]{1,0:T(8,128)(2,1)S(1)}, u32[]{:S(2)}, u32[]{:S(2)}) collective-permute-start(bf16[2112,128]{1,0:T(8,128)(2,1)S(1)} %pad_maximum_fusion.refs_1_.own_ref), channel_id=1, source_target_pairs={{0,32},{1,9},{2,34},{3,11},{4,36},{5,13},{6,38},{7,15},{8,40},{9,1... | collective-permute-start | bytes 1622024 | tf_op jit(solution)/shard_map/ppermute | solution.py:44
  18.2 4.5 %collective-permute-start.12 = (bf16[512,128]{1,0:T(8,128)(2,1)S(1)}, bf16[512,128]{1,0:T(8,128)(2,1)S(1)}, u32[]{:S(2)}, u32[]{:S(2)}) collective-permute-start(bf16[512,128]{1,0:T(8,128)(2,1)S(1)} %get-tuple-element.39), channel_id=1, source_target_pairs={{0,1},{1,0},{2,3},{3,2},{4,5},{5,4},{6,7},{7,6},{8,9},{9,8},{10,11... | collective-permute-start | bytes 393224 | tf_op jit(solution)/shard_map/ppermute | solution.py:49
  22.8 0.4 collective-permute-start.10
  23.2 0.5 collective-permute-done.12.refs_5_
  23.7 0.4 collective-permute-start.9
  24.0 1.7 %collective-permute-start.6 = (bf16[2112,128]{1,0:T(8,128)(2,1)S(1)}, bf16[2112,128]{1,0:T(8,128)(2,1)S(1)}, u32[]{:S(2)}, u32[]{:S(2)}) collective-permute-start(bf16[2112,128]{1,0:T(8,128)(2,1)S(1)} %pad_maximum_fusion.refs_1_.own_ref), channel_id=1, source_target_pairs={{0,64},{1,17},{2,66},{3,19},{4,68},{5,21},{6,70},{7,23},{8,72},{9,... | collective-permute-start | bytes 1622024 | tf_op jit(solution)/shard_map/ppermute | solution.py:44
  25.8 0.5 %shard_map.57.refs_3_ = f32[6144,128]{1,0:T(8,128)S(1)} custom-call(bf16[6144,128]{1,0:T(8,128)(2,1)S(1)} %shard_map.56.refs_0_.sorted_ref, bf16[2112,128]{1,0:T(8,128)(2,1)S(1)} %pad_maximum_fusion.refs_1_.own_ref, bf16[512,128]{1,0:T(8,128)(2,1)S(1)} %collective-permute-done.9.refs_2_, bf16[512,128]{1,0:T(8,128)(2,1)S(1)} %collective-permute-done.10.refs_3_, ...), custom_call_target="tpu_custom_call" | custom-call | flops 1000 | bytes 1000 | tf_op jit(solution)/shard_map/pallas_call | solution.py:205
  26.4 10.8 %collective-permute-start.16 = (bf16[512,128]{1,0:T(8,128)(2,1)S(1)}, bf16[512,128]{1,0:T(8,128)(2,1)S(1)}, u32[]{:S(2)}, u32[]{:S(2)}) collective-permute-start(bf16[512,128]{1,0:T(8,128)(2,1)S(1)} %get-tuple-element.35), channel_id=1, source_target_pairs={{0,1},{1,0},{2,3},{3,2},{4,5},{5,4},{6,7},{7,6},{8,9},{9,8},{10,11... | collective-permute-start | bytes 393224 | tf_op jit(solution)/shard_map/ppermute | solution.py:49
  37.3 0.4 collective-permute-start.14
  38.2 0.4 collective-permute-start.20
  39.3 0.5 %shard_map.58.refs_9_ = f32[6144,128]{1,0:T(8,128)S(1)} custom-call(bf16[6144,128]{1,0:T(8,128)(2,1)S(1)} %shard_map.56.refs_0_.sorted_ref, bf16[2112,128]{1,0:T(8,128)(2,1)S(1)} %collective-permute-done.8.refs_1_.before_ref, bf16[2112,128]{1,0:T(8,128)(2,1)S(1)} %collective-permute-done.7.refs_2_.after_ref, ...), custom_call_target="tpu_custom_call", output_to_operand_aliasing={{}: (3, {})} | custom-call | flops 1000 | bytes 1000 | tf_op jit(solution)/shard_map/pallas_call | solution.py:205
  39.9 0.7 %shard_map.60.base_ref = f32[4096,128]{1,0:T(8,128)S(1)} custom-call(bf16[4096,128]{1,0:T(8,128)(2,1)S(1)} %bitcast.12, bf16[2112,128]{1,0:T(8,128)(2,1)S(1)} %pad_maximum_fusion.refs_1_.own_ref, bf16[2112,128]{1,0:T(8,128)(2,1)S(1)} %collective-permute-done.8.refs_1_.before_ref, bf16[2112,128]{1,0:T(8,128)(2,1)S(1)} %collective-permute-done.7.refs_2_.after_ref, ...), custom_call_target="tpu_custom_call" | custom-call | flops 1000 | bytes 1000 | tf_op jit(solution)/shard_map/pallas_call | solution.py:164
  40.6 0.5 %shard_map.59.refs_5_ = f32[6144,128]{1,0:T(8,128)S(1)} custom-call(bf16[6144,128]{1,0:T(8,128)(2,1)S(1)} %shard_map.56.refs_0_.sorted_ref, bf16[512,128]{1,0:T(8,128)(2,1)S(1)} %collective-permute-done.13.refs_1_, bf16[512,128]{1,0:T(8,128)(2,1)S(1)} %collective-permute-done.14.refs_2_, ...), custom_call_target="tpu_custom_call", output_to_operand_aliasing={{}: (9, {})} | custom-call | flops 1000 | bytes 1000 | tf_op jit(solution)/shard_map/pallas_call | solution.py:205
  43.4 5.8 %shard_map.61 = (f32[4096,128]{1,0:T(8,128)}, f32[6144,128]{1,0:T(8,128)S(1)}) custom-call(s32[4096]{0:T(1024)S(1)} %bitcast.14, f32[4096,128]{1,0:T(8,128)S(1)} %shard_map.60.base_ref, bf16[6144,128]{1,0:T(8,128)(2,1)S(1)} %shard_map.56.refs_0_.sorted_ref, bf16[2112,128]{1,0:T(8,128)(2,1)S(1)} %collective-permute-done.6.refs_0_, ...), custom_call_target="tpu_custom_call", output_to_operand_aliasing={{1}: (8, {})} | custom-call | flops 524288 | bytes 10000000 | tf_op jit(solution)/shard_map/pallas_call | solution.py:245
  (52 shorter events, 4.2 us)
Async XLA Ops:
  0.0 8.4 %collective-permute-start.2 = (bf16[128,128]{1,0:T(8,128)(2,1)}, bf16[128,128]{1,0:T(8,128)(2,1)S(1)}, u32[]{:S(2)}, u32[]{:S(2)}) collective-permute-start(bf16[128,128]{1,0:T(8,128)(2,1)} %bitcast.17), channel_id=1, source_target_pairs={{0,6},{1,7},{2,0},{3,1},{4,2},{5,3},{6,4},{7,5},{8,14},{9,15},{10,... | collective-permute-start | bytes 98312 | tf_op jit(solution)/shard_map/ppermute | solution.py:44
  3.8 4.6 %collective-permute-start.1 = (bf16[128,128]{1,0:T(8,128)(2,1)}, bf16[128,128]{1,0:T(8,128)(2,1)S(1)}, u32[]{:S(2)}, u32[]{:S(2)}) collective-permute-start(bf16[128,128]{1,0:T(8,128)(2,1)} %bitcast.18), channel_id=1, source_target_pairs={{0,2},{1,3},{2,4},{3,5},{4,6},{5,7},{6,0},{7,1},{8,10},{9,11},{10,... | collective-permute-start | bytes 98312 | tf_op jit(solution)/shard_map/ppermute | solution.py:44
  3.8 4.6 %collective-permute-start = (bf16[128,128]{1,0:T(8,128)(2,1)}, bf16[128,128]{1,0:T(8,128)(2,1)S(1)}, u32[]{:S(2)}, u32[]{:S(2)}) collective-permute-start(bf16[128,128]{1,0:T(8,128)(2,1)} %bitcast.19), channel_id=1, source_target_pairs={{0,4},{1,5},{2,6},{3,7},{4,0},{5,1},{6,2},{7,3},{8,12},{9,13},{10,... | collective-permute-start | bytes 98312 | tf_op jit(solution)/shard_map/ppermute | solution.py:44
  8.4 7.2 %collective-permute-start.5 = (bf16[528,128]{1,0:T(8,128)(2,1)S(1)}, bf16[528,128]{1,0:T(8,128)(2,1)S(1)}, u32[]{:S(2)}, u32[]{:S(2)}) collective-permute-start(bf16[528,128]{1,0:T(8,128)(2,1)S(1)} %constant_dynamic-update-slice_fusion), channel_id=1, source_target_pairs={{0,24},{1,97},{2,26},{3,99},{4,28},{5,101},{6,30},{7,103},{8,0},{9... | collective-permute-start | bytes 405512 | tf_op jit(solution)/shard_map/ppermute | solution.py:44
  9.0 6.7 %collective-permute-start.4 = (bf16[528,128]{1,0:T(8,128)(2,1)S(1)}, bf16[528,128]{1,0:T(8,128)(2,1)S(1)}, u32[]{:S(2)}, u32[]{:S(2)}) collective-permute-start(bf16[528,128]{1,0:T(8,128)(2,1)S(1)} %constant_dynamic-update-slice_fusion), channel_id=1, source_target_pairs={{0,8},{1,33},{2,10},{3,35},{4,12},{5,37},{6,14},{7,39},{8,16},{9,4... | collective-permute-start | bytes 405512 | tf_op jit(solution)/shard_map/ppermute | solution.py:44
  11.2 5.4 %collective-permute-start.3 = (bf16[528,128]{1,0:T(8,128)(2,1)S(1)}, bf16[528,128]{1,0:T(8,128)(2,1)S(1)}, u32[]{:S(2)}, u32[]{:S(2)}) collective-permute-start(bf16[528,128]{1,0:T(8,128)(2,1)S(1)} %constant_dynamic-update-slice_fusion), channel_id=1, source_target_pairs={{0,16},{1,65},{2,18},{3,67},{4,20},{5,69},{6,22},{7,71},{8,24},{9,... | collective-permute-start | bytes 405512 | tf_op jit(solution)/shard_map/ppermute | solution.py:44
  16.6 9.7 %collective-permute-start.8 = (bf16[2112,128]{1,0:T(8,128)(2,1)S(1)}, bf16[2112,128]{1,0:T(8,128)(2,1)S(1)}, u32[]{:S(2)}, u32[]{:S(2)}) collective-permute-start(bf16[2112,128]{1,0:T(8,128)(2,1)S(1)} %pad_maximum_fusion.refs_1_.own_ref), channel_id=1, source_target_pairs={{0,32},{1,9},{2,34},{3,11},{4,36},{5,13},{6,38},{7,15},{8,40},{9,1... | collective-permute-start | bytes 1622024 | tf_op jit(solution)/shard_map/ppermute | solution.py:44
  17.9 8.5 %collective-permute-start.7 = (bf16[2112,128]{1,0:T(8,128)(2,1)S(1)}, bf16[2112,128]{1,0:T(8,128)(2,1)S(1)}, u32[]{:S(2)}, u32[]{:S(2)}) collective-permute-start(bf16[2112,128]{1,0:T(8,128)(2,1)S(1)} %pad_maximum_fusion.refs_1_.own_ref), channel_id=1, source_target_pairs={{0,96},{1,25},{2,98},{3,27},{4,100},{5,29},{6,102},{7,31},{8,104},... | collective-permute-start | bytes 1622024 | tf_op jit(solution)/shard_map/ppermute | solution.py:44
  18.2 5.5 %collective-permute-start.12 = (bf16[512,128]{1,0:T(8,128)(2,1)S(1)}, bf16[512,128]{1,0:T(8,128)(2,1)S(1)}, u32[]{:S(2)}, u32[]{:S(2)}) collective-permute-start(bf16[512,128]{1,0:T(8,128)(2,1)S(1)} %get-tuple-element.39), channel_id=1, source_target_pairs={{0,1},{1,0},{2,3},{3,2},{4,5},{5,4},{6,7},{7,6},{8,9},{9,8},{10,11... | collective-permute-start | bytes 393224 | tf_op jit(solution)/shard_map/ppermute | solution.py:49
  22.7 1.4 %collective-permute-start.11 = (bf16[512,128]{1,0:T(8,128)(2,1)S(1)}, bf16[512,128]{1,0:T(8,128)(2,1)S(1)}, u32[]{:S(2)}, u32[]{:S(2)}) collective-permute-start(bf16[512,128]{1,0:T(8,128)(2,1)S(1)} %get-tuple-element.40), channel_id=1, source_target_pairs={{0,1},{1,0},{2,3},{3,2},{4,5},{5,4},{6,7},{7,6},{8,9},{9,8},{10,11... | collective-permute-start | bytes 393224 | tf_op jit(solution)/shard_map/ppermute | solution.py:49
  22.8 3.0 %collective-permute-start.10 = (bf16[512,128]{1,0:T(8,128)(2,1)S(1)}, bf16[512,128]{1,0:T(8,128)(2,1)S(1)}, u32[]{:S(2)}, u32[]{:S(2)}) collective-permute-start(bf16[512,128]{1,0:T(8,128)(2,1)S(1)} %get-tuple-element.41), channel_id=1, source_target_pairs={{0,1},{1,0},{2,3},{3,2},{4,5},{5,4},{6,7},{7,6},{8,9},{9,8},{10,11... | collective-permute-start | bytes 393224 | tf_op jit(solution)/shard_map/ppermute | solution.py:49
  23.7 2.1 %collective-permute-start.9 = (bf16[512,128]{1,0:T(8,128)(2,1)S(1)}, bf16[512,128]{1,0:T(8,128)(2,1)S(1)}, u32[]{:S(2)}, u32[]{:S(2)}) collective-permute-start(bf16[512,128]{1,0:T(8,128)(2,1)S(1)} %get-tuple-element.42), channel_id=1, source_target_pairs={{0,1},{1,0},{2,3},{3,2},{4,5},{5,4},{6,7},{7,6},{8,9},{9,8},{10,11... | collective-permute-start | bytes 393224 | tf_op jit(solution)/shard_map/ppermute | solution.py:49
  24.0 17.1 %collective-permute-start.6 = (bf16[2112,128]{1,0:T(8,128)(2,1)S(1)}, bf16[2112,128]{1,0:T(8,128)(2,1)S(1)}, u32[]{:S(2)}, u32[]{:S(2)}) collective-permute-start(bf16[2112,128]{1,0:T(8,128)(2,1)S(1)} %pad_maximum_fusion.refs_1_.own_ref), channel_id=1, source_target_pairs={{0,64},{1,17},{2,66},{3,19},{4,68},{5,21},{6,70},{7,23},{8,72},{9,... | collective-permute-start | bytes 1622024 | tf_op jit(solution)/shard_map/ppermute | solution.py:44
  26.4 11.8 %collective-permute-start.16 = (bf16[512,128]{1,0:T(8,128)(2,1)S(1)}, bf16[512,128]{1,0:T(8,128)(2,1)S(1)}, u32[]{:S(2)}, u32[]{:S(2)}) collective-permute-start(bf16[512,128]{1,0:T(8,128)(2,1)S(1)} %get-tuple-element.35), channel_id=1, source_target_pairs={{0,1},{1,0},{2,3},{3,2},{4,5},{5,4},{6,7},{7,6},{8,9},{9,8},{10,11... | collective-permute-start | bytes 393224 | tf_op jit(solution)/shard_map/ppermute | solution.py:49
  37.2 1.4 %collective-permute-start.15 = (bf16[512,128]{1,0:T(8,128)(2,1)S(1)}, bf16[512,128]{1,0:T(8,128)(2,1)S(1)}, u32[]{:S(2)}, u32[]{:S(2)}) collective-permute-start(bf16[512,128]{1,0:T(8,128)(2,1)S(1)} %get-tuple-element.36), channel_id=1, source_target_pairs={{0,1},{1,0},{2,3},{3,2},{4,5},{5,4},{6,7},{7,6},{8,9},{9,8},{10,11... | collective-permute-start | bytes 393224 | tf_op jit(solution)/shard_map/ppermute | solution.py:49
  37.3 1.4 %collective-permute-start.14 = (bf16[512,128]{1,0:T(8,128)(2,1)S(1)}, bf16[512,128]{1,0:T(8,128)(2,1)S(1)}, u32[]{:S(2)}, u32[]{:S(2)}) collective-permute-start(bf16[512,128]{1,0:T(8,128)(2,1)S(1)} %get-tuple-element.37), channel_id=1, source_target_pairs={{0,1},{1,0},{2,3},{3,2},{4,5},{5,4},{6,7},{7,6},{8,9},{9,8},{10,11... | collective-permute-start | bytes 393224 | tf_op jit(solution)/shard_map/ppermute | solution.py:49
  37.7 1.4 %collective-permute-start.13 = (bf16[512,128]{1,0:T(8,128)(2,1)S(1)}, bf16[512,128]{1,0:T(8,128)(2,1)S(1)}, u32[]{:S(2)}, u32[]{:S(2)}) collective-permute-start(bf16[512,128]{1,0:T(8,128)(2,1)S(1)} %get-tuple-element.38), channel_id=1, source_target_pairs={{0,1},{1,0},{2,3},{3,2},{4,5},{5,4},{6,7},{7,6},{8,9},{9,8},{10,11... | collective-permute-start | bytes 393224 | tf_op jit(solution)/shard_map/ppermute | solution.py:49
  38.2 2.4 %collective-permute-start.20 = (bf16[512,128]{1,0:T(8,128)(2,1)S(1)}, bf16[512,128]{1,0:T(8,128)(2,1)S(1)}, u32[]{:S(2)}, u32[]{:S(2)}) collective-permute-start(bf16[512,128]{1,0:T(8,128)(2,1)S(1)} %get-tuple-element.31), channel_id=1, source_target_pairs={{0,1},{1,0},{2,3},{3,2},{4,5},{5,4},{6,7},{7,6},{8,9},{9,8},{10,11... | collective-permute-start | bytes 393224 | tf_op jit(solution)/shard_map/ppermute | solution.py:49
  38.6 2.0 %collective-permute-start.19 = (bf16[512,128]{1,0:T(8,128)(2,1)S(1)}, bf16[512,128]{1,0:T(8,128)(2,1)S(1)}, u32[]{:S(2)}, u32[]{:S(2)}) collective-permute-start(bf16[512,128]{1,0:T(8,128)(2,1)S(1)} %get-tuple-element.32), channel_id=1, source_target_pairs={{0,1},{1,0},{2,3},{3,2},{4,5},{5,4},{6,7},{7,6},{8,9},{9,8},{10,11... | collective-permute-start | bytes 393224 | tf_op jit(solution)/shard_map/ppermute | solution.py:49
  38.8 1.8 %collective-permute-start.18 = (bf16[512,128]{1,0:T(8,128)(2,1)S(1)}, bf16[512,128]{1,0:T(8,128)(2,1)S(1)}, u32[]{:S(2)}, u32[]{:S(2)}) collective-permute-start(bf16[512,128]{1,0:T(8,128)(2,1)S(1)} %get-tuple-element.33), channel_id=1, source_target_pairs={{0,1},{1,0},{2,3},{3,2},{4,5},{5,4},{6,7},{7,6},{8,9},{9,8},{10,11... | collective-permute-start | bytes 393224 | tf_op jit(solution)/shard_map/ppermute | solution.py:49
  39.1 1.5 %collective-permute-start.17 = (bf16[512,128]{1,0:T(8,128)(2,1)S(1)}, bf16[512,128]{1,0:T(8,128)(2,1)S(1)}, u32[]{:S(2)}, u32[]{:S(2)}) collective-permute-start(bf16[512,128]{1,0:T(8,128)(2,1)S(1)} %get-tuple-element.34), channel_id=1, source_target_pairs={{0,1},{1,0},{2,3},{3,2},{4,5},{5,4},{6,7},{7,6},{8,9},{9,8},{10,11... | collective-permute-start | bytes 393224 | tf_op jit(solution)/shard_map/ppermute | solution.py:49
  41.2 1.4 %collective-permute-start.24 = (bf16[512,128]{1,0:T(8,128)(2,1)S(1)}, bf16[512,128]{1,0:T(8,128)(2,1)S(1)}, u32[]{:S(2)}, u32[]{:S(2)}) collective-permute-start(bf16[512,128]{1,0:T(8,128)(2,1)S(1)} %get-tuple-element.27), channel_id=1, source_target_pairs={{0,1},{1,0},{2,3},{3,2},{4,5},{5,4},{6,7},{7,6},{8,9},{9,8},{10,11... | collective-permute-start | bytes 393224 | tf_op jit(solution)/shard_map/ppermute | solution.py:49
  41.5 1.3 %collective-permute-start.23 = (bf16[512,128]{1,0:T(8,128)(2,1)S(1)}, bf16[512,128]{1,0:T(8,128)(2,1)S(1)}, u32[]{:S(2)}, u32[]{:S(2)}) collective-permute-start(bf16[512,128]{1,0:T(8,128)(2,1)S(1)} %get-tuple-element.28), channel_id=1, source_target_pairs={{0,1},{1,0},{2,3},{3,2},{4,5},{5,4},{6,7},{7,6},{8,9},{9,8},{10,11... | collective-permute-start | bytes 393224 | tf_op jit(solution)/shard_map/ppermute | solution.py:49
  41.8 1.3 %collective-permute-start.22 = (bf16[512,128]{1,0:T(8,128)(2,1)S(1)}, bf16[512,128]{1,0:T(8,128)(2,1)S(1)}, u32[]{:S(2)}, u32[]{:S(2)}) collective-permute-start(bf16[512,128]{1,0:T(8,128)(2,1)S(1)} %get-tuple-element.29), channel_id=1, source_target_pairs={{0,1},{1,0},{2,3},{3,2},{4,5},{5,4},{6,7},{7,6},{8,9},{9,8},{10,11... | collective-permute-start | bytes 393224 | tf_op jit(solution)/shard_map/ppermute | solution.py:49
  (5 other events, 12.0 us)

commit v5 on v4

--- a/solution.py
+++ b/solution.py
@@ -32,16 +32,19 @@
     return ((y % 4) * 4 + (x % 4)) * 8 + (z % 4) * 2 + (c % 2)
 
 
-def shifted(value, step, axes):
+def shifted(value, moves):
     pairs = []
     for y in range(4):
         for x in range(4):
             for z in range(4):
                 for c in range(2):
-                    place = dict(y=y, x=x, z=z, c=c)
-                    place[axes[c]] += step
-                    pairs.append((device(y, x, z, c), device(**place)))
+                    dy, dx, dz = moves[c]
+                    pairs.append((device(y, x, z, c), device(y + dy, x + dx, z + dz, c)))
     return lax.ppermute(value, axes_all, pairs)
+
+
+def scaled(moves, step):
+    return [tuple(step * part for part in move) for move in moves]
 
 
 def core_swap(value):
@@ -53,8 +56,14 @@
     return [core_swap(value[i : i + group]) for i in range(0, value.shape[0], stride)]
 
 
-def around(value, axes):
-    return [value] + [shifted(value, step, axes) for step in (2, 1, -1)]
+first_moves = [(2, 0, 1), (0, 2, 1)]
+second_moves = [(0, 1, 0), (1, 0, 0)]
+third_moves = [(1, 0, 0), (0, 1, 0)]
+side_moves = [(0, 0, 1), (0, 0, -1)]
+
+
+def around(value, moves):
+    return [value] + [shifted(value, scaled(moves, step)) for step in (2, 1, -1)]
 
 
 def offset(index):
@@ -68,9 +77,12 @@
     third, side = index >> 5, (index >> 4) & 1
     second, first = (index >> 2) & 3, index & 3
     core = side ^ c
-    dx = jnp.where(core == 0, offset(second), offset(third))
-    dy = jnp.where(core == 0, offset(third), offset(second))
-    return ((((y + dy) & 3) << 2) + ((x + dx) & 3)) * 8 + ((z + offset(first)) & 3) * 2 + core
+    turn = offset(first)
+    along = 2 * turn + jnp.where(third == 2, 3, jnp.where(third == 3, 1, 0))
+    up = turn + jnp.where(third == 1, jnp.where(core == 0, 3, 1), 0)
+    dx = jnp.where(core == 0, offset(second), along)
+    dy = jnp.where(core == 0, along, offset(second))
+    return ((((y + dy) & 3) << 2) + ((x + dx) & 3)) * 8 + ((z + up) & 3) * 2 + core
 
 
 def rank_kernel(owner_ref, slot_ref):
@@ -264,13 +276,14 @@
     field = edge_field[0]
     tied = lax.optimization_barrier
     ends = jnp.concatenate([field[:8], field[rows - 8 :]], axis=0)
-    near = jnp.concatenate([*around(profile_op[0], "zz"), ends], axis=0)
+    near = jnp.concatenate([*around(profile_op[0], first_moves), ends], axis=0)
     slot = rank(owner_map.transpose(0, 2, 1)[0]).reshape(rows)
     near, slot = tied((near, slot))
-    plane = jnp.concatenate(around(near, "xy"), axis=0)
+    plane = jnp.concatenate(around(near, second_moves), axis=0)
     sorted_rows = sort_rows(slot, field)
     plane, sorted_rows = tied((plane, sorted_rows))
-    own, across, plus, minus = around(plane, "yx")
+    own, plus, minus = plane, shifted(plane, third_moves), shifted(plane, scaled(third_moves, -1))
+    across = shifted(plane, side_moves)
     effect = effects(sorted_rows, [own, *swap_pieces(own)], (0, 1), None)
     minus, plus, effect = tied((minus, plus, effect))
     effect = effects(sorted_rows, [plus, minus], (4, 6), effect)

time: 49.4 us -> 50.1 us (1.014)
  the two profiles are of different devices: /device:TPU:27 before, /device:TPU:1 now
where the time goes in v5:
time: 50.1 us; the launch traced here: 49.8 us
  starting transfers between devices  28.3 us (56%)
  Pallas kernels  13.2 us (26%)
  waiting for transfers between devices  6.4 us (13%)
  local copies, waits for them, and re-layouts  1.74 us (3%)
    ppermute x9, starting transfers between devices, shifted(): return lax.ppermute(value, axes_all, pairs)  16.3 us
    ppermute x16, starting transfers between devices, core_swap(): return lax.ppermute(value, axes_all, pairs)  12 us
    pallas_call x1, Pallas kernels, finish(): pl.pallas_call(functools.partial(final_kernel, blocks), in_specs=[pl.Bloc...  5.78 us
    pallas_call x1, Pallas kernels, sort_rows(): pl.pallas_call(sort_kernel, in_specs=[pl.BlockSpec(memory_space=pltpu.SME...  4.46 us
    ppermute x9, waiting for transfers between devices, shifted(): return lax.ppermute(value, axes_all, pairs)  4.1 us
    ppermute x16, waiting for transfers between devices, core_swap(): return lax.ppermute(value, axes_all, pairs)  2.29 us
    unnamed x13, local copies, waits for them, and re-layouts  1.59 us
    pallas_call x3, Pallas kernels, effects(): pl.pallas_call(functools.partial(effect_kernel, blocks), in_specs=[in_vme...  1.48 us
  transfers between devices with their start and end apart: 25, of which 11 were waited for; matrix products, arithmetic and copies ran while one was open for 2% of the time, Pallas kernels for 15%

profile of v5, /device:TPU:1, one launch (start us, length us, event | category | flops | bytes accessed | tf_op | source)
XLA Modules:
  0.0 49.8 jit_solution(11153199898038426778)
XLA Ops:
  0.0 7.0 %collective-permute-start.2 = (bf16[128,128]{1,0:T(8,128)(2,1)}, bf16[128,128]{1,0:T(8,128)(2,1)S(1)}, u32[]{:S(2)}, u32[]{:S(2)}) collective-permute-start(bf16[128,128]{1,0:T(8,128)(2,1)} %bitcast.17), channel_id=1, source_target_pairs={{0,70},{1,23},{2,64},{3,17},{4,66},{5,19},{6,68},{7,21},{8,78},{9,... | collective-permute-start | bytes 98312 | tf_op jit(solution)/shard_map/ppermute | solution.py:43
  7.1 1.2 %collective-permute-start = (bf16[128,128]{1,0:T(8,128)(2,1)}, bf16[128,128]{1,0:T(8,128)(2,1)S(1)}, u32[]{:S(2)}, u32[]{:S(2)}) collective-permute-start(bf16[128,128]{1,0:T(8,128)(2,1)} %bitcast.19), channel_id=1, source_target_pairs={{0,4},{1,5},{2,6},{3,7},{4,0},{5,1},{6,2},{7,3},{8,12},{9,13},{10,... | collective-permute-start | bytes 98312 | tf_op jit(solution)/shard_map/ppermute | solution.py:43
  8.3 0.8 %constant_dynamic-update-slice_fusion.5 = bf16[528,128]{1,0:T(8,128)(2,1)S(1)} fusion(bf16[1,128,128]{2,1,0:T(8,128)(2,1)} %param.9), kind=kLoop, calls=%fused_computation.6 | loop fusion | bytes 65536
  9.1 0.7 %copy-done.3 = s32[1,4096,1]{1,2,0:T(1,128)S(1)} copy-done((s32[1,4096,1]{1,2,0:T(1,128)S(1)}, s32[1,4096,1]{1,2,0:T(1,128)}, u32[]{:S(2)}) %copy-start.3) | copy-done | bytes 16408
  9.8 0.8 %shard_map.55 = s32[1,4096]{1,0:T(1,128)S(1)} custom-call(s32[1,4096]{1,0:T(1,128)S(1)} %bitcast.16), custom_call_target="tpu_custom_call" | custom-call | flops 402653184 | bytes 100000 | tf_op jit(solution)/shard_map/pallas_call | solution.py:106
  10.6 0.9 %collective-permute-done = bf16[128,128]{1,0:T(8,128)(2,1)S(1)} collective-permute-done((bf16[128,128]{1,0:T(8,128)(2,1)}, bf16[128,128]{1,0:T(8,128)(2,1)S(1)}, u32[]{:S(2)}, u32[]{:S(2)}) %collective-permute-start) | collective-permute-done | bytes 32800 | tf_op jit(solution)/shard_map/ppermute | solution.py:43
  11.5 2.1 %collective-permute-done.1 = bf16[128,128]{1,0:T(8,128)(2,1)S(1)} collective-permute-done((bf16[128,128]{1,0:T(8,128)(2,1)}, bf16[128,128]{1,0:T(8,128)(2,1)S(1)}, u32[]{:S(2)}, u32[]{:S(2)}) %collective-permute-start.1) | collective-permute-done | bytes 32800 | tf_op jit(solution)/shard_map/ppermute | solution.py:43
  13.7 2.8 %collective-permute-start.5 = (bf16[528,128]{1,0:T(8,128)(2,1)S(1)}, bf16[528,128]{1,0:T(8,128)(2,1)S(1)}, u32[]{:S(2)}, u32[]{:S(2)}) collective-permute-start(bf16[528,128]{1,0:T(8,128)(2,1)S(1)} %constant_dynamic-update-slice_fusion), channel_id=1, source_target_pairs={{0,24},{1,97},{2,26},{3,99},{4,28},{5,101},{6,30},{7,103},{8,0},{9... | collective-permute-start | bytes 405512 | tf_op jit(solution)/shard_map/ppermute | solution.py:43
  16.5 1.6 %collective-permute-start.3 = (bf16[528,128]{1,0:T(8,128)(2,1)S(1)}, bf16[528,128]{1,0:T(8,128)(2,1)S(1)}, u32[]{:S(2)}, u32[]{:S(2)}) collective-permute-start(bf16[528,128]{1,0:T(8,128)(2,1)S(1)} %constant_dynamic-update-slice_fusion), channel_id=1, source_target_pairs={{0,16},{1,65},{2,18},{3,67},{4,20},{5,69},{6,22},{7,71},{8,24},{9,... | collective-permute-start | bytes 405512 | tf_op jit(solution)/shard_map/ppermute | solution.py:43
  18.2 4.5 %shard_map.56.refs_0_.sorted_ref = bf16[6144,128]{1,0:T(8,128)(2,1)S(1)} custom-call(s32[4096]{0:T(1024)S(1)} %bitcast.13, bf16[4096,128]{1,0:T(8,128)(2,1)S(1)} %bitcast.11), custom_call_target="tpu_custom_call" | custom-call | bytes 20000000 | tf_op jit(solution)/shard_map/pallas_call | solution.py:128
  22.6 0.7 %collective-permute-done.4 = bf16[528,128]{1,0:T(8,128)(2,1)S(1)} collective-permute-done((bf16[528,128]{1,0:T(8,128)(2,1)S(1)}, bf16[528,128]{1,0:T(8,128)(2,1)S(1)}, u32[]{:S(2)}, u32[]{:S(2)}) %collective-permute-start.4) | collective-permute-done | bytes 135200 | tf_op jit(solution)/shard_map/ppermute | solution.py:43
  23.7 2.4 %collective-permute-start.7 = (bf16[2112,128]{1,0:T(8,128)(2,1)S(1)}, bf16[2112,128]{1,0:T(8,128)(2,1)S(1)}, u32[]{:S(2)}, u32[]{:S(2)}) collective-permute-start(bf16[2112,128]{1,0:T(8,128)(2,1)S(1)} %pad_maximum_fusion.refs_1_.own_ref), channel_id=1, source_target_pairs={{0,96},{1,25},{2,98},{3,27},{4,100},{5,29},{6,102},{7,31},{8,104},... | collective-permute-start | bytes 1622024 | tf_op jit(solution)/shard_map/ppermute | solution.py:43
  26.1 3.8 %collective-permute-start.12 = (bf16[512,128]{1,0:T(8,128)(2,1)S(1)}, bf16[512,128]{1,0:T(8,128)(2,1)S(1)}, u32[]{:S(2)}, u32[]{:S(2)}) collective-permute-start(bf16[512,128]{1,0:T(8,128)(2,1)S(1)} %get-tuple-element.39), channel_id=1, source_target_pairs={{0,1},{1,0},{2,3},{3,2},{4,5},{5,4},{6,7},{7,6},{8,9},{9,8},{10,11... | collective-permute-start | bytes 393224 | tf_op jit(solution)/shard_map/ppermute | solution.py:52
  30.0 0.4 collective-permute-start.10
  30.5 0.5 collective-permute-done.12.refs_5_
  31.3 0.8 %collective-permute-start.6 = (bf16[2112,128]{1,0:T(8,128)(2,1)S(1)}, bf16[2112,128]{1,0:T(8,128)(2,1)S(1)}, u32[]{:S(2)}, u32[]{:S(2)}) collective-permute-start(bf16[2112,128]{1,0:T(8,128)(2,1)S(1)} %pad_maximum_fusion.refs_1_.own_ref), channel_id=1, source_target_pairs={{0,2},{1,7},{2,4},{3,1},{4,6},{5,3},{6,0},{7,5},{8,10},{9,15},{10,... | collective-permute-start | bytes 1622024 | tf_op jit(solution)/shard_map/ppermute | solution.py:43
  32.3 0.5 shard_map.57.refs_3_
  33.2 4.1 %collective-permute-start.16 = (bf16[512,128]{1,0:T(8,128)(2,1)S(1)}, bf16[512,128]{1,0:T(8,128)(2,1)S(1)}, u32[]{:S(2)}, u32[]{:S(2)}) collective-permute-start(bf16[512,128]{1,0:T(8,128)(2,1)S(1)} %get-tuple-element.35), channel_id=1, source_target_pairs={{0,1},{1,0},{2,3},{3,2},{4,5},{5,4},{6,7},{7,6},{8,9},{9,8},{10,11... | collective-permute-start | bytes 393224 | tf_op jit(solution)/shard_map/ppermute | solution.py:52
  37.4 0.4 collective-permute-start.14
  39.4 0.5 shard_map.58.refs_9_
  39.9 0.7 %shard_map.60.base_ref = f32[4096,128]{1,0:T(8,128)S(1)} custom-call(bf16[4096,128]{1,0:T(8,128)(2,1)S(1)} %bitcast.12, bf16[2112,128]{1,0:T(8,128)(2,1)S(1)} %pad_maximum_fusion.refs_1_.own_ref, bf16[2112,128]{1,0:T(8,128)(2,1)S(1)} %collective-permute-done.8.refs_1_.before_ref, bf16[2112,128]{1,0:T(8,128)(2,1)S(1)} %collective-permute-done.7.refs_2_.after_ref, ...), custom_call_target="tpu_custom_call" | custom-call | flops 1000 | bytes 1000 | tf_op jit(solution)/shard_map/pallas_call | solution.py:176
  40.7 0.5 shard_map.59.refs_5_
  41.2 0.9 %collective-permute-start.24 = (bf16[512,128]{1,0:T(8,128)(2,1)S(1)}, bf16[512,128]{1,0:T(8,128)(2,1)S(1)}, u32[]{:S(2)}, u32[]{:S(2)}) collective-permute-start(bf16[512,128]{1,0:T(8,128)(2,1)S(1)} %get-tuple-element.27), channel_id=1, source_target_pairs={{0,1},{1,0},{2,3},{3,2},{4,5},{5,4},{6,7},{7,6},{8,9},{9,8},{10,11... | collective-permute-start | bytes 393224 | tf_op jit(solution)/shard_map/ppermute | solution.py:52
  44.0 5.8 %shard_map.61 = (f32[4096,128]{1,0:T(8,128)}, f32[6144,128]{1,0:T(8,128)S(1)}) custom-call(s32[4096]{0:T(1024)S(1)} %bitcast.14, f32[4096,128]{1,0:T(8,128)S(1)} %shard_map.60.base_ref, bf16[6144,128]{1,0:T(8,128)(2,1)S(1)} %shard_map.56.refs_0_.sorted_ref, bf16[2112,128]{1,0:T(8,128)(2,1)S(1)} %collective-permute-done.6.refs_0_, ...), custom_call_target="tpu_custom_call", output_to_operand_aliasing={{1}: (8, {})} | custom-call | flops 524288 | bytes 10000000 | tf_op jit(solution)/shard_map/pallas_call | solution.py:257
  (52 shorter events, 5.2 us)
Async XLA Ops:
  0.0 13.6 %collective-permute-start.2 = (bf16[128,128]{1,0:T(8,128)(2,1)}, bf16[128,128]{1,0:T(8,128)(2,1)S(1)}, u32[]{:S(2)}, u32[]{:S(2)}) collective-permute-start(bf16[128,128]{1,0:T(8,128)(2,1)} %bitcast.17), channel_id=1, source_target_pairs={{0,70},{1,23},{2,64},{3,17},{4,66},{5,19},{6,68},{7,21},{8,78},{9,... | collective-permute-start | bytes 98312 | tf_op jit(solution)/shard_map/ppermute | solution.py:43
  7.0 6.6 %collective-permute-start.1 = (bf16[128,128]{1,0:T(8,128)(2,1)}, bf16[128,128]{1,0:T(8,128)(2,1)S(1)}, u32[]{:S(2)}, u32[]{:S(2)}) collective-permute-start(bf16[128,128]{1,0:T(8,128)(2,1)} %bitcast.18), channel_id=1, source_target_pairs={{0,66},{1,19},{2,68},{3,21},{4,70},{5,23},{6,64},{7,17},{8,74},{9,... | collective-permute-start | bytes 98312 | tf_op jit(solution)/shard_map/ppermute | solution.py:43
  7.1 4.5 %collective-permute-start = (bf16[128,128]{1,0:T(8,128)(2,1)}, bf16[128,128]{1,0:T(8,128)(2,1)S(1)}, u32[]{:S(2)}, u32[]{:S(2)}) collective-permute-start(bf16[128,128]{1,0:T(8,128)(2,1)} %bitcast.19), channel_id=1, source_target_pairs={{0,4},{1,5},{2,6},{3,7},{4,0},{5,1},{6,2},{7,3},{8,12},{9,13},{10,... | collective-permute-start | bytes 98312 | tf_op jit(solution)/shard_map/ppermute | solution.py:43
  13.7 8.9 %collective-permute-start.5 = (bf16[528,128]{1,0:T(8,128)(2,1)S(1)}, bf16[528,128]{1,0:T(8,128)(2,1)S(1)}, u32[]{:S(2)}, u32[]{:S(2)}) collective-permute-start(bf16[528,128]{1,0:T(8,128)(2,1)S(1)} %constant_dynamic-update-slice_fusion), channel_id=1, source_target_pairs={{0,24},{1,97},{2,26},{3,99},{4,28},{5,101},{6,30},{7,103},{8,0},{9... | collective-permute-start | bytes 405512 | tf_op jit(solution)/shard_map/ppermute | solution.py:43
  16.5 6.8 %collective-permute-start.4 = (bf16[528,128]{1,0:T(8,128)(2,1)S(1)}, bf16[528,128]{1,0:T(8,128)(2,1)S(1)}, u32[]{:S(2)}, u32[]{:S(2)}) collective-permute-start(bf16[528,128]{1,0:T(8,128)(2,1)S(1)} %constant_dynamic-update-slice_fusion), channel_id=1, source_target_pairs={{0,8},{1,33},{2,10},{3,35},{4,12},{5,37},{6,14},{7,39},{8,16},{9,4... | collective-permute-start | bytes 405512 | tf_op jit(solution)/shard_map/ppermute | solution.py:43
  16.5 6.8 %collective-permute-start.3 = (bf16[528,128]{1,0:T(8,128)(2,1)S(1)}, bf16[528,128]{1,0:T(8,128)(2,1)S(1)}, u32[]{:S(2)}, u32[]{:S(2)}) collective-permute-start(bf16[528,128]{1,0:T(8,128)(2,1)S(1)} %constant_dynamic-update-slice_fusion), channel_id=1, source_target_pairs={{0,16},{1,65},{2,18},{3,67},{4,20},{5,69},{6,22},{7,71},{8,24},{9,... | collective-permute-start | bytes 405512 | tf_op jit(solution)/shard_map/ppermute | solution.py:43
  23.4 9.8 %collective-permute-start.8 = (bf16[2112,128]{1,0:T(8,128)(2,1)S(1)}, bf16[2112,128]{1,0:T(8,128)(2,1)S(1)}, u32[]{:S(2)}, u32[]{:S(2)}) collective-permute-start(bf16[2112,128]{1,0:T(8,128)(2,1)S(1)} %pad_maximum_fusion.refs_1_.own_ref), channel_id=1, source_target_pairs={{0,32},{1,9},{2,34},{3,11},{4,36},{5,13},{6,38},{7,15},{8,40},{9,1... | collective-permute-start | bytes 1622024 | tf_op jit(solution)/shard_map/ppermute | solution.py:43
  23.7 9.4 %collective-permute-start.7 = (bf16[2112,128]{1,0:T(8,128)(2,1)S(1)}, bf16[2112,128]{1,0:T(8,128)(2,1)S(1)}, u32[]{:S(2)}, u32[]{:S(2)}) collective-permute-start(bf16[2112,128]{1,0:T(8,128)(2,1)S(1)} %pad_maximum_fusion.refs_1_.own_ref), channel_id=1, source_target_pairs={{0,96},{1,25},{2,98},{3,27},{4,100},{5,29},{6,102},{7,31},{8,104},... | collective-permute-start | bytes 1622024 | tf_op jit(solution)/shard_map/ppermute | solution.py:43
  26.1 4.8 %collective-permute-start.12 = (bf16[512,128]{1,0:T(8,128)(2,1)S(1)}, bf16[512,128]{1,0:T(8,128)(2,1)S(1)}, u32[]{:S(2)}, u32[]{:S(2)}) collective-permute-start(bf16[512,128]{1,0:T(8,128)(2,1)S(1)} %get-tuple-element.39), channel_id=1, source_target_pairs={{0,1},{1,0},{2,3},{3,2},{4,5},{5,4},{6,7},{7,6},{8,9},{9,8},{10,11... | collective-permute-start | bytes 393224 | tf_op jit(solution)/shard_map/ppermute | solution.py:52
  29.9 1.4 %collective-permute-start.11 = (bf16[512,128]{1,0:T(8,128)(2,1)S(1)}, bf16[512,128]{1,0:T(8,128)(2,1)S(1)}, u32[]{:S(2)}, u32[]{:S(2)}) collective-permute-start(bf16[512,128]{1,0:T(8,128)(2,1)S(1)} %get-tuple-element.40), channel_id=1, source_target_pairs={{0,1},{1,0},{2,3},{3,2},{4,5},{5,4},{6,7},{7,6},{8,9},{9,8},{10,11... | collective-permute-start | bytes 393224 | tf_op jit(solution)/shard_map/ppermute | solution.py:52
  30.0 2.0 %collective-permute-start.10 = (bf16[512,128]{1,0:T(8,128)(2,1)S(1)}, bf16[512,128]{1,0:T(8,128)(2,1)S(1)}, u32[]{:S(2)}, u32[]{:S(2)}) collective-permute-start(bf16[512,128]{1,0:T(8,128)(2,1)S(1)} %get-tuple-element.41), channel_id=1, source_target_pairs={{0,1},{1,0},{2,3},{3,2},{4,5},{5,4},{6,7},{7,6},{8,9},{9,8},{10,11... | collective-permute-start | bytes 393224 | tf_op jit(solution)/shard_map/ppermute | solution.py:52
  30.9 1.3 %collective-permute-start.9 = (bf16[512,128]{1,0:T(8,128)(2,1)S(1)}, bf16[512,128]{1,0:T(8,128)(2,1)S(1)}, u32[]{:S(2)}, u32[]{:S(2)}) collective-permute-start(bf16[512,128]{1,0:T(8,128)(2,1)S(1)} %get-tuple-element.42), channel_id=1, source_target_pairs={{0,1},{1,0},{2,3},{3,2},{4,5},{5,4},{6,7},{7,6},{8,9},{9,8},{10,11... | collective-permute-start | bytes 393224 | tf_op jit(solution)/shard_map/ppermute | solution.py:52
  31.3 9.9 %collective-permute-start.6 = (bf16[2112,128]{1,0:T(8,128)(2,1)S(1)}, bf16[2112,128]{1,0:T(8,128)(2,1)S(1)}, u32[]{:S(2)}, u32[]{:S(2)}) collective-permute-start(bf16[2112,128]{1,0:T(8,128)(2,1)S(1)} %pad_maximum_fusion.refs_1_.own_ref), channel_id=1, source_target_pairs={{0,2},{1,7},{2,4},{3,1},{4,6},{5,3},{6,0},{7,5},{8,10},{9,15},{10,... | collective-permute-start | bytes 1622024 | tf_op jit(solution)/shard_map/ppermute | solution.py:43
  33.2 5.1 %collective-permute-start.16 = (bf16[512,128]{1,0:T(8,128)(2,1)S(1)}, bf16[512,128]{1,0:T(8,128)(2,1)S(1)}, u32[]{:S(2)}, u32[]{:S(2)}) collective-permute-start(bf16[512,128]{1,0:T(8,128)(2,1)S(1)} %get-tuple-element.35), channel_id=1, source_target_pairs={{0,1},{1,0},{2,3},{3,2},{4,5},{5,4},{6,7},{7,6},{8,9},{9,8},{10,11... | collective-permute-start | bytes 393224 | tf_op jit(solution)/shard_map/ppermute | solution.py:52
  37.3 1.4 %collective-permute-start.15 = (bf16[512,128]{1,0:T(8,128)(2,1)S(1)}, bf16[512,128]{1,0:T(8,128)(2,1)S(1)}, u32[]{:S(2)}, u32[]{:S(2)}) collective-permute-start(bf16[512,128]{1,0:T(8,128)(2,1)S(1)} %get-tuple-element.36), channel_id=1, source_target_pairs={{0,1},{1,0},{2,3},{3,2},{4,5},{5,4},{6,7},{7,6},{8,9},{9,8},{10,11... | collective-permute-start | bytes 393224 | tf_op jit(solution)/shard_map/ppermute | solution.py:52
  37.4 1.4 %collective-permute-start.14 = (bf16[512,128]{1,0:T(8,128)(2,1)S(1)}, bf16[512,128]{1,0:T(8,128)(2,1)S(1)}, u32[]{:S(2)}, u32[]{:S(2)}) collective-permute-start(bf16[512,128]{1,0:T(8,128)(2,1)S(1)} %get-tuple-element.37), channel_id=1, source_target_pairs={{0,1},{1,0},{2,3},{3,2},{4,5},{5,4},{6,7},{7,6},{8,9},{9,8},{10,11... | collective-permute-start | bytes 393224 | tf_op jit(solution)/shard_map/ppermute | solution.py:52
  37.8 1.4 %collective-permute-start.13 = (bf16[512,128]{1,0:T(8,128)(2,1)S(1)}, bf16[512,128]{1,0:T(8,128)(2,1)S(1)}, u32[]{:S(2)}, u32[]{:S(2)}) collective-permute-start(bf16[512,128]{1,0:T(8,128)(2,1)S(1)} %get-tuple-element.38), channel_id=1, source_target_pairs={{0,1},{1,0},{2,3},{3,2},{4,5},{5,4},{6,7},{7,6},{8,9},{9,8},{10,11... | collective-permute-start | bytes 393224 | tf_op jit(solution)/shard_map/ppermute | solution.py:52
  38.3 2.4 %collective-permute-start.20 = (bf16[512,128]{1,0:T(8,128)(2,1)S(1)}, bf16[512,128]{1,0:T(8,128)(2,1)S(1)}, u32[]{:S(2)}, u32[]{:S(2)}) collective-permute-start(bf16[512,128]{1,0:T(8,128)(2,1)S(1)} %get-tuple-element.31), channel_id=1, source_target_pairs={{0,1},{1,0},{2,3},{3,2},{4,5},{5,4},{6,7},{7,6},{8,9},{9,8},{10,11... | collective-permute-start | bytes 393224 | tf_op jit(solution)/shard_map/ppermute | solution.py:52
  38.6 2.0 %collective-permute-start.19 = (bf16[512,128]{1,0:T(8,128)(2,1)S(1)}, bf16[512,128]{1,0:T(8,128)(2,1)S(1)}, u32[]{:S(2)}, u32[]{:S(2)}) collective-permute-start(bf16[512,128]{1,0:T(8,128)(2,1)S(1)} %get-tuple-element.32), channel_id=1, source_target_pairs={{0,1},{1,0},{2,3},{3,2},{4,5},{5,4},{6,7},{7,6},{8,9},{9,8},{10,11... | collective-permute-start | bytes 393224 | tf_op jit(solution)/shard_map/ppermute | solution.py:52
  38.8 1.8 %collective-permute-start.18 = (bf16[512,128]{1,0:T(8,128)(2,1)S(1)}, bf16[512,128]{1,0:T(8,128)(2,1)S(1)}, u32[]{:S(2)}, u32[]{:S(2)}) collective-permute-start(bf16[512,128]{1,0:T(8,128)(2,1)S(1)} %get-tuple-element.33), channel_id=1, source_target_pairs={{0,1},{1,0},{2,3},{3,2},{4,5},{5,4},{6,7},{7,6},{8,9},{9,8},{10,11... | collective-permute-start | bytes 393224 | tf_op jit(solution)/shard_map/ppermute | solution.py:52
  39.2 1.5 %collective-permute-start.17 = (bf16[512,128]{1,0:T(8,128)(2,1)S(1)}, bf16[512,128]{1,0:T(8,128)(2,1)S(1)}, u32[]{:S(2)}, u32[]{:S(2)}) collective-permute-start(bf16[512,128]{1,0:T(8,128)(2,1)S(1)} %get-tuple-element.34), channel_id=1, source_target_pairs={{0,1},{1,0},{2,3},{3,2},{4,5},{5,4},{6,7},{7,6},{8,9},{9,8},{10,11... | collective-permute-start | bytes 393224 | tf_op jit(solution)/shard_map/ppermute | solution.py:52
  41.2 1.9 %collective-permute-start.24 = (bf16[512,128]{1,0:T(8,128)(2,1)S(1)}, bf16[512,128]{1,0:T(8,128)(2,1)S(1)}, u32[]{:S(2)}, u32[]{:S(2)}) collective-permute-start(bf16[512,128]{1,0:T(8,128)(2,1)S(1)} %get-tuple-element.27), channel_id=1, source_target_pairs={{0,1},{1,0},{2,3},{3,2},{4,5},{5,4},{6,7},{7,6},{8,9},{9,8},{10,11... | collective-permute-start | bytes 393224 | tf_op jit(solution)/shard_map/ppermute | solution.py:52
  42.2 1.3 %collective-permute-start.23 = (bf16[512,128]{1,0:T(8,128)(2,1)S(1)}, bf16[512,128]{1,0:T(8,128)(2,1)S(1)}, u32[]{:S(2)}, u32[]{:S(2)}) collective-permute-start(bf16[512,128]{1,0:T(8,128)(2,1)S(1)} %get-tuple-element.28), channel_id=1, source_target_pairs={{0,1},{1,0},{2,3},{3,2},{4,5},{5,4},{6,7},{7,6},{8,9},{9,8},{10,11... | collective-permute-start | bytes 393224 | tf_op jit(solution)/shard_map/ppermute | solution.py:52
  42.3 1.4 %collective-permute-start.22 = (bf16[512,128]{1,0:T(8,128)(2,1)S(1)}, bf16[512,128]{1,0:T(8,128)(2,1)S(1)}, u32[]{:S(2)}, u32[]{:S(2)}) collective-permute-start(bf16[512,128]{1,0:T(8,128)(2,1)S(1)} %get-tuple-element.29), channel_id=1, source_target_pairs={{0,1},{1,0},{2,3},{3,2},{4,5},{5,4},{6,7},{7,6},{8,9},{9,8},{10,11... | collective-permute-start | bytes 393224 | tf_op jit(solution)/shard_map/ppermute | solution.py:52
  (5 other events, 17.3 us)

commit v6 on v5

--- a/solution.py
+++ b/solution.py
@@ -14,6 +14,8 @@
 rows = 4096
 vals = 128
 slots = owners * cap
+half = slots // 2
+block = 16 * cap
 chunk = 256
 unroll = 128
 group = 4 * vals
@@ -52,10 +54,6 @@
     return lax.ppermute(value, axes_all, pairs)
 
 
-def swap_pieces(value):
-    return [core_swap(value[i : i + group]) for i in range(0, value.shape[0], stride)]
-
-
 first_moves = [(2, 0, 1), (0, 2, 1)]
 second_moves = [(0, 1, 0), (1, 0, 0)]
 third_moves = [(1, 0, 0), (0, 1, 0)]
@@ -74,7 +72,7 @@
     sub, lam = lax.axis_index("sub"), lax.axis_index("lam")
     y, x, z, c = sub // 4, sub % 4, lam // 2, lam % 2
     index = lax.broadcasted_iota(jnp.int32, (owners, chunk), 0)
-    third, side = index >> 5, (index >> 4) & 1
+    side, third = index >> 6, (index >> 4) & 3
     second, first = (index >> 2) & 3, index & 3
     core = side ^ c
     turn = offset(first)
@@ -111,7 +109,7 @@
     )(owner)
 
 
-def sort_kernel(slot_ref, field_ref, sorted_ref, wide, placed):
+def sort_kernel(slot_ref, field_ref, near_ref, far_ref, wide, placed):
     wide[...] = field_ref[...].astype(jnp.float32)
 
     def body(i, carry):
@@ -121,14 +119,16 @@
         return carry
 
     lax.fori_loop(0, rows // unroll, body, 0)
-    sorted_ref[...] = placed[...].astype(jnp.bfloat16)
+    near_ref[...] = placed[:half].astype(jnp.bfloat16)
+    far_ref[...] = placed[half:].astype(jnp.bfloat16)
 
 
 def sort_rows(slot, field):
     return pl.pallas_call(
         sort_kernel,
-        in_specs=[pl.BlockSpec(memory_space=pltpu.SMEM), pl.BlockSpec(memory_space=pltpu.VMEM)],
-        out_shape=jax.ShapeDtypeStruct((slots, vals), jnp.bfloat16),
+        in_specs=[pl.BlockSpec(memory_space=pltpu.SMEM), in_vmem],
+        out_specs=[in_vmem, in_vmem],
+        out_shape=[jax.ShapeDtypeStruct((half, vals), jnp.bfloat16)] * 2,
         scratch_shapes=[pltpu.VMEM((rows, vals), jnp.float32), pltpu.VMEM((slots, vals), jnp.float32)],
         compiler_params=params(),
         cost_estimate=pl.CostEstimate(flops=0, bytes_accessed=20000000, transcendentals=0),
@@ -192,33 +192,31 @@
     return reluct * response
 
 
-def effect_blocks(sorted_ref, operators, effect_ref, blocks):
-    tiles = [
-        (ref, top + k * vals)
-        for ref in operators
-        for top in range(0, ref.shape[0], stride)
-        for k in range(group // vals)
-    ]
-    for number, (operator_ref, top) in enumerate(tiles[: 16 * len(blocks)]):
-        lo = (blocks[number // 16] * 16 + number % 16) * cap
-        effect_ref[lo : lo + cap, :] = respond(
-            sorted_ref[lo : lo + cap, :], operator_ref[top : top + vals, :]
-        )
-
-
-def effect_kernel(blocks, *refs):
-    effect_blocks(refs[0], refs[1:], refs[-1], blocks)
-
-
-def effects(sorted_rows, operators, blocks, previous):
-    operands = [sorted_rows, *operators]
+def effect_kernel(thirds, near_ref, guest_ref, *refs):
+    operators, (effect_ref, reply_ref) = refs[: len(thirds)], refs[-2:]
+    for number, (third, operator_ref) in enumerate(zip(thirds, operators)):
+        for k in range(16):
+            top = k // 4 * stride + k % 4 * vals
+            operator = operator_ref[top : top + vals, :]
+            lo, out = third * block + k * cap, number * block + k * cap
+            effect_ref[lo : lo + cap, :] = respond(near_ref[lo : lo + cap, :], operator)
+            reply_ref[out : out + cap, :] = respond(guest_ref[lo : lo + cap, :], operator).astype(
+                jnp.bfloat16
+            )
+
+
+def effects(near, guest, operators, thirds, previous):
+    operands = [near, guest, *operators]
     if previous is not None:
         operands.append(previous)
     return pl.pallas_call(
-        functools.partial(effect_kernel, blocks),
+        functools.partial(effect_kernel, thirds),
         in_specs=[in_vmem] * len(operands),
-        out_specs=in_vmem,
-        out_shape=jax.ShapeDtypeStruct((slots, vals), jnp.float32),
+        out_specs=[in_vmem, in_vmem],
+        out_shape=[
+            jax.ShapeDtypeStruct((slots, vals), jnp.float32),
+            jax.ShapeDtypeStruct((len(thirds) * block, vals), jnp.bfloat16),
+        ],
         input_output_aliases={} if previous is None else {len(operands) - 1: 0},
         compiler_params=params(),
         cost_estimate=pl.CostEstimate(flops=1000, bytes_accessed=1000, transcendentals=0),
@@ -228,9 +226,10 @@
 part_rows = 512
 
 
-def final_kernel(blocks, slot_ref, base_ref, sorted_ref, *refs):
-    operators, (_, out_ref, effect_ref, result, sent) = refs[:-5], refs[-5:]
-    effect_blocks(sorted_ref, operators, effect_ref, blocks)
+def final_kernel(slot_ref, base_ref, own_ref, pair_ref, side_ref, _, out_ref, effect_ref, result, sent):
+    for returned_ref, third in ((own_ref, 0), (pair_ref, 2), (side_ref, 1)):
+        lo = half + third * block
+        effect_ref[lo : lo + returned_ref.shape[0], :] = returned_ref[...].astype(jnp.float32)
 
     def copy(part):
         span = pl.ds(pl.multiple_of(part * part_rows, part_rows), part_rows)
@@ -252,10 +251,10 @@
         copy(part).wait()
 
 
-def finish(slot, base, sorted_rows, operators, blocks, previous):
-    operands = [slot, base, sorted_rows, *operators, previous]
-    return pl.pallas_call(
-        functools.partial(final_kernel, blocks),
+def finish(slot, base, returned, effect):
+    operands = [slot, base, *returned, effect]
+    return pl.pallas_call(
+        final_kernel,
         in_specs=[pl.BlockSpec(memory_space=pltpu.SMEM)] + [in_vmem] * (len(operands) - 1),
         out_specs=[pl.BlockSpec(memory_space=pl.ANY), in_vmem],
         out_shape=[
@@ -280,17 +279,21 @@
     slot = rank(owner_map.transpose(0, 2, 1)[0]).reshape(rows)
     near, slot = tied((near, slot))
     plane = jnp.concatenate(around(near, second_moves), axis=0)
-    sorted_rows = sort_rows(slot, field)
-    plane, sorted_rows = tied((plane, sorted_rows))
-    own, plus, minus = plane, shifted(plane, third_moves), shifted(plane, scaled(third_moves, -1))
-    across = shifted(plane, side_moves)
-    effect = effects(sorted_rows, [own, *swap_pieces(own)], (0, 1), None)
+    near_rows, far_rows = sort_rows(slot, field)
+    plane, near_rows, far_rows = tied((plane, near_rows, far_rows))
+    plus, minus = shifted(plane, third_moves), shifted(plane, scaled(third_moves, -1))
+    side = shifted(plane, side_moves)
+    guest = core_swap(far_rows)
+    effect, reply = effects(near_rows, guest, [plane], (0,), None)
+    returned = [core_swap(reply)]
     minus, plus, effect = tied((minus, plus, effect))
-    effect = effects(sorted_rows, [plus, minus], (4, 6), effect)
-    base = stencil(field, own, plus, minus, coupling.reshape(rows // vals, vals), in_plane)
-    effect = effects(sorted_rows, [*swap_pieces(plus), *swap_pieces(minus)], (5, 7), effect)
-    across, effect, base = tied((across, effect, base))
-    return finish(slot, base, sorted_rows, [across, *swap_pieces(across)], (2, 3), effect)[None]
+    effect, reply = effects(near_rows, guest, [plus, minus], (2, 3), effect)
+    returned.append(core_swap(reply))
+    base = stencil(field, plane, plus, minus, coupling.reshape(rows // vals, vals), in_plane)
+    side, effect, base = tied((side, effect, base))
+    effect, reply = effects(near_rows, guest, [side], (1,), effect)
+    returned.append(core_swap(reply))
+    return finish(slot, base, returned, effect)[None]
 
 
 def solution(mesh):

time: 50.1 us -> 47.8 us (0.954)
  starting transfers between devices: 28.3 us -> 22 us
  waiting for transfers between devices: 6.4 us -> 10.7 us
    ppermute x16 -> x4, starting transfers between devices: 12 us -> 5.97 us  [core_swap(): return lax.ppermute(value, axes_all, pairs)]
    ppermute x9, waiting for transfers between devices: 4.1 us -> 9.62 us  [shifted(): return lax.ppermute(value, axes_all, pairs)]
    ppermute x16 -> x4, waiting for transfers between devices: 2.29 us -> 1.08 us  [core_swap(): return lax.ppermute(value, axes_all, pairs)]
  transfers between devices with their start and end apart: 25 -> 13, of which waited for: 11 -> 5; matrix products, arithmetic and copies ran while one was open for 2% -> 2% of each run, Pallas kernels for 15% -> 16%
where the time goes in v6:
time: 47.8 us; the launch traced here: 47.5 us
  starting transfers between devices  22 us (46%)
  Pallas kernels  13.1 us (27%)
  waiting for transfers between devices  10.7 us (22%)
  local copies, waits for them, and re-layouts  1.57 us (3%)
    ppermute x9, starting transfers between devices, shifted(): return lax.ppermute(value, axes_all, pairs)  16.1 us
    ppermute x9, waiting for transfers between devices, shifted(): return lax.ppermute(value, axes_all, pairs)  9.62 us
    ppermute x4, starting transfers between devices, core_swap(): return lax.ppermute(value, axes_all, pairs)  5.97 us
    pallas_call x1, Pallas kernels, finish(): pl.pallas_call(final_kernel, in_specs=[pl.BlockSpec(memory_space=pltpu.SM...  5.39 us
    pallas_call x1, Pallas kernels, sort_rows(): pl.pallas_call(sort_kernel, in_specs=[pl.BlockSpec(memory_space=pltpu.SME...  4.46 us
    pallas_call x3, Pallas kernels, effects(): pl.pallas_call(functools.partial(effect_kernel, thirds), in_specs=[in_vme...  1.77 us
    unnamed x13, local copies, waits for them, and re-layouts  1.56 us
    ppermute x4, waiting for transfers between devices, core_swap(): return lax.ppermute(value, axes_all, pairs)  1.08 us
  transfers between devices with their start and end apart: 13, of which 5 were waited for; matrix products, arithmetic and copies ran while one was open for 2% of the time, Pallas kernels for 16%

profile of v6, /device:TPU:1, one launch (start us, length us, event | category | flops | bytes accessed | tf_op | source)
XLA Modules:
  0.0 47.5 jit_solution(15599756765503182042)
XLA Ops:
  0.0 7.0 %collective-permute-start.2 = (bf16[128,128]{1,0:T(8,128)(2,1)}, bf16[128,128]{1,0:T(8,128)(2,1)S(1)}, u32[]{:S(2)}, u32[]{:S(2)}) collective-permute-start(bf16[128,128]{1,0:T(8,128)(2,1)} %bitcast.17), channel_id=1, source_target_pairs={{0,70},{1,23},{2,64},{3,17},{4,66},{5,19},{6,68},{7,21},{8,78},{9,... | collective-permute-start | bytes 98312 | tf_op jit(solution)/shard_map/ppermute | solution.py:45
  7.1 1.2 %collective-permute-start = (bf16[128,128]{1,0:T(8,128)(2,1)}, bf16[128,128]{1,0:T(8,128)(2,1)S(1)}, u32[]{:S(2)}, u32[]{:S(2)}) collective-permute-start(bf16[128,128]{1,0:T(8,128)(2,1)} %bitcast.19), channel_id=1, source_target_pairs={{0,4},{1,5},{2,6},{3,7},{4,0},{5,1},{6,2},{7,3},{8,12},{9,13},{10,... | collective-permute-start | bytes 98312 | tf_op jit(solution)/shard_map/ppermute | solution.py:45
  8.3 0.8 %constant_dynamic-update-slice_fusion.5 = bf16[528,128]{1,0:T(8,128)(2,1)S(1)} fusion(bf16[1,128,128]{2,1,0:T(8,128)(2,1)} %param.9), kind=kLoop, calls=%fused_computation.6 | loop fusion | bytes 65536
  9.1 0.7 %copy-done.3 = s32[1,4096,1]{1,2,0:T(1,128)S(1)} copy-done((s32[1,4096,1]{1,2,0:T(1,128)S(1)}, s32[1,4096,1]{1,2,0:T(1,128)}, u32[]{:S(2)}) %copy-start.3) | copy-done | bytes 16408
  9.8 0.8 %shard_map.55 = s32[1,4096]{1,0:T(1,128)S(1)} custom-call(s32[1,4096]{1,0:T(1,128)S(1)} %bitcast.16), custom_call_target="tpu_custom_call" | custom-call | flops 402653184 | bytes 100000 | tf_op jit(solution)/shard_map/pallas_call | solution.py:104
  10.6 0.9 %collective-permute-done = bf16[128,128]{1,0:T(8,128)(2,1)S(1)} collective-permute-done((bf16[128,128]{1,0:T(8,128)(2,1)}, bf16[128,128]{1,0:T(8,128)(2,1)S(1)}, u32[]{:S(2)}, u32[]{:S(2)}) %collective-permute-start) | collective-permute-done | bytes 32800 | tf_op jit(solution)/shard_map/ppermute | solution.py:45
  11.5 2.1 %collective-permute-done.1 = bf16[128,128]{1,0:T(8,128)(2,1)S(1)} collective-permute-done((bf16[128,128]{1,0:T(8,128)(2,1)}, bf16[128,128]{1,0:T(8,128)(2,1)S(1)}, u32[]{:S(2)}, u32[]{:S(2)}) %collective-permute-start.1) | collective-permute-done | bytes 32800 | tf_op jit(solution)/shard_map/ppermute | solution.py:45
  13.7 2.8 %collective-permute-start.5 = (bf16[528,128]{1,0:T(8,128)(2,1)S(1)}, bf16[528,128]{1,0:T(8,128)(2,1)S(1)}, u32[]{:S(2)}, u32[]{:S(2)}) collective-permute-start(bf16[528,128]{1,0:T(8,128)(2,1)S(1)} %constant_dynamic-update-slice_fusion), channel_id=1, source_target_pairs={{0,24},{1,97},{2,26},{3,99},{4,28},{5,101},{6,30},{7,103},{8,0},{9... | collective-permute-start | bytes 405512 | tf_op jit(solution)/shard_map/ppermute | solution.py:45
  16.5 1.6 %collective-permute-start.3 = (bf16[528,128]{1,0:T(8,128)(2,1)S(1)}, bf16[528,128]{1,0:T(8,128)(2,1)S(1)}, u32[]{:S(2)}, u32[]{:S(2)}) collective-permute-start(bf16[528,128]{1,0:T(8,128)(2,1)S(1)} %constant_dynamic-update-slice_fusion), channel_id=1, source_target_pairs={{0,16},{1,65},{2,18},{3,67},{4,20},{5,69},{6,22},{7,71},{8,24},{9,... | collective-permute-start | bytes 405512 | tf_op jit(solution)/shard_map/ppermute | solution.py:45
  18.2 4.5 %shard_map.56 = (bf16[3072,128]{1,0:T(8,128)(2,1)S(1)}, bf16[3072,128]{1,0:T(8,128)(2,1)S(1)}) custom-call(s32[4096]{0:T(1024)S(1)} %bitcast.13, bf16[4096,128]{1,0:T(8,128)(2,1)S(1)} %bitcast.11), custom_call_target="tpu_custom_call" | custom-call | bytes 20000000 | tf_op jit(solution)/shard_map/pallas_call | solution.py:127
  22.6 0.7 %collective-permute-done.4 = bf16[528,128]{1,0:T(8,128)(2,1)S(1)} collective-permute-done((bf16[528,128]{1,0:T(8,128)(2,1)S(1)}, bf16[528,128]{1,0:T(8,128)(2,1)S(1)}, u32[]{:S(2)}, u32[]{:S(2)}) %collective-permute-start.4) | collective-permute-done | bytes 135200 | tf_op jit(solution)/shard_map/ppermute | solution.py:45
  23.4 3.2 %collective-permute-start.7 = (bf16[3072,128]{1,0:T(8,128)(2,1)S(1)}, bf16[3072,128]{1,0:T(8,128)(2,1)S(1)}, u32[]{:S(2)}, u32[]{:S(2)}) collective-permute-start(bf16[3072,128]{1,0:T(8,128)(2,1)S(1)} %get-tuple-element.31), channel_id=1, source_target_pairs={{0,1},{1,0},{2,3},{3,2},{4,5},{5,4},{6,7},{7,6},{8,9},{9,8},{10,11... | collective-permute-start | bytes 2359304 | tf_op jit(solution)/shard_map/ppermute | solution.py:54
  26.6 0.6 %collective-permute-start.9 = (bf16[2112,128]{1,0:T(8,128)(2,1)S(1)}, bf16[2112,128]{1,0:T(8,128)(2,1)S(1)}, u32[]{:S(2)}, u32[]{:S(2)}) collective-permute-start(bf16[2112,128]{1,0:T(8,128)(2,1)S(1)} %pad_maximum_fusion.refs_0_.own_ref), channel_id=1, source_target_pairs={{0,32},{1,9},{2,34},{3,11},{4,36},{5,13},{6,38},{7,15},{8,40},{9,1... | collective-permute-start | bytes 1622024 | tf_op jit(solution)/shard_map/ppermute | solution.py:45
  27.2 2.0 %collective-permute-start.8 = (bf16[2112,128]{1,0:T(8,128)(2,1)S(1)}, bf16[2112,128]{1,0:T(8,128)(2,1)S(1)}, u32[]{:S(2)}, u32[]{:S(2)}) collective-permute-start(bf16[2112,128]{1,0:T(8,128)(2,1)S(1)} %pad_maximum_fusion.refs_0_.own_ref), channel_id=1, source_target_pairs={{0,96},{1,25},{2,98},{3,27},{4,100},{5,29},{6,102},{7,31},{8,104},... | collective-permute-start | bytes 1622024 | tf_op jit(solution)/shard_map/ppermute | solution.py:45
  29.3 0.6 %collective-permute-start.6 = (bf16[2112,128]{1,0:T(8,128)(2,1)S(1)}, bf16[2112,128]{1,0:T(8,128)(2,1)S(1)}, u32[]{:S(2)}, u32[]{:S(2)}) collective-permute-start(bf16[2112,128]{1,0:T(8,128)(2,1)S(1)} %pad_maximum_fusion.refs_0_.own_ref), channel_id=1, source_target_pairs={{0,2},{1,7},{2,4},{3,1},{4,6},{5,3},{6,0},{7,5},{8,10},{9,15},{10,... | collective-permute-start | bytes 1622024 | tf_op jit(solution)/shard_map/ppermute | solution.py:45
  29.9 0.5 %shard_map.57 = (f32[6144,128]{1,0:T(8,128)S(1)}, bf16[768,128]{1,0:T(8,128)(2,1)S(1)}) custom-call(bf16[3072,128]{1,0:T(8,128)(2,1)S(1)} %get-tuple-element.30.near_ref, bf16[3072,128]{1,0:T(8,128)(2,1)S(1)} %collective-permute-done.7.guest_ref, bf16[2112,128]{1,0:T(8,128)(2,1)S(1)} %pad_maximum_fusion.refs_0_.own_ref), custom_call_target="tpu_custom_call" | custom-call | flops 1000 | bytes 1000 | tf_op jit(solution)/shard_map/pallas_call | solution.py:212
  30.4 5.9 %collective-permute-done.9.refs_0_.before_ref = bf16[2112,128]{1,0:T(8,128)(2,1)S(1)} collective-permute-done((bf16[2112,128]{1,0:T(8,128)(2,1)S(1)}, bf16[2112,128]{1,0:T(8,128)(2,1)S(1)}, u32[]{:S(2)}, u32[]{:S(2)}) %collective-permute-start.9) | collective-permute-done | bytes 540704 | tf_op jit(solution)/shard_map/ppermute | solution.py:45
  36.3 0.8 %shard_map.58 = (f32[6144,128]{1,0:T(8,128)S(1)}, bf16[1536,128]{1,0:T(8,128)(2,1)S(1)}) custom-call(bf16[3072,128]{1,0:T(8,128)(2,1)S(1)} %get-tuple-element.30.near_ref, bf16[3072,128]{1,0:T(8,128)(2,1)S(1)} %collective-permute-done.7.guest_ref, bf16[2112,128]{1,0:T(8,128)(2,1)S(1)} %collective-permute-done.9.refs_0_.before_ref, ...), custom_call_target="tpu_custom_call", output_to_operand_aliasing={{0}: (4, {})} | custom-call | flops 1000 | bytes 1000 | tf_op jit(solution)/shard_map/pallas_call | solution.py:212
  37.1 1.0 %collective-permute-start.11 = (bf16[1536,128]{1,0:T(8,128)(2,1)S(1)}, bf16[1536,128]{1,0:T(8,128)(2,1)S(1)}, u32[]{:S(2)}, u32[]{:S(2)}) collective-permute-start(bf16[1536,128]{1,0:T(8,128)(2,1)S(1)} %get-tuple-element.39), channel_id=1, source_target_pairs={{0,1},{1,0},{2,3},{3,2},{4,5},{5,4},{6,7},{7,6},{8,9},{9,8},{10,11... | collective-permute-start | bytes 1179656 | tf_op jit(solution)/shard_map/ppermute | solution.py:54
  38.2 0.7 %shard_map.59.base_ref = f32[4096,128]{1,0:T(8,128)S(1)} custom-call(bf16[4096,128]{1,0:T(8,128)(2,1)S(1)} %bitcast.12, bf16[2112,128]{1,0:T(8,128)(2,1)S(1)} %pad_maximum_fusion.refs_0_.own_ref, bf16[2112,128]{1,0:T(8,128)(2,1)S(1)} %collective-permute-done.9.refs_0_.before_ref, bf16[2112,128]{1,0:T(8,128)(2,1)S(1)} %collective-permute-done.8.refs_1_.after_ref, ...), custom_call_target="tpu_custom_call" | custom-call | flops 1000 | bytes 1000 | tf_op jit(solution)/shard_map/pallas_call | solution.py:176
  38.9 0.5 %shard_map.60 = (f32[6144,128]{1,0:T(8,128)S(1)}, bf16[768,128]{1,0:T(8,128)(2,1)S(1)}) custom-call(bf16[3072,128]{1,0:T(8,128)(2,1)S(1)} %get-tuple-element.30.near_ref, bf16[3072,128]{1,0:T(8,128)(2,1)S(1)} %collective-permute-done.7.guest_ref, bf16[2112,128]{1,0:T(8,128)(2,1)S(1)} %collective-permute-done.6.refs_0_, ...), custom_call_target="tpu_custom_call", output_to_operand_aliasing={{0}: (3, {})} | custom-call | flops 1000 | bytes 1000 | tf_op jit(solution)/shard_map/pallas_call | solution.py:212
  39.4 1.6 %collective-permute-start.12 = (bf16[768,128]{1,0:T(8,128)(2,1)S(1)}, bf16[768,128]{1,0:T(8,128)(2,1)S(1)}, u32[]{:S(2)}, u32[]{:S(2)}) collective-permute-start(bf16[768,128]{1,0:T(8,128)(2,1)S(1)} %get-tuple-element.42), channel_id=1, source_target_pairs={{0,1},{1,0},{2,3},{3,2},{4,5},{5,4},{6,7},{7,6},{8,9},{9,8},{10,11... | collective-permute-start | bytes 589832 | tf_op jit(solution)/shard_map/ppermute | solution.py:54
  41.1 1.1 %collective-permute-done.12.side_ref = bf16[768,128]{1,0:T(8,128)(2,1)S(1)} collective-permute-done((bf16[768,128]{1,0:T(8,128)(2,1)S(1)}, bf16[768,128]{1,0:T(8,128)(2,1)S(1)}, u32[]{:S(2)}, u32[]{:S(2)}) %collective-permute-start.12) | collective-permute-done | bytes 196640 | tf_op jit(solution)/shard_map/ppermute | solution.py:54
  42.1 5.4 %shard_map.61 = (f32[4096,128]{1,0:T(8,128)}, f32[6144,128]{1,0:T(8,128)S(1)}) custom-call(s32[4096]{0:T(1024)S(1)} %bitcast.14, f32[4096,128]{1,0:T(8,128)S(1)} %shard_map.59.base_ref, bf16[768,128]{1,0:T(8,128)(2,1)S(1)} %collective-permute-done.10.own_ref, ...), custom_call_target="tpu_custom_call", output_to_operand_aliasing={{1}: (5, {})} | custom-call | flops 524288 | bytes 10000000 | tf_op jit(solution)/shard_map/pallas_call | solution.py:256
  (24 shorter events, 0.2 us)
Async XLA Ops:
  0.0 13.7 %copy-start = (bf16[1,4096,128]{2,1,0:T(8,128)(2,1)S(1)}, bf16[1,4096,128]{2,1,0:T(8,128)(2,1)}, u32[]{:S(2)}) copy-start(bf16[1,4096,128]{2,1,0:T(8,128)(2,1)} %param.5) | copy-start | bytes 3145732
  0.0 13.6 %collective-permute-start.2 = (bf16[128,128]{1,0:T(8,128)(2,1)}, bf16[128,128]{1,0:T(8,128)(2,1)S(1)}, u32[]{:S(2)}, u32[]{:S(2)}) collective-permute-start(bf16[128,128]{1,0:T(8,128)(2,1)} %bitcast.17), channel_id=1, source_target_pairs={{0,70},{1,23},{2,64},{3,17},{4,66},{5,19},{6,68},{7,21},{8,78},{9,... | collective-permute-start | bytes 98312 | tf_op jit(solution)/shard_map/ppermute | solution.py:45
  7.0 6.6 %collective-permute-start.1 = (bf16[128,128]{1,0:T(8,128)(2,1)}, bf16[128,128]{1,0:T(8,128)(2,1)S(1)}, u32[]{:S(2)}, u32[]{:S(2)}) collective-permute-start(bf16[128,128]{1,0:T(8,128)(2,1)} %bitcast.18), channel_id=1, source_target_pairs={{0,66},{1,19},{2,68},{3,21},{4,70},{5,23},{6,64},{7,17},{8,74},{9,... | collective-permute-start | bytes 98312 | tf_op jit(solution)/shard_map/ppermute | solution.py:45
  7.1 4.5 %collective-permute-start = (bf16[128,128]{1,0:T(8,128)(2,1)}, bf16[128,128]{1,0:T(8,128)(2,1)S(1)}, u32[]{:S(2)}, u32[]{:S(2)}) collective-permute-start(bf16[128,128]{1,0:T(8,128)(2,1)} %bitcast.19), channel_id=1, source_target_pairs={{0,4},{1,5},{2,6},{3,7},{4,0},{5,1},{6,2},{7,3},{8,12},{9,13},{10,... | collective-permute-start | bytes 98312 | tf_op jit(solution)/shard_map/ppermute | solution.py:45
  9.1 0.7 %copy-start.3 = (s32[1,4096,1]{1,2,0:T(1,128)S(1)}, s32[1,4096,1]{1,2,0:T(1,128)}, u32[]{:S(2)}) copy-start(s32[1,4096,1]{1,2,0:T(1,128)} %param.7) | copy-start | bytes 49156
  13.7 8.9 %collective-permute-start.5 = (bf16[528,128]{1,0:T(8,128)(2,1)S(1)}, bf16[528,128]{1,0:T(8,128)(2,1)S(1)}, u32[]{:S(2)}, u32[]{:S(2)}) collective-permute-start(bf16[528,128]{1,0:T(8,128)(2,1)S(1)} %constant_dynamic-update-slice_fusion), channel_id=1, source_target_pairs={{0,24},{1,97},{2,26},{3,99},{4,28},{5,101},{6,30},{7,103},{8,0},{9... | collective-permute-start | bytes 405512 | tf_op jit(solution)/shard_map/ppermute | solution.py:45
  16.5 6.8 %collective-permute-start.4 = (bf16[528,128]{1,0:T(8,128)(2,1)S(1)}, bf16[528,128]{1,0:T(8,128)(2,1)S(1)}, u32[]{:S(2)}, u32[]{:S(2)}) collective-permute-start(bf16[528,128]{1,0:T(8,128)(2,1)S(1)} %constant_dynamic-update-slice_fusion), channel_id=1, source_target_pairs={{0,8},{1,33},{2,10},{3,35},{4,12},{5,37},{6,14},{7,39},{8,16},{9,4... | collective-permute-start | bytes 405512 | tf_op jit(solution)/shard_map/ppermute | solution.py:45
  16.5 6.8 %collective-permute-start.3 = (bf16[528,128]{1,0:T(8,128)(2,1)S(1)}, bf16[528,128]{1,0:T(8,128)(2,1)S(1)}, u32[]{:S(2)}, u32[]{:S(2)}) collective-permute-start(bf16[528,128]{1,0:T(8,128)(2,1)S(1)} %constant_dynamic-update-slice_fusion), channel_id=1, source_target_pairs={{0,16},{1,65},{2,18},{3,67},{4,20},{5,69},{6,22},{7,71},{8,24},{9,... | collective-permute-start | bytes 405512 | tf_op jit(solution)/shard_map/ppermute | solution.py:45
  23.4 6.6 %collective-permute-start.7 = (bf16[3072,128]{1,0:T(8,128)(2,1)S(1)}, bf16[3072,128]{1,0:T(8,128)(2,1)S(1)}, u32[]{:S(2)}, u32[]{:S(2)}) collective-permute-start(bf16[3072,128]{1,0:T(8,128)(2,1)S(1)} %get-tuple-element.31), channel_id=1, source_target_pairs={{0,1},{1,0},{2,3},{3,2},{4,5},{5,4},{6,7},{7,6},{8,9},{9,8},{10,11... | collective-permute-start | bytes 2359304 | tf_op jit(solution)/shard_map/ppermute | solution.py:54
  26.6 9.7 %collective-permute-start.9 = (bf16[2112,128]{1,0:T(8,128)(2,1)S(1)}, bf16[2112,128]{1,0:T(8,128)(2,1)S(1)}, u32[]{:S(2)}, u32[]{:S(2)}) collective-permute-start(bf16[2112,128]{1,0:T(8,128)(2,1)S(1)} %pad_maximum_fusion.refs_0_.own_ref), channel_id=1, source_target_pairs={{0,32},{1,9},{2,34},{3,11},{4,36},{5,13},{6,38},{7,15},{8,40},{9,1... | collective-permute-start | bytes 1622024 | tf_op jit(solution)/shard_map/ppermute | solution.py:45
  27.2 9.1 %collective-permute-start.8 = (bf16[2112,128]{1,0:T(8,128)(2,1)S(1)}, bf16[2112,128]{1,0:T(8,128)(2,1)S(1)}, u32[]{:S(2)}, u32[]{:S(2)}) collective-permute-start(bf16[2112,128]{1,0:T(8,128)(2,1)S(1)} %pad_maximum_fusion.refs_0_.own_ref), channel_id=1, source_target_pairs={{0,96},{1,25},{2,98},{3,27},{4,100},{5,29},{6,102},{7,31},{8,104},... | collective-permute-start | bytes 1622024 | tf_op jit(solution)/shard_map/ppermute | solution.py:45
  29.3 9.7 %collective-permute-start.6 = (bf16[2112,128]{1,0:T(8,128)(2,1)S(1)}, bf16[2112,128]{1,0:T(8,128)(2,1)S(1)}, u32[]{:S(2)}, u32[]{:S(2)}) collective-permute-start(bf16[2112,128]{1,0:T(8,128)(2,1)S(1)} %pad_maximum_fusion.refs_0_.own_ref), channel_id=1, source_target_pairs={{0,2},{1,7},{2,4},{3,1},{4,6},{5,3},{6,0},{7,5},{8,10},{9,15},{10,... | collective-permute-start | bytes 1622024 | tf_op jit(solution)/shard_map/ppermute | solution.py:45
  36.3 1.9 %copy-start.1 = (bf16[128,128]{1,0:T(8,128)(2,1)S(1)}, bf16[128,128]{1,0:T(8,128)(2,1)}, u32[]{:S(2)}) copy-start(bf16[128,128]{1,0:T(8,128)(2,1)} %plane_ref.1) | copy-start | bytes 98308
  36.3 1.9 %copy-start.2 = (f32[1,4096]{1,0:T(1,128)S(1)}, f32[1,4096]{1,0:T(1,128)}, u32[]{:S(2)}) copy-start(f32[1,4096]{1,0:T(1,128)} %param.6) | copy-start | bytes 49156
  37.1 5.0 %collective-permute-start.11 = (bf16[1536,128]{1,0:T(8,128)(2,1)S(1)}, bf16[1536,128]{1,0:T(8,128)(2,1)S(1)}, u32[]{:S(2)}, u32[]{:S(2)}) collective-permute-start(bf16[1536,128]{1,0:T(8,128)(2,1)S(1)} %get-tuple-element.39), channel_id=1, source_target_pairs={{0,1},{1,0},{2,3},{3,2},{4,5},{5,4},{6,7},{7,6},{8,9},{9,8},{10,11... | collective-permute-start | bytes 1179656 | tf_op jit(solution)/shard_map/ppermute | solution.py:54
  38.1 3.0 %collective-permute-start.10 = (bf16[768,128]{1,0:T(8,128)(2,1)S(1)}, bf16[768,128]{1,0:T(8,128)(2,1)S(1)}, u32[]{:S(2)}, u32[]{:S(2)}) collective-permute-start(bf16[768,128]{1,0:T(8,128)(2,1)S(1)} %get-tuple-element.38), channel_id=1, source_target_pairs={{0,1},{1,0},{2,3},{3,2},{4,5},{5,4},{6,7},{7,6},{8,9},{9,8},{10,11... | collective-permute-start | bytes 589832 | tf_op jit(solution)/shard_map/ppermute | solution.py:54
  39.4 2.7 %collective-permute-start.12 = (bf16[768,128]{1,0:T(8,128)(2,1)S(1)}, bf16[768,128]{1,0:T(8,128)(2,1)S(1)}, u32[]{:S(2)}, u32[]{:S(2)}) collective-permute-start(bf16[768,128]{1,0:T(8,128)(2,1)S(1)} %get-tuple-element.42), channel_id=1, source_target_pairs={{0,1},{1,0},{2,3},{3,2},{4,5},{5,4},{6,7},{7,6},{8,9},{9,8},{10,11... | collective-permute-start | bytes 589832 | tf_op jit(solution)/shard_map/ppermute | solution.py:54

commit v7 on v6

--- a/solution.py
+++ b/solution.py
@@ -192,38 +192,43 @@
     return reluct * response
 
 
-def effect_kernel(thirds, near_ref, guest_ref, *refs):
-    operators, (effect_ref, reply_ref) = refs[: len(thirds)], refs[-2:]
-    for number, (third, operator_ref) in enumerate(zip(thirds, operators)):
+def effect_kernel(thirds, places, rows_ref, *refs):
+    operators, out_ref = refs[: len(thirds)], refs[-1]
+    for third, place, operator_ref in zip(thirds, places, operators):
         for k in range(16):
             top = k // 4 * stride + k % 4 * vals
-            operator = operator_ref[top : top + vals, :]
-            lo, out = third * block + k * cap, number * block + k * cap
-            effect_ref[lo : lo + cap, :] = respond(near_ref[lo : lo + cap, :], operator)
-            reply_ref[out : out + cap, :] = respond(guest_ref[lo : lo + cap, :], operator).astype(
-                jnp.bfloat16
-            )
-
-
-def effects(near, guest, operators, thirds, previous):
-    operands = [near, guest, *operators]
-    if previous is not None:
-        operands.append(previous)
-    return pl.pallas_call(
-        functools.partial(effect_kernel, thirds),
+            lo, out = third * block + k * cap, place * block + k * cap
+            effect = respond(rows_ref[lo : lo + cap, :], operator_ref[top : top + vals, :])
+            out_ref[out : out + cap, :] = effect.astype(out_ref.dtype)
+
+
+def effect_call(operands, thirds, places, shape, dtype, aliases):
+    return pl.pallas_call(
+        functools.partial(effect_kernel, thirds, places),
         in_specs=[in_vmem] * len(operands),
-        out_specs=[in_vmem, in_vmem],
-        out_shape=[
-            jax.ShapeDtypeStruct((slots, vals), jnp.float32),
-            jax.ShapeDtypeStruct((len(thirds) * block, vals), jnp.bfloat16),
-        ],
-        input_output_aliases={} if previous is None else {len(operands) - 1: 0},
+        out_specs=in_vmem,
+        out_shape=jax.ShapeDtypeStruct((shape, vals), dtype),
+        input_output_aliases=aliases,
         compiler_params=params(),
         cost_estimate=pl.CostEstimate(flops=1000, bytes_accessed=1000, transcendentals=0),
     )(*operands)
 
 
-part_rows = 512
+def replies(guest, operators, thirds):
+    count = len(thirds)
+    return effect_call([guest, *operators], thirds, range(count), count * block, jnp.bfloat16, {})
+
+
+def effects(near, operators, thirds, previous):
+    operands = [near, *operators]
+    aliases = {}
+    if previous is not None:
+        aliases = {len(operands): 0}
+        operands.append(previous)
+    return effect_call(operands, thirds, thirds, slots, jnp.float32, aliases)
+
+
+part_tops = (0, 1024, 2048, 3072, 3584, 3840, rows)
 
 
 def final_kernel(slot_ref, base_ref, own_ref, pair_ref, side_ref, _, out_ref, effect_ref, result, sent):
@@ -231,24 +236,23 @@
         lo = half + third * block
         effect_ref[lo : lo + returned_ref.shape[0], :] = returned_ref[...].astype(jnp.float32)
 
-    def copy(part):
-        span = pl.ds(pl.multiple_of(part * part_rows, part_rows), part_rows)
-        return pltpu.make_async_copy(result.at[span], out_ref.at[span], sent.at[part])
-
-    for part in range(rows // part_rows):
+    copies = []
+    for number, (top, end) in enumerate(zip(part_tops, part_tops[1:])):
 
         def body(i, carry):
-            first = pl.multiple_of(part * part_rows + i * unroll, unroll)
+            first = pl.multiple_of(top + i * unroll, unroll)
             for j in range(unroll):
                 effect = effect_ref[pl.ds(slot_ref[first + j], 1), :]
                 row = pl.ds(first + j, 1)
                 result[row, :] = base_ref[row, :] - step_size * effect
             return carry
 
-        lax.fori_loop(0, part_rows // unroll, body, 0)
-        copy(part).start()
-    for part in range(rows // part_rows):
-        copy(part).wait()
+        lax.fori_loop(0, (end - top) // unroll, body, 0)
+        span = slice(top, end)
+        copies.append(pltpu.make_async_copy(result.at[span], out_ref.at[span], sent.at[number]))
+        copies[-1].start()
+    for copy in copies:
+        copy.wait()
 
 
 def finish(slot, base, returned, effect):
@@ -264,7 +268,7 @@
         input_output_aliases={len(operands) - 1: 1},
         scratch_shapes=[
             pltpu.VMEM((rows, vals), jnp.float32),
-            pltpu.SemaphoreType.DMA((rows // part_rows,)),
+            pltpu.SemaphoreType.DMA((len(part_tops) - 1,)),
         ],
         compiler_params=params(),
         cost_estimate=pl.CostEstimate(flops=4096 * 128, bytes_accessed=10000000, transcendentals=0),
@@ -284,15 +288,14 @@
     plus, minus = shifted(plane, third_moves), shifted(plane, scaled(third_moves, -1))
     side = shifted(plane, side_moves)
     guest = core_swap(far_rows)
-    effect, reply = effects(near_rows, guest, [plane], (0,), None)
+    reply = replies(guest, [plane], (0,))
+    effect = effects(near_rows, [plane], (0,), None)
+    minus, plus, effect, reply = tied((minus, plus, effect, reply))
     returned = [core_swap(reply)]
-    minus, plus, effect = tied((minus, plus, effect))
-    effect, reply = effects(near_rows, guest, [plus, minus], (2, 3), effect)
-    returned.append(core_swap(reply))
+    returned.append(core_swap(replies(guest, [plus, minus], (2, 3))))
+    returned.append(core_swap(replies(guest, [side], (1,))))
+    effect = effects(near_rows, [side, plus, minus], (1, 2, 3), effect)
     base = stencil(field, plane, plus, minus, coupling.reshape(rows // vals, vals), in_plane)
-    side, effect, base = tied((side, effect, base))
-    effect, reply = effects(near_rows, guest, [side], (1,), effect)
-    returned.append(core_swap(reply))
     return finish(slot, base, returned, effect)[None]
 
 

time: 47.8 us -> 46.8 us (0.979)
  waiting for transfers between devices: 10.7 us -> 6.97 us
  starting transfers between devices: 22 us -> 24.4 us
    ppermute x9, starting transfers between devices: 16.1 us -> 19.8 us  [shifted(): return lax.ppermute(value, axes_all, pairs)]
    ppermute x9, waiting for transfers between devices: 9.62 us -> 6.96 us  [shifted(): return lax.ppermute(value, axes_all, pairs)]
    ppermute x4, starting transfers between devices: 5.97 us -> 4.57 us  [core_swap(): return lax.ppermute(value, axes_all, pairs)]
    ppermute x4, waiting for transfers between devices: 1.08 us -> 0.01 us  [core_swap(): return lax.ppermute(value, axes_all, pairs)]
    pallas_call x3 -> x5, Pallas kernels: 1.77 us -> 2.21 us  [effect_call(): pl.pallas_call(functools.partial(effect_kernel, thirds, places), in_specs...]
  transfers between devices with their start and end apart: 13 -> 13, of which waited for: 5 -> 3; matrix products, arithmetic and copies ran while one was open for 2% -> 2% of each run, Pallas kernels for 16% -> 18%
where the time goes in v7:
time: 46.8 us; the launch traced here: 46.6 us
  starting transfers between devices  24.4 us (52%)
  Pallas kernels  13.5 us (29%)
  waiting for transfers between devices  6.97 us (15%)
  local copies, waits for them, and re-layouts  1.57 us (3%)
    ppermute x9, starting transfers between devices, shifted(): return lax.ppermute(value, axes_all, pairs)  19.8 us
    ppermute x9, waiting for transfers between devices, shifted(): return lax.ppermute(value, axes_all, pairs)  6.96 us
    pallas_call x1, Pallas kernels, finish(): pl.pallas_call(final_kernel, in_specs=[pl.BlockSpec(memory_space=pltpu.SM...  5.33 us
    ppermute x4, starting transfers between devices, core_swap(): return lax.ppermute(value, axes_all, pairs)  4.57 us
    pallas_call x1, Pallas kernels, sort_rows(): pl.pallas_call(sort_kernel, in_specs=[pl.BlockSpec(memory_space=pltpu.SME...  4.46 us
    pallas_call x5, Pallas kernels, effect_call(): pl.pallas_call(functools.partial(effect_kernel, thirds, places), in_specs...  2.21 us
    unnamed x13, local copies, waits for them, and re-layouts  1.57 us
  transfers between devices with their start and end apart: 13, of which 3 were waited for; matrix products, arithmetic and copies ran while one was open for 2% of the time, Pallas kernels for 18%

profile of v7, /device:TPU:1, one launch (start us, length us, event | category | flops | bytes accessed | tf_op | source)
XLA Modules:
  0.0 46.6 jit_solution(9535128907571897647)
XLA Ops:
  0.0 4.4 %collective-permute-start = (bf16[128,128]{1,0:T(8,128)(2,1)}, bf16[128,128]{1,0:T(8,128)(2,1)S(1)}, u32[]{:S(2)}, u32[]{:S(2)}) collective-permute-start(bf16[128,128]{1,0:T(8,128)(2,1)} %bitcast.17), channel_id=1, source_target_pairs={{0,4},{1,5},{2,6},{3,7},{4,0},{5,1},{6,2},{7,3},{8,12},{9,13},{10,... | collective-permute-start | bytes 98312 | tf_op jit(solution)/shard_map/ppermute | solution.py:45
  4.4 3.2 %collective-permute-start.1 = (bf16[128,128]{1,0:T(8,128)(2,1)}, bf16[128,128]{1,0:T(8,128)(2,1)S(1)}, u32[]{:S(2)}, u32[]{:S(2)}) collective-permute-start(bf16[128,128]{1,0:T(8,128)(2,1)} %bitcast.18), channel_id=1, source_target_pairs={{0,66},{1,19},{2,68},{3,21},{4,70},{5,23},{6,64},{7,17},{8,74},{9,... | collective-permute-start | bytes 98312 | tf_op jit(solution)/shard_map/ppermute | solution.py:45
  7.6 1.9 %collective-permute-start.2 = (bf16[128,128]{1,0:T(8,128)(2,1)}, bf16[128,128]{1,0:T(8,128)(2,1)S(1)}, u32[]{:S(2)}, u32[]{:S(2)}) collective-permute-start(bf16[128,128]{1,0:T(8,128)(2,1)} %bitcast.19), channel_id=1, source_target_pairs={{0,70},{1,23},{2,64},{3,17},{4,66},{5,19},{6,68},{7,21},{8,78},{9,... | collective-permute-start | bytes 98312 | tf_op jit(solution)/shard_map/ppermute | solution.py:45
  9.5 0.8 %constant_dynamic-update-slice_fusion.5 = bf16[528,128]{1,0:T(8,128)(2,1)S(1)} fusion(bf16[1,128,128]{2,1,0:T(8,128)(2,1)} %param.9), kind=kLoop, calls=%fused_computation.6 | loop fusion | bytes 65536
  10.3 0.7 %copy-done.3 = s32[1,4096,1]{1,2,0:T(1,128)S(1)} copy-done((s32[1,4096,1]{1,2,0:T(1,128)S(1)}, s32[1,4096,1]{1,2,0:T(1,128)}, u32[]{:S(2)}) %copy-start.3) | copy-done | bytes 16408
  11.0 0.8 %shard_map.55 = s32[1,4096]{1,0:T(1,128)S(1)} custom-call(s32[1,4096]{1,0:T(1,128)S(1)} %bitcast.16), custom_call_target="tpu_custom_call" | custom-call | flops 402653184 | bytes 100000 | tf_op jit(solution)/shard_map/pallas_call | solution.py:104
  11.9 1.1 %collective-permute-done.2 = bf16[128,128]{1,0:T(8,128)(2,1)S(1)} collective-permute-done((bf16[128,128]{1,0:T(8,128)(2,1)}, bf16[128,128]{1,0:T(8,128)(2,1)S(1)}, u32[]{:S(2)}, u32[]{:S(2)}) %collective-permute-start.2) | collective-permute-done | bytes 32800 | tf_op jit(solution)/shard_map/ppermute | solution.py:45
  13.0 3.0 %collective-permute-start.3 = (bf16[528,128]{1,0:T(8,128)(2,1)S(1)}, bf16[528,128]{1,0:T(8,128)(2,1)S(1)}, u32[]{:S(2)}, u32[]{:S(2)}) collective-permute-start(bf16[528,128]{1,0:T(8,128)(2,1)S(1)} %constant_dynamic-update-slice_fusion), channel_id=1, source_target_pairs={{0,16},{1,65},{2,18},{3,67},{4,20},{5,69},{6,22},{7,71},{8,24},{9,... | collective-permute-start | bytes 405512 | tf_op jit(solution)/shard_map/ppermute | solution.py:45
  16.0 0.7 %collective-permute-start.4 = (bf16[528,128]{1,0:T(8,128)(2,1)S(1)}, bf16[528,128]{1,0:T(8,128)(2,1)S(1)}, u32[]{:S(2)}, u32[]{:S(2)}) collective-permute-start(bf16[528,128]{1,0:T(8,128)(2,1)S(1)} %constant_dynamic-update-slice_fusion), channel_id=1, source_target_pairs={{0,8},{1,33},{2,10},{3,35},{4,12},{5,37},{6,14},{7,39},{8,16},{9,4... | collective-permute-start | bytes 405512 | tf_op jit(solution)/shard_map/ppermute | solution.py:45
  16.7 2.0 %collective-permute-start.5 = (bf16[528,128]{1,0:T(8,128)(2,1)S(1)}, bf16[528,128]{1,0:T(8,128)(2,1)S(1)}, u32[]{:S(2)}, u32[]{:S(2)}) collective-permute-start(bf16[528,128]{1,0:T(8,128)(2,1)S(1)} %constant_dynamic-update-slice_fusion), channel_id=1, source_target_pairs={{0,24},{1,97},{2,26},{3,99},{4,28},{5,101},{6,30},{7,103},{8,0},{9... | collective-permute-start | bytes 405512 | tf_op jit(solution)/shard_map/ppermute | solution.py:45
  18.7 4.5 %shard_map.56 = (bf16[3072,128]{1,0:T(8,128)(2,1)S(1)}, bf16[3072,128]{1,0:T(8,128)(2,1)S(1)}) custom-call(s32[4096]{0:T(1024)S(1)} %bitcast.13, bf16[4096,128]{1,0:T(8,128)(2,1)S(1)} %bitcast.11), custom_call_target="tpu_custom_call" | custom-call | bytes 20000000 | tf_op jit(solution)/shard_map/pallas_call | solution.py:127
  23.3 3.3 %collective-permute-start.8 = (bf16[3072,128]{1,0:T(8,128)(2,1)S(1)}, bf16[3072,128]{1,0:T(8,128)(2,1)S(1)}, u32[]{:S(2)}, u32[]{:S(2)}) collective-permute-start(bf16[3072,128]{1,0:T(8,128)(2,1)S(1)} %get-tuple-element.23), channel_id=1, source_target_pairs={{0,1},{1,0},{2,3},{3,2},{4,5},{5,4},{6,7},{7,6},{8,9},{9,8},{10,11... | collective-permute-start | bytes 2359304 | tf_op jit(solution)/shard_map/ppermute | solution.py:54
  26.6 1.4 %collective-permute-start.6 = (bf16[2112,128]{1,0:T(8,128)(2,1)S(1)}, bf16[2112,128]{1,0:T(8,128)(2,1)S(1)}, u32[]{:S(2)}, u32[]{:S(2)}) collective-permute-start(bf16[2112,128]{1,0:T(8,128)(2,1)S(1)} %pad_maximum_fusion.refs_0_.own_ref), channel_id=1, source_target_pairs={{0,96},{1,25},{2,98},{3,27},{4,100},{5,29},{6,102},{7,31},{8,104},... | collective-permute-start | bytes 1622024 | tf_op jit(solution)/shard_map/ppermute | solution.py:45
  28.0 3.1 %collective-permute-start.11 = (bf16[2112,128]{1,0:T(8,128)(2,1)S(1)}, bf16[2112,128]{1,0:T(8,128)(2,1)S(1)}, u32[]{:S(2)}, u32[]{:S(2)}) collective-permute-start(bf16[2112,128]{1,0:T(8,128)(2,1)S(1)} %pad_maximum_fusion.refs_0_.own_ref), channel_id=1, source_target_pairs={{0,2},{1,7},{2,4},{3,1},{4,6},{5,3},{6,0},{7,5},{8,10},{9,15},{10,... | collective-permute-start | bytes 1622024 | tf_op jit(solution)/shard_map/ppermute | solution.py:45
  31.6 0.4 shard_map.58
  31.9 3.1 %collective-permute-done.6.after_ref.refs_1_.refs_2_ = bf16[2112,128]{1,0:T(8,128)(2,1)S(1)} collective-permute-done((bf16[2112,128]{1,0:T(8,128)(2,1)S(1)}, bf16[2112,128]{1,0:T(8,128)(2,1)S(1)}, u32[]{:S(2)}, u32[]{:S(2)}) %collective-permute-start.6) | collective-permute-done | bytes 540704 | tf_op jit(solution)/shard_map/ppermute | solution.py:45
  35.1 2.6 %collective-permute-done.7.before_ref.refs_0_.refs_1_ = bf16[2112,128]{1,0:T(8,128)(2,1)S(1)} collective-permute-done((bf16[2112,128]{1,0:T(8,128)(2,1)S(1)}, bf16[2112,128]{1,0:T(8,128)(2,1)S(1)}, u32[]{:S(2)}, u32[]{:S(2)}) %collective-permute-start.7) | collective-permute-done | bytes 540704 | tf_op jit(solution)/shard_map/ppermute | solution.py:45
  37.7 0.5 %shard_map.60 = bf16[1536,128]{1,0:T(8,128)(2,1)S(1)} custom-call(bf16[3072,128]{1,0:T(8,128)(2,1)S(1)} %collective-permute-done.8.rows_ref, bf16[2112,128]{1,0:T(8,128)(2,1)S(1)} %collective-permute-done.7.before_ref.refs_0_.refs_1_, bf16[2112,128]{1,0:T(8,128)(2,1)S(1)} %collective-permute-done.6.after_ref.refs_1_.refs_2_), custom_call_target="tpu_custom_call" | custom-call | flops 1000 | bytes 1000 | tf_op jit(solution)/shard_map/pallas_call | solution.py:206
  38.2 0.6 %collective-permute-start.10 = (bf16[1536,128]{1,0:T(8,128)(2,1)S(1)}, bf16[1536,128]{1,0:T(8,128)(2,1)S(1)}, u32[]{:S(2)}, u32[]{:S(2)}) collective-permute-start(bf16[1536,128]{1,0:T(8,128)(2,1)S(1)} %shard_map.60), channel_id=1, source_target_pairs={{0,1},{1,0},{2,3},{3,2},{4,5},{5,4},{6,7},{7,6},{8,9},{9,8},{10,11... | collective-permute-start | bytes 1179656 | tf_op jit(solution)/shard_map/ppermute | solution.py:54
  39.0 0.4 shard_map.61
  39.3 0.5 %collective-permute-start.12 = (bf16[768,128]{1,0:T(8,128)(2,1)S(1)}, bf16[768,128]{1,0:T(8,128)(2,1)S(1)}, u32[]{:S(2)}, u32[]{:S(2)}) collective-permute-start(bf16[768,128]{1,0:T(8,128)(2,1)S(1)} %shard_map.61), channel_id=1, source_target_pairs={{0,1},{1,0},{2,3},{3,2},{4,5},{5,4},{6,7},{7,6},{8,9},{9,8},{10,11... | collective-permute-start | bytes 589832 | tf_op jit(solution)/shard_map/ppermute | solution.py:54
  39.9 0.7 %shard_map.59.base_ref = f32[4096,128]{1,0:T(8,128)S(1)} custom-call(bf16[4096,128]{1,0:T(8,128)(2,1)S(1)} %bitcast.12, bf16[2112,128]{1,0:T(8,128)(2,1)S(1)} %pad_maximum_fusion.refs_0_.own_ref, bf16[2112,128]{1,0:T(8,128)(2,1)S(1)} %collective-permute-done.7.before_ref.refs_0_.refs_1_, ...), custom_call_target="tpu_custom_call" | custom-call | flops 1000 | bytes 1000 | tf_op jit(solution)/shard_map/pallas_call | solution.py:176
  40.6 0.6 %shard_map.62._ = f32[6144,128]{1,0:T(8,128)S(1)} custom-call(bf16[3072,128]{1,0:T(8,128)(2,1)S(1)} %get-tuple-element.22.rows_ref, bf16[2112,128]{1,0:T(8,128)(2,1)S(1)} %collective-permute-done.11.refs_0_, bf16[2112,128]{1,0:T(8,128)(2,1)S(1)} %collective-permute-done.7.before_ref.refs_0_.refs_1_, ...), custom_call_target="tpu_custom_call", output_to_operand_aliasing={{}: (4, {})} | custom-call | flops 1000 | bytes 1000 | tf_op jit(solution)/shard_map/pallas_call | solution.py:206
  41.3 5.3 %shard_map.63 = (f32[4096,128]{1,0:T(8,128)}, f32[6144,128]{1,0:T(8,128)S(1)}) custom-call(s32[4096]{0:T(1024)S(1)} %bitcast.14, f32[4096,128]{1,0:T(8,128)S(1)} %shard_map.59.base_ref, bf16[768,128]{1,0:T(8,128)(2,1)S(1)} %collective-permute-done.9.own_ref, bf16[1536,128]{1,0:T(8,128)(2,1)S(1)} %collective-permute-done.10.pair_ref, ...), custom_call_target="tpu_custom_call", output_to_operand_aliasing={{1}: (5, {})} | custom-call | flops 524288 | bytes 10000000 | tf_op jit(solution)/shard_map/pallas_call | solution.py:260
  (26 shorter events, 0.6 us)
Async XLA Ops:
  0.0 13.0 %copy-start = (bf16[1,4096,128]{2,1,0:T(8,128)(2,1)S(1)}, bf16[1,4096,128]{2,1,0:T(8,128)(2,1)}, u32[]{:S(2)}) copy-start(bf16[1,4096,128]{2,1,0:T(8,128)(2,1)} %param.5) | copy-start | bytes 3145732
  0.0 11.8 %collective-permute-start = (bf16[128,128]{1,0:T(8,128)(2,1)}, bf16[128,128]{1,0:T(8,128)(2,1)S(1)}, u32[]{:S(2)}, u32[]{:S(2)}) collective-permute-start(bf16[128,128]{1,0:T(8,128)(2,1)} %bitcast.17), channel_id=1, source_target_pairs={{0,4},{1,5},{2,6},{3,7},{4,0},{5,1},{6,2},{7,3},{8,12},{9,13},{10,... | collective-permute-start | bytes 98312 | tf_op jit(solution)/shard_map/ppermute | solution.py:45
  4.4 7.4 %collective-permute-start.1 = (bf16[128,128]{1,0:T(8,128)(2,1)}, bf16[128,128]{1,0:T(8,128)(2,1)S(1)}, u32[]{:S(2)}, u32[]{:S(2)}) collective-permute-start(bf16[128,128]{1,0:T(8,128)(2,1)} %bitcast.18), channel_id=1, source_target_pairs={{0,66},{1,19},{2,68},{3,21},{4,70},{5,23},{6,64},{7,17},{8,74},{9,... | collective-permute-start | bytes 98312 | tf_op jit(solution)/shard_map/ppermute | solution.py:45
  7.6 5.4 %collective-permute-start.2 = (bf16[128,128]{1,0:T(8,128)(2,1)}, bf16[128,128]{1,0:T(8,128)(2,1)S(1)}, u32[]{:S(2)}, u32[]{:S(2)}) collective-permute-start(bf16[128,128]{1,0:T(8,128)(2,1)} %bitcast.19), channel_id=1, source_target_pairs={{0,70},{1,23},{2,64},{3,17},{4,66},{5,19},{6,68},{7,21},{8,78},{9,... | collective-permute-start | bytes 98312 | tf_op jit(solution)/shard_map/ppermute | solution.py:45
  10.3 0.7 %copy-start.3 = (s32[1,4096,1]{1,2,0:T(1,128)S(1)}, s32[1,4096,1]{1,2,0:T(1,128)}, u32[]{:S(2)}) copy-start(s32[1,4096,1]{1,2,0:T(1,128)} %param.7) | copy-start | bytes 49156
  13.0 10.1 %collective-permute-start.3 = (bf16[528,128]{1,0:T(8,128)(2,1)S(1)}, bf16[528,128]{1,0:T(8,128)(2,1)S(1)}, u32[]{:S(2)}, u32[]{:S(2)}) collective-permute-start(bf16[528,128]{1,0:T(8,128)(2,1)S(1)} %constant_dynamic-update-slice_fusion), channel_id=1, source_target_pairs={{0,16},{1,65},{2,18},{3,67},{4,20},{5,69},{6,22},{7,71},{8,24},{9,... | collective-permute-start | bytes 405512 | tf_op jit(solution)/shard_map/ppermute | solution.py:45
  16.0 7.2 %collective-permute-start.4 = (bf16[528,128]{1,0:T(8,128)(2,1)S(1)}, bf16[528,128]{1,0:T(8,128)(2,1)S(1)}, u32[]{:S(2)}, u32[]{:S(2)}) collective-permute-start(bf16[528,128]{1,0:T(8,128)(2,1)S(1)} %constant_dynamic-update-slice_fusion), channel_id=1, source_target_pairs={{0,8},{1,33},{2,10},{3,35},{4,12},{5,37},{6,14},{7,39},{8,16},{9,4... | collective-permute-start | bytes 405512 | tf_op jit(solution)/shard_map/ppermute | solution.py:45
  16.7 6.5 %collective-permute-start.5 = (bf16[528,128]{1,0:T(8,128)(2,1)S(1)}, bf16[528,128]{1,0:T(8,128)(2,1)S(1)}, u32[]{:S(2)}, u32[]{:S(2)}) collective-permute-start(bf16[528,128]{1,0:T(8,128)(2,1)S(1)} %constant_dynamic-update-slice_fusion), channel_id=1, source_target_pairs={{0,24},{1,97},{2,26},{3,99},{4,28},{5,101},{6,30},{7,103},{8,0},{9... | collective-permute-start | bytes 405512 | tf_op jit(solution)/shard_map/ppermute | solution.py:45
  23.3 8.3 %collective-permute-start.8 = (bf16[3072,128]{1,0:T(8,128)(2,1)S(1)}, bf16[3072,128]{1,0:T(8,128)(2,1)S(1)}, u32[]{:S(2)}, u32[]{:S(2)}) collective-permute-start(bf16[3072,128]{1,0:T(8,128)(2,1)S(1)} %get-tuple-element.23), channel_id=1, source_target_pairs={{0,1},{1,0},{2,3},{3,2},{4,5},{5,4},{6,7},{7,6},{8,9},{9,8},{10,11... | collective-permute-start | bytes 2359304 | tf_op jit(solution)/shard_map/ppermute | solution.py:54
  26.6 8.5 %collective-permute-start.6 = (bf16[2112,128]{1,0:T(8,128)(2,1)S(1)}, bf16[2112,128]{1,0:T(8,128)(2,1)S(1)}, u32[]{:S(2)}, u32[]{:S(2)}) collective-permute-start(bf16[2112,128]{1,0:T(8,128)(2,1)S(1)} %pad_maximum_fusion.refs_0_.own_ref), channel_id=1, source_target_pairs={{0,96},{1,25},{2,98},{3,27},{4,100},{5,29},{6,102},{7,31},{8,104},... | collective-permute-start | bytes 1622024 | tf_op jit(solution)/shard_map/ppermute | solution.py:45
  28.0 9.7 %collective-permute-start.7 = (bf16[2112,128]{1,0:T(8,128)(2,1)S(1)}, bf16[2112,128]{1,0:T(8,128)(2,1)S(1)}, u32[]{:S(2)}, u32[]{:S(2)}) collective-permute-start(bf16[2112,128]{1,0:T(8,128)(2,1)S(1)} %pad_maximum_fusion.refs_0_.own_ref), channel_id=1, source_target_pairs={{0,32},{1,9},{2,34},{3,11},{4,36},{5,13},{6,38},{7,15},{8,40},{9,1... | collective-permute-start | bytes 1622024 | tf_op jit(solution)/shard_map/ppermute | solution.py:45
  28.0 10.9 %collective-permute-start.11 = (bf16[2112,128]{1,0:T(8,128)(2,1)S(1)}, bf16[2112,128]{1,0:T(8,128)(2,1)S(1)}, u32[]{:S(2)}, u32[]{:S(2)}) collective-permute-start(bf16[2112,128]{1,0:T(8,128)(2,1)S(1)} %pad_maximum_fusion.refs_0_.own_ref), channel_id=1, source_target_pairs={{0,2},{1,7},{2,4},{3,1},{4,6},{5,3},{6,0},{7,5},{8,10},{9,15},{10,... | collective-permute-start | bytes 1622024 | tf_op jit(solution)/shard_map/ppermute | solution.py:45
  38.2 1.7 %copy-start.1 = (bf16[128,128]{1,0:T(8,128)(2,1)S(1)}, bf16[128,128]{1,0:T(8,128)(2,1)}, u32[]{:S(2)}) copy-start(bf16[128,128]{1,0:T(8,128)(2,1)} %plane_ref.1) | copy-start | bytes 98308
  38.2 1.7 %copy-start.2 = (f32[1,4096]{1,0:T(1,128)S(1)}, f32[1,4096]{1,0:T(1,128)}, u32[]{:S(2)}) copy-start(f32[1,4096]{1,0:T(1,128)} %param.6) | copy-start | bytes 49156
  38.2 3.0 %collective-permute-start.10 = (bf16[1536,128]{1,0:T(8,128)(2,1)S(1)}, bf16[1536,128]{1,0:T(8,128)(2,1)S(1)}, u32[]{:S(2)}, u32[]{:S(2)}) collective-permute-start(bf16[1536,128]{1,0:T(8,128)(2,1)S(1)} %shard_map.60), channel_id=1, source_target_pairs={{0,1},{1,0},{2,3},{3,2},{4,5},{5,4},{6,7},{7,6},{8,9},{9,8},{10,11... | collective-permute-start | bytes 1179656 | tf_op jit(solution)/shard_map/ppermute | solution.py:54
  38.9 2.4 %collective-permute-start.9 = (bf16[768,128]{1,0:T(8,128)(2,1)S(1)}, bf16[768,128]{1,0:T(8,128)(2,1)S(1)}, u32[]{:S(2)}, u32[]{:S(2)}) collective-permute-start(bf16[768,128]{1,0:T(8,128)(2,1)S(1)} %shard_map.58), channel_id=1, source_target_pairs={{0,1},{1,0},{2,3},{3,2},{4,5},{5,4},{6,7},{7,6},{8,9},{9,8},{10,11... | collective-permute-start | bytes 589832 | tf_op jit(solution)/shard_map/ppermute | solution.py:54
  39.3 1.9 %collective-permute-start.12 = (bf16[768,128]{1,0:T(8,128)(2,1)S(1)}, bf16[768,128]{1,0:T(8,128)(2,1)S(1)}, u32[]{:S(2)}, u32[]{:S(2)}) collective-permute-start(bf16[768,128]{1,0:T(8,128)(2,1)S(1)} %shard_map.61), channel_id=1, source_target_pairs={{0,1},{1,0},{2,3},{3,2},{4,5},{5,4},{6,7},{7,6},{8,9},{9,8},{10,11... | collective-permute-start | bytes 589832 | tf_op jit(solution)/shard_map/ppermute | solution.py:54

commit v8 on v7

--- a/solution.py
+++ b/solution.py
@@ -18,6 +18,7 @@
 block = 16 * cap
 chunk = 256
 unroll = 128
+long_unroll = 256
 group = 4 * vals
 stride = group + 16
 vmem_bytes = 20 * 1024 * 1024
@@ -109,7 +110,7 @@
     )(owner)
 
 
-def sort_kernel(slot_ref, field_ref, near_ref, far_ref, wide, placed):
+def sort_kernel(slot_ref, field_ref, near_ref, own_ref, side_ref, pair_ref, wide, placed):
     wide[...] = field_ref[...].astype(jnp.float32)
 
     def body(i, carry):
@@ -120,15 +121,19 @@
 
     lax.fori_loop(0, rows // unroll, body, 0)
     near_ref[...] = placed[:half].astype(jnp.bfloat16)
-    far_ref[...] = placed[half:].astype(jnp.bfloat16)
+    own_ref[...] = placed[half : half + block].astype(jnp.bfloat16)
+    side_ref[...] = placed[half + block : half + 2 * block].astype(jnp.bfloat16)
+    pair_ref[...] = placed[half + 2 * block :].astype(jnp.bfloat16)
 
 
 def sort_rows(slot, field):
     return pl.pallas_call(
         sort_kernel,
         in_specs=[pl.BlockSpec(memory_space=pltpu.SMEM), in_vmem],
-        out_specs=[in_vmem, in_vmem],
-        out_shape=[jax.ShapeDtypeStruct((half, vals), jnp.bfloat16)] * 2,
+        out_specs=[in_vmem] * 4,
+        out_shape=[
+            jax.ShapeDtypeStruct((count * block, vals), jnp.bfloat16) for count in (4, 1, 1, 2)
+        ],
         scratch_shapes=[pltpu.VMEM((rows, vals), jnp.float32), pltpu.VMEM((slots, vals), jnp.float32)],
         compiler_params=params(),
         cost_estimate=pl.CostEstimate(flops=0, bytes_accessed=20000000, transcendentals=0),
@@ -146,9 +151,7 @@
     return jnp.where(choice == 0, ends(own_ref, label), corner).astype(jnp.bfloat16)
 
 
-def stencil_kernel(
-    field_ref, own_ref, before_ref, after_ref, coupling_ref, plane_ref, base_ref, projected
-):
+def ends_kernel(own_ref, before_ref, after_ref, coupling_ref, plane_ref, out_ref):
     plane = plane_ref[...]
     sub, lam = lax.axis_index("sub"), lax.axis_index("lam")
     x, inner = sub % 4, jnp.where(lam % 2 == 0, 0, 2)
@@ -156,8 +159,27 @@
     before = halo(choice, own_ref, before_ref, 2)
     choice = jnp.where(sub == 15, 3, jnp.where(x == 3, 1, inner))
     after = halo(choice, own_ref, after_ref, 3)
-    projected[0:8, :] = jnp.dot(before, plane, preferred_element_type=jnp.float32)[8:16]
-    projected[rows + 8 : rows + 16, :] = jnp.dot(after, plane, preferred_element_type=jnp.float32)[0:8]
+    before = jnp.dot(before, plane, preferred_element_type=jnp.float32)[15:16]
+    after = jnp.dot(after, plane, preferred_element_type=jnp.float32)[0:1]
+    out_ref[0:1, :] = step_size * coupling_ref[0:1, 0:1] * before
+    out_ref[1:2, :] = step_size * coupling_ref[31:32, 127:128] * after
+
+
+def end_terms(own, before, after, coupling, plane):
+    return pl.pallas_call(
+        ends_kernel,
+        in_specs=[in_vmem] * 5,
+        out_specs=in_vmem,
+        out_shape=jax.ShapeDtypeStruct((8, vals), jnp.float32),
+        compiler_params=params(),
+        cost_estimate=pl.CostEstimate(flops=1000, bytes_accessed=1000, transcendentals=0),
+    )(own, before, after, coupling, plane)
+
+
+def stencil_kernel(field_ref, coupling_ref, plane_ref, base_ref, projected):
+    plane = plane_ref[...]
+    projected[0:8, :] = jnp.zeros((8, vals), jnp.float32)
+    projected[rows + 8 : rows + 16, :] = jnp.zeros((8, vals), jnp.float32)
     for j in range(rows // 512):
         projected[8 + j * 512 : 8 + (j + 1) * 512, :] = jnp.dot(
             field_ref[j * 512 : (j + 1) * 512, :], plane, preferred_element_type=jnp.float32
@@ -172,16 +194,16 @@
         base_ref[lo : lo + vals, :] = field - step_size * (weight * (2.0 * here - before - after))
 
 
-def stencil(field, own, before, after, coupling, plane):
+def stencil(field, coupling, plane):
     return pl.pallas_call(
         stencil_kernel,
-        in_specs=[in_vmem] * 6,
+        in_specs=[in_vmem] * 3,
         out_specs=in_vmem,
         out_shape=jax.ShapeDtypeStruct((rows, vals), jnp.float32),
         scratch_shapes=[pltpu.VMEM((rows + 16, vals), jnp.float32)],
         compiler_params=params(),
         cost_estimate=pl.CostEstimate(flops=1000, bytes_accessed=1000, transcendentals=0),
-    )(field, own, before, after, coupling, plane)
+    )(field, coupling, plane)
 
 
 def respond(block, operator):
@@ -192,19 +214,19 @@
     return reluct * response
 
 
-def effect_kernel(thirds, places, rows_ref, *refs):
-    operators, out_ref = refs[: len(thirds)], refs[-1]
-    for third, place, operator_ref in zip(thirds, places, operators):
+def effect_kernel(sources, places, rows_ref, *refs):
+    operators, out_ref = refs[: len(sources)], refs[-1]
+    for source, place, operator_ref in zip(sources, places, operators):
         for k in range(16):
             top = k // 4 * stride + k % 4 * vals
-            lo, out = third * block + k * cap, place * block + k * cap
+            lo, out = source * block + k * cap, place * block + k * cap
             effect = respond(rows_ref[lo : lo + cap, :], operator_ref[top : top + vals, :])
             out_ref[out : out + cap, :] = effect.astype(out_ref.dtype)
 
 
-def effect_call(operands, thirds, places, shape, dtype, aliases):
-    return pl.pallas_call(
-        functools.partial(effect_kernel, thirds, places),
+def effect_call(operands, sources, places, shape, dtype, aliases):
+    return pl.pallas_call(
+        functools.partial(effect_kernel, sources, places),
         in_specs=[in_vmem] * len(operands),
         out_specs=in_vmem,
         out_shape=jax.ShapeDtypeStruct((shape, vals), dtype),
@@ -214,9 +236,9 @@
     )(*operands)
 
 
-def replies(guest, operators, thirds):
-    count = len(thirds)
-    return effect_call([guest, *operators], thirds, range(count), count * block, jnp.bfloat16, {})
+def replies(guest, operators, sources):
+    count = len(sources)
+    return effect_call([guest, *operators], sources, range(count), count * block, jnp.bfloat16, {})
 
 
 def effects(near, operators, thirds, previous):
@@ -231,7 +253,9 @@
 part_tops = (0, 1024, 2048, 3072, 3584, 3840, rows)
 
 
-def final_kernel(slot_ref, base_ref, own_ref, pair_ref, side_ref, _, out_ref, effect_ref, result, sent):
+def final_kernel(
+    slot_ref, base_ref, ends_ref, own_ref, pair_ref, side_ref, _, out_ref, effect_ref, result, sent
+):
     for returned_ref, third in ((own_ref, 0), (pair_ref, 2), (side_ref, 1)):
         lo = half + third * block
         effect_ref[lo : lo + returned_ref.shape[0], :] = returned_ref[...].astype(jnp.float32)
@@ -240,14 +264,18 @@
     for number, (top, end) in enumerate(zip(part_tops, part_tops[1:])):
 
         def body(i, carry):
-            first = pl.multiple_of(top + i * unroll, unroll)
-            for j in range(unroll):
+            first = pl.multiple_of(top + i * long_unroll, long_unroll)
+            for j in range(long_unroll):
                 effect = effect_ref[pl.ds(slot_ref[first + j], 1), :]
                 row = pl.ds(first + j, 1)
                 result[row, :] = base_ref[row, :] - step_size * effect
             return carry
 
-        lax.fori_loop(0, (end - top) // unroll, body, 0)
+        lax.fori_loop(0, (end - top) // long_unroll, body, 0)
+        if top == 0:
+            result[0:1, :] = result[0:1, :] + ends_ref[0:1, :]
+        if end == rows:
+            result[rows - 1 : rows, :] = result[rows - 1 : rows, :] + ends_ref[1:2, :]
         span = slice(top, end)
         copies.append(pltpu.make_async_copy(result.at[span], out_ref.at[span], sent.at[number]))
         copies[-1].start()
@@ -255,8 +283,8 @@
         copy.wait()
 
 
-def finish(slot, base, returned, effect):
-    operands = [slot, base, *returned, effect]
+def finish(slot, base, ends, returned, effect):
+    operands = [slot, base, ends, *returned, effect]
     return pl.pallas_call(
         final_kernel,
         in_specs=[pl.BlockSpec(memory_space=pltpu.SMEM)] + [in_vmem] * (len(operands) - 1),
@@ -278,25 +306,27 @@
 def per_device(edge_field, coupling, owner_map, in_plane, profile_op):
     field = edge_field[0]
     tied = lax.optimization_barrier
-    ends = jnp.concatenate([field[:8], field[rows - 8 :]], axis=0)
-    near = jnp.concatenate([*around(profile_op[0], first_moves), ends], axis=0)
+    tips = jnp.concatenate([field[:8], field[rows - 8 :]], axis=0)
+    near = jnp.concatenate([*around(profile_op[0], first_moves), tips], axis=0)
     slot = rank(owner_map.transpose(0, 2, 1)[0]).reshape(rows)
     near, slot = tied((near, slot))
     plane = jnp.concatenate(around(near, second_moves), axis=0)
-    near_rows, far_rows = sort_rows(slot, field)
-    plane, near_rows, far_rows = tied((plane, near_rows, far_rows))
+    near_rows, *far_rows = sort_rows(slot, field)
+    plane, near_rows, *far_rows = tied((plane, near_rows, *far_rows))
     plus, minus = shifted(plane, third_moves), shifted(plane, scaled(third_moves, -1))
     side = shifted(plane, side_moves)
-    guest = core_swap(far_rows)
-    reply = replies(guest, [plane], (0,))
+    own_guest, side_guest, pair_guest = [core_swap(part) for part in far_rows]
+    weights = coupling.reshape(rows // vals, vals)
+    base = stencil(field, weights, in_plane)
+    reply = core_swap(replies(own_guest, [plane], (0,)))
     effect = effects(near_rows, [plane], (0,), None)
-    minus, plus, effect, reply = tied((minus, plus, effect, reply))
-    returned = [core_swap(reply)]
-    returned.append(core_swap(replies(guest, [plus, minus], (2, 3))))
-    returned.append(core_swap(replies(guest, [side], (1,))))
+    minus, plus, effect, reply, base = tied((minus, plus, effect, reply, base))
+    returned = [reply]
+    returned.append(core_swap(replies(pair_guest, [plus, minus], (0, 1))))
+    returned.append(core_swap(replies(side_guest, [side], (0,))))
     effect = effects(near_rows, [side, plus, minus], (1, 2, 3), effect)
-    base = stencil(field, plane, plus, minus, coupling.reshape(rows // vals, vals), in_plane)
-    return finish(slot, base, returned, effect)[None]
+    ends = end_terms(plane, plus, minus, weights, in_plane)
+    return finish(slot, base, ends, returned, effect)[None]
 
 
 def solution(mesh):

time: 46.8 us -> 47.9 us (1.024)
  starting transfers between devices: 24.4 us -> 27.5 us
  waiting for transfers between devices: 6.97 us -> 4.86 us
    ppermute x4 -> x6, starting transfers between devices: 4.57 us -> 11.2 us  [core_swap(): return lax.ppermute(value, axes_all, pairs)]
    ppermute x9, starting transfers between devices: 19.8 us -> 16.3 us  [shifted(): return lax.ppermute(value, axes_all, pairs)]
    ppermute x9, waiting for transfers between devices: 6.96 us -> 4.3 us  [shifted(): return lax.ppermute(value, axes_all, pairs)]
    ppermute x4 -> x6, waiting for transfers between devices: 0.01 us -> 0.57 us  [core_swap(): return lax.ppermute(value, axes_all, pairs)]
    pallas_call x6 -> x7, Pallas kernels: 2.93 us -> 3.08 us  [the longest x5 2.32 us: effect_call(): pl.pallas_call(functools.partial(effect_kernel, sources, places), in_spec...]
  transfers between devices with their start and end apart: 13 -> 15, of which waited for: 3 -> 6; matrix products, arithmetic and copies ran while one was open for 2% -> 2% of each run, Pallas kernels for 18% -> 17%
where the time goes in v8:
time: 47.9 us; the launch traced here: 47.6 us
  starting transfers between devices  27.5 us (57%)
  Pallas kernels  13.5 us (28%)
  waiting for transfers between devices  4.86 us (10%)
  local copies, waits for them, and re-layouts  1.57 us (3%)
    ppermute x9, starting transfers between devices, shifted(): return lax.ppermute(value, axes_all, pairs)  16.3 us
    ppermute x6, starting transfers between devices, core_swap(): return lax.ppermute(value, axes_all, pairs)  11.2 us
    pallas_call x1, Pallas kernels, finish(): pl.pallas_call(final_kernel, in_specs=[pl.BlockSpec(memory_space=pltpu.SM...  5.19 us
    pallas_call x1, Pallas kernels, sort_rows(): pl.pallas_call(sort_kernel, in_specs=[pl.BlockSpec(memory_space=pltpu.SME...  4.46 us
    ppermute x9, waiting for transfers between devices, shifted(): return lax.ppermute(value, axes_all, pairs)  4.3 us
    pallas_call x5, Pallas kernels, effect_call(): pl.pallas_call(functools.partial(effect_kernel, sources, places), in_spec...  2.32 us
    unnamed x13, local copies, waits for them, and re-layouts  1.56 us
  transfers between devices with their start and end apart: 15, of which 6 were waited for; matrix products, arithmetic and copies ran while one was open for 2% of the time, Pallas kernels for 17%

profile of v8, /device:TPU:1, one launch (start us, length us, event | category | flops | bytes accessed | tf_op | source)
XLA Modules:
  0.0 47.6 jit_solution(13009683813448714835)
XLA Ops:
  0.0 7.0 %collective-permute-start.2 = (bf16[128,128]{1,0:T(8,128)(2,1)}, bf16[128,128]{1,0:T(8,128)(2,1)S(1)}, u32[]{:S(2)}, u32[]{:S(2)}) collective-permute-start(bf16[128,128]{1,0:T(8,128)(2,1)} %bitcast.18), channel_id=1, source_target_pairs={{0,70},{1,23},{2,64},{3,17},{4,66},{5,19},{6,68},{7,21},{8,78},{9,... | collective-permute-start | bytes 98312 | tf_op jit(solution)/shard_map/ppermute | solution.py:46
  7.1 1.2 %collective-permute-start = (bf16[128,128]{1,0:T(8,128)(2,1)}, bf16[128,128]{1,0:T(8,128)(2,1)S(1)}, u32[]{:S(2)}, u32[]{:S(2)}) collective-permute-start(bf16[128,128]{1,0:T(8,128)(2,1)} %bitcast.20), channel_id=1, source_target_pairs={{0,4},{1,5},{2,6},{3,7},{4,0},{5,1},{6,2},{7,3},{8,12},{9,13},{10,... | collective-permute-start | bytes 98312 | tf_op jit(solution)/shard_map/ppermute | solution.py:46
  8.3 0.8 %constant_dynamic-update-slice_fusion.5 = bf16[528,128]{1,0:T(8,128)(2,1)S(1)} fusion(bf16[1,128,128]{2,1,0:T(8,128)(2,1)} %param.9), kind=kLoop, calls=%fused_computation.6 | loop fusion | bytes 65536
  9.1 0.7 %copy-done.3 = s32[1,4096,1]{1,2,0:T(1,128)S(1)} copy-done((s32[1,4096,1]{1,2,0:T(1,128)S(1)}, s32[1,4096,1]{1,2,0:T(1,128)}, u32[]{:S(2)}) %copy-start.3) | copy-done | bytes 16408
  9.8 0.8 %shard_map.55 = s32[1,4096]{1,0:T(1,128)S(1)} custom-call(s32[1,4096]{1,0:T(1,128)S(1)} %bitcast.17), custom_call_target="tpu_custom_call" | custom-call | flops 402653184 | bytes 100000 | tf_op jit(solution)/shard_map/pallas_call | solution.py:105
  10.6 0.9 %collective-permute-done = bf16[128,128]{1,0:T(8,128)(2,1)S(1)} collective-permute-done((bf16[128,128]{1,0:T(8,128)(2,1)}, bf16[128,128]{1,0:T(8,128)(2,1)S(1)}, u32[]{:S(2)}, u32[]{:S(2)}) %collective-permute-start) | collective-permute-done | bytes 32800 | tf_op jit(solution)/shard_map/ppermute | solution.py:46
  11.5 2.1 %collective-permute-done.1 = bf16[128,128]{1,0:T(8,128)(2,1)S(1)} collective-permute-done((bf16[128,128]{1,0:T(8,128)(2,1)}, bf16[128,128]{1,0:T(8,128)(2,1)S(1)}, u32[]{:S(2)}, u32[]{:S(2)}) %collective-permute-start.1) | collective-permute-done | bytes 32800 | tf_op jit(solution)/shard_map/ppermute | solution.py:46
  13.7 2.8 %collective-permute-start.5 = (bf16[528,128]{1,0:T(8,128)(2,1)S(1)}, bf16[528,128]{1,0:T(8,128)(2,1)S(1)}, u32[]{:S(2)}, u32[]{:S(2)}) collective-permute-start(bf16[528,128]{1,0:T(8,128)(2,1)S(1)} %constant_dynamic-update-slice_fusion), channel_id=1, source_target_pairs={{0,24},{1,97},{2,26},{3,99},{4,28},{5,101},{6,30},{7,103},{8,0},{9... | collective-permute-start | bytes 405512 | tf_op jit(solution)/shard_map/ppermute | solution.py:46
  16.5 1.6 %collective-permute-start.3 = (bf16[528,128]{1,0:T(8,128)(2,1)S(1)}, bf16[528,128]{1,0:T(8,128)(2,1)S(1)}, u32[]{:S(2)}, u32[]{:S(2)}) collective-permute-start(bf16[528,128]{1,0:T(8,128)(2,1)S(1)} %constant_dynamic-update-slice_fusion), channel_id=1, source_target_pairs={{0,16},{1,65},{2,18},{3,67},{4,20},{5,69},{6,22},{7,71},{8,24},{9,... | collective-permute-start | bytes 405512 | tf_op jit(solution)/shard_map/ppermute | solution.py:46
  18.2 4.5 %shard_map.56 = (bf16[3072,128]{1,0:T(8,128)(2,1)S(1)}, bf16[768,128]{1,0:T(8,128)(2,1)S(1)}, bf16[768,128]{1,0:T(8,128)(2,1)S(1)}, bf16[1536,128]{1,0:T(8,128)(2,1)S(1)}) custom-call(s32[4096]{0:T(1024)S(1)} %bitcast.15, bf16[4096,128]{1,0:T(8,128)(2,1)S(1)} %bitcast.11), custom_call_target="tpu_custom_call" | custom-call | bytes 20000000 | tf_op jit(solution)/shard_map/pallas_call | solution.py:130
  22.7 0.7 %collective-permute-done.4 = bf16[528,128]{1,0:T(8,128)(2,1)S(1)} collective-permute-done((bf16[528,128]{1,0:T(8,128)(2,1)S(1)}, bf16[528,128]{1,0:T(8,128)(2,1)S(1)}, u32[]{:S(2)}, u32[]{:S(2)}) %collective-permute-start.4) | collective-permute-done | bytes 135200 | tf_op jit(solution)/shard_map/ppermute | solution.py:46
  23.4 0.4 collective-permute-start.7
  23.7 2.4 %collective-permute-start.6 = (bf16[2112,128]{1,0:T(8,128)(2,1)S(1)}, bf16[2112,128]{1,0:T(8,128)(2,1)S(1)}, u32[]{:S(2)}, u32[]{:S(2)}) collective-permute-start(bf16[2112,128]{1,0:T(8,128)(2,1)S(1)} %pad_maximum_fusion.refs_0_.own_ref), channel_id=1, source_target_pairs={{0,96},{1,25},{2,98},{3,27},{4,100},{5,29},{6,102},{7,31},{8,104},... | collective-permute-start | bytes 1622024 | tf_op jit(solution)/shard_map/ppermute | solution.py:46
  26.1 3.7 %collective-permute-start.8 = (bf16[768,128]{1,0:T(8,128)(2,1)S(1)}, bf16[768,128]{1,0:T(8,128)(2,1)S(1)}, u32[]{:S(2)}, u32[]{:S(2)}) collective-permute-start(bf16[768,128]{1,0:T(8,128)(2,1)S(1)} %get-tuple-element.30), channel_id=1, source_target_pairs={{0,1},{1,0},{2,3},{3,2},{4,5},{5,4},{6,7},{7,6},{8,9},{9,8},{10,11... | collective-permute-start | bytes 589832 | tf_op jit(solution)/shard_map/ppermute | solution.py:55
  29.8 0.8 %collective-permute-start.13 = (bf16[2112,128]{1,0:T(8,128)(2,1)S(1)}, bf16[2112,128]{1,0:T(8,128)(2,1)S(1)}, u32[]{:S(2)}, u32[]{:S(2)}) collective-permute-start(bf16[2112,128]{1,0:T(8,128)(2,1)S(1)} %pad_maximum_fusion.refs_0_.own_ref), channel_id=1, source_target_pairs={{0,2},{1,7},{2,4},{3,1},{4,6},{5,3},{6,0},{7,5},{8,10},{9,15},{10,... | collective-permute-start | bytes 1622024 | tf_op jit(solution)/shard_map/ppermute | solution.py:46
  31.3 0.5 collective-permute-start.9
  31.7 0.7 %shard_map.59.base_ref = f32[4096,128]{1,0:T(8,128)S(1)} custom-call(bf16[4096,128]{1,0:T(8,128)(2,1)S(1)} %bitcast.12, f32[32,128]{1,0:T(8,128)S(1)} %bitcast.13, bf16[128,128]{1,0:T(8,128)(2,1)S(1)} %copy-done.1), custom_call_target="tpu_custom_call" | custom-call | flops 1000 | bytes 1000 | tf_op jit(solution)/shard_map/pallas_call | solution.py:198
  32.4 0.4 shard_map.57.refs_3_
  33.2 0.5 %shard_map.61 = bf16[1536,128]{1,0:T(8,128)(2,1)S(1)} custom-call(bf16[1536,128]{1,0:T(8,128)(2,1)S(1)} %collective-permute-done.10.rows_ref, bf16[2112,128]{1,0:T(8,128)(2,1)S(1)} %collective-permute-done.7.before_ref.refs_0_.refs_1_, bf16[2112,128]{1,0:T(8,128)(2,1)S(1)} %collective-permute-done.6.after_ref.refs_1_.refs_2_), custom_call_target="tpu_custom_call" | custom-call | flops 1000 | bytes 1000 | tf_op jit(solution)/shard_map/pallas_call | solution.py:228
  33.7 4.1 %collective-permute-start.11 = (bf16[1536,128]{1,0:T(8,128)(2,1)S(1)}, bf16[1536,128]{1,0:T(8,128)(2,1)S(1)}, u32[]{:S(2)}, u32[]{:S(2)}) collective-permute-start(bf16[1536,128]{1,0:T(8,128)(2,1)S(1)} %shard_map.61), channel_id=1, source_target_pairs={{0,1},{1,0},{2,3},{3,2},{4,5},{5,4},{6,7},{7,6},{8,9},{9,8},{10,11... | collective-permute-start | bytes 1179656 | tf_op jit(solution)/shard_map/ppermute | solution.py:55
  37.8 0.6 %collective-permute-done.13.refs_0_ = bf16[2112,128]{1,0:T(8,128)(2,1)S(1)} collective-permute-done((bf16[2112,128]{1,0:T(8,128)(2,1)S(1)}, bf16[2112,128]{1,0:T(8,128)(2,1)S(1)}, u32[]{:S(2)}, u32[]{:S(2)}) %collective-permute-start.13) | collective-permute-done | bytes 540704 | tf_op jit(solution)/shard_map/ppermute | solution.py:46
  38.7 2.7 %collective-permute-start.14 = (bf16[768,128]{1,0:T(8,128)(2,1)S(1)}, bf16[768,128]{1,0:T(8,128)(2,1)S(1)}, u32[]{:S(2)}, u32[]{:S(2)}) collective-permute-start(bf16[768,128]{1,0:T(8,128)(2,1)S(1)} %shard_map.62), channel_id=1, source_target_pairs={{0,1},{1,0},{2,3},{3,2},{4,5},{5,4},{6,7},{7,6},{8,9},{9,8},{10,11... | collective-permute-start | bytes 589832 | tf_op jit(solution)/shard_map/ppermute | solution.py:55
  41.4 0.7 %shard_map.63._ = f32[6144,128]{1,0:T(8,128)S(1)} custom-call(bf16[3072,128]{1,0:T(8,128)(2,1)S(1)} %get-tuple-element.29.rows_ref, bf16[2112,128]{1,0:T(8,128)(2,1)S(1)} %collective-permute-done.13.refs_0_, bf16[2112,128]{1,0:T(8,128)(2,1)S(1)} %collective-permute-done.7.before_ref.refs_0_.refs_1_, ...), custom_call_target="tpu_custom_call", output_to_operand_aliasing={{}: (4, {})} | custom-call | flops 1000 | bytes 1000 | tf_op jit(solution)/shard_map/pallas_call | solution.py:228
  42.4 5.2 %shard_map.64 = (f32[4096,128]{1,0:T(8,128)}, f32[6144,128]{1,0:T(8,128)S(1)}) custom-call(s32[4096]{0:T(1024)S(1)} %bitcast.16, f32[4096,128]{1,0:T(8,128)S(1)} %shard_map.59.base_ref, f32[8,128]{1,0:T(8,128)S(1)} %shard_map.60.ends_ref, bf16[768,128]{1,0:T(8,128)(2,1)S(1)} %collective-permute-done.9.own_ref, ...), custom_call_target="tpu_custom_call", output_to_operand_aliasing={{1}: (6, {})} | custom-call | flops 524288 | bytes 10000000 | tf_op jit(solution)/shard_map/pallas_call | solution.py:288
  (31 shorter events, 1.8 us)
Async XLA Ops:
  0.0 13.7 %copy-start = (bf16[1,4096,128]{2,1,0:T(8,128)(2,1)S(1)}, bf16[1,4096,128]{2,1,0:T(8,128)(2,1)}, u32[]{:S(2)}) copy-start(bf16[1,4096,128]{2,1,0:T(8,128)(2,1)} %param.5) | copy-start | bytes 3145732
  0.0 13.6 %collective-permute-start.2 = (bf16[128,128]{1,0:T(8,128)(2,1)}, bf16[128,128]{1,0:T(8,128)(2,1)S(1)}, u32[]{:S(2)}, u32[]{:S(2)}) collective-permute-start(bf16[128,128]{1,0:T(8,128)(2,1)} %bitcast.18), channel_id=1, source_target_pairs={{0,70},{1,23},{2,64},{3,17},{4,66},{5,19},{6,68},{7,21},{8,78},{9,... | collective-permute-start | bytes 98312 | tf_op jit(solution)/shard_map/ppermute | solution.py:46
  7.0 6.6 %collective-permute-start.1 = (bf16[128,128]{1,0:T(8,128)(2,1)}, bf16[128,128]{1,0:T(8,128)(2,1)S(1)}, u32[]{:S(2)}, u32[]{:S(2)}) collective-permute-start(bf16[128,128]{1,0:T(8,128)(2,1)} %bitcast.19), channel_id=1, source_target_pairs={{0,66},{1,19},{2,68},{3,21},{4,70},{5,23},{6,64},{7,17},{8,74},{9,... | collective-permute-start | bytes 98312 | tf_op jit(solution)/shard_map/ppermute | solution.py:46
  7.1 4.5 %collective-permute-start = (bf16[128,128]{1,0:T(8,128)(2,1)}, bf16[128,128]{1,0:T(8,128)(2,1)S(1)}, u32[]{:S(2)}, u32[]{:S(2)}) collective-permute-start(bf16[128,128]{1,0:T(8,128)(2,1)} %bitcast.20), channel_id=1, source_target_pairs={{0,4},{1,5},{2,6},{3,7},{4,0},{5,1},{6,2},{7,3},{8,12},{9,13},{10,... | collective-permute-start | bytes 98312 | tf_op jit(solution)/shard_map/ppermute | solution.py:46
  9.1 0.7 %copy-start.3 = (s32[1,4096,1]{1,2,0:T(1,128)S(1)}, s32[1,4096,1]{1,2,0:T(1,128)}, u32[]{:S(2)}) copy-start(s32[1,4096,1]{1,2,0:T(1,128)} %param.7) | copy-start | bytes 49156
  13.7 8.9 %collective-permute-start.5 = (bf16[528,128]{1,0:T(8,128)(2,1)S(1)}, bf16[528,128]{1,0:T(8,128)(2,1)S(1)}, u32[]{:S(2)}, u32[]{:S(2)}) collective-permute-start(bf16[528,128]{1,0:T(8,128)(2,1)S(1)} %constant_dynamic-update-slice_fusion), channel_id=1, source_target_pairs={{0,24},{1,97},{2,26},{3,99},{4,28},{5,101},{6,30},{7,103},{8,0},{9... | collective-permute-start | bytes 405512 | tf_op jit(solution)/shard_map/ppermute | solution.py:46
  16.5 6.8 %collective-permute-start.4 = (bf16[528,128]{1,0:T(8,128)(2,1)S(1)}, bf16[528,128]{1,0:T(8,128)(2,1)S(1)}, u32[]{:S(2)}, u32[]{:S(2)}) collective-permute-start(bf16[528,128]{1,0:T(8,128)(2,1)S(1)} %constant_dynamic-update-slice_fusion), channel_id=1, source_target_pairs={{0,8},{1,33},{2,10},{3,35},{4,12},{5,37},{6,14},{7,39},{8,16},{9,4... | collective-permute-start | bytes 405512 | tf_op jit(solution)/shard_map/ppermute | solution.py:46
  16.5 6.8 %collective-permute-start.3 = (bf16[528,128]{1,0:T(8,128)(2,1)S(1)}, bf16[528,128]{1,0:T(8,128)(2,1)S(1)}, u32[]{:S(2)}, u32[]{:S(2)}) collective-permute-start(bf16[528,128]{1,0:T(8,128)(2,1)S(1)} %constant_dynamic-update-slice_fusion), channel_id=1, source_target_pairs={{0,16},{1,65},{2,18},{3,67},{4,20},{5,69},{6,22},{7,71},{8,24},{9,... | collective-permute-start | bytes 405512 | tf_op jit(solution)/shard_map/ppermute | solution.py:46
  22.6 9.1 %copy-start.1 = (bf16[128,128]{1,0:T(8,128)(2,1)S(1)}, bf16[128,128]{1,0:T(8,128)(2,1)}, u32[]{:S(2)}) copy-start(bf16[128,128]{1,0:T(8,128)(2,1)} %plane_ref.3) | copy-start | bytes 98308
  22.6 9.1 %copy-start.2 = (f32[1,4096]{1,0:T(1,128)S(1)}, f32[1,4096]{1,0:T(1,128)}, u32[]{:S(2)}) copy-start(f32[1,4096]{1,0:T(1,128)} %param.6) | copy-start | bytes 49156
  23.4 9.8 %collective-permute-start.7 = (bf16[2112,128]{1,0:T(8,128)(2,1)S(1)}, bf16[2112,128]{1,0:T(8,128)(2,1)S(1)}, u32[]{:S(2)}, u32[]{:S(2)}) collective-permute-start(bf16[2112,128]{1,0:T(8,128)(2,1)S(1)} %pad_maximum_fusion.refs_0_.own_ref), channel_id=1, source_target_pairs={{0,32},{1,9},{2,34},{3,11},{4,36},{5,13},{6,38},{7,15},{8,40},{9,1... | collective-permute-start | bytes 1622024 | tf_op jit(solution)/shard_map/ppermute | solution.py:46
  23.7 9.4 %collective-permute-start.6 = (bf16[2112,128]{1,0:T(8,128)(2,1)S(1)}, bf16[2112,128]{1,0:T(8,128)(2,1)S(1)}, u32[]{:S(2)}, u32[]{:S(2)}) collective-permute-start(bf16[2112,128]{1,0:T(8,128)(2,1)S(1)} %pad_maximum_fusion.refs_0_.own_ref), channel_id=1, source_target_pairs={{0,96},{1,25},{2,98},{3,27},{4,100},{5,29},{6,102},{7,31},{8,104},... | collective-permute-start | bytes 1622024 | tf_op jit(solution)/shard_map/ppermute | solution.py:46
  26.1 4.8 %collective-permute-start.8 = (bf16[768,128]{1,0:T(8,128)(2,1)S(1)}, bf16[768,128]{1,0:T(8,128)(2,1)S(1)}, u32[]{:S(2)}, u32[]{:S(2)}) collective-permute-start(bf16[768,128]{1,0:T(8,128)(2,1)S(1)} %get-tuple-element.30), channel_id=1, source_target_pairs={{0,1},{1,0},{2,3},{3,2},{4,5},{5,4},{6,7},{7,6},{8,9},{9,8},{10,11... | collective-permute-start | bytes 589832 | tf_op jit(solution)/shard_map/ppermute | solution.py:55
  29.8 3.3 %collective-permute-start.10 = (bf16[1536,128]{1,0:T(8,128)(2,1)S(1)}, bf16[1536,128]{1,0:T(8,128)(2,1)S(1)}, u32[]{:S(2)}, u32[]{:S(2)}) collective-permute-start(bf16[1536,128]{1,0:T(8,128)(2,1)S(1)} %get-tuple-element.35), channel_id=1, source_target_pairs={{0,1},{1,0},{2,3},{3,2},{4,5},{5,4},{6,7},{7,6},{8,9},{9,8},{10,11... | collective-permute-start | bytes 1179656 | tf_op jit(solution)/shard_map/ppermute | solution.py:55
  29.8 8.5 %collective-permute-start.13 = (bf16[2112,128]{1,0:T(8,128)(2,1)S(1)}, bf16[2112,128]{1,0:T(8,128)(2,1)S(1)}, u32[]{:S(2)}, u32[]{:S(2)}) collective-permute-start(bf16[2112,128]{1,0:T(8,128)(2,1)S(1)} %pad_maximum_fusion.refs_0_.own_ref), channel_id=1, source_target_pairs={{0,2},{1,7},{2,4},{3,1},{4,6},{5,3},{6,0},{7,5},{8,10},{9,15},{10,... | collective-permute-start | bytes 1622024 | tf_op jit(solution)/shard_map/ppermute | solution.py:46
  31.3 1.5 %collective-permute-start.9 = (bf16[768,128]{1,0:T(8,128)(2,1)S(1)}, bf16[768,128]{1,0:T(8,128)(2,1)S(1)}, u32[]{:S(2)}, u32[]{:S(2)}) collective-permute-start(bf16[768,128]{1,0:T(8,128)(2,1)S(1)} %shard_map.58), channel_id=1, source_target_pairs={{0,1},{1,0},{2,3},{3,2},{4,5},{5,4},{6,7},{7,6},{8,9},{9,8},{10,11... | collective-permute-start | bytes 589832 | tf_op jit(solution)/shard_map/ppermute | solution.py:55
  32.8 4.9 %collective-permute-start.12 = (bf16[768,128]{1,0:T(8,128)(2,1)S(1)}, bf16[768,128]{1,0:T(8,128)(2,1)S(1)}, u32[]{:S(2)}, u32[]{:S(2)}) collective-permute-start(bf16[768,128]{1,0:T(8,128)(2,1)S(1)} %get-tuple-element.36), channel_id=1, source_target_pairs={{0,1},{1,0},{2,3},{3,2},{4,5},{5,4},{6,7},{7,6},{8,9},{9,8},{10,11... | collective-permute-start | bytes 589832 | tf_op jit(solution)/shard_map/ppermute | solution.py:55
  33.7 8.8 %collective-permute-start.11 = (bf16[1536,128]{1,0:T(8,128)(2,1)S(1)}, bf16[1536,128]{1,0:T(8,128)(2,1)S(1)}, u32[]{:S(2)}, u32[]{:S(2)}) collective-permute-start(bf16[1536,128]{1,0:T(8,128)(2,1)S(1)} %shard_map.61), channel_id=1, source_target_pairs={{0,1},{1,0},{2,3},{3,2},{4,5},{5,4},{6,7},{7,6},{8,9},{9,8},{10,11... | collective-permute-start | bytes 1179656 | tf_op jit(solution)/shard_map/ppermute | solution.py:55
  38.7 3.7 %collective-permute-start.14 = (bf16[768,128]{1,0:T(8,128)(2,1)S(1)}, bf16[768,128]{1,0:T(8,128)(2,1)S(1)}, u32[]{:S(2)}, u32[]{:S(2)}) collective-permute-start(bf16[768,128]{1,0:T(8,128)(2,1)S(1)} %shard_map.62), channel_id=1, source_target_pairs={{0,1},{1,0},{2,3},{3,2},{4,5},{5,4},{6,7},{7,6},{8,9},{9,8},{10,11... | collective-permute-start | bytes 589832 | tf_op jit(solution)/shard_map/ppermute | solution.py:55

commit v9 on v8

--- a/solution.py
+++ b/solution.py
@@ -110,7 +110,7 @@
     )(owner)
 
 
-def sort_kernel(slot_ref, field_ref, near_ref, own_ref, side_ref, pair_ref, wide, placed):
+def sort_kernel(slot_ref, field_ref, near_ref, own_ref, side_ref, plus_ref, minus_ref, wide, placed):
     wide[...] = field_ref[...].astype(jnp.float32)
 
     def body(i, carry):
@@ -121,18 +121,18 @@
 
     lax.fori_loop(0, rows // unroll, body, 0)
     near_ref[...] = placed[:half].astype(jnp.bfloat16)
-    own_ref[...] = placed[half : half + block].astype(jnp.bfloat16)
-    side_ref[...] = placed[half + block : half + 2 * block].astype(jnp.bfloat16)
-    pair_ref[...] = placed[half + 2 * block :].astype(jnp.bfloat16)
+    for third, far_ref in enumerate((own_ref, side_ref, plus_ref, minus_ref)):
+        lo = half + third * block
+        far_ref[...] = placed[lo : lo + block].astype(jnp.bfloat16)
 
 
 def sort_rows(slot, field):
     return pl.pallas_call(
         sort_kernel,
         in_specs=[pl.BlockSpec(memory_space=pltpu.SMEM), in_vmem],
-        out_specs=[in_vmem] * 4,
+        out_specs=[in_vmem] * 5,
         out_shape=[
-            jax.ShapeDtypeStruct((count * block, vals), jnp.bfloat16) for count in (4, 1, 1, 2)
+            jax.ShapeDtypeStruct((count * block, vals), jnp.bfloat16) for count in (4, 1, 1, 1, 1)
         ],
         scratch_shapes=[pltpu.VMEM((rows, vals), jnp.float32), pltpu.VMEM((slots, vals), jnp.float32)],
         compiler_params=params(),
@@ -214,9 +214,10 @@
     return reluct * response
 
 
-def effect_kernel(sources, places, rows_ref, *refs):
+def effect_kernel(sources, places, *refs):
     operators, out_ref = refs[: len(sources)], refs[-1]
-    for source, place, operator_ref in zip(sources, places, operators):
+    for (number, source), place, operator_ref in zip(sources, places, operators):
+        rows_ref = refs[len(sources) + number]
         for k in range(16):
             top = k // 4 * stride + k % 4 * vals
             lo, out = source * block + k * cap, place * block + k * cap
@@ -236,18 +237,20 @@
     )(*operands)
 
 
-def replies(guest, operators, sources):
-    count = len(sources)
-    return effect_call([guest, *operators], sources, range(count), count * block, jnp.bfloat16, {})
+def replies(operators, guests):
+    count = len(guests)
+    sources = [(number, 0) for number in range(count)]
+    return effect_call([*operators, *guests], sources, range(count), count * block, jnp.bfloat16, {})
 
 
 def effects(near, operators, thirds, previous):
-    operands = [near, *operators]
+    operands = [*operators, near]
     aliases = {}
     if previous is not None:
         aliases = {len(operands): 0}
         operands.append(previous)
-    return effect_call(operands, thirds, thirds, slots, jnp.float32, aliases)
+    sources = [(0, third) for third in thirds]
+    return effect_call(operands, sources, thirds, slots, jnp.float32, aliases)
 
 
 part_tops = (0, 1024, 2048, 3072, 3584, 3840, rows)
@@ -256,9 +259,9 @@
 def final_kernel(
     slot_ref, base_ref, ends_ref, own_ref, pair_ref, side_ref, _, out_ref, effect_ref, result, sent
 ):
-    for returned_ref, third in ((own_ref, 0), (pair_ref, 2), (side_ref, 1)):
-        lo = half + third * block
-        effect_ref[lo : lo + returned_ref.shape[0], :] = returned_ref[...].astype(jnp.float32)
+    for returned_ref, first, third in ((own_ref, 0, 0), (pair_ref, 0, 2), (pair_ref, 1, 3), (side_ref, 0, 1)):
+        lo, top = half + third * block, first * block
+        effect_ref[lo : lo + block, :] = returned_ref[top : top + block, :].astype(jnp.float32)
 
     copies = []
     for number, (top, end) in enumerate(zip(part_tops, part_tops[1:])):
@@ -315,15 +318,15 @@
     plane, near_rows, *far_rows = tied((plane, near_rows, *far_rows))
     plus, minus = shifted(plane, third_moves), shifted(plane, scaled(third_moves, -1))
     side = shifted(plane, side_moves)
-    own_guest, side_guest, pair_guest = [core_swap(part) for part in far_rows]
+    own_guest, side_guest, *pair_guests = [core_swap(part) for part in far_rows]
     weights = coupling.reshape(rows // vals, vals)
     base = stencil(field, weights, in_plane)
-    reply = core_swap(replies(own_guest, [plane], (0,)))
     effect = effects(near_rows, [plane], (0,), None)
-    minus, plus, effect, reply, base = tied((minus, plus, effect, reply, base))
-    returned = [reply]
-    returned.append(core_swap(replies(pair_guest, [plus, minus], (0, 1))))
-    returned.append(core_swap(replies(side_guest, [side], (0,))))
+    reply = replies([plane], [own_guest])
+    minus, plus, effect, base, reply = tied((minus, plus, effect, base, reply))
+    returned = [core_swap(reply)]
+    returned.append(core_swap(replies([plus, minus], pair_guests)))
+    returned.append(core_swap(replies([side], [side_guest])))
     effect = effects(near_rows, [side, plus, minus], (1, 2, 3), effect)
     ends = end_terms(plane, plus, minus, weights, in_plane)
     return finish(slot, base, ends, returned, effect)[None]

time: 47.9 us -> 47.7 us (level)
  starting transfers between devices: 27.5 us -> 26.7 us
  waiting for transfers between devices: 4.86 us -> 5.58 us
    ppermute x6 -> x7, starting transfers between devices: 11.2 us -> 10.4 us  [core_swap(): return lax.ppermute(value, axes_all, pairs)]
    ppermute x6 -> x7, waiting for transfers between devices: 0.57 us -> 1.3 us  [core_swap(): return lax.ppermute(value, axes_all, pairs)]
  transfers between devices with their start and end apart: 15 -> 16, of which waited for: 6 -> 9; matrix products, arithmetic and copies ran while one was open for 2% -> 2% of each run, Pallas kernels for 17% -> 18%
where the time goes in v9:
time: 47.7 us; the launch traced here: 47.5 us
  starting transfers between devices  26.7 us (56%)
  Pallas kernels  13.5 us (28%)
  waiting for transfers between devices  5.58 us (12%)
  local copies, waits for them, and re-layouts  1.57 us (3%)
    ppermute x9, starting transfers between devices, shifted(): return lax.ppermute(value, axes_all, pairs)  16.3 us
    ppermute x7, starting transfers between devices, core_swap(): return lax.ppermute(value, axes_all, pairs)  10.4 us
    pallas_call x1, Pallas kernels, finish(): pl.pallas_call(final_kernel, in_specs=[pl.BlockSpec(memory_space=pltpu.SM...  5.19 us
    pallas_call x1, Pallas kernels, sort_rows(): pl.pallas_call(sort_kernel, in_specs=[pl.BlockSpec(memory_space=pltpu.SME...  4.46 us
    ppermute x9, waiting for transfers between devices, shifted(): return lax.ppermute(value, axes_all, pairs)  4.27 us
    pallas_call x5, Pallas kernels, effect_call(): pl.pallas_call(functools.partial(effect_kernel, sources, places), in_spec...  2.31 us
    unnamed x13, local copies, waits for them, and re-layouts  1.56 us
    ppermute x7, waiting for transfers between devices, core_swap(): return lax.ppermute(value, axes_all, pairs)  1.3 us
  transfers between devices with their start and end apart: 16, of which 9 were waited for; matrix products, arithmetic and copies ran while one was open for 2% of the time, Pallas kernels for 18%

profile of v9, /device:TPU:1, one launch (start us, length us, event | category | flops | bytes accessed | tf_op | source)
XLA Modules:
  0.0 47.5 jit_solution(15474192532915442295)
XLA Ops:
  0.0 7.0 %collective-permute-start.2 = (bf16[128,128]{1,0:T(8,128)(2,1)}, bf16[128,128]{1,0:T(8,128)(2,1)S(1)}, u32[]{:S(2)}, u32[]{:S(2)}) collective-permute-start(bf16[128,128]{1,0:T(8,128)(2,1)} %bitcast.18), channel_id=1, source_target_pairs={{0,70},{1,23},{2,64},{3,17},{4,66},{5,19},{6,68},{7,21},{8,78},{9,... | collective-permute-start | bytes 98312 | tf_op jit(solution)/shard_map/ppermute | solution.py:46
  7.1 1.2 %collective-permute-start = (bf16[128,128]{1,0:T(8,128)(2,1)}, bf16[128,128]{1,0:T(8,128)(2,1)S(1)}, u32[]{:S(2)}, u32[]{:S(2)}) collective-permute-start(bf16[128,128]{1,0:T(8,128)(2,1)} %bitcast.20), channel_id=1, source_target_pairs={{0,4},{1,5},{2,6},{3,7},{4,0},{5,1},{6,2},{7,3},{8,12},{9,13},{10,... | collective-permute-start | bytes 98312 | tf_op jit(solution)/shard_map/ppermute | solution.py:46
  8.3 0.8 %constant_dynamic-update-slice_fusion.5 = bf16[528,128]{1,0:T(8,128)(2,1)S(1)} fusion(bf16[1,128,128]{2,1,0:T(8,128)(2,1)} %param.9), kind=kLoop, calls=%fused_computation.6 | loop fusion | bytes 65536
  9.1 0.7 %copy-done.3 = s32[1,4096,1]{1,2,0:T(1,128)S(1)} copy-done((s32[1,4096,1]{1,2,0:T(1,128)S(1)}, s32[1,4096,1]{1,2,0:T(1,128)}, u32[]{:S(2)}) %copy-start.3) | copy-done | bytes 16408
  9.8 0.8 %shard_map.55 = s32[1,4096]{1,0:T(1,128)S(1)} custom-call(s32[1,4096]{1,0:T(1,128)S(1)} %bitcast.17), custom_call_target="tpu_custom_call" | custom-call | flops 402653184 | bytes 100000 | tf_op jit(solution)/shard_map/pallas_call | solution.py:105
  10.6 0.9 %collective-permute-done = bf16[128,128]{1,0:T(8,128)(2,1)S(1)} collective-permute-done((bf16[128,128]{1,0:T(8,128)(2,1)}, bf16[128,128]{1,0:T(8,128)(2,1)S(1)}, u32[]{:S(2)}, u32[]{:S(2)}) %collective-permute-start) | collective-permute-done | bytes 32800 | tf_op jit(solution)/shard_map/ppermute | solution.py:46
  11.5 2.1 %collective-permute-done.1 = bf16[128,128]{1,0:T(8,128)(2,1)S(1)} collective-permute-done((bf16[128,128]{1,0:T(8,128)(2,1)}, bf16[128,128]{1,0:T(8,128)(2,1)S(1)}, u32[]{:S(2)}, u32[]{:S(2)}) %collective-permute-start.1) | collective-permute-done | bytes 32800 | tf_op jit(solution)/shard_map/ppermute | solution.py:46
  13.7 2.8 %collective-permute-start.5 = (bf16[528,128]{1,0:T(8,128)(2,1)S(1)}, bf16[528,128]{1,0:T(8,128)(2,1)S(1)}, u32[]{:S(2)}, u32[]{:S(2)}) collective-permute-start(bf16[528,128]{1,0:T(8,128)(2,1)S(1)} %constant_dynamic-update-slice_fusion), channel_id=1, source_target_pairs={{0,24},{1,97},{2,26},{3,99},{4,28},{5,101},{6,30},{7,103},{8,0},{9... | collective-permute-start | bytes 405512 | tf_op jit(solution)/shard_map/ppermute | solution.py:46
  16.5 1.6 %collective-permute-start.3 = (bf16[528,128]{1,0:T(8,128)(2,1)S(1)}, bf16[528,128]{1,0:T(8,128)(2,1)S(1)}, u32[]{:S(2)}, u32[]{:S(2)}) collective-permute-start(bf16[528,128]{1,0:T(8,128)(2,1)S(1)} %constant_dynamic-update-slice_fusion), channel_id=1, source_target_pairs={{0,16},{1,65},{2,18},{3,67},{4,20},{5,69},{6,22},{7,71},{8,24},{9,... | collective-permute-start | bytes 405512 | tf_op jit(solution)/shard_map/ppermute | solution.py:46
  18.2 4.5 %shard_map.56 = (bf16[3072,128]{1,0:T(8,128)(2,1)S(1)}, bf16[768,128]{1,0:T(8,128)(2,1)S(1)}, bf16[768,128]{1,0:T(8,128)(2,1)S(1)}, bf16[768,128]{1,0:T(8,128)(2,1)S(1)}, bf16[768,128]{1,0:T(8,128)(2,1)S(1)}) custom-call(s32[4096]{0:T(1024)S(1)} %bitcast.15, bf16[4096,128]{1,0:T(8,128)(2,1)S(1)} %bitcast.11), custom_call_target="tpu_custom_call" | custom-call | bytes 20000000 | tf_op jit(solution)/shard_map/pallas_call | solution.py:130
  22.7 0.7 %collective-permute-done.4 = bf16[528,128]{1,0:T(8,128)(2,1)S(1)} collective-permute-done((bf16[528,128]{1,0:T(8,128)(2,1)S(1)}, bf16[528,128]{1,0:T(8,128)(2,1)S(1)}, u32[]{:S(2)}, u32[]{:S(2)}) %collective-permute-start.4) | collective-permute-done | bytes 135200 | tf_op jit(solution)/shard_map/ppermute | solution.py:46
  23.4 0.4 collective-permute-start.7
  23.8 2.4 %collective-permute-start.6 = (bf16[2112,128]{1,0:T(8,128)(2,1)S(1)}, bf16[2112,128]{1,0:T(8,128)(2,1)S(1)}, u32[]{:S(2)}, u32[]{:S(2)}) collective-permute-start(bf16[2112,128]{1,0:T(8,128)(2,1)S(1)} %pad_maximum_fusion.refs_0_.own_ref), channel_id=1, source_target_pairs={{0,96},{1,25},{2,98},{3,27},{4,100},{5,29},{6,102},{7,31},{8,104},... | collective-permute-start | bytes 1622024 | tf_op jit(solution)/shard_map/ppermute | solution.py:46
  26.1 3.7 %collective-permute-start.8 = (bf16[768,128]{1,0:T(8,128)(2,1)S(1)}, bf16[768,128]{1,0:T(8,128)(2,1)S(1)}, u32[]{:S(2)}, u32[]{:S(2)}) collective-permute-start(bf16[768,128]{1,0:T(8,128)(2,1)S(1)} %get-tuple-element.33), channel_id=1, source_target_pairs={{0,1},{1,0},{2,3},{3,2},{4,5},{5,4},{6,7},{7,6},{8,9},{9,8},{10,11... | collective-permute-start | bytes 589832 | tf_op jit(solution)/shard_map/ppermute | solution.py:55
  29.9 0.8 %collective-permute-start.13 = (bf16[2112,128]{1,0:T(8,128)(2,1)S(1)}, bf16[2112,128]{1,0:T(8,128)(2,1)S(1)}, u32[]{:S(2)}, u32[]{:S(2)}) collective-permute-start(bf16[2112,128]{1,0:T(8,128)(2,1)S(1)} %pad_maximum_fusion.refs_0_.own_ref), channel_id=1, source_target_pairs={{0,2},{1,7},{2,4},{3,1},{4,6},{5,3},{6,0},{7,5},{8,10},{9,15},{10,... | collective-permute-start | bytes 1622024 | tf_op jit(solution)/shard_map/ppermute | solution.py:46
  30.9 0.4 collective-permute-start.11
  31.3 0.7 %shard_map.58.base_ref = f32[4096,128]{1,0:T(8,128)S(1)} custom-call(bf16[4096,128]{1,0:T(8,128)(2,1)S(1)} %bitcast.12, f32[32,128]{1,0:T(8,128)S(1)} %bitcast.13, bf16[128,128]{1,0:T(8,128)(2,1)S(1)} %copy-done.1), custom_call_target="tpu_custom_call" | custom-call | flops 1000 | bytes 1000 | tf_op jit(solution)/shard_map/pallas_call | solution.py:198
  32.7 0.4 collective-permute-done.7.before_ref.refs_0_.refs_1_
  33.2 4.0 %collective-permute-start.14 = (bf16[768,128]{1,0:T(8,128)(2,1)S(1)}, bf16[768,128]{1,0:T(8,128)(2,1)S(1)}, u32[]{:S(2)}, u32[]{:S(2)}) collective-permute-start(bf16[768,128]{1,0:T(8,128)(2,1)S(1)} %get-tuple-element.40), channel_id=1, source_target_pairs={{0,1},{1,0},{2,3},{3,2},{4,5},{5,4},{6,7},{7,6},{8,9},{9,8},{10,11... | collective-permute-start | bytes 589832 | tf_op jit(solution)/shard_map/ppermute | solution.py:55
  37.2 0.5 %shard_map.61 = bf16[1536,128]{1,0:T(8,128)(2,1)S(1)} custom-call(bf16[2112,128]{1,0:T(8,128)(2,1)S(1)} %collective-permute-done.7.before_ref.refs_0_.refs_1_, bf16[2112,128]{1,0:T(8,128)(2,1)S(1)} %collective-permute-done.6.after_ref.refs_1_.refs_2_, bf16[768,128]{1,0:T(8,128)(2,1)S(1)} %collective-permute-done.10.refs_2_, ...), custom_call_target="tpu_custom_call" | custom-call | flops 1000 | bytes 1000 | tf_op jit(solution)/shard_map/pallas_call | solution.py:229
  37.8 0.5 collective-permute-done.14.refs_1_
  38.7 2.1 %collective-permute-start.15 = (bf16[768,128]{1,0:T(8,128)(2,1)S(1)}, bf16[768,128]{1,0:T(8,128)(2,1)S(1)}, u32[]{:S(2)}, u32[]{:S(2)}) collective-permute-start(bf16[768,128]{1,0:T(8,128)(2,1)S(1)} %shard_map.62), channel_id=1, source_target_pairs={{0,1},{1,0},{2,3},{3,2},{4,5},{5,4},{6,7},{7,6},{8,9},{9,8},{10,11... | collective-permute-start | bytes 589832 | tf_op jit(solution)/shard_map/ppermute | solution.py:55
  41.0 0.7 %shard_map.63._ = f32[6144,128]{1,0:T(8,128)S(1)} custom-call(bf16[2112,128]{1,0:T(8,128)(2,1)S(1)} %collective-permute-done.13.refs_0_, bf16[2112,128]{1,0:T(8,128)(2,1)S(1)} %collective-permute-done.7.before_ref.refs_0_.refs_1_, bf16[2112,128]{1,0:T(8,128)(2,1)S(1)} %collective-permute-done.6.after_ref.refs_1_.refs_2_, ...), custom_call_target="tpu_custom_call", output_to_operand_aliasing={{}: (4, {})} | custom-call | flops 1000 | bytes 1000 | tf_op jit(solution)/shard_map/pallas_call | solution.py:229
  42.3 5.2 %shard_map.64 = (f32[4096,128]{1,0:T(8,128)}, f32[6144,128]{1,0:T(8,128)S(1)}) custom-call(s32[4096]{0:T(1024)S(1)} %bitcast.16, f32[4096,128]{1,0:T(8,128)S(1)} %shard_map.58.base_ref, f32[8,128]{1,0:T(8,128)S(1)} %shard_map.60.ends_ref, bf16[768,128]{1,0:T(8,128)(2,1)S(1)} %collective-permute-done.9.own_ref, ...), custom_call_target="tpu_custom_call", output_to_operand_aliasing={{1}: (6, {})} | custom-call | flops 524288 | bytes 10000000 | tf_op jit(solution)/shard_map/pallas_call | solution.py:291
  (33 shorter events, 2.4 us)
Async XLA Ops:
  0.0 13.7 %copy-start = (bf16[1,4096,128]{2,1,0:T(8,128)(2,1)S(1)}, bf16[1,4096,128]{2,1,0:T(8,128)(2,1)}, u32[]{:S(2)}) copy-start(bf16[1,4096,128]{2,1,0:T(8,128)(2,1)} %param.5) | copy-start | bytes 3145732
  0.0 13.6 %collective-permute-start.2 = (bf16[128,128]{1,0:T(8,128)(2,1)}, bf16[128,128]{1,0:T(8,128)(2,1)S(1)}, u32[]{:S(2)}, u32[]{:S(2)}) collective-permute-start(bf16[128,128]{1,0:T(8,128)(2,1)} %bitcast.18), channel_id=1, source_target_pairs={{0,70},{1,23},{2,64},{3,17},{4,66},{5,19},{6,68},{7,21},{8,78},{9,... | collective-permute-start | bytes 98312 | tf_op jit(solution)/shard_map/ppermute | solution.py:46
  7.0 6.6 %collective-permute-start.1 = (bf16[128,128]{1,0:T(8,128)(2,1)}, bf16[128,128]{1,0:T(8,128)(2,1)S(1)}, u32[]{:S(2)}, u32[]{:S(2)}) collective-permute-start(bf16[128,128]{1,0:T(8,128)(2,1)} %bitcast.19), channel_id=1, source_target_pairs={{0,66},{1,19},{2,68},{3,21},{4,70},{5,23},{6,64},{7,17},{8,74},{9,... | collective-permute-start | bytes 98312 | tf_op jit(solution)/shard_map/ppermute | solution.py:46
  7.1 4.5 %collective-permute-start = (bf16[128,128]{1,0:T(8,128)(2,1)}, bf16[128,128]{1,0:T(8,128)(2,1)S(1)}, u32[]{:S(2)}, u32[]{:S(2)}) collective-permute-start(bf16[128,128]{1,0:T(8,128)(2,1)} %bitcast.20), channel_id=1, source_target_pairs={{0,4},{1,5},{2,6},{3,7},{4,0},{5,1},{6,2},{7,3},{8,12},{9,13},{10,... | collective-permute-start | bytes 98312 | tf_op jit(solution)/shard_map/ppermute | solution.py:46
  9.1 0.7 %copy-start.3 = (s32[1,4096,1]{1,2,0:T(1,128)S(1)}, s32[1,4096,1]{1,2,0:T(1,128)}, u32[]{:S(2)}) copy-start(s32[1,4096,1]{1,2,0:T(1,128)} %param.7) | copy-start | bytes 49156
  13.7 17.6 %copy-start.1 = (bf16[128,128]{1,0:T(8,128)(2,1)S(1)}, bf16[128,128]{1,0:T(8,128)(2,1)}, u32[]{:S(2)}) copy-start(bf16[128,128]{1,0:T(8,128)(2,1)} %plane_ref.3) | copy-start | bytes 98308
  13.7 17.6 %copy-start.2 = (f32[1,4096]{1,0:T(1,128)S(1)}, f32[1,4096]{1,0:T(1,128)}, u32[]{:S(2)}) copy-start(f32[1,4096]{1,0:T(1,128)} %param.6) | copy-start | bytes 49156
  13.7 8.9 %collective-permute-start.5 = (bf16[528,128]{1,0:T(8,128)(2,1)S(1)}, bf16[528,128]{1,0:T(8,128)(2,1)S(1)}, u32[]{:S(2)}, u32[]{:S(2)}) collective-permute-start(bf16[528,128]{1,0:T(8,128)(2,1)S(1)} %constant_dynamic-update-slice_fusion), channel_id=1, source_target_pairs={{0,24},{1,97},{2,26},{3,99},{4,28},{5,101},{6,30},{7,103},{8,0},{9... | collective-permute-start | bytes 405512 | tf_op jit(solution)/shard_map/ppermute | solution.py:46
  16.5 6.8 %collective-permute-start.4 = (bf16[528,128]{1,0:T(8,128)(2,1)S(1)}, bf16[528,128]{1,0:T(8,128)(2,1)S(1)}, u32[]{:S(2)}, u32[]{:S(2)}) collective-permute-start(bf16[528,128]{1,0:T(8,128)(2,1)S(1)} %constant_dynamic-update-slice_fusion), channel_id=1, source_target_pairs={{0,8},{1,33},{2,10},{3,35},{4,12},{5,37},{6,14},{7,39},{8,16},{9,4... | collective-permute-start | bytes 405512 | tf_op jit(solution)/shard_map/ppermute | solution.py:46
  16.5 6.8 %collective-permute-start.3 = (bf16[528,128]{1,0:T(8,128)(2,1)S(1)}, bf16[528,128]{1,0:T(8,128)(2,1)S(1)}, u32[]{:S(2)}, u32[]{:S(2)}) collective-permute-start(bf16[528,128]{1,0:T(8,128)(2,1)S(1)} %constant_dynamic-update-slice_fusion), channel_id=1, source_target_pairs={{0,16},{1,65},{2,18},{3,67},{4,20},{5,69},{6,22},{7,71},{8,24},{9,... | collective-permute-start | bytes 405512 | tf_op jit(solution)/shard_map/ppermute | solution.py:46
  23.4 9.8 %collective-permute-start.7 = (bf16[2112,128]{1,0:T(8,128)(2,1)S(1)}, bf16[2112,128]{1,0:T(8,128)(2,1)S(1)}, u32[]{:S(2)}, u32[]{:S(2)}) collective-permute-start(bf16[2112,128]{1,0:T(8,128)(2,1)S(1)} %pad_maximum_fusion.refs_0_.own_ref), channel_id=1, source_target_pairs={{0,32},{1,9},{2,34},{3,11},{4,36},{5,13},{6,38},{7,15},{8,40},{9,1... | collective-permute-start | bytes 1622024 | tf_op jit(solution)/shard_map/ppermute | solution.py:46
  23.8 13.4 %collective-permute-start.6 = (bf16[2112,128]{1,0:T(8,128)(2,1)S(1)}, bf16[2112,128]{1,0:T(8,128)(2,1)S(1)}, u32[]{:S(2)}, u32[]{:S(2)}) collective-permute-start(bf16[2112,128]{1,0:T(8,128)(2,1)S(1)} %pad_maximum_fusion.refs_0_.own_ref), channel_id=1, source_target_pairs={{0,96},{1,25},{2,98},{3,27},{4,100},{5,29},{6,102},{7,31},{8,104},... | collective-permute-start | bytes 1622024 | tf_op jit(solution)/shard_map/ppermute | solution.py:46
  26.1 4.8 %collective-permute-start.8 = (bf16[768,128]{1,0:T(8,128)(2,1)S(1)}, bf16[768,128]{1,0:T(8,128)(2,1)S(1)}, u32[]{:S(2)}, u32[]{:S(2)}) collective-permute-start(bf16[768,128]{1,0:T(8,128)(2,1)S(1)} %get-tuple-element.33), channel_id=1, source_target_pairs={{0,1},{1,0},{2,3},{3,2},{4,5},{5,4},{6,7},{7,6},{8,9},{9,8},{10,11... | collective-permute-start | bytes 589832 | tf_op jit(solution)/shard_map/ppermute | solution.py:55
  29.9 8.5 %collective-permute-start.13 = (bf16[2112,128]{1,0:T(8,128)(2,1)S(1)}, bf16[2112,128]{1,0:T(8,128)(2,1)S(1)}, u32[]{:S(2)}, u32[]{:S(2)}) collective-permute-start(bf16[2112,128]{1,0:T(8,128)(2,1)S(1)} %pad_maximum_fusion.refs_0_.own_ref), channel_id=1, source_target_pairs={{0,2},{1,7},{2,4},{3,1},{4,6},{5,3},{6,0},{7,5},{8,10},{9,15},{10,... | collective-permute-start | bytes 1622024 | tf_op jit(solution)/shard_map/ppermute | solution.py:46
  30.6 6.6 %collective-permute-start.10 = (bf16[768,128]{1,0:T(8,128)(2,1)S(1)}, bf16[768,128]{1,0:T(8,128)(2,1)S(1)}, u32[]{:S(2)}, u32[]{:S(2)}) collective-permute-start(bf16[768,128]{1,0:T(8,128)(2,1)S(1)} %get-tuple-element.38), channel_id=1, source_target_pairs={{0,1},{1,0},{2,3},{3,2},{4,5},{5,4},{6,7},{7,6},{8,9},{9,8},{10,11... | collective-permute-start | bytes 589832 | tf_op jit(solution)/shard_map/ppermute | solution.py:55
  30.9 6.3 %collective-permute-start.11 = (bf16[768,128]{1,0:T(8,128)(2,1)S(1)}, bf16[768,128]{1,0:T(8,128)(2,1)S(1)}, u32[]{:S(2)}, u32[]{:S(2)}) collective-permute-start(bf16[768,128]{1,0:T(8,128)(2,1)S(1)} %get-tuple-element.39), channel_id=1, source_target_pairs={{0,1},{1,0},{2,3},{3,2},{4,5},{5,4},{6,7},{7,6},{8,9},{9,8},{10,11... | collective-permute-start | bytes 589832 | tf_op jit(solution)/shard_map/ppermute | solution.py:55
  33.2 5.1 %collective-permute-start.14 = (bf16[768,128]{1,0:T(8,128)(2,1)S(1)}, bf16[768,128]{1,0:T(8,128)(2,1)S(1)}, u32[]{:S(2)}, u32[]{:S(2)}) collective-permute-start(bf16[768,128]{1,0:T(8,128)(2,1)S(1)} %get-tuple-element.40), channel_id=1, source_target_pairs={{0,1},{1,0},{2,3},{3,2},{4,5},{5,4},{6,7},{7,6},{8,9},{9,8},{10,11... | collective-permute-start | bytes 589832 | tf_op jit(solution)/shard_map/ppermute | solution.py:55
  37.7 4.6 %collective-permute-start.12 = (bf16[1536,128]{1,0:T(8,128)(2,1)S(1)}, bf16[1536,128]{1,0:T(8,128)(2,1)S(1)}, u32[]{:S(2)}, u32[]{:S(2)}) collective-permute-start(bf16[1536,128]{1,0:T(8,128)(2,1)S(1)} %shard_map.61), channel_id=1, source_target_pairs={{0,1},{1,0},{2,3},{3,2},{4,5},{5,4},{6,7},{7,6},{8,9},{9,8},{10,11... | collective-permute-start | bytes 1179656 | tf_op jit(solution)/shard_map/ppermute | solution.py:55
  38.7 3.2 %collective-permute-start.15 = (bf16[768,128]{1,0:T(8,128)(2,1)S(1)}, bf16[768,128]{1,0:T(8,128)(2,1)S(1)}, u32[]{:S(2)}, u32[]{:S(2)}) collective-permute-start(bf16[768,128]{1,0:T(8,128)(2,1)S(1)} %shard_map.62), channel_id=1, source_target_pairs={{0,1},{1,0},{2,3},{3,2},{4,5},{5,4},{6,7},{7,6},{8,9},{9,8},{10,11... | collective-permute-start | bytes 589832 | tf_op jit(solution)/shard_map/ppermute | solution.py:55
  40.9 1.4 %collective-permute-start.9 = (bf16[768,128]{1,0:T(8,128)(2,1)S(1)}, bf16[768,128]{1,0:T(8,128)(2,1)S(1)}, u32[]{:S(2)}, u32[]{:S(2)}) collective-permute-start(bf16[768,128]{1,0:T(8,128)(2,1)S(1)} %shard_map.59), channel_id=1, source_target_pairs={{0,1},{1,0},{2,3},{3,2},{4,5},{5,4},{6,7},{7,6},{8,9},{9,8},{10,11... | collective-permute-start | bytes 589832 | tf_op jit(solution)/shard_map/ppermute | solution.py:55

commit v10 on v8

--- a/solution.py
+++ b/solution.py
@@ -62,11 +62,11 @@
 
 
 def around(value, moves):
-    return [value] + [shifted(value, scaled(moves, step)) for step in (2, 1, -1)]
+    return [value] + [shifted(value, scaled(moves, step)) for step in (-1, 1, 2)]
 
 
 def offset(index):
-    return jnp.where(index == 1, 2, jnp.where(index == 2, 3, jnp.where(index == 3, 1, 0)))
+    return jnp.where(index == 1, 1, jnp.where(index == 2, 3, jnp.where(index == 3, 2, 0)))
 
 
 def slot_owners():
@@ -158,7 +158,7 @@
     choice = jnp.where(sub == 0, 3, jnp.where(x == 0, 1, inner))
     before = halo(choice, own_ref, before_ref, 2)
     choice = jnp.where(sub == 15, 3, jnp.where(x == 3, 1, inner))
-    after = halo(choice, own_ref, after_ref, 3)
+    after = halo(choice, own_ref, after_ref, 1)
     before = jnp.dot(before, plane, preferred_element_type=jnp.float32)[15:16]
     after = jnp.dot(after, plane, preferred_element_type=jnp.float32)[0:1]
     out_ref[0:1, :] = step_size * coupling_ref[0:1, 0:1] * before

time: 47.9 us -> 48.1 us (level)
  starting transfers between devices: 27.5 us -> 29.2 us
  waiting for transfers between devices: 4.86 us -> 3.37 us
    ppermute x9, starting transfers between devices: 16.3 us -> 21.1 us  [shifted(): return lax.ppermute(value, axes_all, pairs)]
    ppermute x6, starting transfers between devices: 11.2 us -> 8.13 us  [core_swap(): return lax.ppermute(value, axes_all, pairs)]
    ppermute x9, waiting for transfers between devices: 4.3 us -> 2.75 us  [shifted(): return lax.ppermute(value, axes_all, pairs)]
  transfers between devices with their start and end apart: 15 -> 15, of which waited for: 6 -> 4; matrix products, arithmetic and copies ran while one was open for 2% -> 2% of each run, Pallas kernels for 17% -> 17%
where the time goes in v10:
time: 48.1 us; the launch traced here: 47.9 us
  starting transfers between devices  29.2 us (61%)
  Pallas kernels  13.5 us (28%)
  waiting for transfers between devices  3.37 us (7%)
  local copies, waits for them, and re-layouts  1.57 us (3%)
    ppermute x9, starting transfers between devices, shifted(): return lax.ppermute(value, axes_all, pairs)  21.1 us
    ppermute x6, starting transfers between devices, core_swap(): return lax.ppermute(value, axes_all, pairs)  8.13 us
    pallas_call x1, Pallas kernels, finish(): pl.pallas_call(final_kernel, in_specs=[pl.BlockSpec(memory_space=pltpu.SM...  5.19 us
    pallas_call x1, Pallas kernels, sort_rows(): pl.pallas_call(sort_kernel, in_specs=[pl.BlockSpec(memory_space=pltpu.SME...  4.46 us
    ppermute x9, waiting for transfers between devices, shifted(): return lax.ppermute(value, axes_all, pairs)  2.75 us
    pallas_call x5, Pallas kernels, effect_call(): pl.pallas_call(functools.partial(effect_kernel, sources, places), in_spec...  2.31 us
    unnamed x13, local copies, waits for them, and re-layouts  1.57 us
  transfers between devices with their start and end apart: 15, of which 4 were waited for; matrix products, arithmetic and copies ran while one was open for 2% of the time, Pallas kernels for 17%

profile of v10, /device:TPU:1, one launch (start us, length us, event | category | flops | bytes accessed | tf_op | source)
XLA Modules:
  0.0 47.9 jit_solution(14181424416422673408)
XLA Ops:
  0.0 4.4 %collective-permute-start.2 = (bf16[128,128]{1,0:T(8,128)(2,1)}, bf16[128,128]{1,0:T(8,128)(2,1)S(1)}, u32[]{:S(2)}, u32[]{:S(2)}) collective-permute-start(bf16[128,128]{1,0:T(8,128)(2,1)} %bitcast.18), channel_id=1, source_target_pairs={{0,4},{1,5},{2,6},{3,7},{4,0},{5,1},{6,2},{7,3},{8,12},{9,13},{10,... | collective-permute-start | bytes 98312 | tf_op jit(solution)/shard_map/ppermute | solution.py:46
  4.4 3.2 %collective-permute-start.1 = (bf16[128,128]{1,0:T(8,128)(2,1)}, bf16[128,128]{1,0:T(8,128)(2,1)S(1)}, u32[]{:S(2)}, u32[]{:S(2)}) collective-permute-start(bf16[128,128]{1,0:T(8,128)(2,1)} %bitcast.19), channel_id=1, source_target_pairs={{0,66},{1,19},{2,68},{3,21},{4,70},{5,23},{6,64},{7,17},{8,74},{9,... | collective-permute-start | bytes 98312 | tf_op jit(solution)/shard_map/ppermute | solution.py:46
  7.6 1.9 %collective-permute-start = (bf16[128,128]{1,0:T(8,128)(2,1)}, bf16[128,128]{1,0:T(8,128)(2,1)S(1)}, u32[]{:S(2)}, u32[]{:S(2)}) collective-permute-start(bf16[128,128]{1,0:T(8,128)(2,1)} %bitcast.20), channel_id=1, source_target_pairs={{0,70},{1,23},{2,64},{3,17},{4,66},{5,19},{6,68},{7,21},{8,78},{9,... | collective-permute-start | bytes 98312 | tf_op jit(solution)/shard_map/ppermute | solution.py:46
  9.5 0.8 %constant_dynamic-update-slice_fusion.5 = bf16[528,128]{1,0:T(8,128)(2,1)S(1)} fusion(bf16[1,128,128]{2,1,0:T(8,128)(2,1)} %param.9), kind=kLoop, calls=%fused_computation.6 | loop fusion | bytes 65536
  10.3 0.7 %copy-done.3 = s32[1,4096,1]{1,2,0:T(1,128)S(1)} copy-done((s32[1,4096,1]{1,2,0:T(1,128)S(1)}, s32[1,4096,1]{1,2,0:T(1,128)}, u32[]{:S(2)}) %copy-start.3) | copy-done | bytes 16408
  11.0 0.8 %shard_map.55 = s32[1,4096]{1,0:T(1,128)S(1)} custom-call(s32[1,4096]{1,0:T(1,128)S(1)} %bitcast.17), custom_call_target="tpu_custom_call" | custom-call | flops 402653184 | bytes 100000 | tf_op jit(solution)/shard_map/pallas_call | solution.py:105
  11.8 1.2 %collective-permute-done = bf16[128,128]{1,0:T(8,128)(2,1)S(1)} collective-permute-done((bf16[128,128]{1,0:T(8,128)(2,1)}, bf16[128,128]{1,0:T(8,128)(2,1)S(1)}, u32[]{:S(2)}, u32[]{:S(2)}) %collective-permute-start) | collective-permute-done | bytes 32800 | tf_op jit(solution)/shard_map/ppermute | solution.py:46
  13.1 3.0 %collective-permute-start.5 = (bf16[528,128]{1,0:T(8,128)(2,1)S(1)}, bf16[528,128]{1,0:T(8,128)(2,1)S(1)}, u32[]{:S(2)}, u32[]{:S(2)}) collective-permute-start(bf16[528,128]{1,0:T(8,128)(2,1)S(1)} %constant_dynamic-update-slice_fusion), channel_id=1, source_target_pairs={{0,16},{1,65},{2,18},{3,67},{4,20},{5,69},{6,22},{7,71},{8,24},{9,... | collective-permute-start | bytes 405512 | tf_op jit(solution)/shard_map/ppermute | solution.py:46
  16.1 0.7 %collective-permute-start.4 = (bf16[528,128]{1,0:T(8,128)(2,1)S(1)}, bf16[528,128]{1,0:T(8,128)(2,1)S(1)}, u32[]{:S(2)}, u32[]{:S(2)}) collective-permute-start(bf16[528,128]{1,0:T(8,128)(2,1)S(1)} %constant_dynamic-update-slice_fusion), channel_id=1, source_target_pairs={{0,8},{1,33},{2,10},{3,35},{4,12},{5,37},{6,14},{7,39},{8,16},{9,4... | collective-permute-start | bytes 405512 | tf_op jit(solution)/shard_map/ppermute | solution.py:46
  16.7 2.0 %collective-permute-start.3 = (bf16[528,128]{1,0:T(8,128)(2,1)S(1)}, bf16[528,128]{1,0:T(8,128)(2,1)S(1)}, u32[]{:S(2)}, u32[]{:S(2)}) collective-permute-start(bf16[528,128]{1,0:T(8,128)(2,1)S(1)} %constant_dynamic-update-slice_fusion), channel_id=1, source_target_pairs={{0,24},{1,97},{2,26},{3,99},{4,28},{5,101},{6,30},{7,103},{8,0},{9... | collective-permute-start | bytes 405512 | tf_op jit(solution)/shard_map/ppermute | solution.py:46
  18.8 4.5 %shard_map.56 = (bf16[3072,128]{1,0:T(8,128)(2,1)S(1)}, bf16[768,128]{1,0:T(8,128)(2,1)S(1)}, bf16[768,128]{1,0:T(8,128)(2,1)S(1)}, bf16[1536,128]{1,0:T(8,128)(2,1)S(1)}) custom-call(s32[4096]{0:T(1024)S(1)} %bitcast.15, bf16[4096,128]{1,0:T(8,128)(2,1)S(1)} %bitcast.11), custom_call_target="tpu_custom_call" | custom-call | bytes 20000000 | tf_op jit(solution)/shard_map/pallas_call | solution.py:130
  23.3 0.7 %collective-permute-start.7 = (bf16[2112,128]{1,0:T(8,128)(2,1)S(1)}, bf16[2112,128]{1,0:T(8,128)(2,1)S(1)}, u32[]{:S(2)}, u32[]{:S(2)}) collective-permute-start(bf16[2112,128]{1,0:T(8,128)(2,1)S(1)} %pad_maximum_fusion.refs_0_.own_ref), channel_id=1, source_target_pairs={{0,32},{1,9},{2,34},{3,11},{4,36},{5,13},{6,38},{7,15},{8,40},{9,1... | collective-permute-start | bytes 1622024 | tf_op jit(solution)/shard_map/ppermute | solution.py:46
  24.0 2.1 %collective-permute-start.6 = (bf16[2112,128]{1,0:T(8,128)(2,1)S(1)}, bf16[2112,128]{1,0:T(8,128)(2,1)S(1)}, u32[]{:S(2)}, u32[]{:S(2)}) collective-permute-start(bf16[2112,128]{1,0:T(8,128)(2,1)S(1)} %pad_maximum_fusion.refs_0_.own_ref), channel_id=1, source_target_pairs={{0,96},{1,25},{2,98},{3,27},{4,100},{5,29},{6,102},{7,31},{8,104},... | collective-permute-start | bytes 1622024 | tf_op jit(solution)/shard_map/ppermute | solution.py:46
  26.1 3.8 %collective-permute-start.8 = (bf16[768,128]{1,0:T(8,128)(2,1)S(1)}, bf16[768,128]{1,0:T(8,128)(2,1)S(1)}, u32[]{:S(2)}, u32[]{:S(2)}) collective-permute-start(bf16[768,128]{1,0:T(8,128)(2,1)S(1)} %get-tuple-element.30), channel_id=1, source_target_pairs={{0,1},{1,0},{2,3},{3,2},{4,5},{5,4},{6,7},{7,6},{8,9},{9,8},{10,11... | collective-permute-start | bytes 589832 | tf_op jit(solution)/shard_map/ppermute | solution.py:55
  29.9 3.1 %collective-permute-start.13 = (bf16[2112,128]{1,0:T(8,128)(2,1)S(1)}, bf16[2112,128]{1,0:T(8,128)(2,1)S(1)}, u32[]{:S(2)}, u32[]{:S(2)}) collective-permute-start(bf16[2112,128]{1,0:T(8,128)(2,1)S(1)} %pad_maximum_fusion.refs_0_.own_ref), channel_id=1, source_target_pairs={{0,2},{1,7},{2,4},{3,1},{4,6},{5,3},{6,0},{7,5},{8,10},{9,15},{10,... | collective-permute-start | bytes 1622024 | tf_op jit(solution)/shard_map/ppermute | solution.py:46
  33.5 0.7 %shard_map.59.base_ref = f32[4096,128]{1,0:T(8,128)S(1)} custom-call(bf16[4096,128]{1,0:T(8,128)(2,1)S(1)} %bitcast.12, f32[32,128]{1,0:T(8,128)S(1)} %bitcast.13, bf16[128,128]{1,0:T(8,128)(2,1)S(1)} %copy-done.1), custom_call_target="tpu_custom_call" | custom-call | flops 1000 | bytes 1000 | tf_op jit(solution)/shard_map/pallas_call | solution.py:198
  34.2 0.4 shard_map.57.refs_3_
  35.2 0.5 %shard_map.61 = bf16[1536,128]{1,0:T(8,128)(2,1)S(1)} custom-call(bf16[1536,128]{1,0:T(8,128)(2,1)S(1)} %collective-permute-done.10.rows_ref, bf16[2112,128]{1,0:T(8,128)(2,1)S(1)} %collective-permute-done.7.before_ref.refs_0_.refs_1_, bf16[2112,128]{1,0:T(8,128)(2,1)S(1)} %collective-permute-done.6.after_ref.refs_1_.refs_2_), custom_call_target="tpu_custom_call" | custom-call | flops 1000 | bytes 1000 | tf_op jit(solution)/shard_map/pallas_call | solution.py:228
  35.7 2.1 %collective-permute-start.11 = (bf16[1536,128]{1,0:T(8,128)(2,1)S(1)}, bf16[1536,128]{1,0:T(8,128)(2,1)S(1)}, u32[]{:S(2)}, u32[]{:S(2)}) collective-permute-start(bf16[1536,128]{1,0:T(8,128)(2,1)S(1)} %shard_map.61), channel_id=1, source_target_pairs={{0,1},{1,0},{2,3},{3,2},{4,5},{5,4},{6,7},{7,6},{8,9},{9,8},{10,11... | collective-permute-start | bytes 1179656 | tf_op jit(solution)/shard_map/ppermute | solution.py:55
  37.8 1.5 %collective-permute-done.13.refs_0_ = bf16[2112,128]{1,0:T(8,128)(2,1)S(1)} collective-permute-done((bf16[2112,128]{1,0:T(8,128)(2,1)S(1)}, bf16[2112,128]{1,0:T(8,128)(2,1)S(1)}, u32[]{:S(2)}, u32[]{:S(2)}) %collective-permute-start.13) | collective-permute-done | bytes 540704 | tf_op jit(solution)/shard_map/ppermute | solution.py:46
  39.3 0.4 shard_map.62
  39.7 1.9 %collective-permute-start.14 = (bf16[768,128]{1,0:T(8,128)(2,1)S(1)}, bf16[768,128]{1,0:T(8,128)(2,1)S(1)}, u32[]{:S(2)}, u32[]{:S(2)}) collective-permute-start(bf16[768,128]{1,0:T(8,128)(2,1)S(1)} %shard_map.62), channel_id=1, source_target_pairs={{0,1},{1,0},{2,3},{3,2},{4,5},{5,4},{6,7},{7,6},{8,9},{9,8},{10,11... | collective-permute-start | bytes 589832 | tf_op jit(solution)/shard_map/ppermute | solution.py:55
  41.7 0.7 %shard_map.63._ = f32[6144,128]{1,0:T(8,128)S(1)} custom-call(bf16[3072,128]{1,0:T(8,128)(2,1)S(1)} %get-tuple-element.29.rows_ref, bf16[2112,128]{1,0:T(8,128)(2,1)S(1)} %collective-permute-done.13.refs_0_, bf16[2112,128]{1,0:T(8,128)(2,1)S(1)} %collective-permute-done.7.before_ref.refs_0_.refs_1_, ...), custom_call_target="tpu_custom_call", output_to_operand_aliasing={{}: (4, {})} | custom-call | flops 1000 | bytes 1000 | tf_op jit(solution)/shard_map/pallas_call | solution.py:228
  42.7 5.2 %shard_map.64 = (f32[4096,128]{1,0:T(8,128)}, f32[6144,128]{1,0:T(8,128)S(1)}) custom-call(s32[4096]{0:T(1024)S(1)} %bitcast.16, f32[4096,128]{1,0:T(8,128)S(1)} %shard_map.59.base_ref, f32[8,128]{1,0:T(8,128)S(1)} %shard_map.60.ends_ref, bf16[768,128]{1,0:T(8,128)(2,1)S(1)} %collective-permute-done.9.own_ref, ...), custom_call_target="tpu_custom_call", output_to_operand_aliasing={{1}: (6, {})} | custom-call | flops 524288 | bytes 10000000 | tf_op jit(solution)/shard_map/pallas_call | solution.py:288
  (31 shorter events, 1.5 us)
Async XLA Ops:
  0.0 13.1 %copy-start = (bf16[1,4096,128]{2,1,0:T(8,128)(2,1)S(1)}, bf16[1,4096,128]{2,1,0:T(8,128)(2,1)}, u32[]{:S(2)}) copy-start(bf16[1,4096,128]{2,1,0:T(8,128)(2,1)} %param.5) | copy-start | bytes 3145732
  0.0 13.0 %collective-permute-start.2 = (bf16[128,128]{1,0:T(8,128)(2,1)}, bf16[128,128]{1,0:T(8,128)(2,1)S(1)}, u32[]{:S(2)}, u32[]{:S(2)}) collective-permute-start(bf16[128,128]{1,0:T(8,128)(2,1)} %bitcast.18), channel_id=1, source_target_pairs={{0,4},{1,5},{2,6},{3,7},{4,0},{5,1},{6,2},{7,3},{8,12},{9,13},{10,... | collective-permute-start | bytes 98312 | tf_op jit(solution)/shard_map/ppermute | solution.py:46
  4.4 8.6 %collective-permute-start.1 = (bf16[128,128]{1,0:T(8,128)(2,1)}, bf16[128,128]{1,0:T(8,128)(2,1)S(1)}, u32[]{:S(2)}, u32[]{:S(2)}) collective-permute-start(bf16[128,128]{1,0:T(8,128)(2,1)} %bitcast.19), channel_id=1, source_target_pairs={{0,66},{1,19},{2,68},{3,21},{4,70},{5,23},{6,64},{7,17},{8,74},{9,... | collective-permute-start | bytes 98312 | tf_op jit(solution)/shard_map/ppermute | solution.py:46
  7.6 5.4 %collective-permute-start = (bf16[128,128]{1,0:T(8,128)(2,1)}, bf16[128,128]{1,0:T(8,128)(2,1)S(1)}, u32[]{:S(2)}, u32[]{:S(2)}) collective-permute-start(bf16[128,128]{1,0:T(8,128)(2,1)} %bitcast.20), channel_id=1, source_target_pairs={{0,70},{1,23},{2,64},{3,17},{4,66},{5,19},{6,68},{7,21},{8,78},{9,... | collective-permute-start | bytes 98312 | tf_op jit(solution)/shard_map/ppermute | solution.py:46
  10.3 0.7 %copy-start.3 = (s32[1,4096,1]{1,2,0:T(1,128)S(1)}, s32[1,4096,1]{1,2,0:T(1,128)}, u32[]{:S(2)}) copy-start(s32[1,4096,1]{1,2,0:T(1,128)} %param.7) | copy-start | bytes 49156
  13.1 10.2 %collective-permute-start.5 = (bf16[528,128]{1,0:T(8,128)(2,1)S(1)}, bf16[528,128]{1,0:T(8,128)(2,1)S(1)}, u32[]{:S(2)}, u32[]{:S(2)}) collective-permute-start(bf16[528,128]{1,0:T(8,128)(2,1)S(1)} %constant_dynamic-update-slice_fusion), channel_id=1, source_target_pairs={{0,16},{1,65},{2,18},{3,67},{4,20},{5,69},{6,22},{7,71},{8,24},{9,... | collective-permute-start | bytes 405512 | tf_op jit(solution)/shard_map/ppermute | solution.py:46
  16.1 7.2 %collective-permute-start.4 = (bf16[528,128]{1,0:T(8,128)(2,1)S(1)}, bf16[528,128]{1,0:T(8,128)(2,1)S(1)}, u32[]{:S(2)}, u32[]{:S(2)}) collective-permute-start(bf16[528,128]{1,0:T(8,128)(2,1)S(1)} %constant_dynamic-update-slice_fusion), channel_id=1, source_target_pairs={{0,8},{1,33},{2,10},{3,35},{4,12},{5,37},{6,14},{7,39},{8,16},{9,4... | collective-permute-start | bytes 405512 | tf_op jit(solution)/shard_map/ppermute | solution.py:46
  16.7 6.5 %collective-permute-start.3 = (bf16[528,128]{1,0:T(8,128)(2,1)S(1)}, bf16[528,128]{1,0:T(8,128)(2,1)S(1)}, u32[]{:S(2)}, u32[]{:S(2)}) collective-permute-start(bf16[528,128]{1,0:T(8,128)(2,1)S(1)} %constant_dynamic-update-slice_fusion), channel_id=1, source_target_pairs={{0,24},{1,97},{2,26},{3,99},{4,28},{5,101},{6,30},{7,103},{8,0},{9... | collective-permute-start | bytes 405512 | tf_op jit(solution)/shard_map/ppermute | solution.py:46
  23.2 10.2 %copy-start.1 = (bf16[128,128]{1,0:T(8,128)(2,1)S(1)}, bf16[128,128]{1,0:T(8,128)(2,1)}, u32[]{:S(2)}) copy-start(bf16[128,128]{1,0:T(8,128)(2,1)} %plane_ref.3) | copy-start | bytes 98308
  23.2 10.2 %copy-start.2 = (f32[1,4096]{1,0:T(1,128)S(1)}, f32[1,4096]{1,0:T(1,128)}, u32[]{:S(2)}) copy-start(f32[1,4096]{1,0:T(1,128)} %param.6) | copy-start | bytes 49156
  23.3 11.8 %collective-permute-start.7 = (bf16[2112,128]{1,0:T(8,128)(2,1)S(1)}, bf16[2112,128]{1,0:T(8,128)(2,1)S(1)}, u32[]{:S(2)}, u32[]{:S(2)}) collective-permute-start(bf16[2112,128]{1,0:T(8,128)(2,1)S(1)} %pad_maximum_fusion.refs_0_.own_ref), channel_id=1, source_target_pairs={{0,32},{1,9},{2,34},{3,11},{4,36},{5,13},{6,38},{7,15},{8,40},{9,1... | collective-permute-start | bytes 1622024 | tf_op jit(solution)/shard_map/ppermute | solution.py:46
  24.0 11.1 %collective-permute-start.6 = (bf16[2112,128]{1,0:T(8,128)(2,1)S(1)}, bf16[2112,128]{1,0:T(8,128)(2,1)S(1)}, u32[]{:S(2)}, u32[]{:S(2)}) collective-permute-start(bf16[2112,128]{1,0:T(8,128)(2,1)S(1)} %pad_maximum_fusion.refs_0_.own_ref), channel_id=1, source_target_pairs={{0,96},{1,25},{2,98},{3,27},{4,100},{5,29},{6,102},{7,31},{8,104},... | collective-permute-start | bytes 1622024 | tf_op jit(solution)/shard_map/ppermute | solution.py:46
  26.1 6.9 %collective-permute-start.8 = (bf16[768,128]{1,0:T(8,128)(2,1)S(1)}, bf16[768,128]{1,0:T(8,128)(2,1)S(1)}, u32[]{:S(2)}, u32[]{:S(2)}) collective-permute-start(bf16[768,128]{1,0:T(8,128)(2,1)S(1)} %get-tuple-element.30), channel_id=1, source_target_pairs={{0,1},{1,0},{2,3},{3,2},{4,5},{5,4},{6,7},{7,6},{8,9},{9,8},{10,11... | collective-permute-start | bytes 589832 | tf_op jit(solution)/shard_map/ppermute | solution.py:55
  29.9 5.3 %collective-permute-start.10 = (bf16[1536,128]{1,0:T(8,128)(2,1)S(1)}, bf16[1536,128]{1,0:T(8,128)(2,1)S(1)}, u32[]{:S(2)}, u32[]{:S(2)}) collective-permute-start(bf16[1536,128]{1,0:T(8,128)(2,1)S(1)} %get-tuple-element.35), channel_id=1, source_target_pairs={{0,1},{1,0},{2,3},{3,2},{4,5},{5,4},{6,7},{7,6},{8,9},{9,8},{10,11... | collective-permute-start | bytes 1179656 | tf_op jit(solution)/shard_map/ppermute | solution.py:55
  29.9 9.5 %collective-permute-start.13 = (bf16[2112,128]{1,0:T(8,128)(2,1)S(1)}, bf16[2112,128]{1,0:T(8,128)(2,1)S(1)}, u32[]{:S(2)}, u32[]{:S(2)}) collective-permute-start(bf16[2112,128]{1,0:T(8,128)(2,1)S(1)} %pad_maximum_fusion.refs_0_.own_ref), channel_id=1, source_target_pairs={{0,2},{1,7},{2,4},{3,1},{4,6},{5,3},{6,0},{7,5},{8,10},{9,15},{10,... | collective-permute-start | bytes 1622024 | tf_op jit(solution)/shard_map/ppermute | solution.py:46
  33.4 1.5 %collective-permute-start.9 = (bf16[768,128]{1,0:T(8,128)(2,1)S(1)}, bf16[768,128]{1,0:T(8,128)(2,1)S(1)}, u32[]{:S(2)}, u32[]{:S(2)}) collective-permute-start(bf16[768,128]{1,0:T(8,128)(2,1)S(1)} %shard_map.58), channel_id=1, source_target_pairs={{0,1},{1,0},{2,3},{3,2},{4,5},{5,4},{6,7},{7,6},{8,9},{9,8},{10,11... | collective-permute-start | bytes 589832 | tf_op jit(solution)/shard_map/ppermute | solution.py:55
  34.9 2.9 %collective-permute-start.12 = (bf16[768,128]{1,0:T(8,128)(2,1)S(1)}, bf16[768,128]{1,0:T(8,128)(2,1)S(1)}, u32[]{:S(2)}, u32[]{:S(2)}) collective-permute-start(bf16[768,128]{1,0:T(8,128)(2,1)S(1)} %get-tuple-element.36), channel_id=1, source_target_pairs={{0,1},{1,0},{2,3},{3,2},{4,5},{5,4},{6,7},{7,6},{8,9},{9,8},{10,11... | collective-permute-start | bytes 589832 | tf_op jit(solution)/shard_map/ppermute | solution.py:55
  35.7 7.0 %collective-permute-start.11 = (bf16[1536,128]{1,0:T(8,128)(2,1)S(1)}, bf16[1536,128]{1,0:T(8,128)(2,1)S(1)}, u32[]{:S(2)}, u32[]{:S(2)}) collective-permute-start(bf16[1536,128]{1,0:T(8,128)(2,1)S(1)} %shard_map.61), channel_id=1, source_target_pairs={{0,1},{1,0},{2,3},{3,2},{4,5},{5,4},{6,7},{7,6},{8,9},{9,8},{10,11... | collective-permute-start | bytes 1179656 | tf_op jit(solution)/shard_map/ppermute | solution.py:55
  39.7 3.0 %collective-permute-start.14 = (bf16[768,128]{1,0:T(8,128)(2,1)S(1)}, bf16[768,128]{1,0:T(8,128)(2,1)S(1)}, u32[]{:S(2)}, u32[]{:S(2)}) collective-permute-start(bf16[768,128]{1,0:T(8,128)(2,1)S(1)} %shard_map.62), channel_id=1, source_target_pairs={{0,1},{1,0},{2,3},{3,2},{4,5},{5,4},{6,7},{7,6},{8,9},{9,8},{10,11... | collective-permute-start | bytes 589832 | tf_op jit(solution)/shard_map/ppermute | solution.py:55

commit v11 on v9

--- a/solution.py
+++ b/solution.py
@@ -62,11 +62,11 @@
 
 
 def around(value, moves):
-    return [value] + [shifted(value, scaled(moves, step)) for step in (2, 1, -1)]
+    return [value] + [shifted(value, scaled(moves, step)) for step in (-1, 1, 2)]
 
 
 def offset(index):
-    return jnp.where(index == 1, 2, jnp.where(index == 2, 3, jnp.where(index == 3, 1, 0)))
+    return jnp.where(index == 1, 1, jnp.where(index == 2, 3, jnp.where(index == 3, 2, 0)))
 
 
 def slot_owners():
@@ -158,7 +158,7 @@
     choice = jnp.where(sub == 0, 3, jnp.where(x == 0, 1, inner))
     before = halo(choice, own_ref, before_ref, 2)
     choice = jnp.where(sub == 15, 3, jnp.where(x == 3, 1, inner))
-    after = halo(choice, own_ref, after_ref, 3)
+    after = halo(choice, own_ref, after_ref, 1)
     before = jnp.dot(before, plane, preferred_element_type=jnp.float32)[15:16]
     after = jnp.dot(after, plane, preferred_element_type=jnp.float32)[0:1]
     out_ref[0:1, :] = step_size * coupling_ref[0:1, 0:1] * before
@@ -257,11 +257,11 @@
 
 
 def final_kernel(
-    slot_ref, base_ref, ends_ref, own_ref, pair_ref, side_ref, _, out_ref, effect_ref, result, sent
+    slot_ref, base_ref, ends_ref, own_ref, plus_ref, minus_ref, side_ref, _, out_ref, effect_ref, result, sent
 ):
-    for returned_ref, first, third in ((own_ref, 0, 0), (pair_ref, 0, 2), (pair_ref, 1, 3), (side_ref, 0, 1)):
-        lo, top = half + third * block, first * block
-        effect_ref[lo : lo + block, :] = returned_ref[top : top + block, :].astype(jnp.float32)
+    for returned_ref, third in ((own_ref, 0), (plus_ref, 2), (minus_ref, 3), (side_ref, 1)):
+        lo = half + third * block
+        effect_ref[lo : lo + block, :] = returned_ref[...].astype(jnp.float32)
 
     copies = []
     for number, (top, end) in enumerate(zip(part_tops, part_tops[1:])):
@@ -325,7 +325,8 @@
     reply = replies([plane], [own_guest])
     minus, plus, effect, base, reply = tied((minus, plus, effect, base, reply))
     returned = [core_swap(reply)]
-    returned.append(core_swap(replies([plus, minus], pair_guests)))
+    for part, guest in zip((plus, minus), pair_guests):
+        returned.append(core_swap(replies([part], [guest])))
     returned.append(core_swap(replies([side], [side_guest])))
     effect = effects(near_rows, [side, plus, minus], (1, 2, 3), effect)
     ends = end_terms(plane, plus, minus, weights, in_plane)

time: 47.7 us -> 46.1 us (0.966)
  waiting for transfers between devices: 5.58 us -> 2.81 us
  starting transfers between devices: 26.7 us -> 27.6 us
    ppermute x9, starting transfers between devices: 16.3 us -> 21.1 us  [shifted(): return lax.ppermute(value, axes_all, pairs)]
    ppermute x7 -> x8, starting transfers between devices: 10.4 us -> 6.49 us  [core_swap(): return lax.ppermute(value, axes_all, pairs)]
    ppermute x9, waiting for transfers between devices: 4.27 us -> 1.22 us  [shifted(): return lax.ppermute(value, axes_all, pairs)]
    ppermute x7 -> x8, waiting for transfers between devices: 1.3 us -> 1.59 us  [core_swap(): return lax.ppermute(value, axes_all, pairs)]
    pallas_call x5 -> x6, Pallas kernels: 2.31 us -> 2.53 us  [effect_call(): pl.pallas_call(functools.partial(effect_kernel, sources, places), in_spec...]
  transfers between devices with their start and end apart: 16 -> 17, of which waited for: 9 -> 3; matrix products, arithmetic and copies ran while one was open for 2% -> 2% of each run, Pallas kernels for 18% -> 19%
where the time goes in v11:
time: 46.1 us; the launch traced here: 45.9 us
  starting transfers between devices  27.6 us (60%)
  Pallas kernels  13.7 us (30%)
  waiting for transfers between devices  2.81 us (6%)
  local copies, waits for them, and re-layouts  1.57 us (3%)
    ppermute x9, starting transfers between devices, shifted(): return lax.ppermute(value, axes_all, pairs)  21.1 us
    ppermute x8, starting transfers between devices, core_swap(): return lax.ppermute(value, axes_all, pairs)  6.49 us
    pallas_call x1, Pallas kernels, finish(): pl.pallas_call(final_kernel, in_specs=[pl.BlockSpec(memory_space=pltpu.SM...  5.2 us
    pallas_call x1, Pallas kernels, sort_rows(): pl.pallas_call(sort_kernel, in_specs=[pl.BlockSpec(memory_space=pltpu.SME...  4.46 us
    pallas_call x6, Pallas kernels, effect_call(): pl.pallas_call(functools.partial(effect_kernel, sources, places), in_spec...  2.53 us
    ppermute x8, waiting for transfers between devices, core_swap(): return lax.ppermute(value, axes_all, pairs)  1.59 us
    unnamed x13, local copies, waits for them, and re-layouts  1.57 us
    ppermute x9, waiting for transfers between devices, shifted(): return lax.ppermute(value, axes_all, pairs)  1.22 us
  transfers between devices with their start and end apart: 17, of which 3 were waited for; matrix products, arithmetic and copies ran while one was open for 2% of the time, Pallas kernels for 19%

profile of v11, /device:TPU:1, one launch (start us, length us, event | category | flops | bytes accessed | tf_op | source)
XLA Modules:
  0.0 45.9 jit_solution(7759929228147642791)
XLA Ops:
  0.0 4.4 %collective-permute-start.2 = (bf16[128,128]{1,0:T(8,128)(2,1)}, bf16[128,128]{1,0:T(8,128)(2,1)S(1)}, u32[]{:S(2)}, u32[]{:S(2)}) collective-permute-start(bf16[128,128]{1,0:T(8,128)(2,1)} %bitcast.18), channel_id=1, source_target_pairs={{0,4},{1,5},{2,6},{3,7},{4,0},{5,1},{6,2},{7,3},{8,12},{9,13},{10,... | collective-permute-start | bytes 98312 | tf_op jit(solution)/shard_map/ppermute | solution.py:46
  4.4 3.2 %collective-permute-start.1 = (bf16[128,128]{1,0:T(8,128)(2,1)}, bf16[128,128]{1,0:T(8,128)(2,1)S(1)}, u32[]{:S(2)}, u32[]{:S(2)}) collective-permute-start(bf16[128,128]{1,0:T(8,128)(2,1)} %bitcast.19), channel_id=1, source_target_pairs={{0,66},{1,19},{2,68},{3,21},{4,70},{5,23},{6,64},{7,17},{8,74},{9,... | collective-permute-start | bytes 98312 | tf_op jit(solution)/shard_map/ppermute | solution.py:46
  7.6 1.9 %collective-permute-start = (bf16[128,128]{1,0:T(8,128)(2,1)}, bf16[128,128]{1,0:T(8,128)(2,1)S(1)}, u32[]{:S(2)}, u32[]{:S(2)}) collective-permute-start(bf16[128,128]{1,0:T(8,128)(2,1)} %bitcast.20), channel_id=1, source_target_pairs={{0,70},{1,23},{2,64},{3,17},{4,66},{5,19},{6,68},{7,21},{8,78},{9,... | collective-permute-start | bytes 98312 | tf_op jit(solution)/shard_map/ppermute | solution.py:46
  9.5 0.8 %constant_dynamic-update-slice_fusion.5 = bf16[528,128]{1,0:T(8,128)(2,1)S(1)} fusion(bf16[1,128,128]{2,1,0:T(8,128)(2,1)} %param.9), kind=kLoop, calls=%fused_computation.6 | loop fusion | bytes 65536
  10.3 0.7 %copy-done.3 = s32[1,4096,1]{1,2,0:T(1,128)S(1)} copy-done((s32[1,4096,1]{1,2,0:T(1,128)S(1)}, s32[1,4096,1]{1,2,0:T(1,128)}, u32[]{:S(2)}) %copy-start.3) | copy-done | bytes 16408
  11.0 0.8 %shard_map.55 = s32[1,4096]{1,0:T(1,128)S(1)} custom-call(s32[1,4096]{1,0:T(1,128)S(1)} %bitcast.17), custom_call_target="tpu_custom_call" | custom-call | flops 402653184 | bytes 100000 | tf_op jit(solution)/shard_map/pallas_call | solution.py:105
  11.8 1.2 %collective-permute-done = bf16[128,128]{1,0:T(8,128)(2,1)S(1)} collective-permute-done((bf16[128,128]{1,0:T(8,128)(2,1)}, bf16[128,128]{1,0:T(8,128)(2,1)S(1)}, u32[]{:S(2)}, u32[]{:S(2)}) %collective-permute-start) | collective-permute-done | bytes 32800 | tf_op jit(solution)/shard_map/ppermute | solution.py:46
  13.1 3.0 %collective-permute-start.5 = (bf16[528,128]{1,0:T(8,128)(2,1)S(1)}, bf16[528,128]{1,0:T(8,128)(2,1)S(1)}, u32[]{:S(2)}, u32[]{:S(2)}) collective-permute-start(bf16[528,128]{1,0:T(8,128)(2,1)S(1)} %constant_dynamic-update-slice_fusion), channel_id=1, source_target_pairs={{0,16},{1,65},{2,18},{3,67},{4,20},{5,69},{6,22},{7,71},{8,24},{9,... | collective-permute-start | bytes 405512 | tf_op jit(solution)/shard_map/ppermute | solution.py:46
  16.1 0.7 %collective-permute-start.4 = (bf16[528,128]{1,0:T(8,128)(2,1)S(1)}, bf16[528,128]{1,0:T(8,128)(2,1)S(1)}, u32[]{:S(2)}, u32[]{:S(2)}) collective-permute-start(bf16[528,128]{1,0:T(8,128)(2,1)S(1)} %constant_dynamic-update-slice_fusion), channel_id=1, source_target_pairs={{0,8},{1,33},{2,10},{3,35},{4,12},{5,37},{6,14},{7,39},{8,16},{9,4... | collective-permute-start | bytes 405512 | tf_op jit(solution)/shard_map/ppermute | solution.py:46
  16.8 2.0 %collective-permute-start.3 = (bf16[528,128]{1,0:T(8,128)(2,1)S(1)}, bf16[528,128]{1,0:T(8,128)(2,1)S(1)}, u32[]{:S(2)}, u32[]{:S(2)}) collective-permute-start(bf16[528,128]{1,0:T(8,128)(2,1)S(1)} %constant_dynamic-update-slice_fusion), channel_id=1, source_target_pairs={{0,24},{1,97},{2,26},{3,99},{4,28},{5,101},{6,30},{7,103},{8,0},{9... | collective-permute-start | bytes 405512 | tf_op jit(solution)/shard_map/ppermute | solution.py:46
  18.8 4.5 %shard_map.56 = (bf16[3072,128]{1,0:T(8,128)(2,1)S(1)}, bf16[768,128]{1,0:T(8,128)(2,1)S(1)}, bf16[768,128]{1,0:T(8,128)(2,1)S(1)}, bf16[768,128]{1,0:T(8,128)(2,1)S(1)}, bf16[768,128]{1,0:T(8,128)(2,1)S(1)}) custom-call(s32[4096]{0:T(1024)S(1)} %bitcast.15, bf16[4096,128]{1,0:T(8,128)(2,1)S(1)} %bitcast.11), custom_call_target="tpu_custom_call" | custom-call | bytes 20000000 | tf_op jit(solution)/shard_map/pallas_call | solution.py:130
  23.3 3.2 %collective-permute-start.14 = (bf16[2112,128]{1,0:T(8,128)(2,1)S(1)}, bf16[2112,128]{1,0:T(8,128)(2,1)S(1)}, u32[]{:S(2)}, u32[]{:S(2)}) collective-permute-start(bf16[2112,128]{1,0:T(8,128)(2,1)S(1)} %pad_maximum_fusion.refs_0_.own_ref), channel_id=1, source_target_pairs={{0,2},{1,7},{2,4},{3,1},{4,6},{5,3},{6,0},{7,5},{8,10},{9,15},{10,... | collective-permute-start | bytes 1622024 | tf_op jit(solution)/shard_map/ppermute | solution.py:46
  26.6 0.6 %collective-permute-start.7 = (bf16[2112,128]{1,0:T(8,128)(2,1)S(1)}, bf16[2112,128]{1,0:T(8,128)(2,1)S(1)}, u32[]{:S(2)}, u32[]{:S(2)}) collective-permute-start(bf16[2112,128]{1,0:T(8,128)(2,1)S(1)} %pad_maximum_fusion.refs_0_.own_ref), channel_id=1, source_target_pairs={{0,32},{1,9},{2,34},{3,11},{4,36},{5,13},{6,38},{7,15},{8,40},{9,1... | collective-permute-start | bytes 1622024 | tf_op jit(solution)/shard_map/ppermute | solution.py:46
  27.1 2.1 %collective-permute-start.6 = (bf16[2112,128]{1,0:T(8,128)(2,1)S(1)}, bf16[2112,128]{1,0:T(8,128)(2,1)S(1)}, u32[]{:S(2)}, u32[]{:S(2)}) collective-permute-start(bf16[2112,128]{1,0:T(8,128)(2,1)S(1)} %pad_maximum_fusion.refs_0_.own_ref), channel_id=1, source_target_pairs={{0,96},{1,25},{2,98},{3,27},{4,100},{5,29},{6,102},{7,31},{8,104},... | collective-permute-start | bytes 1622024 | tf_op jit(solution)/shard_map/ppermute | solution.py:46
  29.2 0.7 %collective-permute-start.8 = (bf16[768,128]{1,0:T(8,128)(2,1)S(1)}, bf16[768,128]{1,0:T(8,128)(2,1)S(1)}, u32[]{:S(2)}, u32[]{:S(2)}) collective-permute-start(bf16[768,128]{1,0:T(8,128)(2,1)S(1)} %get-tuple-element.33), channel_id=1, source_target_pairs={{0,1},{1,0},{2,3},{3,2},{4,5},{5,4},{6,7},{7,6},{8,9},{9,8},{10,11... | collective-permute-start | bytes 589832 | tf_op jit(solution)/shard_map/ppermute | solution.py:55
  30.0 1.1 %collective-permute-done.8.refs_1_ = bf16[768,128]{1,0:T(8,128)(2,1)S(1)} collective-permute-done((bf16[768,128]{1,0:T(8,128)(2,1)S(1)}, bf16[768,128]{1,0:T(8,128)(2,1)S(1)}, u32[]{:S(2)}, u32[]{:S(2)}) %collective-permute-start.8) | collective-permute-done | bytes 196640 | tf_op jit(solution)/shard_map/ppermute | solution.py:55
  31.0 0.4 collective-permute-start.12
  31.7 0.7 %shard_map.58.base_ref = f32[4096,128]{1,0:T(8,128)S(1)} custom-call(bf16[4096,128]{1,0:T(8,128)(2,1)S(1)} %bitcast.12, f32[32,128]{1,0:T(8,128)S(1)} %bitcast.13, bf16[128,128]{1,0:T(8,128)(2,1)S(1)} %copy-done.1), custom_call_target="tpu_custom_call" | custom-call | flops 1000 | bytes 1000 | tf_op jit(solution)/shard_map/pallas_call | solution.py:198
  32.4 0.4 shard_map.57.refs_4_
  33.5 4.3 %collective-permute-start.16 = (bf16[768,128]{1,0:T(8,128)(2,1)S(1)}, bf16[768,128]{1,0:T(8,128)(2,1)S(1)}, u32[]{:S(2)}, u32[]{:S(2)}) collective-permute-start(bf16[768,128]{1,0:T(8,128)(2,1)S(1)} %shard_map.63), channel_id=1, source_target_pairs={{0,1},{1,0},{2,3},{3,2},{4,5},{5,4},{6,7},{7,6},{8,9},{9,8},{10,11... | collective-permute-start | bytes 589832 | tf_op jit(solution)/shard_map/ppermute | solution.py:55
  38.3 0.5 %collective-permute-start.13 = (bf16[768,128]{1,0:T(8,128)(2,1)S(1)}, bf16[768,128]{1,0:T(8,128)(2,1)S(1)}, u32[]{:S(2)}, u32[]{:S(2)}) collective-permute-start(bf16[768,128]{1,0:T(8,128)(2,1)S(1)} %shard_map.62), channel_id=1, source_target_pairs={{0,1},{1,0},{2,3},{3,2},{4,5},{5,4},{6,7},{7,6},{8,9},{9,8},{10,11... | collective-permute-start | bytes 589832 | tf_op jit(solution)/shard_map/ppermute | solution.py:55
  39.4 0.7 %shard_map.64._ = f32[6144,128]{1,0:T(8,128)S(1)} custom-call(bf16[2112,128]{1,0:T(8,128)(2,1)S(1)} %collective-permute-done.14.refs_0_, bf16[2112,128]{1,0:T(8,128)(2,1)S(1)} %collective-permute-done.7.before_ref.refs_0_.refs_1_, bf16[2112,128]{1,0:T(8,128)(2,1)S(1)} %collective-permute-done.6.after_ref.refs_0_.refs_2_, ...), custom_call_target="tpu_custom_call", output_to_operand_aliasing={{}: (4, {})} | custom-call | flops 1000 | bytes 1000 | tf_op jit(solution)/shard_map/pallas_call | solution.py:229
  40.2 0.5 %collective-permute-done.11.plus_ref = bf16[768,128]{1,0:T(8,128)(2,1)S(1)} collective-permute-done((bf16[768,128]{1,0:T(8,128)(2,1)S(1)}, bf16[768,128]{1,0:T(8,128)(2,1)S(1)}, u32[]{:S(2)}, u32[]{:S(2)}) %collective-permute-start.11) | collective-permute-done | bytes 196640 | tf_op jit(solution)/shard_map/ppermute | solution.py:55
  40.7 5.2 %shard_map.65 = (f32[4096,128]{1,0:T(8,128)}, f32[6144,128]{1,0:T(8,128)S(1)}) custom-call(s32[4096]{0:T(1024)S(1)} %bitcast.16, f32[4096,128]{1,0:T(8,128)S(1)} %shard_map.58.base_ref, f32[8,128]{1,0:T(8,128)S(1)} %shard_map.60.ends_ref, bf16[768,128]{1,0:T(8,128)(2,1)S(1)} %collective-permute-done.9.own_ref, ...), custom_call_target="tpu_custom_call", output_to_operand_aliasing={{1}: (7, {})} | custom-call | flops 524288 | bytes 10000000 | tf_op jit(solution)/shard_map/pallas_call | solution.py:291
  (36 shorter events, 2.2 us)
Async XLA Ops:
  0.0 13.1 %copy-start = (bf16[1,4096,128]{2,1,0:T(8,128)(2,1)S(1)}, bf16[1,4096,128]{2,1,0:T(8,128)(2,1)}, u32[]{:S(2)}) copy-start(bf16[1,4096,128]{2,1,0:T(8,128)(2,1)} %param.5) | copy-start | bytes 3145732
  0.0 13.0 %collective-permute-start.2 = (bf16[128,128]{1,0:T(8,128)(2,1)}, bf16[128,128]{1,0:T(8,128)(2,1)S(1)}, u32[]{:S(2)}, u32[]{:S(2)}) collective-permute-start(bf16[128,128]{1,0:T(8,128)(2,1)} %bitcast.18), channel_id=1, source_target_pairs={{0,4},{1,5},{2,6},{3,7},{4,0},{5,1},{6,2},{7,3},{8,12},{9,13},{10,... | collective-permute-start | bytes 98312 | tf_op jit(solution)/shard_map/ppermute | solution.py:46
  4.4 8.6 %collective-permute-start.1 = (bf16[128,128]{1,0:T(8,128)(2,1)}, bf16[128,128]{1,0:T(8,128)(2,1)S(1)}, u32[]{:S(2)}, u32[]{:S(2)}) collective-permute-start(bf16[128,128]{1,0:T(8,128)(2,1)} %bitcast.19), channel_id=1, source_target_pairs={{0,66},{1,19},{2,68},{3,21},{4,70},{5,23},{6,64},{7,17},{8,74},{9,... | collective-permute-start | bytes 98312 | tf_op jit(solution)/shard_map/ppermute | solution.py:46
  7.6 5.4 %collective-permute-start = (bf16[128,128]{1,0:T(8,128)(2,1)}, bf16[128,128]{1,0:T(8,128)(2,1)S(1)}, u32[]{:S(2)}, u32[]{:S(2)}) collective-permute-start(bf16[128,128]{1,0:T(8,128)(2,1)} %bitcast.20), channel_id=1, source_target_pairs={{0,70},{1,23},{2,64},{3,17},{4,66},{5,19},{6,68},{7,21},{8,78},{9,... | collective-permute-start | bytes 98312 | tf_op jit(solution)/shard_map/ppermute | solution.py:46
  10.3 0.7 %copy-start.3 = (s32[1,4096,1]{1,2,0:T(1,128)S(1)}, s32[1,4096,1]{1,2,0:T(1,128)}, u32[]{:S(2)}) copy-start(s32[1,4096,1]{1,2,0:T(1,128)} %param.7) | copy-start | bytes 49156
  13.1 18.6 %copy-start.1 = (bf16[128,128]{1,0:T(8,128)(2,1)S(1)}, bf16[128,128]{1,0:T(8,128)(2,1)}, u32[]{:S(2)}) copy-start(bf16[128,128]{1,0:T(8,128)(2,1)} %plane_ref.3) | copy-start | bytes 98308
  13.1 18.6 %copy-start.2 = (f32[1,4096]{1,0:T(1,128)S(1)}, f32[1,4096]{1,0:T(1,128)}, u32[]{:S(2)}) copy-start(f32[1,4096]{1,0:T(1,128)} %param.6) | copy-start | bytes 49156
  13.1 10.1 %collective-permute-start.5 = (bf16[528,128]{1,0:T(8,128)(2,1)S(1)}, bf16[528,128]{1,0:T(8,128)(2,1)S(1)}, u32[]{:S(2)}, u32[]{:S(2)}) collective-permute-start(bf16[528,128]{1,0:T(8,128)(2,1)S(1)} %constant_dynamic-update-slice_fusion), channel_id=1, source_target_pairs={{0,16},{1,65},{2,18},{3,67},{4,20},{5,69},{6,22},{7,71},{8,24},{9,... | collective-permute-start | bytes 405512 | tf_op jit(solution)/shard_map/ppermute | solution.py:46
  16.1 7.2 %collective-permute-start.4 = (bf16[528,128]{1,0:T(8,128)(2,1)S(1)}, bf16[528,128]{1,0:T(8,128)(2,1)S(1)}, u32[]{:S(2)}, u32[]{:S(2)}) collective-permute-start(bf16[528,128]{1,0:T(8,128)(2,1)S(1)} %constant_dynamic-update-slice_fusion), channel_id=1, source_target_pairs={{0,8},{1,33},{2,10},{3,35},{4,12},{5,37},{6,14},{7,39},{8,16},{9,4... | collective-permute-start | bytes 405512 | tf_op jit(solution)/shard_map/ppermute | solution.py:46
  16.8 6.5 %collective-permute-start.3 = (bf16[528,128]{1,0:T(8,128)(2,1)S(1)}, bf16[528,128]{1,0:T(8,128)(2,1)S(1)}, u32[]{:S(2)}, u32[]{:S(2)}) collective-permute-start(bf16[528,128]{1,0:T(8,128)(2,1)S(1)} %constant_dynamic-update-slice_fusion), channel_id=1, source_target_pairs={{0,24},{1,97},{2,26},{3,99},{4,28},{5,101},{6,30},{7,103},{8,0},{9... | collective-permute-start | bytes 405512 | tf_op jit(solution)/shard_map/ppermute | solution.py:46
  23.3 9.8 %collective-permute-start.14 = (bf16[2112,128]{1,0:T(8,128)(2,1)S(1)}, bf16[2112,128]{1,0:T(8,128)(2,1)S(1)}, u32[]{:S(2)}, u32[]{:S(2)}) collective-permute-start(bf16[2112,128]{1,0:T(8,128)(2,1)S(1)} %pad_maximum_fusion.refs_0_.own_ref), channel_id=1, source_target_pairs={{0,2},{1,7},{2,4},{3,1},{4,6},{5,3},{6,0},{7,5},{8,10},{9,15},{10,... | collective-permute-start | bytes 1622024 | tf_op jit(solution)/shard_map/ppermute | solution.py:46
  26.6 11.3 %collective-permute-start.7 = (bf16[2112,128]{1,0:T(8,128)(2,1)S(1)}, bf16[2112,128]{1,0:T(8,128)(2,1)S(1)}, u32[]{:S(2)}, u32[]{:S(2)}) collective-permute-start(bf16[2112,128]{1,0:T(8,128)(2,1)S(1)} %pad_maximum_fusion.refs_0_.own_ref), channel_id=1, source_target_pairs={{0,32},{1,9},{2,34},{3,11},{4,36},{5,13},{6,38},{7,15},{8,40},{9,1... | collective-permute-start | bytes 1622024 | tf_op jit(solution)/shard_map/ppermute | solution.py:46
  27.1 10.7 %collective-permute-start.6 = (bf16[2112,128]{1,0:T(8,128)(2,1)S(1)}, bf16[2112,128]{1,0:T(8,128)(2,1)S(1)}, u32[]{:S(2)}, u32[]{:S(2)}) collective-permute-start(bf16[2112,128]{1,0:T(8,128)(2,1)S(1)} %pad_maximum_fusion.refs_0_.own_ref), channel_id=1, source_target_pairs={{0,96},{1,25},{2,98},{3,27},{4,100},{5,29},{6,102},{7,31},{8,104},... | collective-permute-start | bytes 1622024 | tf_op jit(solution)/shard_map/ppermute | solution.py:46
  29.2 1.8 %collective-permute-start.8 = (bf16[768,128]{1,0:T(8,128)(2,1)S(1)}, bf16[768,128]{1,0:T(8,128)(2,1)S(1)}, u32[]{:S(2)}, u32[]{:S(2)}) collective-permute-start(bf16[768,128]{1,0:T(8,128)(2,1)S(1)} %get-tuple-element.33), channel_id=1, source_target_pairs={{0,1},{1,0},{2,3},{3,2},{4,5},{5,4},{6,7},{7,6},{8,9},{9,8},{10,11... | collective-permute-start | bytes 589832 | tf_op jit(solution)/shard_map/ppermute | solution.py:55
  29.9 1.4 %collective-permute-start.15 = (bf16[768,128]{1,0:T(8,128)(2,1)S(1)}, bf16[768,128]{1,0:T(8,128)(2,1)S(1)}, u32[]{:S(2)}, u32[]{:S(2)}) collective-permute-start(bf16[768,128]{1,0:T(8,128)(2,1)S(1)} %get-tuple-element.40), channel_id=1, source_target_pairs={{0,1},{1,0},{2,3},{3,2},{4,5},{5,4},{6,7},{7,6},{8,9},{9,8},{10,11... | collective-permute-start | bytes 589832 | tf_op jit(solution)/shard_map/ppermute | solution.py:55
  31.0 6.9 %collective-permute-start.12 = (bf16[768,128]{1,0:T(8,128)(2,1)S(1)}, bf16[768,128]{1,0:T(8,128)(2,1)S(1)}, u32[]{:S(2)}, u32[]{:S(2)}) collective-permute-start(bf16[768,128]{1,0:T(8,128)(2,1)S(1)} %get-tuple-element.39), channel_id=1, source_target_pairs={{0,1},{1,0},{2,3},{3,2},{4,5},{5,4},{6,7},{7,6},{8,9},{9,8},{10,11... | collective-permute-start | bytes 589832 | tf_op jit(solution)/shard_map/ppermute | solution.py:55
  31.4 7.4 %collective-permute-start.10 = (bf16[768,128]{1,0:T(8,128)(2,1)S(1)}, bf16[768,128]{1,0:T(8,128)(2,1)S(1)}, u32[]{:S(2)}, u32[]{:S(2)}) collective-permute-start(bf16[768,128]{1,0:T(8,128)(2,1)S(1)} %get-tuple-element.38), channel_id=1, source_target_pairs={{0,1},{1,0},{2,3},{3,2},{4,5},{5,4},{6,7},{7,6},{8,9},{9,8},{10,11... | collective-permute-start | bytes 589832 | tf_op jit(solution)/shard_map/ppermute | solution.py:55
  33.5 6.7 %collective-permute-start.16 = (bf16[768,128]{1,0:T(8,128)(2,1)S(1)}, bf16[768,128]{1,0:T(8,128)(2,1)S(1)}, u32[]{:S(2)}, u32[]{:S(2)}) collective-permute-start(bf16[768,128]{1,0:T(8,128)(2,1)S(1)} %shard_map.63), channel_id=1, source_target_pairs={{0,1},{1,0},{2,3},{3,2},{4,5},{5,4},{6,7},{7,6},{8,9},{9,8},{10,11... | collective-permute-start | bytes 589832 | tf_op jit(solution)/shard_map/ppermute | solution.py:55
  37.8 2.3 %collective-permute-start.9 = (bf16[768,128]{1,0:T(8,128)(2,1)S(1)}, bf16[768,128]{1,0:T(8,128)(2,1)S(1)}, u32[]{:S(2)}, u32[]{:S(2)}) collective-permute-start(bf16[768,128]{1,0:T(8,128)(2,1)S(1)} %shard_map.59), channel_id=1, source_target_pairs={{0,1},{1,0},{2,3},{3,2},{4,5},{5,4},{6,7},{7,6},{8,9},{9,8},{10,11... | collective-permute-start | bytes 589832 | tf_op jit(solution)/shard_map/ppermute | solution.py:55
  38.3 1.9 %collective-permute-start.13 = (bf16[768,128]{1,0:T(8,128)(2,1)S(1)}, bf16[768,128]{1,0:T(8,128)(2,1)S(1)}, u32[]{:S(2)}, u32[]{:S(2)}) collective-permute-start(bf16[768,128]{1,0:T(8,128)(2,1)S(1)} %shard_map.62), channel_id=1, source_target_pairs={{0,1},{1,0},{2,3},{3,2},{4,5},{5,4},{6,7},{7,6},{8,9},{9,8},{10,11... | collective-permute-start | bytes 589832 | tf_op jit(solution)/shard_map/ppermute | solution.py:55
  39.2 1.5 %collective-permute-start.11 = (bf16[768,128]{1,0:T(8,128)(2,1)S(1)}, bf16[768,128]{1,0:T(8,128)(2,1)S(1)}, u32[]{:S(2)}, u32[]{:S(2)}) collective-permute-start(bf16[768,128]{1,0:T(8,128)(2,1)S(1)} %shard_map.61), channel_id=1, source_target_pairs={{0,1},{1,0},{2,3},{3,2},{4,5},{5,4},{6,7},{7,6},{8,9},{9,8},{10,11... | collective-permute-start | bytes 589832 | tf_op jit(solution)/shard_map/ppermute | solution.py:55

commit v12 on v9

--- a/solution.py
+++ b/solution.py
@@ -62,11 +62,11 @@
 
 
 def around(value, moves):
-    return [value] + [shifted(value, scaled(moves, step)) for step in (2, 1, -1)]
+    return [value] + [shifted(value, scaled(moves, step)) for step in (-1, 1, 2)]
 
 
 def offset(index):
-    return jnp.where(index == 1, 2, jnp.where(index == 2, 3, jnp.where(index == 3, 1, 0)))
+    return jnp.where(index == 1, 1, jnp.where(index == 2, 3, jnp.where(index == 3, 2, 0)))
 
 
 def slot_owners():
@@ -158,7 +158,7 @@
     choice = jnp.where(sub == 0, 3, jnp.where(x == 0, 1, inner))
     before = halo(choice, own_ref, before_ref, 2)
     choice = jnp.where(sub == 15, 3, jnp.where(x == 3, 1, inner))
-    after = halo(choice, own_ref, after_ref, 3)
+    after = halo(choice, own_ref, after_ref, 1)
     before = jnp.dot(before, plane, preferred_element_type=jnp.float32)[15:16]
     after = jnp.dot(after, plane, preferred_element_type=jnp.float32)[0:1]
     out_ref[0:1, :] = step_size * coupling_ref[0:1, 0:1] * before
@@ -322,9 +322,8 @@
     weights = coupling.reshape(rows // vals, vals)
     base = stencil(field, weights, in_plane)
     effect = effects(near_rows, [plane], (0,), None)
-    reply = replies([plane], [own_guest])
-    minus, plus, effect, base, reply = tied((minus, plus, effect, base, reply))
-    returned = [core_swap(reply)]
+    minus, plus, effect, base = tied((minus, plus, effect, base))
+    returned = [core_swap(replies([plane], [own_guest]))]
     returned.append(core_swap(replies([plus, minus], pair_guests)))
     returned.append(core_swap(replies([side], [side_guest])))
     effect = effects(near_rows, [side, plus, minus], (1, 2, 3), effect)

time: 47.7 us -> 47.6 us (level)
  waiting for transfers between devices: 5.58 us -> 3.66 us
  starting transfers between devices: 26.7 us -> 28.4 us
    ppermute x9, starting transfers between devices: 16.3 us -> 21.1 us  [shifted(): return lax.ppermute(value, axes_all, pairs)]
    ppermute x7, starting transfers between devices: 10.4 us -> 7.32 us  [core_swap(): return lax.ppermute(value, axes_all, pairs)]
    ppermute x7, waiting for transfers between devices: 1.3 us -> 0.28 us  [core_swap(): return lax.ppermute(value, axes_all, pairs)]
    ppermute x9, waiting for transfers between devices: 4.27 us -> 3.38 us  [shifted(): return lax.ppermute(value, axes_all, pairs)]
  transfers between devices with their start and end apart: 16 -> 16, of which waited for: 9 -> 3; matrix products, arithmetic and copies ran while one was open for 2% -> 2% of each run, Pallas kernels for 18% -> 18%
where the time goes in v12:
time: 47.6 us; the launch traced here: 47.3 us
  starting transfers between devices  28.4 us (60%)
  Pallas kernels  13.5 us (28%)
  waiting for transfers between devices  3.66 us (8%)
  local copies, waits for them, and re-layouts  1.57 us (3%)
    ppermute x9, starting transfers between devices, shifted(): return lax.ppermute(value, axes_all, pairs)  21.1 us
    ppermute x7, starting transfers between devices, core_swap(): return lax.ppermute(value, axes_all, pairs)  7.32 us
    pallas_call x1, Pallas kernels, finish(): pl.pallas_call(final_kernel, in_specs=[pl.BlockSpec(memory_space=pltpu.SM...  5.2 us
    pallas_call x1, Pallas kernels, sort_rows(): pl.pallas_call(sort_kernel, in_specs=[pl.BlockSpec(memory_space=pltpu.SME...  4.46 us
    ppermute x9, waiting for transfers between devices, shifted(): return lax.ppermute(value, axes_all, pairs)  3.38 us
    pallas_call x5, Pallas kernels, effect_call(): pl.pallas_call(functools.partial(effect_kernel, sources, places), in_spec...  2.31 us
    unnamed x13, local copies, waits for them, and re-layouts  1.57 us
  transfers between devices with their start and end apart: 16, of which 3 were waited for; matrix products, arithmetic and copies ran while one was open for 2% of the time, Pallas kernels for 18%

profile of v12, /device:TPU:1, one launch (start us, length us, event | category | flops | bytes accessed | tf_op | source)
XLA Modules:
  0.0 47.3 jit_solution(7697576791244160783)
XLA Ops:
  0.0 4.4 %collective-permute-start.2 = (bf16[128,128]{1,0:T(8,128)(2,1)}, bf16[128,128]{1,0:T(8,128)(2,1)S(1)}, u32[]{:S(2)}, u32[]{:S(2)}) collective-permute-start(bf16[128,128]{1,0:T(8,128)(2,1)} %bitcast.18), channel_id=1, source_target_pairs={{0,4},{1,5},{2,6},{3,7},{4,0},{5,1},{6,2},{7,3},{8,12},{9,13},{10,... | collective-permute-start | bytes 98312 | tf_op jit(solution)/shard_map/ppermute | solution.py:46
  4.4 3.2 %collective-permute-start.1 = (bf16[128,128]{1,0:T(8,128)(2,1)}, bf16[128,128]{1,0:T(8,128)(2,1)S(1)}, u32[]{:S(2)}, u32[]{:S(2)}) collective-permute-start(bf16[128,128]{1,0:T(8,128)(2,1)} %bitcast.19), channel_id=1, source_target_pairs={{0,66},{1,19},{2,68},{3,21},{4,70},{5,23},{6,64},{7,17},{8,74},{9,... | collective-permute-start | bytes 98312 | tf_op jit(solution)/shard_map/ppermute | solution.py:46
  7.6 1.9 %collective-permute-start = (bf16[128,128]{1,0:T(8,128)(2,1)}, bf16[128,128]{1,0:T(8,128)(2,1)S(1)}, u32[]{:S(2)}, u32[]{:S(2)}) collective-permute-start(bf16[128,128]{1,0:T(8,128)(2,1)} %bitcast.20), channel_id=1, source_target_pairs={{0,70},{1,23},{2,64},{3,17},{4,66},{5,19},{6,68},{7,21},{8,78},{9,... | collective-permute-start | bytes 98312 | tf_op jit(solution)/shard_map/ppermute | solution.py:46
  9.5 0.8 %constant_dynamic-update-slice_fusion.5 = bf16[528,128]{1,0:T(8,128)(2,1)S(1)} fusion(bf16[1,128,128]{2,1,0:T(8,128)(2,1)} %param.9), kind=kLoop, calls=%fused_computation.6 | loop fusion | bytes 65536
  10.3 0.7 %copy-done.3 = s32[1,4096,1]{1,2,0:T(1,128)S(1)} copy-done((s32[1,4096,1]{1,2,0:T(1,128)S(1)}, s32[1,4096,1]{1,2,0:T(1,128)}, u32[]{:S(2)}) %copy-start.3) | copy-done | bytes 16408
  11.0 0.8 %shard_map.55 = s32[1,4096]{1,0:T(1,128)S(1)} custom-call(s32[1,4096]{1,0:T(1,128)S(1)} %bitcast.17), custom_call_target="tpu_custom_call" | custom-call | flops 402653184 | bytes 100000 | tf_op jit(solution)/shard_map/pallas_call | solution.py:105
  11.8 1.2 %collective-permute-done = bf16[128,128]{1,0:T(8,128)(2,1)S(1)} collective-permute-done((bf16[128,128]{1,0:T(8,128)(2,1)}, bf16[128,128]{1,0:T(8,128)(2,1)S(1)}, u32[]{:S(2)}, u32[]{:S(2)}) %collective-permute-start) | collective-permute-done | bytes 32800 | tf_op jit(solution)/shard_map/ppermute | solution.py:46
  13.1 3.0 %collective-permute-start.5 = (bf16[528,128]{1,0:T(8,128)(2,1)S(1)}, bf16[528,128]{1,0:T(8,128)(2,1)S(1)}, u32[]{:S(2)}, u32[]{:S(2)}) collective-permute-start(bf16[528,128]{1,0:T(8,128)(2,1)S(1)} %constant_dynamic-update-slice_fusion), channel_id=1, source_target_pairs={{0,16},{1,65},{2,18},{3,67},{4,20},{5,69},{6,22},{7,71},{8,24},{9,... | collective-permute-start | bytes 405512 | tf_op jit(solution)/shard_map/ppermute | solution.py:46
  16.1 0.7 %collective-permute-start.4 = (bf16[528,128]{1,0:T(8,128)(2,1)S(1)}, bf16[528,128]{1,0:T(8,128)(2,1)S(1)}, u32[]{:S(2)}, u32[]{:S(2)}) collective-permute-start(bf16[528,128]{1,0:T(8,128)(2,1)S(1)} %constant_dynamic-update-slice_fusion), channel_id=1, source_target_pairs={{0,8},{1,33},{2,10},{3,35},{4,12},{5,37},{6,14},{7,39},{8,16},{9,4... | collective-permute-start | bytes 405512 | tf_op jit(solution)/shard_map/ppermute | solution.py:46
  16.8 2.0 %collective-permute-start.3 = (bf16[528,128]{1,0:T(8,128)(2,1)S(1)}, bf16[528,128]{1,0:T(8,128)(2,1)S(1)}, u32[]{:S(2)}, u32[]{:S(2)}) collective-permute-start(bf16[528,128]{1,0:T(8,128)(2,1)S(1)} %constant_dynamic-update-slice_fusion), channel_id=1, source_target_pairs={{0,24},{1,97},{2,26},{3,99},{4,28},{5,101},{6,30},{7,103},{8,0},{9... | collective-permute-start | bytes 405512 | tf_op jit(solution)/shard_map/ppermute | solution.py:46
  18.8 4.5 %shard_map.56 = (bf16[3072,128]{1,0:T(8,128)(2,1)S(1)}, bf16[768,128]{1,0:T(8,128)(2,1)S(1)}, bf16[768,128]{1,0:T(8,128)(2,1)S(1)}, bf16[768,128]{1,0:T(8,128)(2,1)S(1)}, bf16[768,128]{1,0:T(8,128)(2,1)S(1)}) custom-call(s32[4096]{0:T(1024)S(1)} %bitcast.15, bf16[4096,128]{1,0:T(8,128)(2,1)S(1)} %bitcast.11), custom_call_target="tpu_custom_call" | custom-call | bytes 20000000 | tf_op jit(solution)/shard_map/pallas_call | solution.py:130
  23.3 0.7 %collective-permute-start.7 = (bf16[2112,128]{1,0:T(8,128)(2,1)S(1)}, bf16[2112,128]{1,0:T(8,128)(2,1)S(1)}, u32[]{:S(2)}, u32[]{:S(2)}) collective-permute-start(bf16[2112,128]{1,0:T(8,128)(2,1)S(1)} %pad_maximum_fusion.refs_0_.own_ref), channel_id=1, source_target_pairs={{0,32},{1,9},{2,34},{3,11},{4,36},{5,13},{6,38},{7,15},{8,40},{9,1... | collective-permute-start | bytes 1622024 | tf_op jit(solution)/shard_map/ppermute | solution.py:46
  24.0 2.1 %collective-permute-start.6 = (bf16[2112,128]{1,0:T(8,128)(2,1)S(1)}, bf16[2112,128]{1,0:T(8,128)(2,1)S(1)}, u32[]{:S(2)}, u32[]{:S(2)}) collective-permute-start(bf16[2112,128]{1,0:T(8,128)(2,1)S(1)} %pad_maximum_fusion.refs_0_.own_ref), channel_id=1, source_target_pairs={{0,96},{1,25},{2,98},{3,27},{4,100},{5,29},{6,102},{7,31},{8,104},... | collective-permute-start | bytes 1622024 | tf_op jit(solution)/shard_map/ppermute | solution.py:46
  26.1 3.1 %collective-permute-start.13 = (bf16[2112,128]{1,0:T(8,128)(2,1)S(1)}, bf16[2112,128]{1,0:T(8,128)(2,1)S(1)}, u32[]{:S(2)}, u32[]{:S(2)}) collective-permute-start(bf16[2112,128]{1,0:T(8,128)(2,1)S(1)} %pad_maximum_fusion.refs_0_.own_ref), channel_id=1, source_target_pairs={{0,2},{1,7},{2,4},{3,1},{4,6},{5,3},{6,0},{7,5},{8,10},{9,15},{10,... | collective-permute-start | bytes 1622024 | tf_op jit(solution)/shard_map/ppermute | solution.py:46
  29.2 0.6 %collective-permute-start.10 = (bf16[768,128]{1,0:T(8,128)(2,1)S(1)}, bf16[768,128]{1,0:T(8,128)(2,1)S(1)}, u32[]{:S(2)}, u32[]{:S(2)}) collective-permute-start(bf16[768,128]{1,0:T(8,128)(2,1)S(1)} %get-tuple-element.36), channel_id=1, source_target_pairs={{0,1},{1,0},{2,3},{3,2},{4,5},{5,4},{6,7},{7,6},{8,9},{9,8},{10,11... | collective-permute-start | bytes 589832 | tf_op jit(solution)/shard_map/ppermute | solution.py:55
  29.9 0.7 %shard_map.58.base_ref = f32[4096,128]{1,0:T(8,128)S(1)} custom-call(bf16[4096,128]{1,0:T(8,128)(2,1)S(1)} %bitcast.12, f32[32,128]{1,0:T(8,128)S(1)} %bitcast.13, bf16[128,128]{1,0:T(8,128)(2,1)S(1)} %copy-done.1), custom_call_target="tpu_custom_call" | custom-call | flops 1000 | bytes 1000 | tf_op jit(solution)/shard_map/pallas_call | solution.py:198
  31.0 2.2 %collective-permute-done.7.before_ref.refs_0_.refs_1_ = bf16[2112,128]{1,0:T(8,128)(2,1)S(1)} collective-permute-done((bf16[2112,128]{1,0:T(8,128)(2,1)S(1)}, bf16[2112,128]{1,0:T(8,128)(2,1)S(1)}, u32[]{:S(2)}, u32[]{:S(2)}) %collective-permute-start.7) | collective-permute-done | bytes 540704 | tf_op jit(solution)/shard_map/ppermute | solution.py:46
  33.1 4.1 %collective-permute-start.8 = (bf16[768,128]{1,0:T(8,128)(2,1)S(1)}, bf16[768,128]{1,0:T(8,128)(2,1)S(1)}, u32[]{:S(2)}, u32[]{:S(2)}) collective-permute-start(bf16[768,128]{1,0:T(8,128)(2,1)S(1)} %get-tuple-element.35), channel_id=1, source_target_pairs={{0,1},{1,0},{2,3},{3,2},{4,5},{5,4},{6,7},{7,6},{8,9},{9,8},{10,11... | collective-permute-start | bytes 589832 | tf_op jit(solution)/shard_map/ppermute | solution.py:55
  37.2 0.5 %shard_map.61 = bf16[1536,128]{1,0:T(8,128)(2,1)S(1)} custom-call(bf16[2112,128]{1,0:T(8,128)(2,1)S(1)} %collective-permute-done.7.before_ref.refs_0_.refs_1_, bf16[2112,128]{1,0:T(8,128)(2,1)S(1)} %collective-permute-done.6.after_ref.refs_1_.refs_2_, bf16[768,128]{1,0:T(8,128)(2,1)S(1)} %collective-permute-done.10.refs_2_, ...), custom_call_target="tpu_custom_call" | custom-call | flops 1000 | bytes 1000 | tf_op jit(solution)/shard_map/pallas_call | solution.py:229
  37.7 0.6 %collective-permute-start.12 = (bf16[1536,128]{1,0:T(8,128)(2,1)S(1)}, bf16[1536,128]{1,0:T(8,128)(2,1)S(1)}, u32[]{:S(2)}, u32[]{:S(2)}) collective-permute-start(bf16[1536,128]{1,0:T(8,128)(2,1)S(1)} %shard_map.61), channel_id=1, source_target_pairs={{0,1},{1,0},{2,3},{3,2},{4,5},{5,4},{6,7},{7,6},{8,9},{9,8},{10,11... | collective-permute-start | bytes 1179656 | tf_op jit(solution)/shard_map/ppermute | solution.py:55
  38.7 0.4 collective-permute-start.9
  39.5 1.6 %collective-permute-start.15 = (bf16[768,128]{1,0:T(8,128)(2,1)S(1)}, bf16[768,128]{1,0:T(8,128)(2,1)S(1)}, u32[]{:S(2)}, u32[]{:S(2)}) collective-permute-start(bf16[768,128]{1,0:T(8,128)(2,1)S(1)} %shard_map.62), channel_id=1, source_target_pairs={{0,1},{1,0},{2,3},{3,2},{4,5},{5,4},{6,7},{7,6},{8,9},{9,8},{10,11... | collective-permute-start | bytes 589832 | tf_op jit(solution)/shard_map/ppermute | solution.py:55
  41.1 0.7 %shard_map.63._ = f32[6144,128]{1,0:T(8,128)S(1)} custom-call(bf16[2112,128]{1,0:T(8,128)(2,1)S(1)} %collective-permute-done.13.refs_0_, bf16[2112,128]{1,0:T(8,128)(2,1)S(1)} %collective-permute-done.7.before_ref.refs_0_.refs_1_, bf16[2112,128]{1,0:T(8,128)(2,1)S(1)} %collective-permute-done.6.after_ref.refs_1_.refs_2_, ...), custom_call_target="tpu_custom_call", output_to_operand_aliasing={{}: (4, {})} | custom-call | flops 1000 | bytes 1000 | tf_op jit(solution)/shard_map/pallas_call | solution.py:229
  42.1 5.2 %shard_map.64 = (f32[4096,128]{1,0:T(8,128)}, f32[6144,128]{1,0:T(8,128)S(1)}) custom-call(s32[4096]{0:T(1024)S(1)} %bitcast.16, f32[4096,128]{1,0:T(8,128)S(1)} %shard_map.58.base_ref, f32[8,128]{1,0:T(8,128)S(1)} %shard_map.59.ends_ref, bf16[768,128]{1,0:T(8,128)(2,1)S(1)} %collective-permute-done.9.own_ref, ...), custom_call_target="tpu_custom_call", output_to_operand_aliasing={{1}: (6, {})} | custom-call | flops 524288 | bytes 10000000 | tf_op jit(solution)/shard_map/pallas_call | solution.py:291
  (33 shorter events, 1.6 us)
Async XLA Ops:
  0.0 13.1 %copy-start = (bf16[1,4096,128]{2,1,0:T(8,128)(2,1)S(1)}, bf16[1,4096,128]{2,1,0:T(8,128)(2,1)}, u32[]{:S(2)}) copy-start(bf16[1,4096,128]{2,1,0:T(8,128)(2,1)} %param.5) | copy-start | bytes 3145732
  0.0 13.0 %collective-permute-start.2 = (bf16[128,128]{1,0:T(8,128)(2,1)}, bf16[128,128]{1,0:T(8,128)(2,1)S(1)}, u32[]{:S(2)}, u32[]{:S(2)}) collective-permute-start(bf16[128,128]{1,0:T(8,128)(2,1)} %bitcast.18), channel_id=1, source_target_pairs={{0,4},{1,5},{2,6},{3,7},{4,0},{5,1},{6,2},{7,3},{8,12},{9,13},{10,... | collective-permute-start | bytes 98312 | tf_op jit(solution)/shard_map/ppermute | solution.py:46
  4.4 8.6 %collective-permute-start.1 = (bf16[128,128]{1,0:T(8,128)(2,1)}, bf16[128,128]{1,0:T(8,128)(2,1)S(1)}, u32[]{:S(2)}, u32[]{:S(2)}) collective-permute-start(bf16[128,128]{1,0:T(8,128)(2,1)} %bitcast.19), channel_id=1, source_target_pairs={{0,66},{1,19},{2,68},{3,21},{4,70},{5,23},{6,64},{7,17},{8,74},{9,... | collective-permute-start | bytes 98312 | tf_op jit(solution)/shard_map/ppermute | solution.py:46
  7.6 5.4 %collective-permute-start = (bf16[128,128]{1,0:T(8,128)(2,1)}, bf16[128,128]{1,0:T(8,128)(2,1)S(1)}, u32[]{:S(2)}, u32[]{:S(2)}) collective-permute-start(bf16[128,128]{1,0:T(8,128)(2,1)} %bitcast.20), channel_id=1, source_target_pairs={{0,70},{1,23},{2,64},{3,17},{4,66},{5,19},{6,68},{7,21},{8,78},{9,... | collective-permute-start | bytes 98312 | tf_op jit(solution)/shard_map/ppermute | solution.py:46
  10.3 0.7 %copy-start.3 = (s32[1,4096,1]{1,2,0:T(1,128)S(1)}, s32[1,4096,1]{1,2,0:T(1,128)}, u32[]{:S(2)}) copy-start(s32[1,4096,1]{1,2,0:T(1,128)} %param.7) | copy-start | bytes 49156
  13.1 16.8 %copy-start.1 = (bf16[128,128]{1,0:T(8,128)(2,1)S(1)}, bf16[128,128]{1,0:T(8,128)(2,1)}, u32[]{:S(2)}) copy-start(bf16[128,128]{1,0:T(8,128)(2,1)} %plane_ref.3) | copy-start | bytes 98308
  13.1 16.8 %copy-start.2 = (f32[1,4096]{1,0:T(1,128)S(1)}, f32[1,4096]{1,0:T(1,128)}, u32[]{:S(2)}) copy-start(f32[1,4096]{1,0:T(1,128)} %param.6) | copy-start | bytes 49156
  13.1 10.1 %collective-permute-start.5 = (bf16[528,128]{1,0:T(8,128)(2,1)S(1)}, bf16[528,128]{1,0:T(8,128)(2,1)S(1)}, u32[]{:S(2)}, u32[]{:S(2)}) collective-permute-start(bf16[528,128]{1,0:T(8,128)(2,1)S(1)} %constant_dynamic-update-slice_fusion), channel_id=1, source_target_pairs={{0,16},{1,65},{2,18},{3,67},{4,20},{5,69},{6,22},{7,71},{8,24},{9,... | collective-permute-start | bytes 405512 | tf_op jit(solution)/shard_map/ppermute | solution.py:46
  16.1 7.2 %collective-permute-start.4 = (bf16[528,128]{1,0:T(8,128)(2,1)S(1)}, bf16[528,128]{1,0:T(8,128)(2,1)S(1)}, u32[]{:S(2)}, u32[]{:S(2)}) collective-permute-start(bf16[528,128]{1,0:T(8,128)(2,1)S(1)} %constant_dynamic-update-slice_fusion), channel_id=1, source_target_pairs={{0,8},{1,33},{2,10},{3,35},{4,12},{5,37},{6,14},{7,39},{8,16},{9,4... | collective-permute-start | bytes 405512 | tf_op jit(solution)/shard_map/ppermute | solution.py:46
  16.8 6.5 %collective-permute-start.3 = (bf16[528,128]{1,0:T(8,128)(2,1)S(1)}, bf16[528,128]{1,0:T(8,128)(2,1)S(1)}, u32[]{:S(2)}, u32[]{:S(2)}) collective-permute-start(bf16[528,128]{1,0:T(8,128)(2,1)S(1)} %constant_dynamic-update-slice_fusion), channel_id=1, source_target_pairs={{0,24},{1,97},{2,26},{3,99},{4,28},{5,101},{6,30},{7,103},{8,0},{9... | collective-permute-start | bytes 405512 | tf_op jit(solution)/shard_map/ppermute | solution.py:46
  23.3 9.8 %collective-permute-start.7 = (bf16[2112,128]{1,0:T(8,128)(2,1)S(1)}, bf16[2112,128]{1,0:T(8,128)(2,1)S(1)}, u32[]{:S(2)}, u32[]{:S(2)}) collective-permute-start(bf16[2112,128]{1,0:T(8,128)(2,1)S(1)} %pad_maximum_fusion.refs_0_.own_ref), channel_id=1, source_target_pairs={{0,32},{1,9},{2,34},{3,11},{4,36},{5,13},{6,38},{7,15},{8,40},{9,1... | collective-permute-start | bytes 1622024 | tf_op jit(solution)/shard_map/ppermute | solution.py:46
  24.0 13.2 %collective-permute-start.6 = (bf16[2112,128]{1,0:T(8,128)(2,1)S(1)}, bf16[2112,128]{1,0:T(8,128)(2,1)S(1)}, u32[]{:S(2)}, u32[]{:S(2)}) collective-permute-start(bf16[2112,128]{1,0:T(8,128)(2,1)S(1)} %pad_maximum_fusion.refs_0_.own_ref), channel_id=1, source_target_pairs={{0,96},{1,25},{2,98},{3,27},{4,100},{5,29},{6,102},{7,31},{8,104},... | collective-permute-start | bytes 1622024 | tf_op jit(solution)/shard_map/ppermute | solution.py:46
  26.1 13.0 %collective-permute-start.13 = (bf16[2112,128]{1,0:T(8,128)(2,1)S(1)}, bf16[2112,128]{1,0:T(8,128)(2,1)S(1)}, u32[]{:S(2)}, u32[]{:S(2)}) collective-permute-start(bf16[2112,128]{1,0:T(8,128)(2,1)S(1)} %pad_maximum_fusion.refs_0_.own_ref), channel_id=1, source_target_pairs={{0,2},{1,7},{2,4},{3,1},{4,6},{5,3},{6,0},{7,5},{8,10},{9,15},{10,... | collective-permute-start | bytes 1622024 | tf_op jit(solution)/shard_map/ppermute | solution.py:46
  29.2 8.0 %collective-permute-start.10 = (bf16[768,128]{1,0:T(8,128)(2,1)S(1)}, bf16[768,128]{1,0:T(8,128)(2,1)S(1)}, u32[]{:S(2)}, u32[]{:S(2)}) collective-permute-start(bf16[768,128]{1,0:T(8,128)(2,1)S(1)} %get-tuple-element.36), channel_id=1, source_target_pairs={{0,1},{1,0},{2,3},{3,2},{4,5},{5,4},{6,7},{7,6},{8,9},{9,8},{10,11... | collective-permute-start | bytes 589832 | tf_op jit(solution)/shard_map/ppermute | solution.py:55
  29.9 7.3 %collective-permute-start.11 = (bf16[768,128]{1,0:T(8,128)(2,1)S(1)}, bf16[768,128]{1,0:T(8,128)(2,1)S(1)}, u32[]{:S(2)}, u32[]{:S(2)}) collective-permute-start(bf16[768,128]{1,0:T(8,128)(2,1)S(1)} %get-tuple-element.37), channel_id=1, source_target_pairs={{0,1},{1,0},{2,3},{3,2},{4,5},{5,4},{6,7},{7,6},{8,9},{9,8},{10,11... | collective-permute-start | bytes 589832 | tf_op jit(solution)/shard_map/ppermute | solution.py:55
  33.1 5.2 %collective-permute-start.8 = (bf16[768,128]{1,0:T(8,128)(2,1)S(1)}, bf16[768,128]{1,0:T(8,128)(2,1)S(1)}, u32[]{:S(2)}, u32[]{:S(2)}) collective-permute-start(bf16[768,128]{1,0:T(8,128)(2,1)S(1)} %get-tuple-element.35), channel_id=1, source_target_pairs={{0,1},{1,0},{2,3},{3,2},{4,5},{5,4},{6,7},{7,6},{8,9},{9,8},{10,11... | collective-permute-start | bytes 589832 | tf_op jit(solution)/shard_map/ppermute | solution.py:55
  37.2 1.9 %collective-permute-start.14 = (bf16[768,128]{1,0:T(8,128)(2,1)S(1)}, bf16[768,128]{1,0:T(8,128)(2,1)S(1)}, u32[]{:S(2)}, u32[]{:S(2)}) collective-permute-start(bf16[768,128]{1,0:T(8,128)(2,1)S(1)} %get-tuple-element.38), channel_id=1, source_target_pairs={{0,1},{1,0},{2,3},{3,2},{4,5},{5,4},{6,7},{7,6},{8,9},{9,8},{10,11... | collective-permute-start | bytes 589832 | tf_op jit(solution)/shard_map/ppermute | solution.py:55
  37.7 4.4 %collective-permute-start.12 = (bf16[1536,128]{1,0:T(8,128)(2,1)S(1)}, bf16[1536,128]{1,0:T(8,128)(2,1)S(1)}, u32[]{:S(2)}, u32[]{:S(2)}) collective-permute-start(bf16[1536,128]{1,0:T(8,128)(2,1)S(1)} %shard_map.61), channel_id=1, source_target_pairs={{0,1},{1,0},{2,3},{3,2},{4,5},{5,4},{6,7},{7,6},{8,9},{9,8},{10,11... | collective-permute-start | bytes 1179656 | tf_op jit(solution)/shard_map/ppermute | solution.py:55
  38.7 3.2 %collective-permute-start.9 = (bf16[768,128]{1,0:T(8,128)(2,1)S(1)}, bf16[768,128]{1,0:T(8,128)(2,1)S(1)}, u32[]{:S(2)}, u32[]{:S(2)}) collective-permute-start(bf16[768,128]{1,0:T(8,128)(2,1)S(1)} %shard_map.60), channel_id=1, source_target_pairs={{0,1},{1,0},{2,3},{3,2},{4,5},{5,4},{6,7},{7,6},{8,9},{9,8},{10,11... | collective-permute-start | bytes 589832 | tf_op jit(solution)/shard_map/ppermute | solution.py:55
  39.5 2.7 %collective-permute-start.15 = (bf16[768,128]{1,0:T(8,128)(2,1)S(1)}, bf16[768,128]{1,0:T(8,128)(2,1)S(1)}, u32[]{:S(2)}, u32[]{:S(2)}) collective-permute-start(bf16[768,128]{1,0:T(8,128)(2,1)S(1)} %shard_map.62), channel_id=1, source_target_pairs={{0,1},{1,0},{2,3},{3,2},{4,5},{5,4},{6,7},{7,6},{8,9},{9,8},{10,11... | collective-permute-start | bytes 589832 | tf_op jit(solution)/shard_map/ppermute | solution.py:55

commit v13 on v11

--- a/solution.py
+++ b/solution.py
@@ -257,11 +257,10 @@
 
 
 def final_kernel(
-    slot_ref, base_ref, ends_ref, own_ref, plus_ref, minus_ref, side_ref, _, out_ref, effect_ref, result, sent
+    slot_ref, base_ref, ends_ref, own_ref, trio_ref, _, out_ref, effect_ref, result, sent
 ):
-    for returned_ref, third in ((own_ref, 0), (plus_ref, 2), (minus_ref, 3), (side_ref, 1)):
-        lo = half + third * block
-        effect_ref[lo : lo + block, :] = returned_ref[...].astype(jnp.float32)
+    effect_ref[half : half + block, :] = own_ref[...].astype(jnp.float32)
+    effect_ref[half + block :, :] = trio_ref[...].astype(jnp.float32)
 
     copies = []
     for number, (top, end) in enumerate(zip(part_tops, part_tops[1:])):
@@ -323,11 +322,11 @@
     base = stencil(field, weights, in_plane)
     effect = effects(near_rows, [plane], (0,), None)
     reply = replies([plane], [own_guest])
-    minus, plus, effect, base, reply = tied((minus, plus, effect, base, reply))
+    effect, base, reply, guests = tied((effect, base, reply, [side_guest, *pair_guests]))
+    side_guest, *pair_guests = guests
+    minus, plus, side, effect, base, reply = tied((minus, plus, side, effect, base, reply))
     returned = [core_swap(reply)]
-    for part, guest in zip((plus, minus), pair_guests):
-        returned.append(core_swap(replies([part], [guest])))
-    returned.append(core_swap(replies([side], [side_guest])))
+    returned.append(core_swap(replies([side, plus, minus], [side_guest, *pair_guests])))
     effect = effects(near_rows, [side, plus, minus], (1, 2, 3), effect)
     ends = end_terms(plane, plus, minus, weights, in_plane)
     return finish(slot, base, ends, returned, effect)[None]

time: 46.1 us -> 45.7 us (level)
  starting transfers between devices: 27.6 us -> 23.7 us
  waiting for transfers between devices: 2.81 us -> 6.42 us
    ppermute x8 -> x6, starting transfers between devices: 6.49 us -> 2.68 us  [core_swap(): return lax.ppermute(value, axes_all, pairs)]
    ppermute x9, waiting for transfers between devices: 1.22 us -> 4.31 us  [shifted(): return lax.ppermute(value, axes_all, pairs)]
    ppermute x8 -> x6, waiting for transfers between devices: 1.59 us -> 2.11 us  [core_swap(): return lax.ppermute(value, axes_all, pairs)]
    pallas_call x6 -> x4, Pallas kernels: 2.53 us -> 2.09 us  [effect_call(): pl.pallas_call(functools.partial(effect_kernel, sources, places), in_spec...]
  transfers between devices with their start and end apart: 17 -> 15, of which waited for: 3 -> 4; matrix products, arithmetic and copies ran while one was open for 2% -> 2% of each run, Pallas kernels for 19% -> 16%
where the time goes in v13:
time: 45.7 us; the launch traced here: 45.2 us
  starting transfers between devices  23.7 us (52%)
  Pallas kernels  13.3 us (29%)
  waiting for transfers between devices  6.42 us (14%)
  local copies, waits for them, and re-layouts  1.57 us (3%)
    ppermute x9, starting transfers between devices, shifted(): return lax.ppermute(value, axes_all, pairs)  21.1 us
    pallas_call x1, Pallas kernels, finish(): pl.pallas_call(final_kernel, in_specs=[pl.BlockSpec(memory_space=pltpu.SM...  5.19 us
    pallas_call x1, Pallas kernels, sort_rows(): pl.pallas_call(sort_kernel, in_specs=[pl.BlockSpec(memory_space=pltpu.SME...  4.46 us
    ppermute x9, waiting for transfers between devices, shifted(): return lax.ppermute(value, axes_all, pairs)  4.31 us
    ppermute x6, starting transfers between devices, core_swap(): return lax.ppermute(value, axes_all, pairs)  2.68 us
    ppermute x6, waiting for transfers between devices, core_swap(): return lax.ppermute(value, axes_all, pairs)  2.11 us
    pallas_call x4, Pallas kernels, effect_call(): pl.pallas_call(functools.partial(effect_kernel, sources, places), in_spec...  2.09 us
    unnamed x13, local copies, waits for them, and re-layouts  1.57 us
  transfers between devices with their start and end apart: 15, of which 4 were waited for; matrix products, arithmetic and copies ran while one was open for 2% of the time, Pallas kernels for 16%

profile of v13, /device:TPU:1, one launch (start us, length us, event | category | flops | bytes accessed | tf_op | source)
XLA Modules:
  0.0 45.2 jit_solution(7719772547243705806)
XLA Ops:
  0.0 4.4 %collective-permute-start.2 = (bf16[128,128]{1,0:T(8,128)(2,1)}, bf16[128,128]{1,0:T(8,128)(2,1)S(1)}, u32[]{:S(2)}, u32[]{:S(2)}) collective-permute-start(bf16[128,128]{1,0:T(8,128)(2,1)} %bitcast.18), channel_id=1, source_target_pairs={{0,4},{1,5},{2,6},{3,7},{4,0},{5,1},{6,2},{7,3},{8,12},{9,13},{10,... | collective-permute-start | bytes 98312 | tf_op jit(solution)/shard_map/ppermute | solution.py:46
  4.4 3.2 %collective-permute-start.1 = (bf16[128,128]{1,0:T(8,128)(2,1)}, bf16[128,128]{1,0:T(8,128)(2,1)S(1)}, u32[]{:S(2)}, u32[]{:S(2)}) collective-permute-start(bf16[128,128]{1,0:T(8,128)(2,1)} %bitcast.19), channel_id=1, source_target_pairs={{0,66},{1,19},{2,68},{3,21},{4,70},{5,23},{6,64},{7,17},{8,74},{9,... | collective-permute-start | bytes 98312 | tf_op jit(solution)/shard_map/ppermute | solution.py:46
  7.6 1.9 %collective-permute-start = (bf16[128,128]{1,0:T(8,128)(2,1)}, bf16[128,128]{1,0:T(8,128)(2,1)S(1)}, u32[]{:S(2)}, u32[]{:S(2)}) collective-permute-start(bf16[128,128]{1,0:T(8,128)(2,1)} %bitcast.20), channel_id=1, source_target_pairs={{0,70},{1,23},{2,64},{3,17},{4,66},{5,19},{6,68},{7,21},{8,78},{9,... | collective-permute-start | bytes 98312 | tf_op jit(solution)/shard_map/ppermute | solution.py:46
  9.5 0.8 %constant_dynamic-update-slice_fusion.5 = bf16[528,128]{1,0:T(8,128)(2,1)S(1)} fusion(bf16[1,128,128]{2,1,0:T(8,128)(2,1)} %param.9), kind=kLoop, calls=%fused_computation.6 | loop fusion | bytes 65536
  10.3 0.7 %copy-done.3 = s32[1,4096,1]{1,2,0:T(1,128)S(1)} copy-done((s32[1,4096,1]{1,2,0:T(1,128)S(1)}, s32[1,4096,1]{1,2,0:T(1,128)}, u32[]{:S(2)}) %copy-start.3) | copy-done | bytes 16408
  11.0 0.8 %shard_map.55 = s32[1,4096]{1,0:T(1,128)S(1)} custom-call(s32[1,4096]{1,0:T(1,128)S(1)} %bitcast.17), custom_call_target="tpu_custom_call" | custom-call | flops 402653184 | bytes 100000 | tf_op jit(solution)/shard_map/pallas_call | solution.py:105
  11.8 1.2 %collective-permute-done = bf16[128,128]{1,0:T(8,128)(2,1)S(1)} collective-permute-done((bf16[128,128]{1,0:T(8,128)(2,1)}, bf16[128,128]{1,0:T(8,128)(2,1)S(1)}, u32[]{:S(2)}, u32[]{:S(2)}) %collective-permute-start) | collective-permute-done | bytes 32800 | tf_op jit(solution)/shard_map/ppermute | solution.py:46
  13.1 3.0 %collective-permute-start.5 = (bf16[528,128]{1,0:T(8,128)(2,1)S(1)}, bf16[528,128]{1,0:T(8,128)(2,1)S(1)}, u32[]{:S(2)}, u32[]{:S(2)}) collective-permute-start(bf16[528,128]{1,0:T(8,128)(2,1)S(1)} %constant_dynamic-update-slice_fusion), channel_id=1, source_target_pairs={{0,16},{1,65},{2,18},{3,67},{4,20},{5,69},{6,22},{7,71},{8,24},{9,... | collective-permute-start | bytes 405512 | tf_op jit(solution)/shard_map/ppermute | solution.py:46
  16.1 0.7 %collective-permute-start.4 = (bf16[528,128]{1,0:T(8,128)(2,1)S(1)}, bf16[528,128]{1,0:T(8,128)(2,1)S(1)}, u32[]{:S(2)}, u32[]{:S(2)}) collective-permute-start(bf16[528,128]{1,0:T(8,128)(2,1)S(1)} %constant_dynamic-update-slice_fusion), channel_id=1, source_target_pairs={{0,8},{1,33},{2,10},{3,35},{4,12},{5,37},{6,14},{7,39},{8,16},{9,4... | collective-permute-start | bytes 405512 | tf_op jit(solution)/shard_map/ppermute | solution.py:46
  16.8 2.0 %collective-permute-start.3 = (bf16[528,128]{1,0:T(8,128)(2,1)S(1)}, bf16[528,128]{1,0:T(8,128)(2,1)S(1)}, u32[]{:S(2)}, u32[]{:S(2)}) collective-permute-start(bf16[528,128]{1,0:T(8,128)(2,1)S(1)} %constant_dynamic-update-slice_fusion), channel_id=1, source_target_pairs={{0,24},{1,97},{2,26},{3,99},{4,28},{5,101},{6,30},{7,103},{8,0},{9... | collective-permute-start | bytes 405512 | tf_op jit(solution)/shard_map/ppermute | solution.py:46
  18.8 4.5 %shard_map.56 = (bf16[3072,128]{1,0:T(8,128)(2,1)S(1)}, bf16[768,128]{1,0:T(8,128)(2,1)S(1)}, bf16[768,128]{1,0:T(8,128)(2,1)S(1)}, bf16[768,128]{1,0:T(8,128)(2,1)S(1)}, bf16[768,128]{1,0:T(8,128)(2,1)S(1)}) custom-call(s32[4096]{0:T(1024)S(1)} %bitcast.15, bf16[4096,128]{1,0:T(8,128)(2,1)S(1)} %bitcast.11), custom_call_target="tpu_custom_call" | custom-call | bytes 20000000 | tf_op jit(solution)/shard_map/pallas_call | solution.py:130
  23.3 3.2 %collective-permute-start.8 = (bf16[2112,128]{1,0:T(8,128)(2,1)S(1)}, bf16[2112,128]{1,0:T(8,128)(2,1)S(1)}, u32[]{:S(2)}, u32[]{:S(2)}) collective-permute-start(bf16[2112,128]{1,0:T(8,128)(2,1)S(1)} %pad_maximum_fusion.refs_0_.own_ref), channel_id=1, source_target_pairs={{0,2},{1,7},{2,4},{3,1},{4,6},{5,3},{6,0},{7,5},{8,10},{9,15},{10,... | collective-permute-start | bytes 1622024 | tf_op jit(solution)/shard_map/ppermute | solution.py:46
  26.6 0.6 %collective-permute-start.7 = (bf16[2112,128]{1,0:T(8,128)(2,1)S(1)}, bf16[2112,128]{1,0:T(8,128)(2,1)S(1)}, u32[]{:S(2)}, u32[]{:S(2)}) collective-permute-start(bf16[2112,128]{1,0:T(8,128)(2,1)S(1)} %pad_maximum_fusion.refs_0_.own_ref), channel_id=1, source_target_pairs={{0,32},{1,9},{2,34},{3,11},{4,36},{5,13},{6,38},{7,15},{8,40},{9,1... | collective-permute-start | bytes 1622024 | tf_op jit(solution)/shard_map/ppermute | solution.py:46
  27.1 2.1 %collective-permute-start.6 = (bf16[2112,128]{1,0:T(8,128)(2,1)S(1)}, bf16[2112,128]{1,0:T(8,128)(2,1)S(1)}, u32[]{:S(2)}, u32[]{:S(2)}) collective-permute-start(bf16[2112,128]{1,0:T(8,128)(2,1)S(1)} %pad_maximum_fusion.refs_0_.own_ref), channel_id=1, source_target_pairs={{0,96},{1,25},{2,98},{3,27},{4,100},{5,29},{6,102},{7,31},{8,104},... | collective-permute-start | bytes 1622024 | tf_op jit(solution)/shard_map/ppermute | solution.py:46
  29.2 0.7 %collective-permute-start.9 = (bf16[768,128]{1,0:T(8,128)(2,1)S(1)}, bf16[768,128]{1,0:T(8,128)(2,1)S(1)}, u32[]{:S(2)}, u32[]{:S(2)}) collective-permute-start(bf16[768,128]{1,0:T(8,128)(2,1)S(1)} %get-tuple-element.40), channel_id=1, source_target_pairs={{0,1},{1,0},{2,3},{3,2},{4,5},{5,4},{6,7},{7,6},{8,9},{9,8},{10,11... | collective-permute-start | bytes 589832 | tf_op jit(solution)/shard_map/ppermute | solution.py:55
  30.0 1.1 %collective-permute-done.9.refs_1_ = bf16[768,128]{1,0:T(8,128)(2,1)S(1)} collective-permute-done((bf16[768,128]{1,0:T(8,128)(2,1)S(1)}, bf16[768,128]{1,0:T(8,128)(2,1)S(1)}, u32[]{:S(2)}, u32[]{:S(2)}) %collective-permute-start.9) | collective-permute-done | bytes 196640 | tf_op jit(solution)/shard_map/ppermute | solution.py:55
  31.7 0.7 %shard_map.58.base_ref = f32[4096,128]{1,0:T(8,128)S(1)} custom-call(bf16[4096,128]{1,0:T(8,128)(2,1)S(1)} %bitcast.12, f32[32,128]{1,0:T(8,128)S(1)} %bitcast.13, bf16[128,128]{1,0:T(8,128)(2,1)S(1)} %copy-done.1), custom_call_target="tpu_custom_call" | custom-call | flops 1000 | bytes 1000 | tf_op jit(solution)/shard_map/pallas_call | solution.py:198
  32.4 0.4 shard_map.57.refs_4_
  33.2 3.1 %collective-permute-done.7.before_ref.refs_1_ = bf16[2112,128]{1,0:T(8,128)(2,1)S(1)} collective-permute-done((bf16[2112,128]{1,0:T(8,128)(2,1)S(1)}, bf16[2112,128]{1,0:T(8,128)(2,1)S(1)}, u32[]{:S(2)}, u32[]{:S(2)}) %collective-permute-start.7) | collective-permute-done | bytes 540704 | tf_op jit(solution)/shard_map/ppermute | solution.py:46
  36.3 0.6 %shard_map.61 = bf16[2304,128]{1,0:T(8,128)(2,1)S(1)} custom-call(bf16[2112,128]{1,0:T(8,128)(2,1)S(1)} %collective-permute-done.8.refs_0_, bf16[2112,128]{1,0:T(8,128)(2,1)S(1)} %collective-permute-done.7.before_ref.refs_1_, bf16[2112,128]{1,0:T(8,128)(2,1)S(1)} %collective-permute-done.6.after_ref.refs_2_, ...), custom_call_target="tpu_custom_call" | custom-call | flops 1000 | bytes 1000 | tf_op jit(solution)/shard_map/pallas_call | solution.py:229
  36.9 1.2 %collective-permute-start.14 = (bf16[2304,128]{1,0:T(8,128)(2,1)S(1)}, bf16[2304,128]{1,0:T(8,128)(2,1)S(1)}, u32[]{:S(2)}, u32[]{:S(2)}) collective-permute-start(bf16[2304,128]{1,0:T(8,128)(2,1)S(1)} %shard_map.61), channel_id=1, source_target_pairs={{0,1},{1,0},{2,3},{3,2},{4,5},{5,4},{6,7},{7,6},{8,9},{9,8},{10,11... | collective-permute-start | bytes 1769480 | tf_op jit(solution)/shard_map/ppermute | solution.py:55
  38.3 0.7 %shard_map.62._ = f32[6144,128]{1,0:T(8,128)S(1)} custom-call(bf16[2112,128]{1,0:T(8,128)(2,1)S(1)} %collective-permute-done.8.refs_0_, bf16[2112,128]{1,0:T(8,128)(2,1)S(1)} %collective-permute-done.7.before_ref.refs_1_, bf16[2112,128]{1,0:T(8,128)(2,1)S(1)} %collective-permute-done.6.after_ref.refs_2_, ...), custom_call_target="tpu_custom_call", output_to_operand_aliasing={{}: (4, {})} | custom-call | flops 1000 | bytes 1000 | tf_op jit(solution)/shard_map/pallas_call | solution.py:229
  39.0 1.0 %collective-permute-done.13.own_ref = bf16[768,128]{1,0:T(8,128)(2,1)S(1)} collective-permute-done((bf16[768,128]{1,0:T(8,128)(2,1)S(1)}, bf16[768,128]{1,0:T(8,128)(2,1)S(1)}, u32[]{:S(2)}, u32[]{:S(2)}) %collective-permute-start.13) | collective-permute-done | bytes 196640 | tf_op jit(solution)/shard_map/ppermute | solution.py:55
  40.0 5.2 %shard_map.63 = (f32[4096,128]{1,0:T(8,128)}, f32[6144,128]{1,0:T(8,128)S(1)}) custom-call(s32[4096]{0:T(1024)S(1)} %bitcast.16, f32[4096,128]{1,0:T(8,128)S(1)} %shard_map.58.base_ref, f32[8,128]{1,0:T(8,128)S(1)} %shard_map.60.ends_ref, bf16[768,128]{1,0:T(8,128)(2,1)S(1)} %collective-permute-done.13.own_ref, ...), custom_call_target="tpu_custom_call", output_to_operand_aliasing={{1}: (5, {})} | custom-call | flops 524288 | bytes 10000000 | tf_op jit(solution)/shard_map/pallas_call | solution.py:290
  (30 shorter events, 1.3 us)
Async XLA Ops:
  0.0 13.1 %copy-start = (bf16[1,4096,128]{2,1,0:T(8,128)(2,1)S(1)}, bf16[1,4096,128]{2,1,0:T(8,128)(2,1)}, u32[]{:S(2)}) copy-start(bf16[1,4096,128]{2,1,0:T(8,128)(2,1)} %param.5) | copy-start | bytes 3145732
  0.0 13.0 %collective-permute-start.2 = (bf16[128,128]{1,0:T(8,128)(2,1)}, bf16[128,128]{1,0:T(8,128)(2,1)S(1)}, u32[]{:S(2)}, u32[]{:S(2)}) collective-permute-start(bf16[128,128]{1,0:T(8,128)(2,1)} %bitcast.18), channel_id=1, source_target_pairs={{0,4},{1,5},{2,6},{3,7},{4,0},{5,1},{6,2},{7,3},{8,12},{9,13},{10,... | collective-permute-start | bytes 98312 | tf_op jit(solution)/shard_map/ppermute | solution.py:46
  4.4 8.6 %collective-permute-start.1 = (bf16[128,128]{1,0:T(8,128)(2,1)}, bf16[128,128]{1,0:T(8,128)(2,1)S(1)}, u32[]{:S(2)}, u32[]{:S(2)}) collective-permute-start(bf16[128,128]{1,0:T(8,128)(2,1)} %bitcast.19), channel_id=1, source_target_pairs={{0,66},{1,19},{2,68},{3,21},{4,70},{5,23},{6,64},{7,17},{8,74},{9,... | collective-permute-start | bytes 98312 | tf_op jit(solution)/shard_map/ppermute | solution.py:46
  7.6 5.4 %collective-permute-start = (bf16[128,128]{1,0:T(8,128)(2,1)}, bf16[128,128]{1,0:T(8,128)(2,1)S(1)}, u32[]{:S(2)}, u32[]{:S(2)}) collective-permute-start(bf16[128,128]{1,0:T(8,128)(2,1)} %bitcast.20), channel_id=1, source_target_pairs={{0,70},{1,23},{2,64},{3,17},{4,66},{5,19},{6,68},{7,21},{8,78},{9,... | collective-permute-start | bytes 98312 | tf_op jit(solution)/shard_map/ppermute | solution.py:46
  10.3 0.7 %copy-start.3 = (s32[1,4096,1]{1,2,0:T(1,128)S(1)}, s32[1,4096,1]{1,2,0:T(1,128)}, u32[]{:S(2)}) copy-start(s32[1,4096,1]{1,2,0:T(1,128)} %param.7) | copy-start | bytes 49156
  13.1 18.6 %copy-start.1 = (bf16[128,128]{1,0:T(8,128)(2,1)S(1)}, bf16[128,128]{1,0:T(8,128)(2,1)}, u32[]{:S(2)}) copy-start(bf16[128,128]{1,0:T(8,128)(2,1)} %plane_ref.3) | copy-start | bytes 98308
  13.1 18.6 %copy-start.2 = (f32[1,4096]{1,0:T(1,128)S(1)}, f32[1,4096]{1,0:T(1,128)}, u32[]{:S(2)}) copy-start(f32[1,4096]{1,0:T(1,128)} %param.6) | copy-start | bytes 49156
  13.1 10.1 %collective-permute-start.5 = (bf16[528,128]{1,0:T(8,128)(2,1)S(1)}, bf16[528,128]{1,0:T(8,128)(2,1)S(1)}, u32[]{:S(2)}, u32[]{:S(2)}) collective-permute-start(bf16[528,128]{1,0:T(8,128)(2,1)S(1)} %constant_dynamic-update-slice_fusion), channel_id=1, source_target_pairs={{0,16},{1,65},{2,18},{3,67},{4,20},{5,69},{6,22},{7,71},{8,24},{9,... | collective-permute-start | bytes 405512 | tf_op jit(solution)/shard_map/ppermute | solution.py:46
  16.1 7.2 %collective-permute-start.4 = (bf16[528,128]{1,0:T(8,128)(2,1)S(1)}, bf16[528,128]{1,0:T(8,128)(2,1)S(1)}, u32[]{:S(2)}, u32[]{:S(2)}) collective-permute-start(bf16[528,128]{1,0:T(8,128)(2,1)S(1)} %constant_dynamic-update-slice_fusion), channel_id=1, source_target_pairs={{0,8},{1,33},{2,10},{3,35},{4,12},{5,37},{6,14},{7,39},{8,16},{9,4... | collective-permute-start | bytes 405512 | tf_op jit(solution)/shard_map/ppermute | solution.py:46
  16.8 6.5 %collective-permute-start.3 = (bf16[528,128]{1,0:T(8,128)(2,1)S(1)}, bf16[528,128]{1,0:T(8,128)(2,1)S(1)}, u32[]{:S(2)}, u32[]{:S(2)}) collective-permute-start(bf16[528,128]{1,0:T(8,128)(2,1)S(1)} %constant_dynamic-update-slice_fusion), channel_id=1, source_target_pairs={{0,24},{1,97},{2,26},{3,99},{4,28},{5,101},{6,30},{7,103},{8,0},{9... | collective-permute-start | bytes 405512 | tf_op jit(solution)/shard_map/ppermute | solution.py:46
  23.3 9.8 %collective-permute-start.8 = (bf16[2112,128]{1,0:T(8,128)(2,1)S(1)}, bf16[2112,128]{1,0:T(8,128)(2,1)S(1)}, u32[]{:S(2)}, u32[]{:S(2)}) collective-permute-start(bf16[2112,128]{1,0:T(8,128)(2,1)S(1)} %pad_maximum_fusion.refs_0_.own_ref), channel_id=1, source_target_pairs={{0,2},{1,7},{2,4},{3,1},{4,6},{5,3},{6,0},{7,5},{8,10},{9,15},{10,... | collective-permute-start | bytes 1622024 | tf_op jit(solution)/shard_map/ppermute | solution.py:46
  26.6 9.7 %collective-permute-start.7 = (bf16[2112,128]{1,0:T(8,128)(2,1)S(1)}, bf16[2112,128]{1,0:T(8,128)(2,1)S(1)}, u32[]{:S(2)}, u32[]{:S(2)}) collective-permute-start(bf16[2112,128]{1,0:T(8,128)(2,1)S(1)} %pad_maximum_fusion.refs_0_.own_ref), channel_id=1, source_target_pairs={{0,32},{1,9},{2,34},{3,11},{4,36},{5,13},{6,38},{7,15},{8,40},{9,1... | collective-permute-start | bytes 1622024 | tf_op jit(solution)/shard_map/ppermute | solution.py:46
  27.1 9.1 %collective-permute-start.6 = (bf16[2112,128]{1,0:T(8,128)(2,1)S(1)}, bf16[2112,128]{1,0:T(8,128)(2,1)S(1)}, u32[]{:S(2)}, u32[]{:S(2)}) collective-permute-start(bf16[2112,128]{1,0:T(8,128)(2,1)S(1)} %pad_maximum_fusion.refs_0_.own_ref), channel_id=1, source_target_pairs={{0,96},{1,25},{2,98},{3,27},{4,100},{5,29},{6,102},{7,31},{8,104},... | collective-permute-start | bytes 1622024 | tf_op jit(solution)/shard_map/ppermute | solution.py:46
  29.2 1.8 %collective-permute-start.9 = (bf16[768,128]{1,0:T(8,128)(2,1)S(1)}, bf16[768,128]{1,0:T(8,128)(2,1)S(1)}, u32[]{:S(2)}, u32[]{:S(2)}) collective-permute-start(bf16[768,128]{1,0:T(8,128)(2,1)S(1)} %get-tuple-element.40), channel_id=1, source_target_pairs={{0,1},{1,0},{2,3},{3,2},{4,5},{5,4},{6,7},{7,6},{8,9},{9,8},{10,11... | collective-permute-start | bytes 589832 | tf_op jit(solution)/shard_map/ppermute | solution.py:55
  29.9 1.4 %collective-permute-start.10 = (bf16[768,128]{1,0:T(8,128)(2,1)S(1)}, bf16[768,128]{1,0:T(8,128)(2,1)S(1)}, u32[]{:S(2)}, u32[]{:S(2)}) collective-permute-start(bf16[768,128]{1,0:T(8,128)(2,1)S(1)} %get-tuple-element.41), channel_id=1, source_target_pairs={{0,1},{1,0},{2,3},{3,2},{4,5},{5,4},{6,7},{7,6},{8,9},{9,8},{10,11... | collective-permute-start | bytes 589832 | tf_op jit(solution)/shard_map/ppermute | solution.py:55
  31.0 2.1 %collective-permute-start.11 = (bf16[768,128]{1,0:T(8,128)(2,1)S(1)}, bf16[768,128]{1,0:T(8,128)(2,1)S(1)}, u32[]{:S(2)}, u32[]{:S(2)}) collective-permute-start(bf16[768,128]{1,0:T(8,128)(2,1)S(1)} %get-tuple-element.42), channel_id=1, source_target_pairs={{0,1},{1,0},{2,3},{3,2},{4,5},{5,4},{6,7},{7,6},{8,9},{9,8},{10,11... | collective-permute-start | bytes 589832 | tf_op jit(solution)/shard_map/ppermute | solution.py:55
  31.4 1.8 %collective-permute-start.12 = (bf16[768,128]{1,0:T(8,128)(2,1)S(1)}, bf16[768,128]{1,0:T(8,128)(2,1)S(1)}, u32[]{:S(2)}, u32[]{:S(2)}) collective-permute-start(bf16[768,128]{1,0:T(8,128)(2,1)S(1)} %get-tuple-element.43), channel_id=1, source_target_pairs={{0,1},{1,0},{2,3},{3,2},{4,5},{5,4},{6,7},{7,6},{8,9},{9,8},{10,11... | collective-permute-start | bytes 589832 | tf_op jit(solution)/shard_map/ppermute | solution.py:55
  36.9 3.1 %collective-permute-start.14 = (bf16[2304,128]{1,0:T(8,128)(2,1)S(1)}, bf16[2304,128]{1,0:T(8,128)(2,1)S(1)}, u32[]{:S(2)}, u32[]{:S(2)}) collective-permute-start(bf16[2304,128]{1,0:T(8,128)(2,1)S(1)} %shard_map.61), channel_id=1, source_target_pairs={{0,1},{1,0},{2,3},{3,2},{4,5},{5,4},{6,7},{7,6},{8,9},{9,8},{10,11... | collective-permute-start | bytes 1769480 | tf_op jit(solution)/shard_map/ppermute | solution.py:55
  38.1 1.9 %collective-permute-start.13 = (bf16[768,128]{1,0:T(8,128)(2,1)S(1)}, bf16[768,128]{1,0:T(8,128)(2,1)S(1)}, u32[]{:S(2)}, u32[]{:S(2)}) collective-permute-start(bf16[768,128]{1,0:T(8,128)(2,1)S(1)} %shard_map.59), channel_id=1, source_target_pairs={{0,1},{1,0},{2,3},{3,2},{4,5},{5,4},{6,7},{7,6},{8,9},{9,8},{10,11... | collective-permute-start | bytes 589832 | tf_op jit(solution)/shard_map/ppermute | solution.py:55

commit v14 on v13

--- a/solution.py
+++ b/solution.py
@@ -243,6 +243,25 @@
     return effect_call([*operators, *guests], sources, range(count), count * block, jnp.bfloat16, {})
 
 
+def own_reply_kernel(operator_ref, guest_ref, *out_refs):
+    for k in range(16):
+        top = k // 4 * stride + k % 4 * vals
+        lo, out = k * cap, k % 8 * cap
+        effect = respond(guest_ref[lo : lo + cap, :], operator_ref[top : top + vals, :])
+        out_refs[k // 8][out : out + cap, :] = effect.astype(jnp.bfloat16)
+
+
+def own_replies(operator, guest):
+    return pl.pallas_call(
+        own_reply_kernel,
+        in_specs=[in_vmem] * 2,
+        out_specs=[in_vmem] * 2,
+        out_shape=[jax.ShapeDtypeStruct((block // 2, vals), jnp.bfloat16)] * 2,
+        compiler_params=params(),
+        cost_estimate=pl.CostEstimate(flops=1000, bytes_accessed=1000, transcendentals=0),
+    )(operator, guest)
+
+
 def effects(near, operators, thirds, previous):
     operands = [*operators, near]
     aliases = {}
@@ -257,9 +276,10 @@
 
 
 def final_kernel(
-    slot_ref, base_ref, ends_ref, own_ref, trio_ref, _, out_ref, effect_ref, result, sent
+    slot_ref, base_ref, ends_ref, own_ref, rest_ref, trio_ref, _, out_ref, effect_ref, result, sent
 ):
-    effect_ref[half : half + block, :] = own_ref[...].astype(jnp.float32)
+    effect_ref[half : half + block // 2, :] = own_ref[...].astype(jnp.float32)
+    effect_ref[half + block // 2 : half + block, :] = rest_ref[...].astype(jnp.float32)
     effect_ref[half + block :, :] = trio_ref[...].astype(jnp.float32)
 
     copies = []
@@ -321,11 +341,11 @@
     weights = coupling.reshape(rows // vals, vals)
     base = stencil(field, weights, in_plane)
     effect = effects(near_rows, [plane], (0,), None)
-    reply = replies([plane], [own_guest])
+    reply = [core_swap(part) for part in own_replies(plane, own_guest)]
     effect, base, reply, guests = tied((effect, base, reply, [side_guest, *pair_guests]))
     side_guest, *pair_guests = guests
     minus, plus, side, effect, base, reply = tied((minus, plus, side, effect, base, reply))
-    returned = [core_swap(reply)]
+    returned = [*reply]
     returned.append(core_swap(replies([side, plus, minus], [side_guest, *pair_guests])))
     effect = effects(near_rows, [side, plus, minus], (1, 2, 3), effect)
     ends = end_terms(plane, plus, minus, weights, in_plane)

time: 45.7 us -> 45.4 us (level)
  waiting for transfers between devices: 6.42 us -> 5.61 us
  starting transfers between devices: 23.7 us -> 24.3 us
    ppermute x9, waiting for transfers between devices: 4.31 us -> 3.26 us  [shifted(): return lax.ppermute(value, axes_all, pairs)]
    ppermute x6 -> x7, starting transfers between devices: 2.68 us -> 3.24 us  [core_swap(): return lax.ppermute(value, axes_all, pairs)]
    pallas_call x4 -> x3, Pallas kernels: 2.09 us -> 1.71 us  [effect_call(): pl.pallas_call(functools.partial(effect_kernel, sources, places), in_spec...]
    ppermute x6 -> x7, waiting for transfers between devices: 2.11 us -> 2.35 us  [core_swap(): return lax.ppermute(value, axes_all, pairs)]
  transfers between devices with their start and end apart: 15 -> 16, of which waited for: 4 -> 5; matrix products, arithmetic and copies ran while one was open for 2% -> 2% of each run, Pallas kernels for 16% -> 17%
where the time goes in v14:
time: 45.4 us; the launch traced here: 45 us
  starting transfers between devices  24.3 us (54%)
  Pallas kernels  13.3 us (29%)
  waiting for transfers between devices  5.61 us (12%)
  local copies, waits for them, and re-layouts  1.57 us (3%)
    ppermute x9, starting transfers between devices, shifted(): return lax.ppermute(value, axes_all, pairs)  21.1 us
    pallas_call x1, Pallas kernels, finish(): pl.pallas_call(final_kernel, in_specs=[pl.BlockSpec(memory_space=pltpu.SM...  5.19 us
    pallas_call x1, Pallas kernels, sort_rows(): pl.pallas_call(sort_kernel, in_specs=[pl.BlockSpec(memory_space=pltpu.SME...  4.46 us
    ppermute x9, waiting for transfers between devices, shifted(): return lax.ppermute(value, axes_all, pairs)  3.26 us
    ppermute x7, starting transfers between devices, core_swap(): return lax.ppermute(value, axes_all, pairs)  3.24 us
    ppermute x7, waiting for transfers between devices, core_swap(): return lax.ppermute(value, axes_all, pairs)  2.35 us
    pallas_call x3, Pallas kernels, effect_call(): pl.pallas_call(functools.partial(effect_kernel, sources, places), in_spec...  1.71 us
    unnamed x13, local copies, waits for them, and re-layouts  1.57 us
  transfers between devices with their start and end apart: 16, of which 5 were waited for; matrix products, arithmetic and copies ran while one was open for 2% of the time, Pallas kernels for 17%

profile of v14, /device:TPU:1, one launch (start us, length us, event | category | flops | bytes accessed | tf_op | source)
XLA Modules:
  0.0 45.0 jit_solution(6969977731943770170)
XLA Ops:
  0.0 4.4 %collective-permute-start.2 = (bf16[128,128]{1,0:T(8,128)(2,1)}, bf16[128,128]{1,0:T(8,128)(2,1)S(1)}, u32[]{:S(2)}, u32[]{:S(2)}) collective-permute-start(bf16[128,128]{1,0:T(8,128)(2,1)} %bitcast.18), channel_id=1, source_target_pairs={{0,4},{1,5},{2,6},{3,7},{4,0},{5,1},{6,2},{7,3},{8,12},{9,13},{10,... | collective-permute-start | bytes 98312 | tf_op jit(solution)/shard_map/ppermute | solution.py:46
  4.4 3.2 %collective-permute-start.1 = (bf16[128,128]{1,0:T(8,128)(2,1)}, bf16[128,128]{1,0:T(8,128)(2,1)S(1)}, u32[]{:S(2)}, u32[]{:S(2)}) collective-permute-start(bf16[128,128]{1,0:T(8,128)(2,1)} %bitcast.19), channel_id=1, source_target_pairs={{0,66},{1,19},{2,68},{3,21},{4,70},{5,23},{6,64},{7,17},{8,74},{9,... | collective-permute-start | bytes 98312 | tf_op jit(solution)/shard_map/ppermute | solution.py:46
  7.6 1.9 %collective-permute-start = (bf16[128,128]{1,0:T(8,128)(2,1)}, bf16[128,128]{1,0:T(8,128)(2,1)S(1)}, u32[]{:S(2)}, u32[]{:S(2)}) collective-permute-start(bf16[128,128]{1,0:T(8,128)(2,1)} %bitcast.20), channel_id=1, source_target_pairs={{0,70},{1,23},{2,64},{3,17},{4,66},{5,19},{6,68},{7,21},{8,78},{9,... | collective-permute-start | bytes 98312 | tf_op jit(solution)/shard_map/ppermute | solution.py:46
  9.5 0.8 %constant_dynamic-update-slice_fusion.5 = bf16[528,128]{1,0:T(8,128)(2,1)S(1)} fusion(bf16[1,128,128]{2,1,0:T(8,128)(2,1)} %param.9), kind=kLoop, calls=%fused_computation.6 | loop fusion | bytes 65536
  10.3 0.7 %copy-done.3 = s32[1,4096,1]{1,2,0:T(1,128)S(1)} copy-done((s32[1,4096,1]{1,2,0:T(1,128)S(1)}, s32[1,4096,1]{1,2,0:T(1,128)}, u32[]{:S(2)}) %copy-start.3) | copy-done | bytes 16408
  11.0 0.8 %shard_map.55 = s32[1,4096]{1,0:T(1,128)S(1)} custom-call(s32[1,4096]{1,0:T(1,128)S(1)} %bitcast.17), custom_call_target="tpu_custom_call" | custom-call | flops 402653184 | bytes 100000 | tf_op jit(solution)/shard_map/pallas_call | solution.py:105
  11.8 1.2 %collective-permute-done = bf16[128,128]{1,0:T(8,128)(2,1)S(1)} collective-permute-done((bf16[128,128]{1,0:T(8,128)(2,1)}, bf16[128,128]{1,0:T(8,128)(2,1)S(1)}, u32[]{:S(2)}, u32[]{:S(2)}) %collective-permute-start) | collective-permute-done | bytes 32800 | tf_op jit(solution)/shard_map/ppermute | solution.py:46
  13.1 3.0 %collective-permute-start.5 = (bf16[528,128]{1,0:T(8,128)(2,1)S(1)}, bf16[528,128]{1,0:T(8,128)(2,1)S(1)}, u32[]{:S(2)}, u32[]{:S(2)}) collective-permute-start(bf16[528,128]{1,0:T(8,128)(2,1)S(1)} %constant_dynamic-update-slice_fusion), channel_id=1, source_target_pairs={{0,16},{1,65},{2,18},{3,67},{4,20},{5,69},{6,22},{7,71},{8,24},{9,... | collective-permute-start | bytes 405512 | tf_op jit(solution)/shard_map/ppermute | solution.py:46
  16.1 0.7 %collective-permute-start.4 = (bf16[528,128]{1,0:T(8,128)(2,1)S(1)}, bf16[528,128]{1,0:T(8,128)(2,1)S(1)}, u32[]{:S(2)}, u32[]{:S(2)}) collective-permute-start(bf16[528,128]{1,0:T(8,128)(2,1)S(1)} %constant_dynamic-update-slice_fusion), channel_id=1, source_target_pairs={{0,8},{1,33},{2,10},{3,35},{4,12},{5,37},{6,14},{7,39},{8,16},{9,4... | collective-permute-start | bytes 405512 | tf_op jit(solution)/shard_map/ppermute | solution.py:46
  16.7 2.0 %collective-permute-start.3 = (bf16[528,128]{1,0:T(8,128)(2,1)S(1)}, bf16[528,128]{1,0:T(8,128)(2,1)S(1)}, u32[]{:S(2)}, u32[]{:S(2)}) collective-permute-start(bf16[528,128]{1,0:T(8,128)(2,1)S(1)} %constant_dynamic-update-slice_fusion), channel_id=1, source_target_pairs={{0,24},{1,97},{2,26},{3,99},{4,28},{5,101},{6,30},{7,103},{8,0},{9... | collective-permute-start | bytes 405512 | tf_op jit(solution)/shard_map/ppermute | solution.py:46
  18.8 4.5 %shard_map.56 = (bf16[3072,128]{1,0:T(8,128)(2,1)S(1)}, bf16[768,128]{1,0:T(8,128)(2,1)S(1)}, bf16[768,128]{1,0:T(8,128)(2,1)S(1)}, bf16[768,128]{1,0:T(8,128)(2,1)S(1)}, bf16[768,128]{1,0:T(8,128)(2,1)S(1)}) custom-call(s32[4096]{0:T(1024)S(1)} %bitcast.15, bf16[4096,128]{1,0:T(8,128)(2,1)S(1)} %bitcast.11), custom_call_target="tpu_custom_call" | custom-call | bytes 20000000 | tf_op jit(solution)/shard_map/pallas_call | solution.py:130
  23.3 3.2 %collective-permute-start.8 = (bf16[2112,128]{1,0:T(8,128)(2,1)S(1)}, bf16[2112,128]{1,0:T(8,128)(2,1)S(1)}, u32[]{:S(2)}, u32[]{:S(2)}) collective-permute-start(bf16[2112,128]{1,0:T(8,128)(2,1)S(1)} %pad_maximum_fusion.refs_0_.operator_ref.own_ref), channel_id=1, source_target_pairs={{0,2},{1,7},{2,4},{3,1},{4,6},{5,3},{6,0},{7,5},{8,10},{9,15},{10,... | collective-permute-start | bytes 1622024 | tf_op jit(solution)/shard_map/ppermute | solution.py:46
  26.6 0.6 %collective-permute-start.7 = (bf16[2112,128]{1,0:T(8,128)(2,1)S(1)}, bf16[2112,128]{1,0:T(8,128)(2,1)S(1)}, u32[]{:S(2)}, u32[]{:S(2)}) collective-permute-start(bf16[2112,128]{1,0:T(8,128)(2,1)S(1)} %pad_maximum_fusion.refs_0_.operator_ref.own_ref), channel_id=1, source_target_pairs={{0,32},{1,9},{2,34},{3,11},{4,36},{5,13},{6,38},{7,15},{8,40},{9,1... | collective-permute-start | bytes 1622024 | tf_op jit(solution)/shard_map/ppermute | solution.py:46
  27.1 2.1 %collective-permute-start.6 = (bf16[2112,128]{1,0:T(8,128)(2,1)S(1)}, bf16[2112,128]{1,0:T(8,128)(2,1)S(1)}, u32[]{:S(2)}, u32[]{:S(2)}) collective-permute-start(bf16[2112,128]{1,0:T(8,128)(2,1)S(1)} %pad_maximum_fusion.refs_0_.operator_ref.own_ref), channel_id=1, source_target_pairs={{0,96},{1,25},{2,98},{3,27},{4,100},{5,29},{6,102},{7,31},{8,104},... | collective-permute-start | bytes 1622024 | tf_op jit(solution)/shard_map/ppermute | solution.py:46
  29.2 0.7 %collective-permute-start.9 = (bf16[768,128]{1,0:T(8,128)(2,1)S(1)}, bf16[768,128]{1,0:T(8,128)(2,1)S(1)}, u32[]{:S(2)}, u32[]{:S(2)}) collective-permute-start(bf16[768,128]{1,0:T(8,128)(2,1)S(1)} %get-tuple-element.44), channel_id=1, source_target_pairs={{0,1},{1,0},{2,3},{3,2},{4,5},{5,4},{6,7},{7,6},{8,9},{9,8},{10,11... | collective-permute-start | bytes 589832 | tf_op jit(solution)/shard_map/ppermute | solution.py:55
  30.0 1.1 %collective-permute-done.9.guest_ref = bf16[768,128]{1,0:T(8,128)(2,1)S(1)} collective-permute-done((bf16[768,128]{1,0:T(8,128)(2,1)S(1)}, bf16[768,128]{1,0:T(8,128)(2,1)S(1)}, u32[]{:S(2)}, u32[]{:S(2)}) %collective-permute-start.9) | collective-permute-done | bytes 196640 | tf_op jit(solution)/shard_map/ppermute | solution.py:55
  32.0 0.4 collective-permute-done.13.refs_4_
  33.1 0.7 %shard_map.58.base_ref = f32[4096,128]{1,0:T(8,128)S(1)} custom-call(bf16[4096,128]{1,0:T(8,128)(2,1)S(1)} %bitcast.12, f32[32,128]{1,0:T(8,128)S(1)} %bitcast.13, bf16[128,128]{1,0:T(8,128)(2,1)S(1)} %copy-done.1), custom_call_target="tpu_custom_call" | custom-call | flops 1000 | bytes 1000 | tf_op jit(solution)/shard_map/pallas_call | solution.py:198
  34.2 2.0 %collective-permute-done.7.before_ref.refs_1_ = bf16[2112,128]{1,0:T(8,128)(2,1)S(1)} collective-permute-done((bf16[2112,128]{1,0:T(8,128)(2,1)S(1)}, bf16[2112,128]{1,0:T(8,128)(2,1)S(1)}, u32[]{:S(2)}, u32[]{:S(2)}) %collective-permute-start.7) | collective-permute-done | bytes 540704 | tf_op jit(solution)/shard_map/ppermute | solution.py:46
  36.3 0.6 %shard_map.61 = bf16[2304,128]{1,0:T(8,128)(2,1)S(1)} custom-call(bf16[2112,128]{1,0:T(8,128)(2,1)S(1)} %collective-permute-done.8.refs_0_, bf16[2112,128]{1,0:T(8,128)(2,1)S(1)} %collective-permute-done.7.before_ref.refs_1_, bf16[2112,128]{1,0:T(8,128)(2,1)S(1)} %collective-permute-done.6.after_ref.refs_2_, ...), custom_call_target="tpu_custom_call" | custom-call | flops 1000 | bytes 1000 | tf_op jit(solution)/shard_map/pallas_call | solution.py:229
  36.9 1.2 %collective-permute-start.15 = (bf16[2304,128]{1,0:T(8,128)(2,1)S(1)}, bf16[2304,128]{1,0:T(8,128)(2,1)S(1)}, u32[]{:S(2)}, u32[]{:S(2)}) collective-permute-start(bf16[2304,128]{1,0:T(8,128)(2,1)S(1)} %shard_map.61), channel_id=1, source_target_pairs={{0,1},{1,0},{2,3},{3,2},{4,5},{5,4},{6,7},{7,6},{8,9},{9,8},{10,11... | collective-permute-start | bytes 1769480 | tf_op jit(solution)/shard_map/ppermute | solution.py:55
  38.2 0.7 %shard_map.62._ = f32[6144,128]{1,0:T(8,128)S(1)} custom-call(bf16[2112,128]{1,0:T(8,128)(2,1)S(1)} %collective-permute-done.8.refs_0_, bf16[2112,128]{1,0:T(8,128)(2,1)S(1)} %collective-permute-done.7.before_ref.refs_1_, bf16[2112,128]{1,0:T(8,128)(2,1)S(1)} %collective-permute-done.6.after_ref.refs_2_, ...), custom_call_target="tpu_custom_call", output_to_operand_aliasing={{}: (4, {})} | custom-call | flops 1000 | bytes 1000 | tf_op jit(solution)/shard_map/pallas_call | solution.py:229
  38.9 0.8 %collective-permute-done.15.trio_ref = bf16[2304,128]{1,0:T(8,128)(2,1)S(1)} collective-permute-done((bf16[2304,128]{1,0:T(8,128)(2,1)S(1)}, bf16[2304,128]{1,0:T(8,128)(2,1)S(1)}, u32[]{:S(2)}, u32[]{:S(2)}) %collective-permute-start.15) | collective-permute-done | bytes 589856 | tf_op jit(solution)/shard_map/ppermute | solution.py:55
  39.8 5.2 %shard_map.63 = (f32[4096,128]{1,0:T(8,128)}, f32[6144,128]{1,0:T(8,128)S(1)}) custom-call(s32[4096]{0:T(1024)S(1)} %bitcast.16, f32[4096,128]{1,0:T(8,128)S(1)} %shard_map.58.base_ref, f32[8,128]{1,0:T(8,128)S(1)} %shard_map.60.ends_ref, bf16[384,128]{1,0:T(8,128)(2,1)S(1)} %collective-permute-done.10.own_ref, ...), custom_call_target="tpu_custom_call", output_to_operand_aliasing={{1}: (6, {})} | custom-call | flops 524288 | bytes 10000000 | tf_op jit(solution)/shard_map/pallas_call | solution.py:310
  (32 shorter events, 2.2 us)
Async XLA Ops:
  0.0 13.1 %copy-start = (bf16[1,4096,128]{2,1,0:T(8,128)(2,1)S(1)}, bf16[1,4096,128]{2,1,0:T(8,128)(2,1)}, u32[]{:S(2)}) copy-start(bf16[1,4096,128]{2,1,0:T(8,128)(2,1)} %param.5) | copy-start | bytes 3145732
  0.0 13.0 %collective-permute-start.2 = (bf16[128,128]{1,0:T(8,128)(2,1)}, bf16[128,128]{1,0:T(8,128)(2,1)S(1)}, u32[]{:S(2)}, u32[]{:S(2)}) collective-permute-start(bf16[128,128]{1,0:T(8,128)(2,1)} %bitcast.18), channel_id=1, source_target_pairs={{0,4},{1,5},{2,6},{3,7},{4,0},{5,1},{6,2},{7,3},{8,12},{9,13},{10,... | collective-permute-start | bytes 98312 | tf_op jit(solution)/shard_map/ppermute | solution.py:46
  4.4 8.6 %collective-permute-start.1 = (bf16[128,128]{1,0:T(8,128)(2,1)}, bf16[128,128]{1,0:T(8,128)(2,1)S(1)}, u32[]{:S(2)}, u32[]{:S(2)}) collective-permute-start(bf16[128,128]{1,0:T(8,128)(2,1)} %bitcast.19), channel_id=1, source_target_pairs={{0,66},{1,19},{2,68},{3,21},{4,70},{5,23},{6,64},{7,17},{8,74},{9,... | collective-permute-start | bytes 98312 | tf_op jit(solution)/shard_map/ppermute | solution.py:46
  7.6 5.4 %collective-permute-start = (bf16[128,128]{1,0:T(8,128)(2,1)}, bf16[128,128]{1,0:T(8,128)(2,1)S(1)}, u32[]{:S(2)}, u32[]{:S(2)}) collective-permute-start(bf16[128,128]{1,0:T(8,128)(2,1)} %bitcast.20), channel_id=1, source_target_pairs={{0,70},{1,23},{2,64},{3,17},{4,66},{5,19},{6,68},{7,21},{8,78},{9,... | collective-permute-start | bytes 98312 | tf_op jit(solution)/shard_map/ppermute | solution.py:46
  10.3 0.7 %copy-start.3 = (s32[1,4096,1]{1,2,0:T(1,128)S(1)}, s32[1,4096,1]{1,2,0:T(1,128)}, u32[]{:S(2)}) copy-start(s32[1,4096,1]{1,2,0:T(1,128)} %param.7) | copy-start | bytes 49156
  13.1 10.2 %collective-permute-start.5 = (bf16[528,128]{1,0:T(8,128)(2,1)S(1)}, bf16[528,128]{1,0:T(8,128)(2,1)S(1)}, u32[]{:S(2)}, u32[]{:S(2)}) collective-permute-start(bf16[528,128]{1,0:T(8,128)(2,1)S(1)} %constant_dynamic-update-slice_fusion), channel_id=1, source_target_pairs={{0,16},{1,65},{2,18},{3,67},{4,20},{5,69},{6,22},{7,71},{8,24},{9,... | collective-permute-start | bytes 405512 | tf_op jit(solution)/shard_map/ppermute | solution.py:46
  16.1 7.2 %collective-permute-start.4 = (bf16[528,128]{1,0:T(8,128)(2,1)S(1)}, bf16[528,128]{1,0:T(8,128)(2,1)S(1)}, u32[]{:S(2)}, u32[]{:S(2)}) collective-permute-start(bf16[528,128]{1,0:T(8,128)(2,1)S(1)} %constant_dynamic-update-slice_fusion), channel_id=1, source_target_pairs={{0,8},{1,33},{2,10},{3,35},{4,12},{5,37},{6,14},{7,39},{8,16},{9,4... | collective-permute-start | bytes 405512 | tf_op jit(solution)/shard_map/ppermute | solution.py:46
  16.7 6.5 %collective-permute-start.3 = (bf16[528,128]{1,0:T(8,128)(2,1)S(1)}, bf16[528,128]{1,0:T(8,128)(2,1)S(1)}, u32[]{:S(2)}, u32[]{:S(2)}) collective-permute-start(bf16[528,128]{1,0:T(8,128)(2,1)S(1)} %constant_dynamic-update-slice_fusion), channel_id=1, source_target_pairs={{0,24},{1,97},{2,26},{3,99},{4,28},{5,101},{6,30},{7,103},{8,0},{9... | collective-permute-start | bytes 405512 | tf_op jit(solution)/shard_map/ppermute | solution.py:46
  23.2 9.9 %copy-start.1 = (bf16[128,128]{1,0:T(8,128)(2,1)S(1)}, bf16[128,128]{1,0:T(8,128)(2,1)}, u32[]{:S(2)}) copy-start(bf16[128,128]{1,0:T(8,128)(2,1)} %plane_ref.3) | copy-start | bytes 98308
  23.2 9.9 %copy-start.2 = (f32[1,4096]{1,0:T(1,128)S(1)}, f32[1,4096]{1,0:T(1,128)}, u32[]{:S(2)}) copy-start(f32[1,4096]{1,0:T(1,128)} %param.6) | copy-start | bytes 49156
  23.3 10.9 %collective-permute-start.8 = (bf16[2112,128]{1,0:T(8,128)(2,1)S(1)}, bf16[2112,128]{1,0:T(8,128)(2,1)S(1)}, u32[]{:S(2)}, u32[]{:S(2)}) collective-permute-start(bf16[2112,128]{1,0:T(8,128)(2,1)S(1)} %pad_maximum_fusion.refs_0_.operator_ref.own_ref), channel_id=1, source_target_pairs={{0,2},{1,7},{2,4},{3,1},{4,6},{5,3},{6,0},{7,5},{8,10},{9,15},{10,... | collective-permute-start | bytes 1622024 | tf_op jit(solution)/shard_map/ppermute | solution.py:46
  26.6 9.7 %collective-permute-start.7 = (bf16[2112,128]{1,0:T(8,128)(2,1)S(1)}, bf16[2112,128]{1,0:T(8,128)(2,1)S(1)}, u32[]{:S(2)}, u32[]{:S(2)}) collective-permute-start(bf16[2112,128]{1,0:T(8,128)(2,1)S(1)} %pad_maximum_fusion.refs_0_.operator_ref.own_ref), channel_id=1, source_target_pairs={{0,32},{1,9},{2,34},{3,11},{4,36},{5,13},{6,38},{7,15},{8,40},{9,1... | collective-permute-start | bytes 1622024 | tf_op jit(solution)/shard_map/ppermute | solution.py:46
  27.1 9.1 %collective-permute-start.6 = (bf16[2112,128]{1,0:T(8,128)(2,1)S(1)}, bf16[2112,128]{1,0:T(8,128)(2,1)S(1)}, u32[]{:S(2)}, u32[]{:S(2)}) collective-permute-start(bf16[2112,128]{1,0:T(8,128)(2,1)S(1)} %pad_maximum_fusion.refs_0_.operator_ref.own_ref), channel_id=1, source_target_pairs={{0,96},{1,25},{2,98},{3,27},{4,100},{5,29},{6,102},{7,31},{8,104},... | collective-permute-start | bytes 1622024 | tf_op jit(solution)/shard_map/ppermute | solution.py:46
  29.2 1.8 %collective-permute-start.9 = (bf16[768,128]{1,0:T(8,128)(2,1)S(1)}, bf16[768,128]{1,0:T(8,128)(2,1)S(1)}, u32[]{:S(2)}, u32[]{:S(2)}) collective-permute-start(bf16[768,128]{1,0:T(8,128)(2,1)S(1)} %get-tuple-element.44), channel_id=1, source_target_pairs={{0,1},{1,0},{2,3},{3,2},{4,5},{5,4},{6,7},{7,6},{8,9},{9,8},{10,11... | collective-permute-start | bytes 589832 | tf_op jit(solution)/shard_map/ppermute | solution.py:55
  29.9 1.4 %collective-permute-start.12 = (bf16[768,128]{1,0:T(8,128)(2,1)S(1)}, bf16[768,128]{1,0:T(8,128)(2,1)S(1)}, u32[]{:S(2)}, u32[]{:S(2)}) collective-permute-start(bf16[768,128]{1,0:T(8,128)(2,1)S(1)} %get-tuple-element.47), channel_id=1, source_target_pairs={{0,1},{1,0},{2,3},{3,2},{4,5},{5,4},{6,7},{7,6},{8,9},{9,8},{10,11... | collective-permute-start | bytes 589832 | tf_op jit(solution)/shard_map/ppermute | solution.py:55
  31.0 1.4 %collective-permute-start.13 = (bf16[768,128]{1,0:T(8,128)(2,1)S(1)}, bf16[768,128]{1,0:T(8,128)(2,1)S(1)}, u32[]{:S(2)}, u32[]{:S(2)}) collective-permute-start(bf16[768,128]{1,0:T(8,128)(2,1)S(1)} %get-tuple-element.48), channel_id=1, source_target_pairs={{0,1},{1,0},{2,3},{3,2},{4,5},{5,4},{6,7},{7,6},{8,9},{9,8},{10,11... | collective-permute-start | bytes 589832 | tf_op jit(solution)/shard_map/ppermute | solution.py:55
  31.4 1.4 %collective-permute-start.14 = (bf16[768,128]{1,0:T(8,128)(2,1)S(1)}, bf16[768,128]{1,0:T(8,128)(2,1)S(1)}, u32[]{:S(2)}, u32[]{:S(2)}) collective-permute-start(bf16[768,128]{1,0:T(8,128)(2,1)S(1)} %get-tuple-element.49), channel_id=1, source_target_pairs={{0,1},{1,0},{2,3},{3,2},{4,5},{5,4},{6,7},{7,6},{8,9},{9,8},{10,11... | collective-permute-start | bytes 589832 | tf_op jit(solution)/shard_map/ppermute | solution.py:55
  32.5 1.7 %collective-permute-start.10 = (bf16[384,128]{1,0:T(8,128)(2,1)S(1)}, bf16[384,128]{1,0:T(8,128)(2,1)S(1)}, u32[]{:S(2)}, u32[]{:S(2)}) collective-permute-start(bf16[384,128]{1,0:T(8,128)(2,1)S(1)} %get-tuple-element.45), channel_id=1, source_target_pairs={{0,1},{1,0},{2,3},{3,2},{4,5},{5,4},{6,7},{7,6},{8,9},{9,8},{10,11... | collective-permute-start | bytes 294920 | tf_op jit(solution)/shard_map/ppermute | solution.py:55
  32.8 1.4 %collective-permute-start.11 = (bf16[384,128]{1,0:T(8,128)(2,1)S(1)}, bf16[384,128]{1,0:T(8,128)(2,1)S(1)}, u32[]{:S(2)}, u32[]{:S(2)}) collective-permute-start(bf16[384,128]{1,0:T(8,128)(2,1)S(1)} %get-tuple-element.46), channel_id=1, source_target_pairs={{0,1},{1,0},{2,3},{3,2},{4,5},{5,4},{6,7},{7,6},{8,9},{9,8},{10,11... | collective-permute-start | bytes 294920 | tf_op jit(solution)/shard_map/ppermute | solution.py:55
  36.9 2.8 %collective-permute-start.15 = (bf16[2304,128]{1,0:T(8,128)(2,1)S(1)}, bf16[2304,128]{1,0:T(8,128)(2,1)S(1)}, u32[]{:S(2)}, u32[]{:S(2)}) collective-permute-start(bf16[2304,128]{1,0:T(8,128)(2,1)S(1)} %shard_map.61), channel_id=1, source_target_pairs={{0,1},{1,0},{2,3},{3,2},{4,5},{5,4},{6,7},{7,6},{8,9},{9,8},{10,11... | collective-permute-start | bytes 1769480 | tf_op jit(solution)/shard_map/ppermute | solution.py:55

commit v15 on v14

--- a/solution.py
+++ b/solution.py
@@ -280,7 +280,9 @@
 ):
     effect_ref[half : half + block // 2, :] = own_ref[...].astype(jnp.float32)
     effect_ref[half + block // 2 : half + block, :] = rest_ref[...].astype(jnp.float32)
-    effect_ref[half + block :, :] = trio_ref[...].astype(jnp.float32)
+    effect_ref[half + block : half + 2 * block, :] = trio_ref[:block].astype(jnp.float32)
+    effect_ref[half + 2 * block : half + 3 * block, :] = trio_ref[2 * block :].astype(jnp.float32)
+    effect_ref[half + 3 * block :, :] = trio_ref[block : 2 * block].astype(jnp.float32)
 
     copies = []
     for number, (top, end) in enumerate(zip(part_tops, part_tops[1:])):
@@ -344,9 +346,9 @@
     reply = [core_swap(part) for part in own_replies(plane, own_guest)]
     effect, base, reply, guests = tied((effect, base, reply, [side_guest, *pair_guests]))
     side_guest, *pair_guests = guests
-    minus, plus, side, effect, base, reply = tied((minus, plus, side, effect, base, reply))
+    plus, minus, side, effect, base, reply = tied((plus, minus, side, effect, base, reply))
     returned = [*reply]
-    returned.append(core_swap(replies([side, plus, minus], [side_guest, *pair_guests])))
+    returned.append(core_swap(replies([side, minus, plus], [side_guest, *reversed(pair_guests)])))
     effect = effects(near_rows, [side, plus, minus], (1, 2, 3), effect)
     ends = end_terms(plane, plus, minus, weights, in_plane)
     return finish(slot, base, ends, returned, effect)[None]

time: 45.4 us -> 46.2 us (1.018)
  waiting for transfers between devices: 5.61 us -> 7.68 us
  starting transfers between devices: 24.3 us -> 23.2 us
    ppermute x9, waiting for transfers between devices: 3.26 us -> 5.33 us  [shifted(): return lax.ppermute(value, axes_all, pairs)]
    ppermute x9, starting transfers between devices: 21.1 us -> 19.9 us  [shifted(): return lax.ppermute(value, axes_all, pairs)]
  transfers between devices with their start and end apart: 16 -> 16, of which waited for: 5 -> 6; matrix products, arithmetic and copies ran while one was open for 2% -> 2% of each run, Pallas kernels for 17% -> 16%
where the time goes in v15:
time: 46.2 us; the launch traced here: 45.9 us
  starting transfers between devices  23.2 us (50%)
  Pallas kernels  13.3 us (29%)
  waiting for transfers between devices  7.68 us (17%)
  local copies, waits for them, and re-layouts  1.57 us (3%)
    ppermute x9, starting transfers between devices, shifted(): return lax.ppermute(value, axes_all, pairs)  19.9 us
    ppermute x9, waiting for transfers between devices, shifted(): return lax.ppermute(value, axes_all, pairs)  5.33 us
    pallas_call x1, Pallas kernels, finish(): pl.pallas_call(final_kernel, in_specs=[pl.BlockSpec(memory_space=pltpu.SM...  5.19 us
    pallas_call x1, Pallas kernels, sort_rows(): pl.pallas_call(sort_kernel, in_specs=[pl.BlockSpec(memory_space=pltpu.SME...  4.46 us
    ppermute x7, starting transfers between devices, core_swap(): return lax.ppermute(value, axes_all, pairs)  3.3 us
    ppermute x7, waiting for transfers between devices, core_swap(): return lax.ppermute(value, axes_all, pairs)  2.35 us
    pallas_call x3, Pallas kernels, effect_call(): pl.pallas_call(functools.partial(effect_kernel, sources, places), in_spec...  1.72 us
    unnamed x13, local copies, waits for them, and re-layouts  1.57 us
  transfers between devices with their start and end apart: 16, of which 6 were waited for; matrix products, arithmetic and copies ran while one was open for 2% of the time, Pallas kernels for 16%

profile of v15, /device:TPU:1, one launch (start us, length us, event | category | flops | bytes accessed | tf_op | source)
XLA Modules:
  0.0 45.9 jit_solution(11502955295975281909)
XLA Ops:
  0.0 4.4 %collective-permute-start.2 = (bf16[128,128]{1,0:T(8,128)(2,1)}, bf16[128,128]{1,0:T(8,128)(2,1)S(1)}, u32[]{:S(2)}, u32[]{:S(2)}) collective-permute-start(bf16[128,128]{1,0:T(8,128)(2,1)} %bitcast.18), channel_id=1, source_target_pairs={{0,4},{1,5},{2,6},{3,7},{4,0},{5,1},{6,2},{7,3},{8,12},{9,13},{10,... | collective-permute-start | bytes 98312 | tf_op jit(solution)/shard_map/ppermute | solution.py:46
  4.4 3.2 %collective-permute-start.1 = (bf16[128,128]{1,0:T(8,128)(2,1)}, bf16[128,128]{1,0:T(8,128)(2,1)S(1)}, u32[]{:S(2)}, u32[]{:S(2)}) collective-permute-start(bf16[128,128]{1,0:T(8,128)(2,1)} %bitcast.19), channel_id=1, source_target_pairs={{0,66},{1,19},{2,68},{3,21},{4,70},{5,23},{6,64},{7,17},{8,74},{9,... | collective-permute-start | bytes 98312 | tf_op jit(solution)/shard_map/ppermute | solution.py:46
  7.6 1.9 %collective-permute-start = (bf16[128,128]{1,0:T(8,128)(2,1)}, bf16[128,128]{1,0:T(8,128)(2,1)S(1)}, u32[]{:S(2)}, u32[]{:S(2)}) collective-permute-start(bf16[128,128]{1,0:T(8,128)(2,1)} %bitcast.20), channel_id=1, source_target_pairs={{0,70},{1,23},{2,64},{3,17},{4,66},{5,19},{6,68},{7,21},{8,78},{9,... | collective-permute-start | bytes 98312 | tf_op jit(solution)/shard_map/ppermute | solution.py:46
  9.5 0.8 %constant_dynamic-update-slice_fusion.5 = bf16[528,128]{1,0:T(8,128)(2,1)S(1)} fusion(bf16[1,128,128]{2,1,0:T(8,128)(2,1)} %param.9), kind=kLoop, calls=%fused_computation.6 | loop fusion | bytes 65536
  10.3 0.7 %copy-done.3 = s32[1,4096,1]{1,2,0:T(1,128)S(1)} copy-done((s32[1,4096,1]{1,2,0:T(1,128)S(1)}, s32[1,4096,1]{1,2,0:T(1,128)}, u32[]{:S(2)}) %copy-start.3) | copy-done | bytes 16408
  11.0 0.8 %shard_map.55 = s32[1,4096]{1,0:T(1,128)S(1)} custom-call(s32[1,4096]{1,0:T(1,128)S(1)} %bitcast.17), custom_call_target="tpu_custom_call" | custom-call | flops 402653184 | bytes 100000 | tf_op jit(solution)/shard_map/pallas_call | solution.py:105
  11.8 1.2 %collective-permute-done = bf16[128,128]{1,0:T(8,128)(2,1)S(1)} collective-permute-done((bf16[128,128]{1,0:T(8,128)(2,1)}, bf16[128,128]{1,0:T(8,128)(2,1)S(1)}, u32[]{:S(2)}, u32[]{:S(2)}) %collective-permute-start) | collective-permute-done | bytes 32800 | tf_op jit(solution)/shard_map/ppermute | solution.py:46
  13.1 3.0 %collective-permute-start.5 = (bf16[528,128]{1,0:T(8,128)(2,1)S(1)}, bf16[528,128]{1,0:T(8,128)(2,1)S(1)}, u32[]{:S(2)}, u32[]{:S(2)}) collective-permute-start(bf16[528,128]{1,0:T(8,128)(2,1)S(1)} %constant_dynamic-update-slice_fusion), channel_id=1, source_target_pairs={{0,16},{1,65},{2,18},{3,67},{4,20},{5,69},{6,22},{7,71},{8,24},{9,... | collective-permute-start | bytes 405512 | tf_op jit(solution)/shard_map/ppermute | solution.py:46
  16.1 0.7 %collective-permute-start.4 = (bf16[528,128]{1,0:T(8,128)(2,1)S(1)}, bf16[528,128]{1,0:T(8,128)(2,1)S(1)}, u32[]{:S(2)}, u32[]{:S(2)}) collective-permute-start(bf16[528,128]{1,0:T(8,128)(2,1)S(1)} %constant_dynamic-update-slice_fusion), channel_id=1, source_target_pairs={{0,8},{1,33},{2,10},{3,35},{4,12},{5,37},{6,14},{7,39},{8,16},{9,4... | collective-permute-start | bytes 405512 | tf_op jit(solution)/shard_map/ppermute | solution.py:46
  16.7 2.0 %collective-permute-start.3 = (bf16[528,128]{1,0:T(8,128)(2,1)S(1)}, bf16[528,128]{1,0:T(8,128)(2,1)S(1)}, u32[]{:S(2)}, u32[]{:S(2)}) collective-permute-start(bf16[528,128]{1,0:T(8,128)(2,1)S(1)} %constant_dynamic-update-slice_fusion), channel_id=1, source_target_pairs={{0,24},{1,97},{2,26},{3,99},{4,28},{5,101},{6,30},{7,103},{8,0},{9... | collective-permute-start | bytes 405512 | tf_op jit(solution)/shard_map/ppermute | solution.py:46
  18.8 4.5 %shard_map.56 = (bf16[3072,128]{1,0:T(8,128)(2,1)S(1)}, bf16[768,128]{1,0:T(8,128)(2,1)S(1)}, bf16[768,128]{1,0:T(8,128)(2,1)S(1)}, bf16[768,128]{1,0:T(8,128)(2,1)S(1)}, bf16[768,128]{1,0:T(8,128)(2,1)S(1)}) custom-call(s32[4096]{0:T(1024)S(1)} %bitcast.15, bf16[4096,128]{1,0:T(8,128)(2,1)S(1)} %bitcast.11), custom_call_target="tpu_custom_call" | custom-call | bytes 20000000 | tf_op jit(solution)/shard_map/pallas_call | solution.py:130
  23.3 3.2 %collective-permute-start.8 = (bf16[2112,128]{1,0:T(8,128)(2,1)S(1)}, bf16[2112,128]{1,0:T(8,128)(2,1)S(1)}, u32[]{:S(2)}, u32[]{:S(2)}) collective-permute-start(bf16[2112,128]{1,0:T(8,128)(2,1)S(1)} %pad_maximum_fusion.refs_0_.operator_ref.own_ref), channel_id=1, source_target_pairs={{0,2},{1,7},{2,4},{3,1},{4,6},{5,3},{6,0},{7,5},{8,10},{9,15},{10,... | collective-permute-start | bytes 1622024 | tf_op jit(solution)/shard_map/ppermute | solution.py:46
  26.6 0.9 %collective-permute-start.7 = (bf16[2112,128]{1,0:T(8,128)(2,1)S(1)}, bf16[2112,128]{1,0:T(8,128)(2,1)S(1)}, u32[]{:S(2)}, u32[]{:S(2)}) collective-permute-start(bf16[2112,128]{1,0:T(8,128)(2,1)S(1)} %pad_maximum_fusion.refs_0_.operator_ref.own_ref), channel_id=1, source_target_pairs={{0,96},{1,25},{2,98},{3,27},{4,100},{5,29},{6,102},{7,31},{8,104},... | collective-permute-start | bytes 1622024 | tf_op jit(solution)/shard_map/ppermute | solution.py:46
  27.4 0.6 %collective-permute-start.6 = (bf16[2112,128]{1,0:T(8,128)(2,1)S(1)}, bf16[2112,128]{1,0:T(8,128)(2,1)S(1)}, u32[]{:S(2)}, u32[]{:S(2)}) collective-permute-start(bf16[2112,128]{1,0:T(8,128)(2,1)S(1)} %pad_maximum_fusion.refs_0_.operator_ref.own_ref), channel_id=1, source_target_pairs={{0,32},{1,9},{2,34},{3,11},{4,36},{5,13},{6,38},{7,15},{8,40},{9,1... | collective-permute-start | bytes 1622024 | tf_op jit(solution)/shard_map/ppermute | solution.py:46
  28.0 0.7 %collective-permute-start.9 = (bf16[768,128]{1,0:T(8,128)(2,1)S(1)}, bf16[768,128]{1,0:T(8,128)(2,1)S(1)}, u32[]{:S(2)}, u32[]{:S(2)}) collective-permute-start(bf16[768,128]{1,0:T(8,128)(2,1)S(1)} %get-tuple-element.44), channel_id=1, source_target_pairs={{0,1},{1,0},{2,3},{3,2},{4,5},{5,4},{6,7},{7,6},{8,9},{9,8},{10,11... | collective-permute-start | bytes 589832 | tf_op jit(solution)/shard_map/ppermute | solution.py:55
  28.7 1.1 %collective-permute-done.9.guest_ref = bf16[768,128]{1,0:T(8,128)(2,1)S(1)} collective-permute-done((bf16[768,128]{1,0:T(8,128)(2,1)S(1)}, bf16[768,128]{1,0:T(8,128)(2,1)S(1)}, u32[]{:S(2)}, u32[]{:S(2)}) %collective-permute-start.9) | collective-permute-done | bytes 196640 | tf_op jit(solution)/shard_map/ppermute | solution.py:55
  31.9 0.7 %shard_map.58.base_ref = f32[4096,128]{1,0:T(8,128)S(1)} custom-call(bf16[4096,128]{1,0:T(8,128)(2,1)S(1)} %bitcast.12, f32[32,128]{1,0:T(8,128)S(1)} %bitcast.13, bf16[128,128]{1,0:T(8,128)(2,1)S(1)} %copy-done.1), custom_call_target="tpu_custom_call" | custom-call | flops 1000 | bytes 1000 | tf_op jit(solution)/shard_map/pallas_call | solution.py:198
  33.0 2.0 %collective-permute-done.7.after_ref.refs_1_.refs_2_ = bf16[2112,128]{1,0:T(8,128)(2,1)S(1)} collective-permute-done((bf16[2112,128]{1,0:T(8,128)(2,1)S(1)}, bf16[2112,128]{1,0:T(8,128)(2,1)S(1)}, u32[]{:S(2)}, u32[]{:S(2)}) %collective-permute-start.7) | collective-permute-done | bytes 540704 | tf_op jit(solution)/shard_map/ppermute | solution.py:46
  35.1 2.1 %collective-permute-done.6.before_ref.refs_2_.refs_1_ = bf16[2112,128]{1,0:T(8,128)(2,1)S(1)} collective-permute-done((bf16[2112,128]{1,0:T(8,128)(2,1)S(1)}, bf16[2112,128]{1,0:T(8,128)(2,1)S(1)}, u32[]{:S(2)}, u32[]{:S(2)}) %collective-permute-start.6) | collective-permute-done | bytes 540704 | tf_op jit(solution)/shard_map/ppermute | solution.py:46
  37.1 0.6 %shard_map.61 = bf16[2304,128]{1,0:T(8,128)(2,1)S(1)} custom-call(bf16[2112,128]{1,0:T(8,128)(2,1)S(1)} %collective-permute-done.8.refs_0_, bf16[2112,128]{1,0:T(8,128)(2,1)S(1)} %collective-permute-done.7.after_ref.refs_1_.refs_2_, bf16[2112,128]{1,0:T(8,128)(2,1)S(1)} %collective-permute-done.6.before_ref.refs_2_.refs_1_, ...), custom_call_target="tpu_custom_call" | custom-call | flops 1000 | bytes 1000 | tf_op jit(solution)/shard_map/pallas_call | solution.py:229
  37.8 1.3 %collective-permute-start.15 = (bf16[2304,128]{1,0:T(8,128)(2,1)S(1)}, bf16[2304,128]{1,0:T(8,128)(2,1)S(1)}, u32[]{:S(2)}, u32[]{:S(2)}) collective-permute-start(bf16[2304,128]{1,0:T(8,128)(2,1)S(1)} %shard_map.61), channel_id=1, source_target_pairs={{0,1},{1,0},{2,3},{3,2},{4,5},{5,4},{6,7},{7,6},{8,9},{9,8},{10,11... | collective-permute-start | bytes 1769480 | tf_op jit(solution)/shard_map/ppermute | solution.py:55
  39.1 0.7 %shard_map.62._ = f32[6144,128]{1,0:T(8,128)S(1)} custom-call(bf16[2112,128]{1,0:T(8,128)(2,1)S(1)} %collective-permute-done.8.refs_0_, bf16[2112,128]{1,0:T(8,128)(2,1)S(1)} %collective-permute-done.6.before_ref.refs_2_.refs_1_, bf16[2112,128]{1,0:T(8,128)(2,1)S(1)} %collective-permute-done.7.after_ref.refs_1_.refs_2_, ...), custom_call_target="tpu_custom_call", output_to_operand_aliasing={{}: (4, {})} | custom-call | flops 1000 | bytes 1000 | tf_op jit(solution)/shard_map/pallas_call | solution.py:229
  39.8 0.8 %collective-permute-done.15.trio_ref = bf16[2304,128]{1,0:T(8,128)(2,1)S(1)} collective-permute-done((bf16[2304,128]{1,0:T(8,128)(2,1)S(1)}, bf16[2304,128]{1,0:T(8,128)(2,1)S(1)}, u32[]{:S(2)}, u32[]{:S(2)}) %collective-permute-start.15) | collective-permute-done | bytes 589856 | tf_op jit(solution)/shard_map/ppermute | solution.py:55
  40.7 5.2 %shard_map.63 = (f32[4096,128]{1,0:T(8,128)}, f32[6144,128]{1,0:T(8,128)S(1)}) custom-call(s32[4096]{0:T(1024)S(1)} %bitcast.16, f32[4096,128]{1,0:T(8,128)S(1)} %shard_map.58.base_ref, f32[8,128]{1,0:T(8,128)S(1)} %shard_map.60.ends_ref, bf16[384,128]{1,0:T(8,128)(2,1)S(1)} %collective-permute-done.10.own_ref, ...), custom_call_target="tpu_custom_call", output_to_operand_aliasing={{1}: (6, {})} | custom-call | flops 524288 | bytes 10000000 | tf_op jit(solution)/shard_map/pallas_call | solution.py:312
  (32 shorter events, 2.7 us)
Async XLA Ops:
  0.0 13.1 %copy-start = (bf16[1,4096,128]{2,1,0:T(8,128)(2,1)S(1)}, bf16[1,4096,128]{2,1,0:T(8,128)(2,1)}, u32[]{:S(2)}) copy-start(bf16[1,4096,128]{2,1,0:T(8,128)(2,1)} %param.5) | copy-start | bytes 3145732
  0.0 13.0 %collective-permute-start.2 = (bf16[128,128]{1,0:T(8,128)(2,1)}, bf16[128,128]{1,0:T(8,128)(2,1)S(1)}, u32[]{:S(2)}, u32[]{:S(2)}) collective-permute-start(bf16[128,128]{1,0:T(8,128)(2,1)} %bitcast.18), channel_id=1, source_target_pairs={{0,4},{1,5},{2,6},{3,7},{4,0},{5,1},{6,2},{7,3},{8,12},{9,13},{10,... | collective-permute-start | bytes 98312 | tf_op jit(solution)/shard_map/ppermute | solution.py:46
  4.4 8.6 %collective-permute-start.1 = (bf16[128,128]{1,0:T(8,128)(2,1)}, bf16[128,128]{1,0:T(8,128)(2,1)S(1)}, u32[]{:S(2)}, u32[]{:S(2)}) collective-permute-start(bf16[128,128]{1,0:T(8,128)(2,1)} %bitcast.19), channel_id=1, source_target_pairs={{0,66},{1,19},{2,68},{3,21},{4,70},{5,23},{6,64},{7,17},{8,74},{9,... | collective-permute-start | bytes 98312 | tf_op jit(solution)/shard_map/ppermute | solution.py:46
  7.6 5.4 %collective-permute-start = (bf16[128,128]{1,0:T(8,128)(2,1)}, bf16[128,128]{1,0:T(8,128)(2,1)S(1)}, u32[]{:S(2)}, u32[]{:S(2)}) collective-permute-start(bf16[128,128]{1,0:T(8,128)(2,1)} %bitcast.20), channel_id=1, source_target_pairs={{0,70},{1,23},{2,64},{3,17},{4,66},{5,19},{6,68},{7,21},{8,78},{9,... | collective-permute-start | bytes 98312 | tf_op jit(solution)/shard_map/ppermute | solution.py:46
  10.3 0.7 %copy-start.3 = (s32[1,4096,1]{1,2,0:T(1,128)S(1)}, s32[1,4096,1]{1,2,0:T(1,128)}, u32[]{:S(2)}) copy-start(s32[1,4096,1]{1,2,0:T(1,128)} %param.7) | copy-start | bytes 49156
  13.1 10.2 %collective-permute-start.5 = (bf16[528,128]{1,0:T(8,128)(2,1)S(1)}, bf16[528,128]{1,0:T(8,128)(2,1)S(1)}, u32[]{:S(2)}, u32[]{:S(2)}) collective-permute-start(bf16[528,128]{1,0:T(8,128)(2,1)S(1)} %constant_dynamic-update-slice_fusion), channel_id=1, source_target_pairs={{0,16},{1,65},{2,18},{3,67},{4,20},{5,69},{6,22},{7,71},{8,24},{9,... | collective-permute-start | bytes 405512 | tf_op jit(solution)/shard_map/ppermute | solution.py:46
  16.1 7.2 %collective-permute-start.4 = (bf16[528,128]{1,0:T(8,128)(2,1)S(1)}, bf16[528,128]{1,0:T(8,128)(2,1)S(1)}, u32[]{:S(2)}, u32[]{:S(2)}) collective-permute-start(bf16[528,128]{1,0:T(8,128)(2,1)S(1)} %constant_dynamic-update-slice_fusion), channel_id=1, source_target_pairs={{0,8},{1,33},{2,10},{3,35},{4,12},{5,37},{6,14},{7,39},{8,16},{9,4... | collective-permute-start | bytes 405512 | tf_op jit(solution)/shard_map/ppermute | solution.py:46
  16.7 6.5 %collective-permute-start.3 = (bf16[528,128]{1,0:T(8,128)(2,1)S(1)}, bf16[528,128]{1,0:T(8,128)(2,1)S(1)}, u32[]{:S(2)}, u32[]{:S(2)}) collective-permute-start(bf16[528,128]{1,0:T(8,128)(2,1)S(1)} %constant_dynamic-update-slice_fusion), channel_id=1, source_target_pairs={{0,24},{1,97},{2,26},{3,99},{4,28},{5,101},{6,30},{7,103},{8,0},{9... | collective-permute-start | bytes 405512 | tf_op jit(solution)/shard_map/ppermute | solution.py:46
  23.2 8.7 %copy-start.1 = (bf16[128,128]{1,0:T(8,128)(2,1)S(1)}, bf16[128,128]{1,0:T(8,128)(2,1)}, u32[]{:S(2)}) copy-start(bf16[128,128]{1,0:T(8,128)(2,1)} %plane_ref.3) | copy-start | bytes 98308
  23.2 8.7 %copy-start.2 = (f32[1,4096]{1,0:T(1,128)S(1)}, f32[1,4096]{1,0:T(1,128)}, u32[]{:S(2)}) copy-start(f32[1,4096]{1,0:T(1,128)} %param.6) | copy-start | bytes 49156
  23.3 9.7 %collective-permute-start.8 = (bf16[2112,128]{1,0:T(8,128)(2,1)S(1)}, bf16[2112,128]{1,0:T(8,128)(2,1)S(1)}, u32[]{:S(2)}, u32[]{:S(2)}) collective-permute-start(bf16[2112,128]{1,0:T(8,128)(2,1)S(1)} %pad_maximum_fusion.refs_0_.operator_ref.own_ref), channel_id=1, source_target_pairs={{0,2},{1,7},{2,4},{3,1},{4,6},{5,3},{6,0},{7,5},{8,10},{9,15},{10,... | collective-permute-start | bytes 1622024 | tf_op jit(solution)/shard_map/ppermute | solution.py:46
  26.6 8.5 %collective-permute-start.7 = (bf16[2112,128]{1,0:T(8,128)(2,1)S(1)}, bf16[2112,128]{1,0:T(8,128)(2,1)S(1)}, u32[]{:S(2)}, u32[]{:S(2)}) collective-permute-start(bf16[2112,128]{1,0:T(8,128)(2,1)S(1)} %pad_maximum_fusion.refs_0_.operator_ref.own_ref), channel_id=1, source_target_pairs={{0,96},{1,25},{2,98},{3,27},{4,100},{5,29},{6,102},{7,31},{8,104},... | collective-permute-start | bytes 1622024 | tf_op jit(solution)/shard_map/ppermute | solution.py:46
  27.4 9.7 %collective-permute-start.6 = (bf16[2112,128]{1,0:T(8,128)(2,1)S(1)}, bf16[2112,128]{1,0:T(8,128)(2,1)S(1)}, u32[]{:S(2)}, u32[]{:S(2)}) collective-permute-start(bf16[2112,128]{1,0:T(8,128)(2,1)S(1)} %pad_maximum_fusion.refs_0_.operator_ref.own_ref), channel_id=1, source_target_pairs={{0,32},{1,9},{2,34},{3,11},{4,36},{5,13},{6,38},{7,15},{8,40},{9,1... | collective-permute-start | bytes 1622024 | tf_op jit(solution)/shard_map/ppermute | solution.py:46
  28.0 1.8 %collective-permute-start.9 = (bf16[768,128]{1,0:T(8,128)(2,1)S(1)}, bf16[768,128]{1,0:T(8,128)(2,1)S(1)}, u32[]{:S(2)}, u32[]{:S(2)}) collective-permute-start(bf16[768,128]{1,0:T(8,128)(2,1)S(1)} %get-tuple-element.44), channel_id=1, source_target_pairs={{0,1},{1,0},{2,3},{3,2},{4,5},{5,4},{6,7},{7,6},{8,9},{9,8},{10,11... | collective-permute-start | bytes 589832 | tf_op jit(solution)/shard_map/ppermute | solution.py:55
  28.7 1.4 %collective-permute-start.12 = (bf16[768,128]{1,0:T(8,128)(2,1)S(1)}, bf16[768,128]{1,0:T(8,128)(2,1)S(1)}, u32[]{:S(2)}, u32[]{:S(2)}) collective-permute-start(bf16[768,128]{1,0:T(8,128)(2,1)S(1)} %get-tuple-element.47), channel_id=1, source_target_pairs={{0,1},{1,0},{2,3},{3,2},{4,5},{5,4},{6,7},{7,6},{8,9},{9,8},{10,11... | collective-permute-start | bytes 589832 | tf_op jit(solution)/shard_map/ppermute | solution.py:55
  29.8 1.4 %collective-permute-start.13 = (bf16[768,128]{1,0:T(8,128)(2,1)S(1)}, bf16[768,128]{1,0:T(8,128)(2,1)S(1)}, u32[]{:S(2)}, u32[]{:S(2)}) collective-permute-start(bf16[768,128]{1,0:T(8,128)(2,1)S(1)} %get-tuple-element.48), channel_id=1, source_target_pairs={{0,1},{1,0},{2,3},{3,2},{4,5},{5,4},{6,7},{7,6},{8,9},{9,8},{10,11... | collective-permute-start | bytes 589832 | tf_op jit(solution)/shard_map/ppermute | solution.py:55
  30.2 1.4 %collective-permute-start.14 = (bf16[768,128]{1,0:T(8,128)(2,1)S(1)}, bf16[768,128]{1,0:T(8,128)(2,1)S(1)}, u32[]{:S(2)}, u32[]{:S(2)}) collective-permute-start(bf16[768,128]{1,0:T(8,128)(2,1)S(1)} %get-tuple-element.49), channel_id=1, source_target_pairs={{0,1},{1,0},{2,3},{3,2},{4,5},{5,4},{6,7},{7,6},{8,9},{9,8},{10,11... | collective-permute-start | bytes 589832 | tf_op jit(solution)/shard_map/ppermute | solution.py:55
  31.3 1.7 %collective-permute-start.10 = (bf16[384,128]{1,0:T(8,128)(2,1)S(1)}, bf16[384,128]{1,0:T(8,128)(2,1)S(1)}, u32[]{:S(2)}, u32[]{:S(2)}) collective-permute-start(bf16[384,128]{1,0:T(8,128)(2,1)S(1)} %get-tuple-element.45), channel_id=1, source_target_pairs={{0,1},{1,0},{2,3},{3,2},{4,5},{5,4},{6,7},{7,6},{8,9},{9,8},{10,11... | collective-permute-start | bytes 294920 | tf_op jit(solution)/shard_map/ppermute | solution.py:55
  31.6 1.4 %collective-permute-start.11 = (bf16[384,128]{1,0:T(8,128)(2,1)S(1)}, bf16[384,128]{1,0:T(8,128)(2,1)S(1)}, u32[]{:S(2)}, u32[]{:S(2)}) collective-permute-start(bf16[384,128]{1,0:T(8,128)(2,1)S(1)} %get-tuple-element.46), channel_id=1, source_target_pairs={{0,1},{1,0},{2,3},{3,2},{4,5},{5,4},{6,7},{7,6},{8,9},{9,8},{10,11... | collective-permute-start | bytes 294920 | tf_op jit(solution)/shard_map/ppermute | solution.py:55
  37.8 2.9 %collective-permute-start.15 = (bf16[2304,128]{1,0:T(8,128)(2,1)S(1)}, bf16[2304,128]{1,0:T(8,128)(2,1)S(1)}, u32[]{:S(2)}, u32[]{:S(2)}) collective-permute-start(bf16[2304,128]{1,0:T(8,128)(2,1)S(1)} %shard_map.61), channel_id=1, source_target_pairs={{0,1},{1,0},{2,3},{3,2},{4,5},{5,4},{6,7},{7,6},{8,9},{9,8},{10,11... | collective-permute-start | bytes 1769480 | tf_op jit(solution)/shard_map/ppermute | solution.py:55
